TPU v7x, 128 devices: a whole 4x4x4 slice. The times are simulated.
128 devices in a mesh: feat: 4 (over y), vert: 32 (over x, z, core).
Axes of the slice: x: 4, y: 4, z: 4, core: 2. Of those that a mesh axis runs over, the one named last changes fastest.
Arguments:
- features: bfloat16 [12288, 768], P('vert', 'feat'), may hold values from -18 to 18
- counts: int32 [12288, 12288], P('vert'), may hold values from 0 to 3, as said below
- tile_mask: int32 [96, 96], P('vert'), may hold values 0 or 1
- w_in: bfloat16 [768, 1024], P('feat'), may hold values from -0.21875 to 0.21875
- b_in: float32 [1024], P('feat'), may hold values from -3 to 3
- w_out: bfloat16 [1024, 153], P('feat'), may hold values from -0.5625 to 0.5625
- b_out: float32 [153], replicated, may hold values from -6 to 6
Outputs:
- logits: float32 [12288, 153], P('vert')
Inputs may be any that keep to these rules, and one draw needn't show every extreme that they name: Entry (i, j) counts edges from vertex j to vertex i; only entries inside tiles whose tile_mask entry is 1 are edges. `tile_mask`: 1 marks a stored tile of 128 x 128 entries of counts.
All inputs are finite; a program needn't handle non-finite values. No bound on the sum of `tile_mask` on one device may be relied on, other than what follows from the above.
Results may differ from a plain program's by a relative error of at most 0.007.
Values may be sent and summed in bfloat16 or wider, within the bound.
No kernel may reach another device: no remote copies, remote signals or barrier semaphores. Data moves between devices by JAX's collectives and lax.ppermute only.
A program may use at most 128 MiB of HBM per device.

v0:
```python
import jax
import jax.numpy as jnp
from jax import lax
from jax.sharding import PartitionSpec as P

TILE = 128


def local(features, counts, tile_mask, w_in, b_in, w_out, b_out):
    rows = features.shape[0]
    me_vert = lax.axis_index("vert")
    spread = jnp.repeat(jnp.repeat(tile_mask, TILE, axis=0), TILE, axis=1)
    shape = counts.shape
    columns = lax.broadcasted_iota(jnp.int32, shape, 1)
    diagonal = lax.broadcasted_iota(jnp.int32, shape, 0) + me_vert * rows
    adj_int = counts * spread + (columns == diagonal).astype(jnp.int32)
    degree = jnp.sum(adj_int, axis=1).astype(jnp.float32)[:, None]
    adj = adj_int.astype(jnp.bfloat16)
    partial_value = jnp.dot(features, w_in, preferred_element_type=jnp.float32)
    projected = lax.psum_scatter(partial_value, "feat", scatter_dimension=1, tiled=True)
    piece = lax.all_gather(projected, "vert", axis=0, tiled=True)
    block = adj
    upper = piece.astype(jnp.bfloat16)
    lower = (piece - upper.astype(jnp.float32)).astype(jnp.bfloat16)
    total = jnp.dot(block, upper, preferred_element_type=jnp.float32)
    summed = total + jnp.dot(block, lower, preferred_element_type=jnp.float32)
    pre = summed / degree + b_in
    hidden = jnp.maximum(pre, 0.0).astype(jnp.bfloat16)
    block = adj
    summed_two = jnp.dot(
        block,
        lax.all_gather(hidden, "vert", axis=0, tiled=True),
        preferred_element_type=jnp.float32,
    )
    mean_two = summed_two / degree
    partial_scores = jnp.dot(mean_two, w_out.astype(jnp.float32), precision=lax.Precision.HIGHEST)
    return lax.psum(partial_scores, "feat") + b_out


def solution(mesh):
    placed = (
        P("vert", "feat"),
        P("vert", None),
        P("vert", None),
        P("feat", None),
        P("feat"),
        P("feat", None),
        P(),
    )
    return jax.shard_map(
        local, mesh=mesh, in_specs=placed, out_specs=P("vert", None), check_vma=False
    )
```

profile of v0, /device:TPU:1, one launch (start us, length us, event | category | flops | bytes accessed | tf_op | source)
XLA Modules:
  0.0 228.4 jit_solution(802584782397351652)
XLA Ops:
  6.5 0.0 copy-start
  6.5 0.0 reduce-scatter.2.cloned.1.call-start
  6.5 1.0 copy-done
  7.5 2.5 %fusion.22 = f32[384,1024]{1,0:T(8,128)} fusion(bf16[384,192]{0,1:T(8,128)(2,1)} %param.7, bf16[192,1024]{1,0:T(8,128)(2,1)S(1)} %copy-done), kind=kOutput, calls=%fused_computation.18 | convolution fusion | flops 150994944 | bytes 2113536 | tf_op jit(solution)/shard_map/dot_general | solution.py:19
  10.0 0.0 reduce-scatter.2.cloned.1.call-update
  10.0 0.0 all-gather.3.cloned.1.call-start
  10.1 28.0 %reduce-scatter.2.cloned.1.call-done = f32[384,256]{1,0:T(8,128)} async-done(((f32[384,1024]{1,0:T(8,128)}), f32[384,256]{1,0:T(8,128)}) %reduce-scatter.2.cloned.1.call-update) | async-done | bytes 393232 | tf_op jit(solution)/shard_map/reduce_scatter | solution.py:20
  38.1 0.0 all-gather.3.cloned.1.call-update
  38.1 0.0 all-gather.5.cloned.1.call-start
  38.2 0.7 broadcast_in_dim.4
  38.9 0.0 copy-start.3
  38.9 5.3 %broadcast_in_dim.10 = s32[384,96,128]{2,1,0:T(8,128)S(1)} broadcast(s32[384,96]{1,0:T(8,128)S(1)} %bitcast.19), dimensions={0,1} | broadcast | bytes 19021824 | tf_op jit(solution)/shard_map/broadcast_in_dim | solution.py:12
  44.2 1.1 copy-done.3
  45.3 23.9 %fusion.20 = (s32[384]{0:T(512)S(1)}, bf16[384,12288]{1,0:T(8,128)(2,1)}) fusion(s32[384]{0:T(512)S(1)} %iota_add_fusion, s32[384,12288]{1,0:T(8,128)S(1)} %copy-done.3, s32[48,8,96,128]{3,2,1,0:T(8,128)S(1)} %bitcast.18), kind=kLoop, calls=%fused_computation.14 | loop fusion | flops 28311168 | bytes 47188992 | tf_op jit(solution)/shard_map/reduce_sum | solution.py:17
  69.2 35.3 %all-gather.3.cloned.1.call-done = f32[12288,256]{1,0:T(8,128)} async-done(((f32[384,256]{1,0:T(8,128)}), f32[12288,256]{1,0:T(8,128)}) %all-gather.3.cloned.1.call-update) | async-done | bytes 12582928 | tf_op jit(solution)/shard_map/all_gather | solution.py:21
  104.5 0.0 copy-start.2
  104.5 0.0 copy-start.4
  104.5 0.0 copy-start.6
  104.5 14.1 %fusion.1 = f32[384,256]{1,0:T(8,128)S(1)} fusion(bf16[384,12288]{1,0:T(8,128)(2,1)} %get-tuple-element.6, f32[12288,256]{1,0:T(8,128)} %all-gather.3.cloned.1.call-done), kind=kOutput, calls=%fused_computation.4 | convolution fusion | flops 2428502016 | bytes 22413312 | tf_op jit(solution)/shard_map/dot_general | solution.py:26
  118.6 0.0 copy-done.2
  118.6 3.1 %copy-done.4 = f32[12288,256]{1,0:T(8,128)S(1)} copy-done((f32[12288,256]{1,0:T(8,128)S(1)}, f32[12288,256]{1,0:T(8,128)}, u32[]{:S(2)}) %copy-start.4) | copy-done | bytes 12582936
  121.7 0.0 copy-done.6
  121.7 3.3 %fusion.17 = bf16[384,256]{1,0:T(8,128)(2,1)} fusion(f32[384,256]{1,0:T(8,128)S(1)} %fusion.1, bf16[384,12288]{1,0:T(8,128)(2,1)S(1)} %copy-done.2, f32[12288,256]{1,0:T(8,128)S(1)} %copy-done.4, f32[256]{0:T(256)S(1)} %copy-done.6, f32[384]{0:T(512)S(1)} %convert_element_type.31), kind=kOutput, calls=%fused_computation.12 | convolution fusion | flops 2419556352 | bytes 22612480 | tf_op jit(solution)/shard_map/dot_general | solution.py:25
  124.9 0.0 all-gather.5.cloned.1.call-update
  125.0 0.0 copy-start.5
  125.0 0.0 copy-start.7
  125.0 0.0 copy-start.1
  125.0 0.0 all-reduce.2.cloned.1.call-start
  125.0 48.8 %all-gather.5.cloned.1.call-done = bf16[12288,256]{1,0:T(8,128)(2,1)} async-done(((bf16[384,256]{1,0:T(8,128)(2,1)}), bf16[12288,256]{1,0:T(8,128)(2,1)}) %all-gather.5.cloned.1.call-update) | async-done | bytes 6291472 | tf_op jit(solution)/shard_map/all_gather | solution.py:32
  173.8 7.0 %convolution_divide_fusion = f32[384,256]{1,0:T(8,128)S(1)} fusion(bf16[384,12288]{1,0:T(8,128)(2,1)} %get-tuple-element.6, bf16[12288,256]{1,0:T(8,128)(2,1)} %all-gather.5.cloned.1.call-done, f32[384]{0:T(512)S(1)} %convert_element_type.31), kind=kOutput, calls=%fused_computation.13 | convolution fusion | flops 2416017408 | bytes 16123392 | tf_op jit(solution)/shard_map/dot_general | solution.py:30
  180.9 0.0 copy-done.5
  180.9 1.1 fusion.23
  181.9 0.0 all-reduce.2.cloned.1.call-update
  182.0 38.2 %all-reduce.2.cloned.1.call-done = f32[384,153]{0,1:T(8,128)} async-done(((f32[384,153]{0,1:T(8,128)}), f32[384,153]{0,1:T(8,128)}) %all-reduce.2.cloned.1.call-update) | async-done | bytes 235024 | tf_op jit(solution)/shard_map/psum | solution.py:37
  220.1 0.0 copy-done.7
  220.1 1.7 broadcast_add_fusion
  221.8 0.0 copy-done.1
  (2 shorter events, 0.0 us)
Async XLA Ops:
  6.5 1.0 copy-start
  6.5 31.6 %reduce-scatter.2.cloned.1.call-start = ((), (), s32[]{:S(2)}) async-start(), calls=%async_computation.1 | async-start | bytes 1966080 | tf_op jit(solution)/shard_map/reduce_scatter | solution.py:20
  10.0 94.4 %all-gather.3.cloned.1.call-start = ((), (), s32[]{:S(2)}) async-start(), calls=%async_computation.2 | async-start | bytes 12976128 | tf_op jit(solution)/shard_map/all_gather | solution.py:21
  38.1 135.7 %all-gather.5.cloned.1.call-start = ((), (), s32[]{:S(2)}) async-start(), calls=%async_computation.3 | async-start | bytes 6488064 | tf_op jit(solution)/shard_map/all_gather | solution.py:32
  38.9 6.4 %copy-start.3 = (s32[384,12288]{1,0:T(8,128)S(1)}, s32[384,12288]{1,0:T(8,128)}, u32[]{:S(2)}) copy-start(s32[384,12288]{1,0:T(8,128)} %param.8) | copy-start | bytes 56623108
  104.5 14.1 %copy-start.2 = (bf16[384,12288]{1,0:T(8,128)(2,1)S(1)}, bf16[384,12288]{1,0:T(8,128)(2,1)}, u32[]{:S(2)}) copy-start(bf16[384,12288]{1,0:T(8,128)(2,1)} %get-tuple-element.6) | copy-start | bytes 28311556
  104.5 17.2 %copy-start.4 = (f32[12288,256]{1,0:T(8,128)S(1)}, f32[12288,256]{1,0:T(8,128)}, u32[]{:S(2)}) copy-start(f32[12288,256]{1,0:T(8,128)} %all-gather.3.cloned.1.call-done) | copy-start | bytes 37748740
  104.5 17.2 %copy-start.6 = (f32[256]{0:T(256)S(1)}, f32[256]{0:T(256)}, u32[]{:S(2)}) copy-start(f32[256]{0:T(256)} %param.11) | copy-start | bytes 3076
  125.0 55.9 %copy-start.5 = (bf16[256,153]{0,1:T(8,128)(2,1)S(1)}, bf16[256,153]{0,1:T(8,128)(2,1)}, u32[]{:S(2)}) copy-start(bf16[256,153]{0,1:T(8,128)(2,1)} %param.12) | copy-start | bytes 235012
  125.0 95.1 %copy-start.7 = (f32[153]{0:T(256)S(1)}, f32[153]{0:T(256)}, u32[]{:S(2)}) copy-start(f32[153]{0:T(256)} %param.13) | copy-start | bytes 1840
  125.0 96.9 %copy-start.1 = (bf16[192,1024]{1,0:T(8,128)(2,1)S(1)}, bf16[192,1024]{1,0:T(8,128)(2,1)}, u32[]{:S(2)}) copy-start(bf16[192,1024]{1,0:T(8,128)(2,1)} %param.10) | copy-start | bytes 1179652
  125.0 95.1 %all-reduce.2.cloned.1.call-start = ((), (), s32[]{:S(2)}) async-start(), calls=%async_computation.4 | async-start | bytes 491520 | tf_op jit(solution)/shard_map/psum | solution.py:37
Sparse Core Ops, SparseCore 0:
  10.1 27.9 reduce-scatter.1
  40.4 64.0 all-gather.2
  125.1 48.6 all-gather.4
  182.1 37.9 all-reduce.1
where the time goes:
time: 230 us; the launch traced here: 228 us
  waiting for transfers between devices  150 us (65%)
  matrix products  27.9 us (12%)
  other arithmetic  25.7 us (11%)
  between operations  13.2 us (6%)
  local copies, waits for them, and re-layouts  11.1 us (5%)
    all_gather x1, waiting for transfers between devices, local(): lax.all_gather(hidden, 'vert', axis=0, tiled=True)  48.8 us
    psum x1, waiting for transfers between devices, local(): return lax.psum(partial_scores, 'feat') + b_out  38.2 us
    all_gather x1, waiting for transfers between devices, local(): piece = lax.all_gather(projected, 'vert', axis=0, tiled=True)  35.3 us
    reduce_scatter x1, waiting for transfers between devices, local(): lax.psum_scatter(partial_value, 'feat', scatter_dimension=1, tiled=True)  28 us
    reduce_sum x1, other arithmetic, local(): degree = jnp.sum(adj_int, axis=1).astype(jnp.float32)[:, None]  23.9 us
    dot_general x1, matrix products, local(): summed = total + jnp.dot(block, lower, preferred_element_type=jnp.float32)  14.1 us
    dot_general x1, matrix products, local(): jnp.dot(block, lax.all_gather(hidden, 'vert', axis=0, tiled=True), prefer...  7.04 us
    broadcast_in_dim x2, local copies, waits for them, and re-layouts, local(): spread = jnp.repeat(jnp.repeat(tile_mask, TILE, axis=0), TILE, axis=1)  5.98 us
  transfers between devices with their start and end apart: 4, of which 4 were waited for; matrix products, arithmetic and copies ran while one was open for 13% of the time, Pallas kernels for 0%

commit v1 on v0

v1 whole, which is shorter than its diff:
```python
import jax
import jax.numpy as jnp
from jax import lax
from jax.experimental import pallas as pl
from jax.experimental.pallas import tpu as pltpu
from jax.sharding import PartitionSpec as P

TILE = 128
ROWS = 384
NV = 32
NF = 4
SHARE = ROWS // NF
CLS = 153
bf16 = jnp.bfloat16
f32 = jnp.float32
NT = (((1,), (1,)), ((), ()))
VM = pl.BlockSpec(memory_space=pltpu.VMEM)
SM = pl.BlockSpec(memory_space=pltpu.SMEM)


def params(mib=16):
    return pltpu.CompilerParams(vmem_limit_bytes=mib * 2**20)


def cost(flops, nbytes):
    return pl.CostEstimate(flops=int(flops), bytes_accessed=int(nbytes), transcendentals=0)


def positions(move):
    pairs = []
    for x in range(4):
        for z in range(4):
            for c in range(2):
                xx, zz, cc = move(x, z, c)
                pairs.append(((x * 4 + z) * 2 + c, (xx % 4 * 4 + zz % 4) * 2 + cc % 2))
    return pairs


def first_axis(value, shift):
    return lax.ppermute(value, "vert", positions(lambda x, z, c: (x + shift * (1 - c), z + shift * c, c)))


def second_axis(value, shift):
    return lax.ppermute(value, "vert", positions(lambda x, z, c: (x + shift * c, z + shift * (1 - c), c)))


def swap(value):
    return lax.ppermute(value, "vert", positions(lambda x, z, c: (x, z, 1 - c)))


def along_feat(value, shift):
    return lax.ppermute(value, "feat", [(i, (i + shift) % NF) for i in range(NF)])


CHUNK = 2 * ROWS


def adjacency_kernel(mask, where, counts, adj, adj2, degree):
    step = pl.program_id(0)
    me, feat = where[0], where[1]
    row = lax.broadcasted_iota(jnp.int32, (TILE, TILE), 0)
    col = lax.broadcasted_iota(jnp.int32, (TILE, TILE), 1)
    eye = (row == col).astype(f32)

    @pl.when(step == 0)
    def _():
        degree[...] = jnp.zeros_like(degree)

    for i in range(ROWS // TILE):
        total = degree[i * TILE : (i + 1) * TILE, :]
        for j in range(CHUNK // TILE):
            tile_col = step * (CHUNK // TILE) + j
            stored = mask[i, tile_col].astype(f32)
            own = (me * (ROWS // TILE) + i == tile_col).astype(f32)
            tile = counts[i * TILE : (i + 1) * TILE, j * TILE : (j + 1) * TILE].astype(f32)
            tile = tile * stored + eye * own
            total = total + tile
            adj[i * TILE : (i + 1) * TILE, j * TILE : (j + 1) * TILE] = tile.astype(bf16)
        degree[i * TILE : (i + 1) * TILE, :] = total

    source = lax.broadcasted_iota(jnp.int32, (ROWS, TILE), 0)
    target = lax.broadcasted_iota(jnp.int32, (ROWS, TILE), 1)
    pick = ((source == target + feat * SHARE) & (target < SHARE)).astype(f32).astype(bf16)
    for j in range(CHUNK // ROWS):
        part = jnp.dot(adj[:, j * ROWS : (j + 1) * ROWS], pick, preferred_element_type=f32)
        adj2[:, j * TILE : (j + 1) * TILE] = part.astype(bf16)

    @pl.when(step == pl.num_programs(0) - 1)
    def _():
        degree[...] = jnp.broadcast_to(jnp.sum(degree[...], axis=1, keepdims=True), degree.shape)


def make_adjacency(tile_mask, where, counts):
    n = NV * ROWS // CHUNK
    return pl.pallas_call(
        adjacency_kernel,
        grid_spec=pltpu.PrefetchScalarGridSpec(
            num_scalar_prefetch=2,
            grid=(n,),
            in_specs=[pl.BlockSpec((ROWS, CHUNK), lambda i, *_: (0, i))],
            out_specs=[
                pl.BlockSpec((ROWS, CHUNK), lambda i, *_: (0, i)),
                pl.BlockSpec((ROWS, CHUNK // ROWS * TILE), lambda i, *_: (0, i)),
                pl.BlockSpec((ROWS, TILE), lambda i, *_: (0, 0)),
            ],
        ),
        out_shape=[
            jax.ShapeDtypeStruct((ROWS, NV * ROWS), bf16),
            jax.ShapeDtypeStruct((ROWS, NV * TILE), bf16),
            jax.ShapeDtypeStruct((ROWS, TILE), f32),
        ],
        compiler_params=params(),
        cost_estimate=cost(2.4e9, 31e6),
        name="adjacency",
    )(tile_mask, where, counts)


def add_blocks(order, adj, total, pieces):
    k = 0
    for piece in pieces:
        for b in range(piece.shape[0]):
            src = pl.multiple_of(order[k] * ROWS, ROWS)
            total = total + lax.dot_general(adj[:, pl.ds(src, ROWS)], piece[b], NT, preferred_element_type=f32)
            k += 1
    return total


def product_first(order, adj, *refs):
    refs[-1][...] = add_blocks(order, adj, jnp.zeros(refs[-1].shape, f32), refs[:-1])


def product_next(order, adj, before, *refs):
    refs[-1][...] = add_blocks(order, adj, before[...], refs[:-1])


def product_last(order, where, adj, before, degree, *refs):
    pieces, outs, mean = refs[:-5], refs[-5:-1], refs[-1]
    total = add_blocks(order, adj, before[...], pieces)
    mean[...] = total / degree[:, :1]
    for s in range(NF):
        q = (where[1] + s) % NF
        outs[s][...] = mean[pl.ds(pl.multiple_of(q * SHARE, SHARE), SHARE), :].astype(bf16)


def blocks_cost(pieces):
    n = sum(p.shape[0] for p in pieces)
    return cost(2 * 384 * 384 * 256 * n, n * 450e3)


def hidden_kernel(where, g0, g1, g2, g3, own, near, far, z_out, hid):
    feat, core = where[1], where[2]
    gs = (g0, g1, g2, g3)
    total = jnp.zeros((SHARE, 256), f32)
    for h in range(2):
        half = (core + h) % 2
        def part(s, rows, h=h, half=half):
            if s == 0:
                return own[half, rows, :]
            return (near, far)[h][s - 1, rows, :]
        pre = jnp.zeros((SHARE, 512), f32)
        for s in range(NF):
            pre = pre + jnp.dot(gs[s][...], part(s, slice(0, 192)), preferred_element_type=f32)
        hid[...] = pre
        for s in range(NF):
            owner = (feat + NF - s) % NF
            lanes = pl.ds(pl.multiple_of(owner * TILE, TILE), TILE)
            b = part(s, slice(256, 272))[:, :TILE].astype(f32)
            bias = b[0:1] + b[1:2] + b[2:3]
            unit = jnp.maximum(hid[:, lanes] + bias, 0.0).astype(bf16)
            w = part(s, slice(192, 256))
            total = total + jnp.dot(unit[:, :64], w[:, :256], preferred_element_type=f32)
            total = total + jnp.dot(unit[:, 64:], w[:, 256:], preferred_element_type=f32)
    z_out[0:SHARE, :] = total[:, :TILE].astype(bf16)
    tail = total[:, TILE : TILE + 32]
    packed = jnp.concatenate([tail[0:32], tail[32:64], tail[64:96], jnp.zeros((32, 32), f32)], axis=1)
    z_out[SHARE:, :] = packed.astype(bf16)


def scores_kernel(order, adj2, degree, z_near, z_far, out, z_all):
    k = 0
    for piece in (z_near, z_far):
        for b in range(piece.shape[0]):
            src = pl.multiple_of(order[k] * TILE, TILE)
            z_all[pl.ds(src, TILE), :TILE] = piece[b]
            tail = piece[b, SHARE:, :].astype(f32)
            tail = jnp.concatenate([tail[:, 0:32], tail[:, 32:64], tail[:, 64:96], jnp.zeros((32, 32), f32)], axis=0)
            tail = jnp.concatenate([tail, jnp.zeros((TILE, 96), f32)], axis=1)
            z_all[pl.ds(src, TILE), TILE:] = tail.astype(bf16)
            k += 1
    part = jnp.dot(adj2[...], z_all[...], preferred_element_type=f32) / degree[:, :1]
    out[0:ROWS, :] = part[:, :TILE].astype(bf16)
    tail = part[:, TILE : TILE + 32]
    packed = jnp.concatenate([tail[i * SHARE : (i + 1) * SHARE] for i in range(NF)], axis=1)
    out[ROWS:, :] = packed.astype(bf16)


def sum_kernel(p0, p1, p2, p3, b_out, out):
    total = (p0[...].astype(f32) + p2[...].astype(f32)) + (p1[...].astype(f32) + p3[...].astype(f32))
    out[:, :TILE] = total[:ROWS] + b_out[:, :TILE]
    for i in range(NF):
        out[i * SHARE : (i + 1) * SHARE, TILE:] = (
            total[ROWS:, i * 32 : i * 32 + CLS - TILE] + b_out[:, TILE:]
        )


def local(features, counts, tile_mask, w_in, b_in, w_out, b_out):
    me = lax.axis_index("vert").astype(jnp.int32)
    feat = lax.axis_index("feat").astype(jnp.int32)
    core, spot = me % 2, me // 2
    x, z = spot // 4, spot % 4
    where = jnp.stack([me, feat, core])

    def source(s, t, c):
        first, second = jnp.where(c == 0, x, z), jnp.where(c == 0, z, x)
        first, second = (first + NF - s) % NF, (second + NF - t) % NF
        xx, zz = jnp.where(c == 0, first, second), jnp.where(c == 0, second, first)
        return (xx * 4 + zz) * 2 + c

    order = jnp.stack([source(s, t, c) for t in (0, 1, 3, 2) for c in (core, 1 - core) for s in (0, 1, 3, 2)])

    mine = features.T
    ring = [first_axis(mine, s) for s in (1, 3, 2)]
    four = jnp.stack([mine] + ring)
    rows = {t: second_axis(four, t) for t in (1, 3, 2)}

    tail = jnp.pad(w_out, ((0, 0), (0, 256 - CLS))).reshape(2, 2, 64, 256).transpose(0, 2, 1, 3).reshape(2, 64, 512)
    hi = lax.reduce_precision(b_in, 8, 7)
    mid = lax.reduce_precision(b_in - hi, 8, 7)
    low = b_in - hi - mid
    bias = jnp.stack([hi, mid, low]).astype(bf16).reshape(3, 2, TILE).transpose(1, 0, 2)
    bias = jnp.pad(bias, ((0, 0), (0, 13), (0, 512 - TILE)))
    halves = w_in.reshape(192, 4, 2, TILE).transpose(2, 0, 1, 3).reshape(2, 192, 512)
    own = jnp.concatenate([halves, tail, bias], axis=1)
    half = lax.dynamic_index_in_dim(own, core, 0, keepdims=False)
    near = jnp.stack([along_feat(half, s) for s in (1, 2, 3)])
    far = swap(near)

    adj, adj2, degree = make_adjacency(tile_mask, where, counts)

    total_shape = jax.ShapeDtypeStruct((ROWS, 192), f32)
    pieces = [four, swap(four)]
    total = pl.pallas_call(
        product_first, out_shape=total_shape, in_specs=[SM] + [VM] * 3, out_specs=VM,
        compiler_params=params(), cost_estimate=blocks_cost(pieces), name="product_first",
    )(order[0:8], adj, *pieces)
    pieces = [rows[1], swap(rows[1]), rows[3], swap(rows[3])]
    total = pl.pallas_call(
        product_next, out_shape=total_shape, in_specs=[SM] + [VM] * 6, out_specs=VM,
        compiler_params=params(), cost_estimate=blocks_cost(pieces), name="product_next",
    )(order[8:24], adj, total, *pieces)
    pieces = [rows[2], swap(rows[2])]
    means = pl.pallas_call(
        product_last, out_shape=[jax.ShapeDtypeStruct((SHARE, 192), bf16)] * NF,
        in_specs=[SM] * 2 + [VM] * 5, out_specs=[VM] * NF,
        scratch_shapes=[pltpu.VMEM((ROWS, 192), f32)],
        compiler_params=params(), cost_estimate=blocks_cost(pieces), name="product_last",
    )(order[24:32], where, adj, total, degree, *pieces)

    g = [means[0]] + [along_feat(means[s], s) for s in (1, 2, 3)]
    z_block = pl.pallas_call(
        hidden_kernel, out_shape=jax.ShapeDtypeStruct((TILE, TILE), bf16),
        in_specs=[SM] + [VM] * 7, out_specs=VM,
        scratch_shapes=[pltpu.VMEM((SHARE, 512), f32)],
        compiler_params=params(), cost_estimate=cost(2 * 96 * 768 * 1024, 2e6), name="hidden",
    )(where, *g, own, near, far)

    z_four = jnp.stack([z_block] + [first_axis(z_block, s) for s in (1, 3, 2)])
    z_near = jnp.concatenate([z_four] + [second_axis(z_four, t) for t in (1, 3, 2)])
    z_far = swap(z_near)
    order2 = jnp.stack([source(s, t, c) for c in (core, 1 - core) for t in (0, 1, 3, 2) for s in (0, 1, 3, 2)])
    part = pl.pallas_call(
        scores_kernel, out_shape=jax.ShapeDtypeStruct((ROWS + SHARE, TILE), bf16),
        in_specs=[SM] + [VM] * 4, out_specs=VM,
        scratch_shapes=[pltpu.VMEM((NV * TILE, 256), bf16)],
        compiler_params=params(), cost_estimate=cost(2 * 384 * 4096 * 256, 5e6), name="scores",
    )(order2, adj2, degree, z_near, z_far)
    parts = [part] + [along_feat(part, s) for s in (1, 2, 3)]
    return pl.pallas_call(
        sum_kernel, out_shape=jax.ShapeDtypeStruct((ROWS, CLS), f32),
        in_specs=[VM] * 5, out_specs=VM,
        compiler_params=params(), cost_estimate=cost(3e5, 8e5), name="sum",
    )(*parts, b_out.reshape(1, CLS))


def solution(mesh):
    placed = (
        P("vert", "feat"),
        P("vert", None),
        P("vert", None),
        P("feat", None),
        P("feat"),
        P("feat", None),
        P(),
    )
    return jax.shard_map(
        local, mesh=mesh, in_specs=placed, out_specs=P("vert", None), check_vma=False
    )
```

time: 230 us -> 105 us (0.46)
  waiting for transfers between devices: 150 us -> 22.8 us
  starting transfers between devices: 0.12 us -> 45.4 us
  matrix products: 27.9 us -> 0 us
  other arithmetic: 25.7 us -> 1.02 us
  Pallas kernels: 0 us -> 22.9 us
  between operations: 13.2 us -> 0.67 us
    all_gather x2 -> x0, waiting for transfers between devices: 84.1 us -> none  [the longest x1 48.8 us: local(): lax.all_gather(hidden, 'vert', axis=0, tiled=True)]
    ppermute x0 -> x27, starting transfers between devices: none -> 45.4 us  [the longest x6 14.2 us: swap(): return lax.ppermute(value, 'vert', positions(lambda x, z, c: (x, z, 1 - c)))]
    psum x1 -> x0, waiting for transfers between devices: 38.2 us -> none  [local(): return lax.psum(partial_scores, 'feat') + b_out]
    reduce_scatter x1 -> x0, waiting for transfers between devices: 28 us -> none  [local(): lax.psum_scatter(partial_value, 'feat', scatter_dimension=1, tiled=True)]
    dot_general x5 -> x0, matrix products: 27.9 us -> none  [the longest x1 14.1 us: local(): summed = total + jnp.dot(block, lower, preferred_element_type=jnp.float32)]
    reduce_sum x1 -> x0, other arithmetic: 23.9 us -> none  [local(): degree = jnp.sum(adj_int, axis=1).astype(jnp.float32)[:, None]]
    pallas_call x0 -> x7, Pallas kernels: none -> 22.9 us  [the longest x1 10.9 us: make_adjacency(): pl.pallas_call(adjacency_kernel, grid_spec=pltpu.PrefetchScalarGridSpec(n...]
    ppermute x0 -> x27, waiting for transfers between devices: none -> 22.8 us  [the longest x9 14 us: along_feat(): lax.ppermute(value, 'feat', [(i, (i + shift) % NF) for i in range(NF)])]
  transfers between devices with their start and end apart: 4 -> 27, of which waited for: 4 -> 13; matrix products, arithmetic and copies ran while one was open for 13% -> 4% of each run, Pallas kernels for 0% -> 18%
where the time goes in v1:
time: 105 us
  starting transfers between devices  45.4 us (43%)
  Pallas kernels  22.9 us (22%)
  waiting for transfers between devices  22.8 us (22%)
  local copies, waits for them, and re-layouts  12.2 us (12%)
    ppermute x6, starting transfers between devices, swap(): return lax.ppermute(value, 'vert', positions(lambda x, z, c: (x, z, 1 - c)))  14.2 us
    ppermute x9, waiting for transfers between devices, along_feat(): lax.ppermute(value, 'feat', [(i, (i + shift) % NF) for i in range(NF)])  14 us
    ppermute x9, starting transfers between devices, along_feat(): lax.ppermute(value, 'feat', [(i, (i + shift) % NF) for i in range(NF)])  11.1 us
    pallas_call x1, Pallas kernels, make_adjacency(): pl.pallas_call(adjacency_kernel, grid_spec=pltpu.PrefetchScalarGridSpec(n...  10.9 us
    ppermute x6, starting transfers between devices, second_axis(): lax.ppermute(value, 'vert', positions(lambda x, z, c: (x + shift * c, z +...  10.2 us
    ppermute x6, starting transfers between devices, first_axis(): lax.ppermute(value, 'vert', positions(lambda x, z, c: (x + shift * (1 - c...  9.98 us
    unnamed x19, local copies, waits for them, and re-layouts  9.33 us
    ppermute x6, waiting for transfers between devices, second_axis(): lax.ppermute(value, 'vert', positions(lambda x, z, c: (x + shift * c, z +...  4.15 us
  transfers between devices with their start and end apart: 27, of which 13 were waited for; matrix products, arithmetic and copies ran while one was open for 4% of the time, Pallas kernels for 18%

profile of v1, /device:TPU:1, one launch (start us, length us, event | category | flops | bytes accessed | tf_op | source)
XLA Modules:
  0.0 105.0 jit_solution(11218782270472894338)
XLA Ops:
  0.0 4.4 %collective-permute-start.2 = (bf16[192,384]{1,0:T(8,128)(2,1)}, bf16[192,384]{1,0:T(8,128)(2,1)S(1)}, u32[]{:S(2)}, u32[]{:S(2)}) collective-permute-start(bf16[192,384]{1,0:T(8,128)(2,1)} %bitcast.79), channel_id=1, source_target_pairs={{0,16},{1,5},{2,18},{3,7},{4,20},{5,1},{6,22},{7,3},{8,24},{9,13},... | collective-permute-start | bytes 442376 | tf_op jit(solution)/shard_map/ppermute | solution.py:40
  4.4 0.4 collective-permute-start.1
  4.9 1.0 collective-permute-start
  5.9 0.7 fusion.3
  6.6 1.0 copy.12
  7.6 1.3 %reshape.25 = bf16[192,4,2,128]{3,2,1,0:T(2,128)(2,1)S(1)} reshape(bf16[192,1024]{1,0:T(8,128)(2,1)} %param.10) | data formatting | bytes 786432 | tf_op jit(solution)/shard_map/reshape | solution.py:232
  8.9 0.1 copy.20
  9.0 0.0 copy-start.5
  9.0 0.2 reshape.26
  9.3 2.8 %collective-permute-start.15 = (bf16[272,512]{1,0:T(8,128)(2,1)S(1)}, bf16[272,512]{1,0:T(8,128)(2,1)S(1)}, u32[]{:S(2)}, u32[]{:S(2)}) collective-permute-start(bf16[272,512]{1,0:T(8,128)(2,1)S(1)} %dynamic-slice_bitcast_fusion), channel_id=1, source_target_pairs={{0,96},{32,0},{64,32},{96,64},{1,97},{33,1},{65,33},{97,65},{2,98}... | collective-permute-start | bytes 835592 | tf_op jit(solution)/shard_map/ppermute | solution.py:52
  12.1 0.0 collective-permute-done.2
  12.1 0.1 pad_maximum_fusion.1.refs_0_
  12.2 1.3 %collective-permute-start.4 = (bf16[4,192,384]{2,1,0:T(8,128)(2,1)S(1)}, bf16[4,192,384]{2,1,0:T(8,128)(2,1)}, u32[]{:S(2)}, u32[]{:S(2)}) collective-permute-start(bf16[4,192,384]{2,1,0:T(8,128)(2,1)S(1)} %pad_maximum_fusion.1.refs_0_), channel_id=1, source_target_pairs={{0,2},{1,9},{2,4},{3,11},{4,6},{5,13},{6,0},{7,15},{8,10},{9,17},{... | collective-permute-start | bytes 1769480 | tf_op jit(solution)/shard_map/ppermute | solution.py:44
  13.5 1.5 %collective-permute-start.6 = (bf16[4,192,384]{2,1,0:T(8,128)(2,1)S(1)}, bf16[4,192,384]{2,1,0:T(8,128)(2,1)}, u32[]{:S(2)}, u32[]{:S(2)}) collective-permute-start(bf16[4,192,384]{2,1,0:T(8,128)(2,1)S(1)} %pad_maximum_fusion.1.refs_0_), channel_id=1, source_target_pairs={{0,6},{1,25},{2,0},{3,27},{4,2},{5,29},{6,4},{7,31},{8,14},{9,1},{... | collective-permute-start | bytes 1769480 | tf_op jit(solution)/shard_map/ppermute | solution.py:44
  15.0 1.5 %collective-permute-start.8 = (bf16[4,192,384]{2,1,0:T(8,128)(2,1)S(1)}, bf16[4,192,384]{2,1,0:T(8,128)(2,1)}, u32[]{:S(2)}, u32[]{:S(2)}) collective-permute-start(bf16[4,192,384]{2,1,0:T(8,128)(2,1)S(1)} %pad_maximum_fusion.1.refs_0_), channel_id=1, source_target_pairs={{0,4},{1,17},{2,6},{3,19},{4,0},{5,21},{6,2},{7,23},{8,12},{9,25},... | collective-permute-start | bytes 1769480 | tf_op jit(solution)/shard_map/ppermute | solution.py:44
  16.5 1.1 %collective-permute-start.14 = (bf16[272,512]{1,0:T(8,128)(2,1)S(1)}, bf16[272,512]{1,0:T(8,128)(2,1)S(1)}, u32[]{:S(2)}, u32[]{:S(2)}) collective-permute-start(bf16[272,512]{1,0:T(8,128)(2,1)S(1)} %dynamic-slice_bitcast_fusion), channel_id=1, source_target_pairs={{0,64},{32,96},{64,0},{96,32},{1,65},{33,97},{65,1},{97,33},{2,66}... | collective-permute-start | bytes 835592 | tf_op jit(solution)/shard_map/ppermute | solution.py:52
  17.6 0.6 collective-permute-start.13
  18.2 5.3 %collective-permute-done.14 = bf16[272,512]{1,0:T(8,128)(2,1)S(1)} collective-permute-done((bf16[272,512]{1,0:T(8,128)(2,1)S(1)}, bf16[272,512]{1,0:T(8,128)(2,1)S(1)}, u32[]{:S(2)}, u32[]{:S(2)}) %collective-permute-start.14) | collective-permute-done | bytes 278560 | tf_op jit(solution)/shard_map/ppermute | solution.py:52
  23.5 6.6 %collective-permute-start.3 = (bf16[4,192,384]{2,1,0:T(8,128)(2,1)S(1)}, bf16[4,192,384]{2,1,0:T(8,128)(2,1)}, u32[]{:S(2)}, u32[]{:S(2)}) collective-permute-start(bf16[4,192,384]{2,1,0:T(8,128)(2,1)S(1)} %pad_maximum_fusion.1.refs_0_), channel_id=1, source_target_pairs={{0,1},{1,0},{2,3},{3,2},{4,5},{5,4},{6,7},{7,6},{8,9},{9,8},{10,11... | collective-permute-start | bytes 1769480 | tf_op jit(solution)/shard_map/ppermute | solution.py:48
  30.1 1.0 collective-permute-done.13
  31.1 0.1 pad_maximum_fusion.near
  31.2 2.1 %collective-permute-start.16 = (bf16[3,272,512]{2,1,0:T(8,128)(2,1)S(1)}, bf16[3,272,512]{2,1,0:T(8,128)(2,1)S(1)}, u32[]{:S(2)}, u32[]{:S(2)}) collective-permute-start(bf16[3,272,512]{2,1,0:T(8,128)(2,1)S(1)} %pad_maximum_fusion.near), channel_id=1, source_target_pairs={{0,1},{1,0},{2,3},{3,2},{4,5},{5,4},{6,7},{7,6},{8,9},{9,8},{10,11... | collective-permute-start | bytes 2506760 | tf_op jit(solution)/shard_map/ppermute | solution.py:48
  33.2 0.1 collective-permute-start.5
  33.3 0.4 collective-permute-start.7
  33.8 0.1 collective-permute-start.9
  34.3 0.1 stack.243.order
  34.3 0.1 stack.245.order
  34.4 0.1 stack.244.order
  34.5 0.1 pad_add_fusion.where
  34.6 6.4 %copy-done = s32[384,12288]{1,0:T(8,128)S(1)} copy-done((s32[384,12288]{1,0:T(8,128)S(1)}, s32[384,12288]{1,0:T(8,128)}, u32[]{:S(2)}) %copy-start) | copy-done | bytes 18874392
  41.0 10.9 %adjacency.1 = (bf16[384,12288]{1,0:T(8,128)(2,1)S(1)}, bf16[384,4096]{1,0:T(8,128)(2,1)S(1)}, f32[384,128]{1,0:T(8,128)S(1)}) custom-call(s32[3,96]{1,0:T(4,128)S(1)} %copy-done.3, s32[3]{0:T(128)S(1)} %pad_add_fusion.where, s32[384,12288]{1,0:T(8,128)S(1)} %copy-done), custom_call_target="tpu_custom_call" | custom-call | flops 2400000000 | bytes 31000000 | tf_op jit(solution)/shard_map/adjacency/pallas_call | solution.py:95
  51.9 2.5 %product_first.1.before = f32[384,192]{1,0:T(8,128)S(1)} custom-call(s32[8]{0:T(128)S(1)} %stack.245.order, bf16[384,12288]{1,0:T(8,128)(2,1)S(1)} %get-tuple-element.14.adj, bf16[4,192,384]{2,1,0:T(8,128)(2,1)S(1)} %pad_maximum_fusion.1.refs_0_, bf16[4,192,384]{2,1,0:T(8,128)(2,1)} %collective-permute-done.3.refs_1_), custom_call_target="tpu_custom_call" | custom-call | flops 603979776 | bytes 3600000 | tf_op jit(solution)/shard_map/product_first/pallas_call | solution.py:242
  54.4 3.4 %product_next.1.before = f32[384,192]{1,0:T(8,128)S(1)} custom-call(s32[16]{0:T(128)S(1)} %stack.244.order, bf16[384,12288]{1,0:T(8,128)(2,1)S(1)} %get-tuple-element.14.adj, f32[384,192]{1,0:T(8,128)S(1)} %product_first.1.before, bf16[4,192,384]{2,1,0:T(8,128)(2,1)} %collective-permute-done.4.refs_0_, bf16[4,192,384]{2,1,0:T(8,128)(2,1)} %collective-permute-done.5.refs_1_, ...), custom_call_target="tpu_custom_call" | custom-call | flops 1207959552 | bytes 7200000 | tf_op jit(solution)/shard_map/product_next/pallas_call | solution.py:247
  57.9 2.3 %product_last.1 = (bf16[96,192]{1,0:T(8,128)(2,1)S(1)}, bf16[96,192]{1,0:T(8,128)(2,1)S(1)}, bf16[96,192]{1,0:T(8,128)(2,1)S(1)}, bf16[96,192]{1,0:T(8,128)(2,1)S(1)}) custom-call(s32[8]{0:T(128)S(1)} %stack.243.order, s32[3]{0:T(128)S(1)} %pad_add_fusion.where, bf16[384,12288]{1,0:T(8,128)(2,1)S(1)} %get-tuple-element.14.adj, ...), custom_call_target="tpu_custom_call" | custom-call | flops 603979776 | bytes 3600000 | tf_op jit(solution)/shard_map/product_last/pallas_call | solution.py:252
  60.2 0.1 collective-permute-start.10
  60.2 1.8 %collective-permute-start.11 = (bf16[96,192]{1,0:T(8,128)(2,1)S(1)}, bf16[96,192]{1,0:T(8,128)(2,1)S(1)}, u32[]{:S(2)}, u32[]{:S(2)}) collective-permute-start(bf16[96,192]{1,0:T(8,128)(2,1)S(1)} %get-tuple-element.17), channel_id=1, source_target_pairs={{0,64},{32,96},{64,0},{96,32},{1,65},{33,97},{65,1},{97,33},{2,66}... | collective-permute-start | bytes 110600 | tf_op jit(solution)/shard_map/ppermute | solution.py:52
  62.1 1.3 %collective-permute-start.12 = (bf16[96,192]{1,0:T(8,128)(2,1)S(1)}, bf16[96,192]{1,0:T(8,128)(2,1)S(1)}, u32[]{:S(2)}, u32[]{:S(2)}) collective-permute-start(bf16[96,192]{1,0:T(8,128)(2,1)S(1)} %get-tuple-element.18), channel_id=1, source_target_pairs={{0,96},{32,0},{64,32},{96,64},{1,97},{33,1},{65,33},{97,65},{2,98}... | collective-permute-start | bytes 110600 | tf_op jit(solution)/shard_map/ppermute | solution.py:52
  63.4 1.9 %collective-permute-done.10.g1 = bf16[96,192]{1,0:T(8,128)(2,1)S(1)} collective-permute-done((bf16[96,192]{1,0:T(8,128)(2,1)S(1)}, bf16[96,192]{1,0:T(8,128)(2,1)S(1)}, u32[]{:S(2)}, u32[]{:S(2)}) %collective-permute-start.10) | collective-permute-done | bytes 36896 | tf_op jit(solution)/shard_map/ppermute | solution.py:52
  65.3 0.5 collective-permute-done.12.g3
  65.8 1.7 %hidden.1 = bf16[128,128]{1,0:T(8,128)(2,1)S(1)} custom-call(s32[3]{0:T(128)S(1)} %pad_add_fusion.where, bf16[96,192]{1,0:T(8,128)(2,1)S(1)} %get-tuple-element.15.g0, bf16[96,192]{1,0:T(8,128)(2,1)S(1)} %collective-permute-done.10.g1, bf16[96,192]{1,0:T(8,128)(2,1)S(1)} %collective-permute-done.11.g2, bf16[96,192]{1,0:T(8,128)(2,1)S(1)} %collective-permute-done.12.g3, ...), custom_call_target="tpu_custom_call" | custom-call | flops 150994944 | bytes 2000000 | tf_op jit(solution)/shard_map/hidden/pallas_call | solution.py:260
  67.5 0.8 collective-permute-start.17
  68.3 2.2 %collective-permute-start.18 = (bf16[128,128]{1,0:T(8,128)(2,1)S(1)}, bf16[128,128]{1,0:T(8,128)(2,1)S(1)}, u32[]{:S(2)}, u32[]{:S(2)}) collective-permute-start(bf16[128,128]{1,0:T(8,128)(2,1)S(1)} %hidden.1), channel_id=1, source_target_pairs={{0,24},{1,7},{2,26},{3,1},{4,28},{5,3},{6,30},{7,5},{8,0},{9,15},{... | collective-permute-start | bytes 98312 | tf_op jit(solution)/shard_map/ppermute | solution.py:40
  70.5 1.1 %collective-permute-start.19 = (bf16[128,128]{1,0:T(8,128)(2,1)S(1)}, bf16[128,128]{1,0:T(8,128)(2,1)S(1)}, u32[]{:S(2)}, u32[]{:S(2)}) collective-permute-start(bf16[128,128]{1,0:T(8,128)(2,1)S(1)} %hidden.1), channel_id=1, source_target_pairs={{0,16},{1,5},{2,18},{3,7},{4,20},{5,1},{6,22},{7,3},{8,24},{9,13},... | collective-permute-start | bytes 98312 | tf_op jit(solution)/shard_map/ppermute | solution.py:40
  71.6 0.1 collective-permute-done.17
  71.7 3.0 %collective-permute-done.19 = bf16[128,128]{1,0:T(8,128)(2,1)S(1)} collective-permute-done((bf16[128,128]{1,0:T(8,128)(2,1)S(1)}, bf16[128,128]{1,0:T(8,128)(2,1)S(1)}, u32[]{:S(2)}, u32[]{:S(2)}) %collective-permute-start.19) | collective-permute-done | bytes 32800 | tf_op jit(solution)/shard_map/ppermute | solution.py:40
  74.8 3.9 %collective-permute-start.20 = (bf16[4,128,128]{2,1,0:T(8,128)(2,1)S(1)}, bf16[4,128,128]{2,1,0:T(8,128)(2,1)S(1)}, u32[]{:S(2)}, u32[]{:S(2)}) collective-permute-start(bf16[4,128,128]{2,1,0:T(8,128)(2,1)S(1)} %pad_maximum_fusion.2), channel_id=1, source_target_pairs={{0,2},{1,9},{2,4},{3,11},{4,6},{5,13},{6,0},{7,15},{8,10},{9,17},{... | collective-permute-start | bytes 393224 | tf_op jit(solution)/shard_map/ppermute | solution.py:44
  78.7 0.9 collective-permute-start.21
  79.6 1.1 %collective-permute-start.22 = (bf16[4,128,128]{2,1,0:T(8,128)(2,1)S(1)}, bf16[4,128,128]{2,1,0:T(8,128)(2,1)S(1)}, u32[]{:S(2)}, u32[]{:S(2)}) collective-permute-start(bf16[4,128,128]{2,1,0:T(8,128)(2,1)S(1)} %pad_maximum_fusion.2), channel_id=1, source_target_pairs={{0,4},{1,17},{2,6},{3,19},{4,0},{5,21},{6,2},{7,23},{8,12},{9,25},... | collective-permute-start | bytes 393224 | tf_op jit(solution)/shard_map/ppermute | solution.py:44
  80.7 1.1 %collective-permute-done.20 = bf16[4,128,128]{2,1,0:T(8,128)(2,1)S(1)} collective-permute-done((bf16[4,128,128]{2,1,0:T(8,128)(2,1)S(1)}, bf16[4,128,128]{2,1,0:T(8,128)(2,1)S(1)}, u32[]{:S(2)}, u32[]{:S(2)}) %collective-permute-start.20) | collective-permute-done | bytes 131104 | tf_op jit(solution)/shard_map/ppermute | solution.py:44
  81.9 0.6 collective-permute-done.21
  82.5 2.4 %collective-permute-done.22 = bf16[4,128,128]{2,1,0:T(8,128)(2,1)S(1)} collective-permute-done((bf16[4,128,128]{2,1,0:T(8,128)(2,1)S(1)}, bf16[4,128,128]{2,1,0:T(8,128)(2,1)S(1)}, u32[]{:S(2)}, u32[]{:S(2)}) %collective-permute-start.22) | collective-permute-done | bytes 131104 | tf_op jit(solution)/shard_map/ppermute | solution.py:44
  84.9 4.9 %collective-permute-start.23 = (bf16[16,128,128]{2,1,0:T(8,128)(2,1)S(1)}, bf16[16,128,128]{2,1,0:T(8,128)(2,1)S(1)}, u32[]{:S(2)}, u32[]{:S(2)}) collective-permute-start(bf16[16,128,128]{2,1,0:T(8,128)(2,1)S(1)} %constant_dynamic-update-slice_fusion.z_near), channel_id=1, source_target_pairs={{0,1},{1,0},{2,3},{3,2},{4,5},{5,4},{6,7},{7,6},{8,9},{9,8},{10,11... | collective-permute-start | bytes 1572872 | tf_op jit(solution)/shard_map/ppermute | solution.py:48
  89.8 0.1 stack.238.order
  89.9 1.4 %collective-permute-done.23.z_far = bf16[16,128,128]{2,1,0:T(8,128)(2,1)S(1)} collective-permute-done((bf16[16,128,128]{2,1,0:T(8,128)(2,1)S(1)}, bf16[16,128,128]{2,1,0:T(8,128)(2,1)S(1)}, u32[]{:S(2)}, u32[]{:S(2)}) %collective-permute-start.23) | collective-permute-done | bytes 524320 | tf_op jit(solution)/shard_map/ppermute | solution.py:48
  91.4 1.9 %copy-done.2 = bf16[384,4096]{1,0:T(8,128)(2,1)S(1)} copy-done((bf16[384,4096]{1,0:T(8,128)(2,1)S(1)}, bf16[384,4096]{1,0:T(8,128)(2,1)}, u32[]{:S(2)}) %copy-start.2) | copy-done | bytes 3145752
  93.3 2.0 %scores.1.p0 = bf16[480,128]{1,0:T(8,128)(2,1)S(1)} custom-call(s32[32]{0:T(128)S(1)} %stack.238.order, bf16[384,4096]{1,0:T(8,128)(2,1)S(1)} %copy-done.2, f32[384,128]{1,0:T(8,128)S(1)} %get-tuple-element.13.degree, bf16[16,128,128]{2,1,0:T(8,128)(2,1)S(1)} %constant_dynamic-update-slice_fusion.z_near, bf16[16,128,128]{2,1,0:T(8,128)(2,1)S(1)} %collective-permute-done.23.z_far), custom_call_target="tpu_custom_call" | custom-call | flops 805306368 | bytes 5000000 | tf_op jit(solution)/shard_map/scores/pallas_call | solution.py:271
  95.2 0.7 collective-permute-start.24
  95.9 2.2 %collective-permute-start.25 = (bf16[480,128]{1,0:T(8,128)(2,1)S(1)}, bf16[480,128]{1,0:T(8,128)(2,1)S(1)}, u32[]{:S(2)}, u32[]{:S(2)}) collective-permute-start(bf16[480,128]{1,0:T(8,128)(2,1)S(1)} %scores.1.p0), channel_id=1, source_target_pairs={{0,64},{32,96},{64,0},{96,32},{1,65},{33,97},{65,1},{97,33},{2,66}... | collective-permute-start | bytes 368648 | tf_op jit(solution)/shard_map/ppermute | solution.py:52
  98.1 0.5 collective-permute-start.26
  98.6 2.4 %collective-permute-done.24.p1 = bf16[480,128]{1,0:T(8,128)(2,1)S(1)} collective-permute-done((bf16[480,128]{1,0:T(8,128)(2,1)S(1)}, bf16[480,128]{1,0:T(8,128)(2,1)S(1)}, u32[]{:S(2)}, u32[]{:S(2)}) %collective-permute-start.24) | collective-permute-done | bytes 122912 | tf_op jit(solution)/shard_map/ppermute | solution.py:52
  101.0 2.8 %collective-permute-done.25.p2 = bf16[480,128]{1,0:T(8,128)(2,1)S(1)} collective-permute-done((bf16[480,128]{1,0:T(8,128)(2,1)S(1)}, bf16[480,128]{1,0:T(8,128)(2,1)S(1)}, u32[]{:S(2)}, u32[]{:S(2)}) %collective-permute-start.25) | collective-permute-done | bytes 122912 | tf_op jit(solution)/shard_map/ppermute | solution.py:52
  103.8 0.1 collective-permute-done.26.p3
  103.9 0.2 sum.1
  104.1 0.8 copy.17
  (38 shorter events, 0.3 us)
Async XLA Ops:
  0.0 12.1 %collective-permute-start.2 = (bf16[192,384]{1,0:T(8,128)(2,1)}, bf16[192,384]{1,0:T(8,128)(2,1)S(1)}, u32[]{:S(2)}, u32[]{:S(2)}) collective-permute-start(bf16[192,384]{1,0:T(8,128)(2,1)} %bitcast.79), channel_id=1, source_target_pairs={{0,16},{1,5},{2,18},{3,7},{4,20},{5,1},{6,22},{7,3},{8,24},{9,13},... | collective-permute-start | bytes 442376 | tf_op jit(solution)/shard_map/ppermute | solution.py:40
  4.4 7.7 %collective-permute-start.1 = (bf16[192,384]{1,0:T(8,128)(2,1)}, bf16[192,384]{1,0:T(8,128)(2,1)S(1)}, u32[]{:S(2)}, u32[]{:S(2)}) collective-permute-start(bf16[192,384]{1,0:T(8,128)(2,1)} %bitcast.80), channel_id=1, source_target_pairs={{0,24},{1,7},{2,26},{3,1},{4,28},{5,3},{6,30},{7,5},{8,0},{9,15},{... | collective-permute-start | bytes 442376 | tf_op jit(solution)/shard_map/ppermute | solution.py:40
  4.9 7.3 %collective-permute-start = (bf16[192,384]{1,0:T(8,128)(2,1)}, bf16[192,384]{1,0:T(8,128)(2,1)S(1)}, u32[]{:S(2)}, u32[]{:S(2)}) collective-permute-start(bf16[192,384]{1,0:T(8,128)(2,1)} %bitcast.81), channel_id=1, source_target_pairs={{0,8},{1,3},{2,10},{3,5},{4,12},{5,7},{6,14},{7,1},{8,16},{9,11},{... | collective-permute-start | bytes 442376 | tf_op jit(solution)/shard_map/ppermute | solution.py:40
  9.0 3.1 %copy-start.5 = (bf16[384,192]{0,1:T(8,128)(2,1)S(1)}, bf16[384,192]{0,1:T(8,128)(2,1)}, u32[]{:S(2)}) copy-start(bf16[384,192]{0,1:T(8,128)(2,1)} %param.7) | copy-start | bytes 442372
  9.3 8.3 %collective-permute-start.15 = (bf16[272,512]{1,0:T(8,128)(2,1)S(1)}, bf16[272,512]{1,0:T(8,128)(2,1)S(1)}, u32[]{:S(2)}, u32[]{:S(2)}) collective-permute-start(bf16[272,512]{1,0:T(8,128)(2,1)S(1)} %dynamic-slice_bitcast_fusion), channel_id=1, source_target_pairs={{0,96},{32,0},{64,32},{96,64},{1,97},{33,1},{65,33},{97,65},{2,98}... | collective-permute-start | bytes 835592 | tf_op jit(solution)/shard_map/ppermute | solution.py:52
  12.2 21.0 %collective-permute-start.4 = (bf16[4,192,384]{2,1,0:T(8,128)(2,1)S(1)}, bf16[4,192,384]{2,1,0:T(8,128)(2,1)}, u32[]{:S(2)}, u32[]{:S(2)}) collective-permute-start(bf16[4,192,384]{2,1,0:T(8,128)(2,1)S(1)} %pad_maximum_fusion.1.refs_0_), channel_id=1, source_target_pairs={{0,2},{1,9},{2,4},{3,11},{4,6},{5,13},{6,0},{7,15},{8,10},{9,17},{... | collective-permute-start | bytes 1769480 | tf_op jit(solution)/shard_map/ppermute | solution.py:44
  13.5 19.8 %collective-permute-start.6 = (bf16[4,192,384]{2,1,0:T(8,128)(2,1)S(1)}, bf16[4,192,384]{2,1,0:T(8,128)(2,1)}, u32[]{:S(2)}, u32[]{:S(2)}) collective-permute-start(bf16[4,192,384]{2,1,0:T(8,128)(2,1)S(1)} %pad_maximum_fusion.1.refs_0_), channel_id=1, source_target_pairs={{0,6},{1,25},{2,0},{3,27},{4,2},{5,29},{6,4},{7,31},{8,14},{9,1},{... | collective-permute-start | bytes 1769480 | tf_op jit(solution)/shard_map/ppermute | solution.py:44
  15.0 18.8 %collective-permute-start.8 = (bf16[4,192,384]{2,1,0:T(8,128)(2,1)S(1)}, bf16[4,192,384]{2,1,0:T(8,128)(2,1)}, u32[]{:S(2)}, u32[]{:S(2)}) collective-permute-start(bf16[4,192,384]{2,1,0:T(8,128)(2,1)S(1)} %pad_maximum_fusion.1.refs_0_), channel_id=1, source_target_pairs={{0,4},{1,17},{2,6},{3,19},{4,0},{5,21},{6,2},{7,23},{8,12},{9,25},... | collective-permute-start | bytes 1769480 | tf_op jit(solution)/shard_map/ppermute | solution.py:44
  16.5 7.0 %collective-permute-start.14 = (bf16[272,512]{1,0:T(8,128)(2,1)S(1)}, bf16[272,512]{1,0:T(8,128)(2,1)S(1)}, u32[]{:S(2)}, u32[]{:S(2)}) collective-permute-start(bf16[272,512]{1,0:T(8,128)(2,1)S(1)} %dynamic-slice_bitcast_fusion), channel_id=1, source_target_pairs={{0,64},{32,96},{64,0},{96,32},{1,65},{33,97},{65,1},{97,33},{2,66}... | collective-permute-start | bytes 835592 | tf_op jit(solution)/shard_map/ppermute | solution.py:52
  17.6 13.5 %collective-permute-start.13 = (bf16[272,512]{1,0:T(8,128)(2,1)S(1)}, bf16[272,512]{1,0:T(8,128)(2,1)S(1)}, u32[]{:S(2)}, u32[]{:S(2)}) collective-permute-start(bf16[272,512]{1,0:T(8,128)(2,1)S(1)} %dynamic-slice_bitcast_fusion), channel_id=1, source_target_pairs={{0,32},{32,64},{64,96},{96,0},{1,33},{33,65},{65,97},{97,1},{2,34}... | collective-permute-start | bytes 835592 | tf_op jit(solution)/shard_map/ppermute | solution.py:52
  23.5 28.3 %collective-permute-start.3 = (bf16[4,192,384]{2,1,0:T(8,128)(2,1)S(1)}, bf16[4,192,384]{2,1,0:T(8,128)(2,1)}, u32[]{:S(2)}, u32[]{:S(2)}) collective-permute-start(bf16[4,192,384]{2,1,0:T(8,128)(2,1)S(1)} %pad_maximum_fusion.1.refs_0_), channel_id=1, source_target_pairs={{0,1},{1,0},{2,3},{3,2},{4,5},{5,4},{6,7},{7,6},{8,9},{9,8},{10,11... | collective-permute-start | bytes 1769480 | tf_op jit(solution)/shard_map/ppermute | solution.py:48
  31.1 3.5 %copy-start.3 = (s32[3,96]{1,0:T(4,128)S(1)}, s32[3,96]{1,0:T(4,128)}, u32[]{:S(2)}) copy-start(s32[3,96]{1,0:T(4,128)} %mask.1) | copy-start | bytes 3460
  31.2 32.2 %collective-permute-start.16 = (bf16[3,272,512]{2,1,0:T(8,128)(2,1)S(1)}, bf16[3,272,512]{2,1,0:T(8,128)(2,1)S(1)}, u32[]{:S(2)}, u32[]{:S(2)}) collective-permute-start(bf16[3,272,512]{2,1,0:T(8,128)(2,1)S(1)} %pad_maximum_fusion.near), channel_id=1, source_target_pairs={{0,1},{1,0},{2,3},{3,2},{4,5},{5,4},{6,7},{7,6},{8,9},{9,8},{10,11... | collective-permute-start | bytes 2506760 | tf_op jit(solution)/shard_map/ppermute | solution.py:48
  33.2 21.2 %collective-permute-start.5 = (bf16[4,192,384]{2,1,0:T(8,128)(2,1)}, bf16[4,192,384]{2,1,0:T(8,128)(2,1)}, u32[]{:S(2)}, u32[]{:S(2)}) collective-permute-start(bf16[4,192,384]{2,1,0:T(8,128)(2,1)} %collective-permute-done.4.refs_0_), channel_id=1, source_target_pairs={{0,1},{1,0},{2,3},{3,2},{4,5},{5,4},{6,7},{7,6},{8,9},{9,8},{10,11... | collective-permute-start | bytes 1769480 | tf_op jit(solution)/shard_map/ppermute | solution.py:48
  33.3 21.1 %collective-permute-start.7 = (bf16[4,192,384]{2,1,0:T(8,128)(2,1)}, bf16[4,192,384]{2,1,0:T(8,128)(2,1)}, u32[]{:S(2)}, u32[]{:S(2)}) collective-permute-start(bf16[4,192,384]{2,1,0:T(8,128)(2,1)} %collective-permute-done.6.refs_2_), channel_id=1, source_target_pairs={{0,1},{1,0},{2,3},{3,2},{4,5},{5,4},{6,7},{7,6},{8,9},{9,8},{10,11... | collective-permute-start | bytes 1769480 | tf_op jit(solution)/shard_map/ppermute | solution.py:48
  33.8 24.1 %collective-permute-start.9 = (bf16[4,192,384]{2,1,0:T(8,128)(2,1)}, bf16[4,192,384]{2,1,0:T(8,128)(2,1)}, u32[]{:S(2)}, u32[]{:S(2)}) collective-permute-start(bf16[4,192,384]{2,1,0:T(8,128)(2,1)} %collective-permute-done.8.refs_0_), channel_id=1, source_target_pairs={{0,1},{1,0},{2,3},{3,2},{4,5},{5,4},{6,7},{7,6},{8,9},{9,8},{10,11... | collective-permute-start | bytes 1769480 | tf_op jit(solution)/shard_map/ppermute | solution.py:48
  34.6 6.4 %copy-start = (s32[384,12288]{1,0:T(8,128)S(1)}, s32[384,12288]{1,0:T(8,128)}, u32[]{:S(2)}) copy-start(s32[384,12288]{1,0:T(8,128)} %counts.1) | copy-start | bytes 56623108
  51.9 2.5 %copy-start.1 = (bf16[384,4096]{1,0:T(8,128)(2,1)}, bf16[384,4096]{1,0:T(8,128)(2,1)S(1)}, u32[]{:S(2)}) copy-start(bf16[384,4096]{1,0:T(8,128)(2,1)S(1)} %get-tuple-element.12.adj2) | copy-start | bytes 9437188
  60.2 5.1 %collective-permute-start.10 = (bf16[96,192]{1,0:T(8,128)(2,1)S(1)}, bf16[96,192]{1,0:T(8,128)(2,1)S(1)}, u32[]{:S(2)}, u32[]{:S(2)}) collective-permute-start(bf16[96,192]{1,0:T(8,128)(2,1)S(1)} %get-tuple-element.16), channel_id=1, source_target_pairs={{0,32},{32,64},{64,96},{96,0},{1,33},{33,65},{65,97},{97,1},{2,34}... | collective-permute-start | bytes 110600 | tf_op jit(solution)/shard_map/ppermute | solution.py:52
  60.2 5.0 %collective-permute-start.11 = (bf16[96,192]{1,0:T(8,128)(2,1)S(1)}, bf16[96,192]{1,0:T(8,128)(2,1)S(1)}, u32[]{:S(2)}, u32[]{:S(2)}) collective-permute-start(bf16[96,192]{1,0:T(8,128)(2,1)S(1)} %get-tuple-element.17), channel_id=1, source_target_pairs={{0,64},{32,96},{64,0},{96,32},{1,65},{33,97},{65,1},{97,33},{2,66}... | collective-permute-start | bytes 110600 | tf_op jit(solution)/shard_map/ppermute | solution.py:52
  62.1 3.7 %collective-permute-start.12 = (bf16[96,192]{1,0:T(8,128)(2,1)S(1)}, bf16[96,192]{1,0:T(8,128)(2,1)S(1)}, u32[]{:S(2)}, u32[]{:S(2)}) collective-permute-start(bf16[96,192]{1,0:T(8,128)(2,1)S(1)} %get-tuple-element.18), channel_id=1, source_target_pairs={{0,96},{32,0},{64,32},{96,64},{1,97},{33,1},{65,33},{97,65},{2,98}... | collective-permute-start | bytes 110600 | tf_op jit(solution)/shard_map/ppermute | solution.py:52
  67.5 4.2 %collective-permute-start.17 = (bf16[128,128]{1,0:T(8,128)(2,1)S(1)}, bf16[128,128]{1,0:T(8,128)(2,1)S(1)}, u32[]{:S(2)}, u32[]{:S(2)}) collective-permute-start(bf16[128,128]{1,0:T(8,128)(2,1)S(1)} %hidden.1), channel_id=1, source_target_pairs={{0,8},{1,3},{2,10},{3,5},{4,12},{5,7},{6,14},{7,1},{8,16},{9,11},{... | collective-permute-start | bytes 98312 | tf_op jit(solution)/shard_map/ppermute | solution.py:40
  68.3 3.4 %collective-permute-start.18 = (bf16[128,128]{1,0:T(8,128)(2,1)S(1)}, bf16[128,128]{1,0:T(8,128)(2,1)S(1)}, u32[]{:S(2)}, u32[]{:S(2)}) collective-permute-start(bf16[128,128]{1,0:T(8,128)(2,1)S(1)} %hidden.1), channel_id=1, source_target_pairs={{0,24},{1,7},{2,26},{3,1},{4,28},{5,3},{6,30},{7,5},{8,0},{9,15},{... | collective-permute-start | bytes 98312 | tf_op jit(solution)/shard_map/ppermute | solution.py:40
  70.5 4.3 %collective-permute-start.19 = (bf16[128,128]{1,0:T(8,128)(2,1)S(1)}, bf16[128,128]{1,0:T(8,128)(2,1)S(1)}, u32[]{:S(2)}, u32[]{:S(2)}) collective-permute-start(bf16[128,128]{1,0:T(8,128)(2,1)S(1)} %hidden.1), channel_id=1, source_target_pairs={{0,16},{1,5},{2,18},{3,7},{4,20},{5,1},{6,22},{7,3},{8,24},{9,13},... | collective-permute-start | bytes 98312 | tf_op jit(solution)/shard_map/ppermute | solution.py:40
  74.8 7.1 %collective-permute-start.20 = (bf16[4,128,128]{2,1,0:T(8,128)(2,1)S(1)}, bf16[4,128,128]{2,1,0:T(8,128)(2,1)S(1)}, u32[]{:S(2)}, u32[]{:S(2)}) collective-permute-start(bf16[4,128,128]{2,1,0:T(8,128)(2,1)S(1)} %pad_maximum_fusion.2), channel_id=1, source_target_pairs={{0,2},{1,9},{2,4},{3,11},{4,6},{5,13},{6,0},{7,15},{8,10},{9,17},{... | collective-permute-start | bytes 393224 | tf_op jit(solution)/shard_map/ppermute | solution.py:44
  78.7 3.8 %collective-permute-start.21 = (bf16[4,128,128]{2,1,0:T(8,128)(2,1)S(1)}, bf16[4,128,128]{2,1,0:T(8,128)(2,1)S(1)}, u32[]{:S(2)}, u32[]{:S(2)}) collective-permute-start(bf16[4,128,128]{2,1,0:T(8,128)(2,1)S(1)} %pad_maximum_fusion.2), channel_id=1, source_target_pairs={{0,6},{1,25},{2,0},{3,27},{4,2},{5,29},{6,4},{7,31},{8,14},{9,1},{... | collective-permute-start | bytes 393224 | tf_op jit(solution)/shard_map/ppermute | solution.py:44
  79.6 5.3 %collective-permute-start.22 = (bf16[4,128,128]{2,1,0:T(8,128)(2,1)S(1)}, bf16[4,128,128]{2,1,0:T(8,128)(2,1)S(1)}, u32[]{:S(2)}, u32[]{:S(2)}) collective-permute-start(bf16[4,128,128]{2,1,0:T(8,128)(2,1)S(1)} %pad_maximum_fusion.2), channel_id=1, source_target_pairs={{0,4},{1,17},{2,6},{3,19},{4,0},{5,21},{6,2},{7,23},{8,12},{9,25},... | collective-permute-start | bytes 393224 | tf_op jit(solution)/shard_map/ppermute | solution.py:44
  84.9 6.5 %collective-permute-start.23 = (bf16[16,128,128]{2,1,0:T(8,128)(2,1)S(1)}, bf16[16,128,128]{2,1,0:T(8,128)(2,1)S(1)}, u32[]{:S(2)}, u32[]{:S(2)}) collective-permute-start(bf16[16,128,128]{2,1,0:T(8,128)(2,1)S(1)} %constant_dynamic-update-slice_fusion.z_near), channel_id=1, source_target_pairs={{0,1},{1,0},{2,3},{3,2},{4,5},{5,4},{6,7},{7,6},{8,9},{9,8},{10,11... | collective-permute-start | bytes 1572872 | tf_op jit(solution)/shard_map/ppermute | solution.py:48
  91.4 1.9 %copy-start.2 = (bf16[384,4096]{1,0:T(8,128)(2,1)S(1)}, bf16[384,4096]{1,0:T(8,128)(2,1)}, u32[]{:S(2)}) copy-start(bf16[384,4096]{1,0:T(8,128)(2,1)} %copy-done.1) | copy-start | bytes 9437188
  93.3 10.7 %copy-start.4 = (f32[153]{0:T(256)S(1)}, f32[153]{0:T(256)}, u32[]{:S(2)}) copy-start(f32[153]{0:T(256)} %param.13) | copy-start | bytes 1840
  95.2 5.8 %collective-permute-start.24 = (bf16[480,128]{1,0:T(8,128)(2,1)S(1)}, bf16[480,128]{1,0:T(8,128)(2,1)S(1)}, u32[]{:S(2)}, u32[]{:S(2)}) collective-permute-start(bf16[480,128]{1,0:T(8,128)(2,1)S(1)} %scores.1.p0), channel_id=1, source_target_pairs={{0,32},{32,64},{64,96},{96,0},{1,33},{33,65},{65,97},{97,1},{2,34}... | collective-permute-start | bytes 368648 | tf_op jit(solution)/shard_map/ppermute | solution.py:52
  95.9 7.9 %collective-permute-start.25 = (bf16[480,128]{1,0:T(8,128)(2,1)S(1)}, bf16[480,128]{1,0:T(8,128)(2,1)S(1)}, u32[]{:S(2)}, u32[]{:S(2)}) collective-permute-start(bf16[480,128]{1,0:T(8,128)(2,1)S(1)} %scores.1.p0), channel_id=1, source_target_pairs={{0,64},{32,96},{64,0},{96,32},{1,65},{33,97},{65,1},{97,33},{2,66}... | collective-permute-start | bytes 368648 | tf_op jit(solution)/shard_map/ppermute | solution.py:52
  98.1 5.8 %collective-permute-start.26 = (bf16[480,128]{1,0:T(8,128)(2,1)S(1)}, bf16[480,128]{1,0:T(8,128)(2,1)S(1)}, u32[]{:S(2)}, u32[]{:S(2)}) collective-permute-start(bf16[480,128]{1,0:T(8,128)(2,1)S(1)} %scores.1.p0), channel_id=1, source_target_pairs={{0,96},{32,0},{64,32},{96,64},{1,97},{33,1},{65,33},{97,65},{2,98}... | collective-permute-start | bytes 368648 | tf_op jit(solution)/shard_map/ppermute | solution.py:52

commit v2 on v1

v2 whole, which is shorter than its diff:
```python
import jax
import jax.numpy as jnp
from jax import lax
from jax.experimental import pallas as pl
from jax.experimental.pallas import tpu as pltpu
from jax.sharding import PartitionSpec as P

TILE = 128
ROWS = 384
NV = 32
NF = 4
SHARE = ROWS // NF
CLS = 153
bf16 = jnp.bfloat16
f32 = jnp.float32
NT = (((1,), (1,)), ((), ()))
VM = pl.BlockSpec(memory_space=pltpu.VMEM)
SM = pl.BlockSpec(memory_space=pltpu.SMEM)


def here():
    return lax.axis_index("vert").astype(jnp.int32), lax.axis_index("feat").astype(jnp.int32)


def source(me, s, t, c):
    spot = lax.div(me, 2)
    x, z = lax.div(spot, NF), lax.rem(spot, NF)
    x = lax.rem(x + NF - jnp.where(c == 0, s, t), NF)
    z = lax.rem(z + NF - jnp.where(c == 0, t, s), NF)
    return (x * NF + z) * 2 + c


SHIFTS = (0, 1, 3, 2)


def params(mib=16):
    return pltpu.CompilerParams(vmem_limit_bytes=mib * 2**20)


def cost(flops, nbytes):
    return pl.CostEstimate(flops=int(flops), bytes_accessed=int(nbytes), transcendentals=0)


def positions(move):
    pairs = []
    for x in range(4):
        for z in range(4):
            for c in range(2):
                xx, zz, cc = move(x, z, c)
                pairs.append(((x * 4 + z) * 2 + c, (xx % 4 * 4 + zz % 4) * 2 + cc % 2))
    return pairs


def first_axis(value, shift):
    return lax.ppermute(value, "vert", positions(lambda x, z, c: (x + shift * (1 - c), z + shift * c, c)))


def second_axis(value, shift):
    return lax.ppermute(value, "vert", positions(lambda x, z, c: (x + shift * c, z + shift * (1 - c), c)))


def swap(value):
    return lax.ppermute(value, "vert", positions(lambda x, z, c: (x, z, 1 - c)))


def along_feat(value, shift):
    return lax.ppermute(value, "feat", [(i, (i + shift) % NF) for i in range(NF)])


CHUNK = 2 * ROWS
STEPS = NV * ROWS // CHUNK
SLOTS = 4


def adjacency_kernel(mask, counts, adj, adj2, degree, slots, sems):
    me, feat = here()
    row = lax.broadcasted_iota(jnp.int32, (TILE, TILE), 0)
    col = lax.broadcasted_iota(jnp.int32, (TILE, TILE), 1)
    eye = (row == col).astype(f32)
    source = lax.broadcasted_iota(jnp.int32, (ROWS, TILE), 0)
    target = lax.broadcasted_iota(jnp.int32, (ROWS, TILE), 1)
    pick = ((source == target + feat * SHARE) & (target < SHARE)).astype(f32).astype(bf16)

    def fetch(step, slot):
        start = pl.multiple_of(step * CHUNK, CHUNK)
        return pltpu.make_async_copy(counts.at[:, pl.ds(start, CHUNK)], slots.at[slot], sems.at[slot])

    for i in range(SLOTS - 1):
        fetch(i, i).start()
    degree[...] = jnp.zeros_like(degree)

    @pl.loop(0, STEPS)
    def _(step):
        slot = lax.rem(step, SLOTS)

        @pl.when(step + SLOTS - 1 < STEPS)
        def _():
            fetch(step + SLOTS - 1, lax.rem(step + SLOTS - 1, SLOTS)).start()

        fetch(step, slot).wait()
        for j in range(CHUNK // ROWS):
            base = pl.multiple_of(step * CHUNK + j * ROWS, ROWS)
            for k in range(ROWS // TILE):
                tile_col = step * (CHUNK // TILE) + j * (ROWS // TILE) + k
                for i in range(ROWS // TILE):
                    stored = mask[i, tile_col].astype(f32)
                    own = (me * (ROWS // TILE) + i == tile_col).astype(f32)
                    tile = slots[slot, i * TILE : (i + 1) * TILE, j * ROWS + k * TILE : j * ROWS + (k + 1) * TILE]
                    tile = tile.astype(f32) * stored + eye * own
                    degree[i * TILE : (i + 1) * TILE, :] += tile
                    adj[i * TILE : (i + 1) * TILE, pl.ds(base + k * TILE, TILE)] = tile.astype(bf16)
            part = jnp.dot(adj[:, pl.ds(base, ROWS)], pick, preferred_element_type=f32)
            place = pl.multiple_of((step * (CHUNK // ROWS) + j) * TILE, TILE)
            adj2[:, pl.ds(place, TILE)] = part.astype(bf16)

    degree[...] = jnp.broadcast_to(jnp.sum(degree[...], axis=1, keepdims=True), degree.shape)


def make_adjacency(tile_mask, counts):
    counts = pltpu.with_memory_space_constraint(counts, pltpu.HBM)
    return pl.pallas_call(
        adjacency_kernel,
        in_specs=[SM, pl.BlockSpec(memory_space=pltpu.HBM)],
        out_specs=[VM] * 3,
        out_shape=[
            pltpu.VMEM((ROWS, NV * ROWS), bf16),
            pltpu.VMEM((ROWS, NV * TILE), bf16),
            pltpu.VMEM((ROWS, TILE), f32),
        ],
        scratch_shapes=[pltpu.VMEM((SLOTS, ROWS, CHUNK), jnp.int32), pltpu.SemaphoreType.DMA((SLOTS,))],
        compiler_params=params(),
        cost_estimate=cost(2.4e9, 31e6),
        name="adjacency",
    )(tile_mask, counts)


def pack_kernel(w_in, w_out_t, b_in, after, mine, other):
    core = lax.rem(here()[0], 2)
    zero = jnp.zeros((192 - CLS, TILE), f32)
    for out, half in ((mine, core), (other, 1 - core)):
        for k in range(NF):
            lanes = pl.ds(pl.multiple_of(256 * k + TILE * half, TILE), TILE)
            out[0:192, k * TILE : (k + 1) * TILE] = w_in[:, lanes]
        lanes = pl.ds(pl.multiple_of(TILE * half, TILE), TILE)
        w = jnp.concatenate([w_out_t[:, lanes].astype(f32), zero], axis=0)
        for k in range(NF):
            out[192:240, k * TILE : (k + 1) * TILE] = w[48 * k : 48 * (k + 1)].astype(bf16)
        b = jnp.broadcast_to(b_in[:, lanes], (16, TILE))
        hi = b.astype(bf16).astype(f32)
        mid = (b - hi).astype(bf16).astype(f32)
        low = b - hi - mid
        row = lax.broadcasted_iota(jnp.int32, (16, TILE), 0)
        b = jnp.where(row == 0, hi, jnp.where(row == 1, mid, jnp.where(row == 2, low, 0.0)))
        out[240:256, 0:TILE] = b.astype(bf16)
        out[240:256, TILE:] = jnp.zeros((16, 512 - TILE), bf16)


def stack_kernel(a, b, c, d, after, out):
    for i, part in enumerate((a, b, c, d)):
        out[i] = part[...]


def add_blocks(shifts, adj, total, pieces):
    me, _ = here()
    for p, piece in enumerate(pieces):
        core = lax.rem(me + p, 2)
        for b in range(NF):
            src = source(me, SHIFTS[b], shifts[p // 2], core)
            src = pl.multiple_of(src * ROWS, ROWS)
            total = total + lax.dot_general(adj[:, pl.ds(src, ROWS)], piece[b], NT, preferred_element_type=f32)
    return total


def product_first(adj, *refs):
    refs[-1][...] = add_blocks((0,), adj, jnp.zeros(refs[-1].shape, f32), refs[:-1])


def product_next(adj, before, *refs):
    refs[-1][...] = add_blocks((1, 3), adj, before[...], refs[:-1])


def product_last(adj, before, degree, *refs):
    pieces, outs, mean = refs[:-5], refs[-5:-1], refs[-1]
    feat = here()[1]
    total = add_blocks((2,), adj, before[...], pieces)
    mean[...] = total / degree[:, :1]
    for s in range(NF):
        q = lax.rem(feat + s, NF)
        outs[s][...] = mean[pl.ds(pl.multiple_of(q * SHARE, SHARE), SHARE), :].astype(bf16)


def blocks_cost(pieces):
    n = sum(p.shape[0] for p in pieces)
    return cost(2 * 384 * 384 * 256 * n, n * 450e3)


def hidden_kernel(g0, g1, g2, g3, n0, n1, n2, n3, f0, f1, f2, f3, z_out, hid):
    feat = here()[1]
    gs = (g0, g1, g2, g3)
    total = jnp.zeros((SHARE, 192), f32)
    for parts in ((n0, n1, n2, n3), (f0, f1, f2, f3)):
        pre = jnp.zeros((SHARE, 512), f32)
        for s in range(NF):
            pre = pre + jnp.dot(gs[s][...], parts[s][0:192, :], preferred_element_type=f32)
        hid[...] = pre
        for s in range(NF):
            owner = lax.rem(feat + NF - s, NF)
            lanes = pl.ds(pl.multiple_of(owner * TILE, TILE), TILE)
            b = parts[s][240:256, 0:TILE].astype(f32)
            bias = b[0:1] + b[1:2] + b[2:3]
            unit = jnp.maximum(hid[:, lanes] + bias, 0.0).astype(bf16)
            w = parts[s][192:240, :]
            w = jnp.concatenate([w[:, k * TILE : (k + 1) * TILE] for k in range(NF)], axis=0)
            total = total + lax.dot_general(unit, w, NT, preferred_element_type=f32)
    z_out[0:SHARE, :] = total[:, :TILE].astype(bf16)
    tail = total[:, TILE : TILE + 32]
    packed = jnp.concatenate([tail[0:32], tail[32:64], tail[64:96], jnp.zeros((32, 32), f32)], axis=1)
    z_out[SHARE:, :] = packed.astype(bf16)


def scores_kernel(adj2, degree, *refs):
    pieces, out, z_all = refs[:-2], refs[-2], refs[-1]
    me, _ = here()
    for p, piece in enumerate(pieces):
        for b in range(NF):
            src = source(me, SHIFTS[b], SHIFTS[p // 2], lax.rem(me + p, 2))
            src = pl.multiple_of(src * TILE, TILE)
            z_all[pl.ds(src, TILE), :TILE] = piece[b]
            tail = piece[b, SHARE:, :].astype(f32)
            tail = jnp.concatenate([tail[:, 0:32], tail[:, 32:64], tail[:, 64:96], jnp.zeros((32, 32), f32)], axis=0)
            tail = jnp.concatenate([tail, jnp.zeros((TILE, 96), f32)], axis=1)
            z_all[pl.ds(src, TILE), TILE:] = tail.astype(bf16)
    part = jnp.dot(adj2[...], z_all[...], preferred_element_type=f32) / degree[:, :1]
    out[...] = part.T[0:160].astype(bf16)


def sum_kernel(p0, p1, p2, p3, b_out, out):
    total = (p0[...].astype(f32) + p2[...].astype(f32)) + (p1[...].astype(f32) + p3[...].astype(f32))
    bias = jnp.broadcast_to(b_out[...], (TILE, 256)).T[:, 0:1]
    out[...] = total[0:CLS] + bias[0:CLS]


def local(features, counts, tile_mask, w_in, b_in, w_out, b_out):
    adj, adj2, degree = make_adjacency(tile_mask, counts)

    mine = features.T
    ring = [first_axis(mine, s) for s in (1, 3, 2)]
    four = pl.pallas_call(
        stack_kernel, out_shape=jax.ShapeDtypeStruct((NF, 192, ROWS), bf16),
        in_specs=[VM] * 4 + [pl.BlockSpec(memory_space=pl.ANY)], out_specs=VM,
        compiler_params=params(), cost_estimate=cost(1e5, 1.2e6), name="stack",
    )(mine, *ring, degree)
    rows = {t: second_axis(four, t) for t in (1, 3, 2)}

    near, far = pl.pallas_call(
        pack_kernel, out_shape=[jax.ShapeDtypeStruct((256, 512), bf16)] * 2,
        in_specs=[VM] * 3 + [pl.BlockSpec(memory_space=pl.ANY)], out_specs=[VM] * 2,
        compiler_params=params(), cost_estimate=cost(1e5, 1.2e6), name="pack",
    )(w_in, w_out.T, b_in.reshape(1, 256), four)
    near = [near] + [along_feat(near, s) for s in (1, 2, 3)]
    far = [far] + [swap(w) for w in near[1:]]

    total_shape = jax.ShapeDtypeStruct((ROWS, 192), f32)
    pieces = [four, swap(four)]
    total = pl.pallas_call(
        product_first, out_shape=total_shape, in_specs=[VM] * 3, out_specs=VM,
        compiler_params=params(), cost_estimate=blocks_cost(pieces), name="product_first",
    )(adj, *pieces)
    total, rows[2] = lax.optimization_barrier((total, rows[2]))
    pieces = [rows[1], swap(rows[1]), rows[3], swap(rows[3])]
    total = pl.pallas_call(
        product_next, out_shape=total_shape, in_specs=[VM] * 6, out_specs=VM,
        compiler_params=params(), cost_estimate=blocks_cost(pieces), name="product_next",
    )(adj, total, *pieces)
    pieces = [rows[2], swap(rows[2])]
    means = pl.pallas_call(
        product_last, out_shape=[jax.ShapeDtypeStruct((SHARE, 192), bf16)] * NF,
        in_specs=[VM] * 5, out_specs=[VM] * NF,
        scratch_shapes=[pltpu.VMEM((ROWS, 192), f32)],
        compiler_params=params(), cost_estimate=blocks_cost(pieces), name="product_last",
    )(adj, total, degree, *pieces)

    g = [means[0]] + [along_feat(means[s], s) for s in (1, 2, 3)]
    z_block = pl.pallas_call(
        hidden_kernel, out_shape=jax.ShapeDtypeStruct((TILE, TILE), bf16),
        in_specs=[VM] * 12, out_specs=VM,
        scratch_shapes=[pltpu.VMEM((SHARE, 512), f32)],
        compiler_params=params(), cost_estimate=cost(2 * 96 * 768 * 1024, 2e6), name="hidden",
    )(*g, *near, *far)

    z_four = jnp.stack([z_block] + [first_axis(z_block, s) for s in (1, 3, 2)])
    z_rows = [z_four] + [second_axis(z_four, t) for t in (1, 3, 2)]
    z_pieces = [z for row in z_rows for z in (row, swap(row))]
    part = pl.pallas_call(
        scores_kernel, out_shape=jax.ShapeDtypeStruct((160, ROWS), bf16),
        in_specs=[VM] * 10, out_specs=VM,
        scratch_shapes=[pltpu.VMEM((NV * TILE, 256), bf16)],
        compiler_params=params(), cost_estimate=cost(2 * 384 * 4096 * 256, 5e6), name="scores",
    )(adj2, degree, *z_pieces)
    parts = [part] + [along_feat(part, s) for s in (1, 2, 3)]
    return pl.pallas_call(
        sum_kernel, out_shape=jax.ShapeDtypeStruct((CLS, ROWS), f32),
        in_specs=[VM] * 5, out_specs=VM,
        compiler_params=params(), cost_estimate=cost(3e5, 8e5), name="sum",
    )(*parts, jnp.pad(b_out, (0, 256 - CLS)).reshape(1, 256)).T


def solution(mesh):
    placed = (
        P("vert", "feat"),
        P("vert", None),
        P("vert", None),
        P("feat", None),
        P("feat"),
        P("feat", None),
        P(),
    )
    return jax.shard_map(
        local, mesh=mesh, in_specs=placed, out_specs=P("vert", None), check_vma=False
    )
```

time: 105 us -> 104 us (level)
  starting transfers between devices: 45.4 us -> 57.8 us
  local copies, waits for them, and re-layouts: 12.2 us -> 0.71 us
  Pallas kernels: 22.9 us -> 20.3 us
  waiting for transfers between devices: 22.8 us -> 24.8 us
    ppermute x6 -> x11, starting transfers between devices: 14.2 us -> 23.4 us  [swap(): return lax.ppermute(value, 'vert', positions(lambda x, z, c: (x, z, 1 - c)))]
    unnamed x19 -> x12, local copies, waits for them, and re-layouts: 9.33 us -> 0.7 us
    ppermute x9, starting transfers between devices: 11.1 us -> 17.3 us  [along_feat(): lax.ppermute(value, 'feat', [(i, (i + shift) % NF) for i in range(NF)])]
    ppermute x6, starting transfers between devices: 10.2 us -> 7.13 us  [second_axis(): lax.ppermute(value, 'vert', positions(lambda x, z, c: (x + shift * c, z +...]
    ppermute x9, waiting for transfers between devices: 14 us -> 16.3 us  [along_feat(): lax.ppermute(value, 'feat', [(i, (i + shift) % NF) for i in range(NF)])]
    reshape x4 -> x0, local copies, waits for them, and re-layouts: 1.53 us -> none  [the longest x3 1.52 us: local(): w_in.reshape(192, 4, 2, TILE).transpose(2, 0, 1, 3).reshape(2, 192, 512)]
    pallas_call x1, Pallas kernels: 2.27 us -> 1.04 us  [local(): pl.pallas_call(product_last, out_shape=[jax.ShapeDtypeStruct((SHARE, 192)...]
    pallas_call x5 -> x7, Pallas kernels: 18.9 us -> 18.2 us  [the longest x1 12.9 us: make_adjacency(): pl.pallas_call(adjacency_kernel, in_specs=[SM, pl.BlockSpec(memory_space=...]
  transfers between devices with their start and end apart: 27 -> 32, of which waited for: 13 -> 11; matrix products, arithmetic and copies ran while one was open for 4% -> 0% of each run, Pallas kernels for 18% -> 16%
where the time goes in v2:
time: 104 us
  starting transfers between devices  57.8 us (56%)
  waiting for transfers between devices  24.8 us (24%)
  Pallas kernels  20.3 us (20%)
    ppermute x11, starting transfers between devices, swap(): return lax.ppermute(value, 'vert', positions(lambda x, z, c: (x, z, 1 - c)))  23.4 us
    ppermute x9, starting transfers between devices, along_feat(): lax.ppermute(value, 'feat', [(i, (i + shift) % NF) for i in range(NF)])  17.3 us
    ppermute x9, waiting for transfers between devices, along_feat(): lax.ppermute(value, 'feat', [(i, (i + shift) % NF) for i in range(NF)])  16.3 us
    pallas_call x1, Pallas kernels, make_adjacency(): pl.pallas_call(adjacency_kernel, in_specs=[SM, pl.BlockSpec(memory_space=...  12.9 us
    ppermute x6, starting transfers between devices, first_axis(): lax.ppermute(value, 'vert', positions(lambda x, z, c: (x + shift * (1 - c...  9.99 us
    ppermute x6, starting transfers between devices, second_axis(): lax.ppermute(value, 'vert', positions(lambda x, z, c: (x + shift * c, z +...  7.13 us
    ppermute x6, waiting for transfers between devices, second_axis(): lax.ppermute(value, 'vert', positions(lambda x, z, c: (x + shift * c, z +...  4.03 us
    ppermute x6, waiting for transfers between devices, first_axis(): lax.ppermute(value, 'vert', positions(lambda x, z, c: (x + shift * (1 - c...  3.48 us
  transfers between devices with their start and end apart: 32, of which 11 were waited for; matrix products, arithmetic and copies ran while one was open for 0% of the time, Pallas kernels for 16%

profile of v2, /device:TPU:1, one launch (start us, length us, event | category | flops | bytes accessed | tf_op | source)
XLA Modules:
  0.0 103.9 jit_solution(5609689808148851040)
XLA Ops:
  0.0 2.5 %collective-permute-start = (bf16[192,384]{1,0:T(8,128)(2,1)}, bf16[192,384]{1,0:T(8,128)(2,1)S(1)}, u32[]{:S(2)}, u32[]{:S(2)}) collective-permute-start(bf16[192,384]{1,0:T(8,128)(2,1)} %bitcast.9), channel_id=1, source_target_pairs={{0,8},{1,3},{2,10},{3,5},{4,12},{5,7},{6,14},{7,1},{8,16},{9,11},{... | collective-permute-start | bytes 442376 | tf_op jit(solution)/shard_map/ppermute | solution.py:55
  2.6 2.2 %collective-permute-start.1 = (bf16[192,384]{1,0:T(8,128)(2,1)}, bf16[192,384]{1,0:T(8,128)(2,1)S(1)}, u32[]{:S(2)}, u32[]{:S(2)}) collective-permute-start(bf16[192,384]{1,0:T(8,128)(2,1)} %bitcast.10), channel_id=1, source_target_pairs={{0,24},{1,7},{2,26},{3,1},{4,28},{5,3},{6,30},{7,5},{8,0},{9,15},{... | collective-permute-start | bytes 442376 | tf_op jit(solution)/shard_map/ppermute | solution.py:55
  4.8 1.2 %collective-permute-start.2 = (bf16[192,384]{1,0:T(8,128)(2,1)}, bf16[192,384]{1,0:T(8,128)(2,1)S(1)}, u32[]{:S(2)}, u32[]{:S(2)}) collective-permute-start(bf16[192,384]{1,0:T(8,128)(2,1)} %bitcast.11), channel_id=1, source_target_pairs={{0,16},{1,5},{2,18},{3,7},{4,20},{5,1},{6,22},{7,3},{8,24},{9,13},... | collective-permute-start | bytes 442376 | tf_op jit(solution)/shard_map/ppermute | solution.py:55
  6.0 0.7 copy-done.3
  6.7 12.9 %adjacency.1 = (bf16[384,12288]{1,0:T(8,128)(2,1)S(1)}, bf16[384,4096]{1,0:T(8,128)(2,1)S(1)}, f32[384,128]{1,0:T(8,128)S(1)}) custom-call(s32[3,96]{1,0:T(4,128)S(1)} %copy-done.3, s32[384,12288]{1,0:T(8,128)} %counts.1), custom_call_target="tpu_custom_call" | custom-call | flops 2400000000 | bytes 31000000 | tf_op jit(solution)/shard_map/adjacency/pallas_call | solution.py:121
  19.6 0.0 collective-permute-done.b
  19.6 0.0 collective-permute-done.2.d
  19.6 0.1 stack.21.refs_0_.after
  19.7 1.3 %collective-permute-start.5 = (bf16[4,192,384]{2,1,0:T(8,128)(2,1)S(1)}, bf16[4,192,384]{2,1,0:T(8,128)(2,1)S(1)}, u32[]{:S(2)}, u32[]{:S(2)}) collective-permute-start(bf16[4,192,384]{2,1,0:T(8,128)(2,1)S(1)} %stack.21.refs_0_.after), channel_id=1, source_target_pairs={{0,2},{1,9},{2,4},{3,11},{4,6},{5,13},{6,0},{7,15},{8,10},{9,17},{... | collective-permute-start | bytes 1769480 | tf_op jit(solution)/shard_map/ppermute | solution.py:59
  21.0 1.5 %collective-permute-start.7 = (bf16[4,192,384]{2,1,0:T(8,128)(2,1)S(1)}, bf16[4,192,384]{2,1,0:T(8,128)(2,1)S(1)}, u32[]{:S(2)}, u32[]{:S(2)}) collective-permute-start(bf16[4,192,384]{2,1,0:T(8,128)(2,1)S(1)} %stack.21.refs_0_.after), channel_id=1, source_target_pairs={{0,6},{1,25},{2,0},{3,27},{4,2},{5,29},{6,4},{7,31},{8,14},{9,1},{... | collective-permute-start | bytes 1769480 | tf_op jit(solution)/shard_map/ppermute | solution.py:59
  22.4 2.1 %collective-permute-start.3 = (bf16[4,192,384]{2,1,0:T(8,128)(2,1)S(1)}, bf16[4,192,384]{2,1,0:T(8,128)(2,1)S(1)}, u32[]{:S(2)}, u32[]{:S(2)}) collective-permute-start(bf16[4,192,384]{2,1,0:T(8,128)(2,1)S(1)} %stack.21.refs_0_.after), channel_id=1, source_target_pairs={{0,1},{1,0},{2,3},{3,2},{4,5},{5,4},{6,7},{7,6},{8,9},{9,8},{10,11... | collective-permute-start | bytes 1769480 | tf_op jit(solution)/shard_map/ppermute | solution.py:63
  24.5 1.4 %collective-permute-start.4 = (bf16[4,192,384]{2,1,0:T(8,128)(2,1)S(1)}, bf16[4,192,384]{2,1,0:T(8,128)(2,1)S(1)}, u32[]{:S(2)}, u32[]{:S(2)}) collective-permute-start(bf16[4,192,384]{2,1,0:T(8,128)(2,1)S(1)} %stack.21.refs_0_.after), channel_id=1, source_target_pairs={{0,4},{1,17},{2,6},{3,19},{4,0},{5,21},{6,2},{7,23},{8,12},{9,25},... | collective-permute-start | bytes 1769480 | tf_op jit(solution)/shard_map/ppermute | solution.py:59
  26.0 4.0 %collective-permute-done.5.refs_0_ = bf16[4,192,384]{2,1,0:T(8,128)(2,1)S(1)} collective-permute-done((bf16[4,192,384]{2,1,0:T(8,128)(2,1)S(1)}, bf16[4,192,384]{2,1,0:T(8,128)(2,1)S(1)}, u32[]{:S(2)}, u32[]{:S(2)}) %collective-permute-start.5) | collective-permute-done | bytes 589856 | tf_op jit(solution)/shard_map/ppermute | solution.py:59
  30.0 2.3 %collective-permute-start.6 = (bf16[4,192,384]{2,1,0:T(8,128)(2,1)S(1)}, bf16[4,192,384]{2,1,0:T(8,128)(2,1)S(1)}, u32[]{:S(2)}, u32[]{:S(2)}) collective-permute-start(bf16[4,192,384]{2,1,0:T(8,128)(2,1)S(1)} %collective-permute-done.5.refs_0_), channel_id=1, source_target_pairs={{0,1},{1,0},{2,3},{3,2},{4,5},{5,4},{6,7},{7,6},{8,9},{9,8},{10,11... | collective-permute-start | bytes 1769480 | tf_op jit(solution)/shard_map/ppermute | solution.py:63
  32.3 0.0 collective-permute-done.7.refs_2_
  32.3 6.0 %collective-permute-start.8 = (bf16[4,192,384]{2,1,0:T(8,128)(2,1)S(1)}, bf16[4,192,384]{2,1,0:T(8,128)(2,1)S(1)}, u32[]{:S(2)}, u32[]{:S(2)}) collective-permute-start(bf16[4,192,384]{2,1,0:T(8,128)(2,1)S(1)} %collective-permute-done.7.refs_2_), channel_id=1, source_target_pairs={{0,1},{1,0},{2,3},{3,2},{4,5},{5,4},{6,7},{7,6},{8,9},{9,8},{10,11... | collective-permute-start | bytes 1769480 | tf_op jit(solution)/shard_map/ppermute | solution.py:63
  38.3 0.1 pack.1
  38.4 1.4 %collective-permute-start.13 = (bf16[256,512]{1,0:T(8,128)(2,1)S(1)}, bf16[256,512]{1,0:T(8,128)(2,1)S(1)}, u32[]{:S(2)}, u32[]{:S(2)}) collective-permute-start(bf16[256,512]{1,0:T(8,128)(2,1)S(1)} %get-tuple-element.25.n0), channel_id=1, source_target_pairs={{0,32},{32,64},{64,96},{96,0},{1,33},{33,65},{65,97},{97,1},{2,34}... | collective-permute-start | bytes 786440 | tf_op jit(solution)/shard_map/ppermute | solution.py:67
  39.8 0.0 collective-permute-done.3.refs_1_
  39.8 1.0 product_first.1.before
  40.8 0.0 collective-permute-done.4.refs_0_
  40.8 0.4 collective-permute-start.9
  41.2 2.6 %collective-permute-start.14 = (bf16[256,512]{1,0:T(8,128)(2,1)S(1)}, bf16[256,512]{1,0:T(8,128)(2,1)S(1)}, u32[]{:S(2)}, u32[]{:S(2)}) collective-permute-start(bf16[256,512]{1,0:T(8,128)(2,1)S(1)} %get-tuple-element.25.n0), channel_id=1, source_target_pairs={{0,64},{32,96},{64,0},{96,32},{1,65},{33,97},{65,1},{97,33},{2,66}... | collective-permute-start | bytes 786440 | tf_op jit(solution)/shard_map/ppermute | solution.py:67
  43.8 4.0 %collective-permute-done.13.n1 = bf16[256,512]{1,0:T(8,128)(2,1)S(1)} collective-permute-done((bf16[256,512]{1,0:T(8,128)(2,1)S(1)}, bf16[256,512]{1,0:T(8,128)(2,1)S(1)}, u32[]{:S(2)}, u32[]{:S(2)}) %collective-permute-start.13) | collective-permute-done | bytes 262176 | tf_op jit(solution)/shard_map/ppermute | solution.py:67
  47.8 1.4 %collective-permute-start.15 = (bf16[256,512]{1,0:T(8,128)(2,1)S(1)}, bf16[256,512]{1,0:T(8,128)(2,1)S(1)}, u32[]{:S(2)}, u32[]{:S(2)}) collective-permute-start(bf16[256,512]{1,0:T(8,128)(2,1)S(1)} %get-tuple-element.25.n0), channel_id=1, source_target_pairs={{0,96},{32,0},{64,32},{96,64},{1,97},{33,1},{65,33},{97,65},{2,98}... | collective-permute-start | bytes 786440 | tf_op jit(solution)/shard_map/ppermute | solution.py:67
  49.2 5.3 %collective-permute-done.14.n2 = bf16[256,512]{1,0:T(8,128)(2,1)S(1)} collective-permute-done((bf16[256,512]{1,0:T(8,128)(2,1)S(1)}, bf16[256,512]{1,0:T(8,128)(2,1)S(1)}, u32[]{:S(2)}, u32[]{:S(2)}) %collective-permute-start.14) | collective-permute-done | bytes 262176 | tf_op jit(solution)/shard_map/ppermute | solution.py:67
  54.5 0.8 collective-permute-start.16
  55.3 0.0 collective-permute-done.15.n3
  55.3 1.2 %collective-permute-start.17 = (bf16[256,512]{1,0:T(8,128)(2,1)S(1)}, bf16[256,512]{1,0:T(8,128)(2,1)S(1)}, u32[]{:S(2)}, u32[]{:S(2)}) collective-permute-start(bf16[256,512]{1,0:T(8,128)(2,1)S(1)} %collective-permute-done.14.n2), channel_id=1, source_target_pairs={{0,1},{1,0},{2,3},{3,2},{4,5},{5,4},{6,7},{7,6},{8,9},{9,8},{10,11... | collective-permute-start | bytes 786440 | tf_op jit(solution)/shard_map/ppermute | solution.py:63
  56.5 0.0 collective-permute-start.18
  56.5 1.8 %product_next.1.before = f32[384,192]{1,0:T(8,128)S(1)} custom-call(bf16[384,12288]{1,0:T(8,128)(2,1)S(1)} %get-tuple-element.18.adj, f32[384,192]{1,0:T(8,128)S(1)} %product_first.1.before, bf16[4,192,384]{2,1,0:T(8,128)(2,1)S(1)} %collective-permute-done.5.refs_0_, bf16[4,192,384]{2,1,0:T(8,128)(2,1)S(1)} %collective-permute-done.6.refs_1_, ...), custom_call_target="tpu_custom_call" | custom-call | flops 1207959552 | bytes 7200000 | tf_op jit(solution)/shard_map/product_next/pallas_call | solution.py:271
  58.3 0.0 copy-start.5
  58.4 0.0 collective-permute-done.9.refs_1_
  58.4 1.0 %product_last.1 = (bf16[96,192]{1,0:T(8,128)(2,1)S(1)}, bf16[96,192]{1,0:T(8,128)(2,1)S(1)}, bf16[96,192]{1,0:T(8,128)(2,1)S(1)}, bf16[96,192]{1,0:T(8,128)(2,1)S(1)}) custom-call(bf16[384,12288]{1,0:T(8,128)(2,1)S(1)} %get-tuple-element.18.adj, f32[384,192]{1,0:T(8,128)S(1)} %product_next.1.before, f32[384,128]{1,0:T(8,128)S(1)} %get-tuple-element.17.after.degree, ...), custom_call_target="tpu_custom_call" | custom-call | flops 603979776 | bytes 3600000 | tf_op jit(solution)/shard_map/product_last/pallas_call | solution.py:276
  59.4 3.6 %collective-permute-start.10 = (bf16[96,192]{1,0:T(8,128)(2,1)S(1)}, bf16[96,192]{1,0:T(8,128)(2,1)S(1)}, u32[]{:S(2)}, u32[]{:S(2)}) collective-permute-start(bf16[96,192]{1,0:T(8,128)(2,1)S(1)} %get-tuple-element.22), channel_id=1, source_target_pairs={{0,32},{32,64},{64,96},{96,0},{1,33},{33,65},{65,97},{97,1},{2,34}... | collective-permute-start | bytes 110600 | tf_op jit(solution)/shard_map/ppermute | solution.py:67
  63.0 2.2 %collective-permute-start.11 = (bf16[96,192]{1,0:T(8,128)(2,1)S(1)}, bf16[96,192]{1,0:T(8,128)(2,1)S(1)}, u32[]{:S(2)}, u32[]{:S(2)}) collective-permute-start(bf16[96,192]{1,0:T(8,128)(2,1)S(1)} %get-tuple-element.23), channel_id=1, source_target_pairs={{0,64},{32,96},{64,0},{96,32},{1,65},{33,97},{65,1},{97,33},{2,66}... | collective-permute-start | bytes 110600 | tf_op jit(solution)/shard_map/ppermute | solution.py:67
  65.2 2.0 %collective-permute-start.12 = (bf16[96,192]{1,0:T(8,128)(2,1)S(1)}, bf16[96,192]{1,0:T(8,128)(2,1)S(1)}, u32[]{:S(2)}, u32[]{:S(2)}) collective-permute-start(bf16[96,192]{1,0:T(8,128)(2,1)S(1)} %get-tuple-element.24), channel_id=1, source_target_pairs={{0,96},{32,0},{64,32},{96,64},{1,97},{33,1},{65,33},{97,65},{2,98}... | collective-permute-start | bytes 110600 | tf_op jit(solution)/shard_map/ppermute | solution.py:67
  67.2 0.0 collective-permute-done.17.f2
  67.2 0.0 collective-permute-done.18.f3
  67.2 0.0 collective-permute-done.10.g1
  67.2 0.6 collective-permute-done.11.g2
  67.8 0.6 collective-permute-done.12.g3
  68.4 1.1 %hidden.1 = bf16[128,128]{1,0:T(8,128)(2,1)S(1)} custom-call(bf16[96,192]{1,0:T(8,128)(2,1)S(1)} %get-tuple-element.21.g0, bf16[96,192]{1,0:T(8,128)(2,1)S(1)} %collective-permute-done.10.g1, bf16[96,192]{1,0:T(8,128)(2,1)S(1)} %collective-permute-done.11.g2, bf16[96,192]{1,0:T(8,128)(2,1)S(1)} %collective-permute-done.12.g3, ...), custom_call_target="tpu_custom_call" | custom-call | flops 150994944 | bytes 2000000 | tf_op jit(solution)/shard_map/hidden/pallas_call | solution.py:284
  69.5 2.0 %collective-permute-start.21 = (bf16[128,128]{1,0:T(8,128)(2,1)S(1)}, bf16[128,128]{1,0:T(8,128)(2,1)S(1)}, u32[]{:S(2)}, u32[]{:S(2)}) collective-permute-start(bf16[128,128]{1,0:T(8,128)(2,1)S(1)} %hidden.1), channel_id=1, source_target_pairs={{0,16},{1,5},{2,18},{3,7},{4,20},{5,1},{6,22},{7,3},{8,24},{9,13},... | collective-permute-start | bytes 98312 | tf_op jit(solution)/shard_map/ppermute | solution.py:55
  71.5 1.5 %collective-permute-start.20 = (bf16[128,128]{1,0:T(8,128)(2,1)S(1)}, bf16[128,128]{1,0:T(8,128)(2,1)S(1)}, u32[]{:S(2)}, u32[]{:S(2)}) collective-permute-start(bf16[128,128]{1,0:T(8,128)(2,1)S(1)} %hidden.1), channel_id=1, source_target_pairs={{0,24},{1,7},{2,26},{3,1},{4,28},{5,3},{6,30},{7,5},{8,0},{9,15},{... | collective-permute-start | bytes 98312 | tf_op jit(solution)/shard_map/ppermute | solution.py:55
  73.0 0.5 collective-permute-start.19
  73.5 0.3 collective-permute-done.21
  73.8 1.6 %collective-permute-done.20 = bf16[128,128]{1,0:T(8,128)(2,1)S(1)} collective-permute-done((bf16[128,128]{1,0:T(8,128)(2,1)S(1)}, bf16[128,128]{1,0:T(8,128)(2,1)S(1)}, u32[]{:S(2)}, u32[]{:S(2)}) %collective-permute-start.20) | collective-permute-done | bytes 32800 | tf_op jit(solution)/shard_map/ppermute | solution.py:55
  75.5 1.5 %collective-permute-done.19 = bf16[128,128]{1,0:T(8,128)(2,1)S(1)} collective-permute-done((bf16[128,128]{1,0:T(8,128)(2,1)S(1)}, bf16[128,128]{1,0:T(8,128)(2,1)S(1)}, u32[]{:S(2)}, u32[]{:S(2)}) %collective-permute-start.19) | collective-permute-done | bytes 32800 | tf_op jit(solution)/shard_map/ppermute | solution.py:55
  77.0 0.4 collective-permute-start.23
  77.4 2.4 %collective-permute-start.25 = (bf16[4,128,128]{2,1,0:T(8,128)(2,1)S(1)}, bf16[4,128,128]{2,1,0:T(8,128)(2,1)S(1)}, u32[]{:S(2)}, u32[]{:S(2)}) collective-permute-start(bf16[4,128,128]{2,1,0:T(8,128)(2,1)S(1)} %pad_maximum_fusion.refs_0_), channel_id=1, source_target_pairs={{0,6},{1,25},{2,0},{3,27},{4,2},{5,29},{6,4},{7,31},{8,14},{9,1},{... | collective-permute-start | bytes 393224 | tf_op jit(solution)/shard_map/ppermute | solution.py:59
  79.8 0.2 collective-permute-start.27
  80.0 5.4 %collective-permute-start.22 = (bf16[4,128,128]{2,1,0:T(8,128)(2,1)S(1)}, bf16[4,128,128]{2,1,0:T(8,128)(2,1)S(1)}, u32[]{:S(2)}, u32[]{:S(2)}) collective-permute-start(bf16[4,128,128]{2,1,0:T(8,128)(2,1)S(1)} %pad_maximum_fusion.refs_0_), channel_id=1, source_target_pairs={{0,1},{1,0},{2,3},{3,2},{4,5},{5,4},{6,7},{7,6},{8,9},{9,8},{10,11... | collective-permute-start | bytes 393224 | tf_op jit(solution)/shard_map/ppermute | solution.py:63
  85.4 1.5 %collective-permute-start.24 = (bf16[4,128,128]{2,1,0:T(8,128)(2,1)S(1)}, bf16[4,128,128]{2,1,0:T(8,128)(2,1)S(1)}, u32[]{:S(2)}, u32[]{:S(2)}) collective-permute-start(bf16[4,128,128]{2,1,0:T(8,128)(2,1)S(1)} %collective-permute-done.23.refs_2_), channel_id=1, source_target_pairs={{0,1},{1,0},{2,3},{3,2},{4,5},{5,4},{6,7},{7,6},{8,9},{9,8},{10,11... | collective-permute-start | bytes 393224 | tf_op jit(solution)/shard_map/ppermute | solution.py:63
  86.8 0.0 collective-permute-done.25.refs_4_
  86.8 0.0 collective-permute-start.26
  86.8 3.8 %collective-permute-start.28 = (bf16[4,128,128]{2,1,0:T(8,128)(2,1)S(1)}, bf16[4,128,128]{2,1,0:T(8,128)(2,1)S(1)}, u32[]{:S(2)}, u32[]{:S(2)}) collective-permute-start(bf16[4,128,128]{2,1,0:T(8,128)(2,1)S(1)} %collective-permute-done.27.refs_6_), channel_id=1, source_target_pairs={{0,1},{1,0},{2,3},{3,2},{4,5},{5,4},{6,7},{7,6},{8,9},{9,8},{10,11... | collective-permute-start | bytes 393224 | tf_op jit(solution)/shard_map/ppermute | solution.py:63
  90.6 1.0 collective-permute-done.28.refs_7_
  91.6 1.5 %scores.1.p0 = bf16[160,384]{1,0:T(8,128)(2,1)S(1)} custom-call(bf16[384,4096]{1,0:T(8,128)(2,1)S(1)} %get-tuple-element.16.adj2, f32[384,128]{1,0:T(8,128)S(1)} %get-tuple-element.17.after.degree, bf16[4,128,128]{2,1,0:T(8,128)(2,1)S(1)} %pad_maximum_fusion.refs_0_, bf16[4,128,128]{2,1,0:T(8,128)(2,1)S(1)} %collective-permute-done.22.refs_1_, ...), custom_call_target="tpu_custom_call" | custom-call | flops 805306368 | bytes 5000000 | tf_op jit(solution)/shard_map/scores/pallas_call | solution.py:294
  93.1 1.0 collective-permute-start.29
  94.1 3.2 %collective-permute-start.30 = (bf16[160,384]{1,0:T(8,128)(2,1)S(1)}, bf16[160,384]{1,0:T(8,128)(2,1)S(1)}, u32[]{:S(2)}, u32[]{:S(2)}) collective-permute-start(bf16[160,384]{1,0:T(8,128)(2,1)S(1)} %scores.1.p0), channel_id=1, source_target_pairs={{0,64},{32,96},{64,0},{96,32},{1,65},{33,97},{65,1},{97,33},{2,66}... | collective-permute-start | bytes 368648 | tf_op jit(solution)/shard_map/ppermute | solution.py:67
  97.3 2.2 %collective-permute-done.29.p1 = bf16[160,384]{1,0:T(8,128)(2,1)S(1)} collective-permute-done((bf16[160,384]{1,0:T(8,128)(2,1)S(1)}, bf16[160,384]{1,0:T(8,128)(2,1)S(1)}, u32[]{:S(2)}, u32[]{:S(2)}) %collective-permute-start.29) | collective-permute-done | bytes 122912 | tf_op jit(solution)/shard_map/ppermute | solution.py:67
  99.4 3.5 %collective-permute-done.30.p2 = bf16[160,384]{1,0:T(8,128)(2,1)S(1)} collective-permute-done((bf16[160,384]{1,0:T(8,128)(2,1)S(1)}, bf16[160,384]{1,0:T(8,128)(2,1)S(1)}, u32[]{:S(2)}, u32[]{:S(2)}) %collective-permute-start.30) | collective-permute-done | bytes 122912 | tf_op jit(solution)/shard_map/ppermute | solution.py:67
  103.0 0.9 sum.1
  (23 shorter events, 0.1 us)
Async XLA Ops:
  0.0 38.3 %copy-start.4 = (f32[256]{0:T(256)S(1)}, f32[256]{0:T(256)}, u32[]{:S(2)}) copy-start(f32[256]{0:T(256)} %param.11) | copy-start | bytes 3076
  0.0 19.6 %copy-start.1 = (bf16[384,192]{0,1:T(8,128)(2,1)S(1)}, bf16[384,192]{0,1:T(8,128)(2,1)}, u32[]{:S(2)}) copy-start(bf16[384,192]{0,1:T(8,128)(2,1)} %param.7) | copy-start | bytes 442372
  0.0 38.3 %copy-start = (bf16[192,1024]{1,0:T(8,128)(2,1)S(1)}, bf16[192,1024]{1,0:T(8,128)(2,1)}, u32[]{:S(2)}) copy-start(bf16[192,1024]{1,0:T(8,128)(2,1)} %w_in.1) | copy-start | bytes 1179652
  0.0 38.3 %copy-start.2 = (bf16[256,153]{0,1:T(8,128)(2,1)S(1)}, bf16[256,153]{0,1:T(8,128)(2,1)}, u32[]{:S(2)}) copy-start(bf16[256,153]{0,1:T(8,128)(2,1)} %param.12) | copy-start | bytes 235012
  0.0 19.6 %collective-permute-start = (bf16[192,384]{1,0:T(8,128)(2,1)}, bf16[192,384]{1,0:T(8,128)(2,1)S(1)}, u32[]{:S(2)}, u32[]{:S(2)}) collective-permute-start(bf16[192,384]{1,0:T(8,128)(2,1)} %bitcast.9), channel_id=1, source_target_pairs={{0,8},{1,3},{2,10},{3,5},{4,12},{5,7},{6,14},{7,1},{8,16},{9,11},{... | collective-permute-start | bytes 442376 | tf_op jit(solution)/shard_map/ppermute | solution.py:55
  2.6 17.0 %collective-permute-start.1 = (bf16[192,384]{1,0:T(8,128)(2,1)}, bf16[192,384]{1,0:T(8,128)(2,1)S(1)}, u32[]{:S(2)}, u32[]{:S(2)}) collective-permute-start(bf16[192,384]{1,0:T(8,128)(2,1)} %bitcast.10), channel_id=1, source_target_pairs={{0,24},{1,7},{2,26},{3,1},{4,28},{5,3},{6,30},{7,5},{8,0},{9,15},{... | collective-permute-start | bytes 442376 | tf_op jit(solution)/shard_map/ppermute | solution.py:55
  4.8 14.8 %collective-permute-start.2 = (bf16[192,384]{1,0:T(8,128)(2,1)}, bf16[192,384]{1,0:T(8,128)(2,1)S(1)}, u32[]{:S(2)}, u32[]{:S(2)}) collective-permute-start(bf16[192,384]{1,0:T(8,128)(2,1)} %bitcast.11), channel_id=1, source_target_pairs={{0,16},{1,5},{2,18},{3,7},{4,20},{5,1},{6,22},{7,3},{8,24},{9,13},... | collective-permute-start | bytes 442376 | tf_op jit(solution)/shard_map/ppermute | solution.py:55
  6.0 0.7 copy-start.3
  19.7 10.3 %collective-permute-start.5 = (bf16[4,192,384]{2,1,0:T(8,128)(2,1)S(1)}, bf16[4,192,384]{2,1,0:T(8,128)(2,1)S(1)}, u32[]{:S(2)}, u32[]{:S(2)}) collective-permute-start(bf16[4,192,384]{2,1,0:T(8,128)(2,1)S(1)} %stack.21.refs_0_.after), channel_id=1, source_target_pairs={{0,2},{1,9},{2,4},{3,11},{4,6},{5,13},{6,0},{7,15},{8,10},{9,17},{... | collective-permute-start | bytes 1769480 | tf_op jit(solution)/shard_map/ppermute | solution.py:59
  21.0 11.4 %collective-permute-start.7 = (bf16[4,192,384]{2,1,0:T(8,128)(2,1)S(1)}, bf16[4,192,384]{2,1,0:T(8,128)(2,1)S(1)}, u32[]{:S(2)}, u32[]{:S(2)}) collective-permute-start(bf16[4,192,384]{2,1,0:T(8,128)(2,1)S(1)} %stack.21.refs_0_.after), channel_id=1, source_target_pairs={{0,6},{1,25},{2,0},{3,27},{4,2},{5,29},{6,4},{7,31},{8,14},{9,1},{... | collective-permute-start | bytes 1769480 | tf_op jit(solution)/shard_map/ppermute | solution.py:59
  22.4 17.4 %collective-permute-start.3 = (bf16[4,192,384]{2,1,0:T(8,128)(2,1)S(1)}, bf16[4,192,384]{2,1,0:T(8,128)(2,1)S(1)}, u32[]{:S(2)}, u32[]{:S(2)}) collective-permute-start(bf16[4,192,384]{2,1,0:T(8,128)(2,1)S(1)} %stack.21.refs_0_.after), channel_id=1, source_target_pairs={{0,1},{1,0},{2,3},{3,2},{4,5},{5,4},{6,7},{7,6},{8,9},{9,8},{10,11... | collective-permute-start | bytes 1769480 | tf_op jit(solution)/shard_map/ppermute | solution.py:63
  24.5 16.3 %collective-permute-start.4 = (bf16[4,192,384]{2,1,0:T(8,128)(2,1)S(1)}, bf16[4,192,384]{2,1,0:T(8,128)(2,1)S(1)}, u32[]{:S(2)}, u32[]{:S(2)}) collective-permute-start(bf16[4,192,384]{2,1,0:T(8,128)(2,1)S(1)} %stack.21.refs_0_.after), channel_id=1, source_target_pairs={{0,4},{1,17},{2,6},{3,19},{4,0},{5,21},{6,2},{7,23},{8,12},{9,25},... | collective-permute-start | bytes 1769480 | tf_op jit(solution)/shard_map/ppermute | solution.py:59
  30.0 26.5 %collective-permute-start.6 = (bf16[4,192,384]{2,1,0:T(8,128)(2,1)S(1)}, bf16[4,192,384]{2,1,0:T(8,128)(2,1)S(1)}, u32[]{:S(2)}, u32[]{:S(2)}) collective-permute-start(bf16[4,192,384]{2,1,0:T(8,128)(2,1)S(1)} %collective-permute-done.5.refs_0_), channel_id=1, source_target_pairs={{0,1},{1,0},{2,3},{3,2},{4,5},{5,4},{6,7},{7,6},{8,9},{9,8},{10,11... | collective-permute-start | bytes 1769480 | tf_op jit(solution)/shard_map/ppermute | solution.py:63
  32.3 24.2 %collective-permute-start.8 = (bf16[4,192,384]{2,1,0:T(8,128)(2,1)S(1)}, bf16[4,192,384]{2,1,0:T(8,128)(2,1)S(1)}, u32[]{:S(2)}, u32[]{:S(2)}) collective-permute-start(bf16[4,192,384]{2,1,0:T(8,128)(2,1)S(1)} %collective-permute-done.7.refs_2_), channel_id=1, source_target_pairs={{0,1},{1,0},{2,3},{3,2},{4,5},{5,4},{6,7},{7,6},{8,9},{9,8},{10,11... | collective-permute-start | bytes 1769480 | tf_op jit(solution)/shard_map/ppermute | solution.py:63
  38.4 9.4 %collective-permute-start.13 = (bf16[256,512]{1,0:T(8,128)(2,1)S(1)}, bf16[256,512]{1,0:T(8,128)(2,1)S(1)}, u32[]{:S(2)}, u32[]{:S(2)}) collective-permute-start(bf16[256,512]{1,0:T(8,128)(2,1)S(1)} %get-tuple-element.25.n0), channel_id=1, source_target_pairs={{0,32},{32,64},{64,96},{96,0},{1,33},{33,65},{65,97},{97,1},{2,34}... | collective-permute-start | bytes 786440 | tf_op jit(solution)/shard_map/ppermute | solution.py:67
  40.8 17.5 %collective-permute-start.9 = (bf16[4,192,384]{2,1,0:T(8,128)(2,1)S(1)}, bf16[4,192,384]{2,1,0:T(8,128)(2,1)S(1)}, u32[]{:S(2)}, u32[]{:S(2)}) collective-permute-start(bf16[4,192,384]{2,1,0:T(8,128)(2,1)S(1)} %collective-permute-done.4.refs_0_), channel_id=1, source_target_pairs={{0,1},{1,0},{2,3},{3,2},{4,5},{5,4},{6,7},{7,6},{8,9},{9,8},{10,11... | collective-permute-start | bytes 1769480 | tf_op jit(solution)/shard_map/ppermute | solution.py:63
  41.2 13.3 %collective-permute-start.14 = (bf16[256,512]{1,0:T(8,128)(2,1)S(1)}, bf16[256,512]{1,0:T(8,128)(2,1)S(1)}, u32[]{:S(2)}, u32[]{:S(2)}) collective-permute-start(bf16[256,512]{1,0:T(8,128)(2,1)S(1)} %get-tuple-element.25.n0), channel_id=1, source_target_pairs={{0,64},{32,96},{64,0},{96,32},{1,65},{33,97},{65,1},{97,33},{2,66}... | collective-permute-start | bytes 786440 | tf_op jit(solution)/shard_map/ppermute | solution.py:67
  47.8 7.5 %collective-permute-start.15 = (bf16[256,512]{1,0:T(8,128)(2,1)S(1)}, bf16[256,512]{1,0:T(8,128)(2,1)S(1)}, u32[]{:S(2)}, u32[]{:S(2)}) collective-permute-start(bf16[256,512]{1,0:T(8,128)(2,1)S(1)} %get-tuple-element.25.n0), channel_id=1, source_target_pairs={{0,96},{32,0},{64,32},{96,64},{1,97},{33,1},{65,33},{97,65},{2,98}... | collective-permute-start | bytes 786440 | tf_op jit(solution)/shard_map/ppermute | solution.py:67
  54.5 10.7 %collective-permute-start.16 = (bf16[256,512]{1,0:T(8,128)(2,1)S(1)}, bf16[256,512]{1,0:T(8,128)(2,1)S(1)}, u32[]{:S(2)}, u32[]{:S(2)}) collective-permute-start(bf16[256,512]{1,0:T(8,128)(2,1)S(1)} %collective-permute-done.13.n1), channel_id=1, source_target_pairs={{0,1},{1,0},{2,3},{3,2},{4,5},{5,4},{6,7},{7,6},{8,9},{9,8},{10,11... | collective-permute-start | bytes 786440 | tf_op jit(solution)/shard_map/ppermute | solution.py:63
  55.3 11.9 %collective-permute-start.17 = (bf16[256,512]{1,0:T(8,128)(2,1)S(1)}, bf16[256,512]{1,0:T(8,128)(2,1)S(1)}, u32[]{:S(2)}, u32[]{:S(2)}) collective-permute-start(bf16[256,512]{1,0:T(8,128)(2,1)S(1)} %collective-permute-done.14.n2), channel_id=1, source_target_pairs={{0,1},{1,0},{2,3},{3,2},{4,5},{5,4},{6,7},{7,6},{8,9},{9,8},{10,11... | collective-permute-start | bytes 786440 | tf_op jit(solution)/shard_map/ppermute | solution.py:63
  56.5 10.7 %collective-permute-start.18 = (bf16[256,512]{1,0:T(8,128)(2,1)S(1)}, bf16[256,512]{1,0:T(8,128)(2,1)S(1)}, u32[]{:S(2)}, u32[]{:S(2)}) collective-permute-start(bf16[256,512]{1,0:T(8,128)(2,1)S(1)} %collective-permute-done.15.n3), channel_id=1, source_target_pairs={{0,1},{1,0},{2,3},{3,2},{4,5},{5,4},{6,7},{7,6},{8,9},{9,8},{10,11... | collective-permute-start | bytes 786440 | tf_op jit(solution)/shard_map/ppermute | solution.py:63
  58.3 38.9 %copy-start.5 = (f32[153]{0:T(256)S(1)}, f32[153]{0:T(256)}, u32[]{:S(2)}) copy-start(f32[153]{0:T(256)} %param.13) | copy-start | bytes 1840
  59.4 7.8 %collective-permute-start.10 = (bf16[96,192]{1,0:T(8,128)(2,1)S(1)}, bf16[96,192]{1,0:T(8,128)(2,1)S(1)}, u32[]{:S(2)}, u32[]{:S(2)}) collective-permute-start(bf16[96,192]{1,0:T(8,128)(2,1)S(1)} %get-tuple-element.22), channel_id=1, source_target_pairs={{0,32},{32,64},{64,96},{96,0},{1,33},{33,65},{65,97},{97,1},{2,34}... | collective-permute-start | bytes 110600 | tf_op jit(solution)/shard_map/ppermute | solution.py:67
  63.0 4.8 %collective-permute-start.11 = (bf16[96,192]{1,0:T(8,128)(2,1)S(1)}, bf16[96,192]{1,0:T(8,128)(2,1)S(1)}, u32[]{:S(2)}, u32[]{:S(2)}) collective-permute-start(bf16[96,192]{1,0:T(8,128)(2,1)S(1)} %get-tuple-element.23), channel_id=1, source_target_pairs={{0,64},{32,96},{64,0},{96,32},{1,65},{33,97},{65,1},{97,33},{2,66}... | collective-permute-start | bytes 110600 | tf_op jit(solution)/shard_map/ppermute | solution.py:67
  65.2 3.2 %collective-permute-start.12 = (bf16[96,192]{1,0:T(8,128)(2,1)S(1)}, bf16[96,192]{1,0:T(8,128)(2,1)S(1)}, u32[]{:S(2)}, u32[]{:S(2)}) collective-permute-start(bf16[96,192]{1,0:T(8,128)(2,1)S(1)} %get-tuple-element.24), channel_id=1, source_target_pairs={{0,96},{32,0},{64,32},{96,64},{1,97},{33,1},{65,33},{97,65},{2,98}... | collective-permute-start | bytes 110600 | tf_op jit(solution)/shard_map/ppermute | solution.py:67
  69.5 4.3 %collective-permute-start.21 = (bf16[128,128]{1,0:T(8,128)(2,1)S(1)}, bf16[128,128]{1,0:T(8,128)(2,1)S(1)}, u32[]{:S(2)}, u32[]{:S(2)}) collective-permute-start(bf16[128,128]{1,0:T(8,128)(2,1)S(1)} %hidden.1), channel_id=1, source_target_pairs={{0,16},{1,5},{2,18},{3,7},{4,20},{5,1},{6,22},{7,3},{8,24},{9,13},... | collective-permute-start | bytes 98312 | tf_op jit(solution)/shard_map/ppermute | solution.py:55
  71.5 4.0 %collective-permute-start.20 = (bf16[128,128]{1,0:T(8,128)(2,1)S(1)}, bf16[128,128]{1,0:T(8,128)(2,1)S(1)}, u32[]{:S(2)}, u32[]{:S(2)}) collective-permute-start(bf16[128,128]{1,0:T(8,128)(2,1)S(1)} %hidden.1), channel_id=1, source_target_pairs={{0,24},{1,7},{2,26},{3,1},{4,28},{5,3},{6,30},{7,5},{8,0},{9,15},{... | collective-permute-start | bytes 98312 | tf_op jit(solution)/shard_map/ppermute | solution.py:55
  73.0 4.0 %collective-permute-start.19 = (bf16[128,128]{1,0:T(8,128)(2,1)S(1)}, bf16[128,128]{1,0:T(8,128)(2,1)S(1)}, u32[]{:S(2)}, u32[]{:S(2)}) collective-permute-start(bf16[128,128]{1,0:T(8,128)(2,1)S(1)} %hidden.1), channel_id=1, source_target_pairs={{0,8},{1,3},{2,10},{3,5},{4,12},{5,7},{6,14},{7,1},{8,16},{9,11},{... | collective-permute-start | bytes 98312 | tf_op jit(solution)/shard_map/ppermute | solution.py:55
  77.0 8.3 %collective-permute-start.23 = (bf16[4,128,128]{2,1,0:T(8,128)(2,1)S(1)}, bf16[4,128,128]{2,1,0:T(8,128)(2,1)S(1)}, u32[]{:S(2)}, u32[]{:S(2)}) collective-permute-start(bf16[4,128,128]{2,1,0:T(8,128)(2,1)S(1)} %pad_maximum_fusion.refs_0_), channel_id=1, source_target_pairs={{0,2},{1,9},{2,4},{3,11},{4,6},{5,13},{6,0},{7,15},{8,10},{9,17},{... | collective-permute-start | bytes 393224 | tf_op jit(solution)/shard_map/ppermute | solution.py:59
  77.4 9.4 %collective-permute-start.25 = (bf16[4,128,128]{2,1,0:T(8,128)(2,1)S(1)}, bf16[4,128,128]{2,1,0:T(8,128)(2,1)S(1)}, u32[]{:S(2)}, u32[]{:S(2)}) collective-permute-start(bf16[4,128,128]{2,1,0:T(8,128)(2,1)S(1)} %pad_maximum_fusion.refs_0_), channel_id=1, source_target_pairs={{0,6},{1,25},{2,0},{3,27},{4,2},{5,29},{6,4},{7,31},{8,14},{9,1},{... | collective-permute-start | bytes 393224 | tf_op jit(solution)/shard_map/ppermute | solution.py:59
  79.8 7.1 %collective-permute-start.27 = (bf16[4,128,128]{2,1,0:T(8,128)(2,1)S(1)}, bf16[4,128,128]{2,1,0:T(8,128)(2,1)S(1)}, u32[]{:S(2)}, u32[]{:S(2)}) collective-permute-start(bf16[4,128,128]{2,1,0:T(8,128)(2,1)S(1)} %pad_maximum_fusion.refs_0_), channel_id=1, source_target_pairs={{0,4},{1,17},{2,6},{3,19},{4,0},{5,21},{6,2},{7,23},{8,12},{9,25},... | collective-permute-start | bytes 393224 | tf_op jit(solution)/shard_map/ppermute | solution.py:59
  80.0 10.6 %collective-permute-start.22 = (bf16[4,128,128]{2,1,0:T(8,128)(2,1)S(1)}, bf16[4,128,128]{2,1,0:T(8,128)(2,1)S(1)}, u32[]{:S(2)}, u32[]{:S(2)}) collective-permute-start(bf16[4,128,128]{2,1,0:T(8,128)(2,1)S(1)} %pad_maximum_fusion.refs_0_), channel_id=1, source_target_pairs={{0,1},{1,0},{2,3},{3,2},{4,5},{5,4},{6,7},{7,6},{8,9},{9,8},{10,11... | collective-permute-start | bytes 393224 | tf_op jit(solution)/shard_map/ppermute | solution.py:63
  85.4 5.3 %collective-permute-start.24 = (bf16[4,128,128]{2,1,0:T(8,128)(2,1)S(1)}, bf16[4,128,128]{2,1,0:T(8,128)(2,1)S(1)}, u32[]{:S(2)}, u32[]{:S(2)}) collective-permute-start(bf16[4,128,128]{2,1,0:T(8,128)(2,1)S(1)} %collective-permute-done.23.refs_2_), channel_id=1, source_target_pairs={{0,1},{1,0},{2,3},{3,2},{4,5},{5,4},{6,7},{7,6},{8,9},{9,8},{10,11... | collective-permute-start | bytes 393224 | tf_op jit(solution)/shard_map/ppermute | solution.py:63
  86.8 3.8 %collective-permute-start.26 = (bf16[4,128,128]{2,1,0:T(8,128)(2,1)S(1)}, bf16[4,128,128]{2,1,0:T(8,128)(2,1)S(1)}, u32[]{:S(2)}, u32[]{:S(2)}) collective-permute-start(bf16[4,128,128]{2,1,0:T(8,128)(2,1)S(1)} %collective-permute-done.25.refs_4_), channel_id=1, source_target_pairs={{0,1},{1,0},{2,3},{3,2},{4,5},{5,4},{6,7},{7,6},{8,9},{9,8},{10,11... | collective-permute-start | bytes 393224 | tf_op jit(solution)/shard_map/ppermute | solution.py:63
  86.8 4.8 %collective-permute-start.28 = (bf16[4,128,128]{2,1,0:T(8,128)(2,1)S(1)}, bf16[4,128,128]{2,1,0:T(8,128)(2,1)S(1)}, u32[]{:S(2)}, u32[]{:S(2)}) collective-permute-start(bf16[4,128,128]{2,1,0:T(8,128)(2,1)S(1)} %collective-permute-done.27.refs_6_), channel_id=1, source_target_pairs={{0,1},{1,0},{2,3},{3,2},{4,5},{5,4},{6,7},{7,6},{8,9},{9,8},{10,11... | collective-permute-start | bytes 393224 | tf_op jit(solution)/shard_map/ppermute | solution.py:63
  93.1 6.3 %collective-permute-start.29 = (bf16[160,384]{1,0:T(8,128)(2,1)S(1)}, bf16[160,384]{1,0:T(8,128)(2,1)S(1)}, u32[]{:S(2)}, u32[]{:S(2)}) collective-permute-start(bf16[160,384]{1,0:T(8,128)(2,1)S(1)} %scores.1.p0), channel_id=1, source_target_pairs={{0,32},{32,64},{64,96},{96,0},{1,33},{33,65},{65,97},{97,1},{2,34}... | collective-permute-start | bytes 368648 | tf_op jit(solution)/shard_map/ppermute | solution.py:67
  94.1 8.9 %collective-permute-start.30 = (bf16[160,384]{1,0:T(8,128)(2,1)S(1)}, bf16[160,384]{1,0:T(8,128)(2,1)S(1)}, u32[]{:S(2)}, u32[]{:S(2)}) collective-permute-start(bf16[160,384]{1,0:T(8,128)(2,1)S(1)} %scores.1.p0), channel_id=1, source_target_pairs={{0,64},{32,96},{64,0},{96,32},{1,65},{33,97},{65,1},{97,33},{2,66}... | collective-permute-start | bytes 368648 | tf_op jit(solution)/shard_map/ppermute | solution.py:67
  97.3 5.7 %collective-permute-start.31 = (bf16[160,384]{1,0:T(8,128)(2,1)S(1)}, bf16[160,384]{1,0:T(8,128)(2,1)S(1)}, u32[]{:S(2)}, u32[]{:S(2)}) collective-permute-start(bf16[160,384]{1,0:T(8,128)(2,1)S(1)} %scores.1.p0), channel_id=1, source_target_pairs={{0,96},{32,0},{64,32},{96,64},{1,97},{33,1},{65,33},{97,65},{2,98}... | collective-permute-start | bytes 368648 | tf_op jit(solution)/shard_map/ppermute | solution.py:67

commit v3 on v2

--- a/solution.py
+++ b/solution.py
@@ -16,6 +16,7 @@
 NT = (((1,), (1,)), ((), ()))
 VM = pl.BlockSpec(memory_space=pltpu.VMEM)
 SM = pl.BlockSpec(memory_space=pltpu.SMEM)
+ANY = pl.BlockSpec(memory_space=pl.ANY)
 
 
 def here():
@@ -67,19 +68,24 @@
     return lax.ppermute(value, "feat", [(i, (i + shift) % NF) for i in range(NF)])
 
 
-CHUNK = 2 * ROWS
+def both_sides(value):
+    pairs = [(f * NV + v, (f + 1 - 2 * (v % 2)) % NF * NV + v) for v in range(NV) for f in range(NF)]
+    return lax.ppermute(value, ("feat", "vert"), pairs)
+
+
+CHUNK = 4 * ROWS
 STEPS = NV * ROWS // CHUNK
-SLOTS = 4
-
-
-def adjacency_kernel(mask, counts, adj, adj2, degree, slots, sems):
+SLOTS = 3
+
+
+def adjacency_kernel(mask, counts, *refs):
+    adj, adj2, degree, slots, sems = refs[-5:]
     me, feat = here()
-    row = lax.broadcasted_iota(jnp.int32, (TILE, TILE), 0)
-    col = lax.broadcasted_iota(jnp.int32, (TILE, TILE), 1)
-    eye = (row == col).astype(f32)
-    source = lax.broadcasted_iota(jnp.int32, (ROWS, TILE), 0)
+    source_row = lax.broadcasted_iota(jnp.int32, (ROWS, TILE), 0)
     target = lax.broadcasted_iota(jnp.int32, (ROWS, TILE), 1)
-    pick = ((source == target + feat * SHARE) & (target < SHARE)).astype(f32).astype(bf16)
+    chosen = (source_row == target + feat * SHARE) & (target < SHARE)
+    pick = (chosen | (target == SHARE)).astype(f32).astype(bf16)
+    inside = lax.broadcasted_iota(jnp.int32, (TILE, TILE), 1) < SHARE
 
     def fetch(step, slot):
         start = pl.multiple_of(step * CHUNK, CHUNK)
@@ -100,27 +106,34 @@
         fetch(step, slot).wait()
         for j in range(CHUNK // ROWS):
             base = pl.multiple_of(step * CHUNK + j * ROWS, ROWS)
-            for k in range(ROWS // TILE):
-                tile_col = step * (CHUNK // TILE) + j * (ROWS // TILE) + k
-                for i in range(ROWS // TILE):
-                    stored = mask[i, tile_col].astype(f32)
-                    own = (me * (ROWS // TILE) + i == tile_col).astype(f32)
-                    tile = slots[slot, i * TILE : (i + 1) * TILE, j * ROWS + k * TILE : j * ROWS + (k + 1) * TILE]
-                    tile = tile.astype(f32) * stored + eye * own
-                    degree[i * TILE : (i + 1) * TILE, :] += tile
-                    adj[i * TILE : (i + 1) * TILE, pl.ds(base + k * TILE, TILE)] = tile.astype(bf16)
-            part = jnp.dot(adj[:, pl.ds(base, ROWS)], pick, preferred_element_type=f32)
             place = pl.multiple_of((step * (CHUNK // ROWS) + j) * TILE, TILE)
-            adj2[:, pl.ds(place, TILE)] = part.astype(bf16)
-
-    degree[...] = jnp.broadcast_to(jnp.sum(degree[...], axis=1, keepdims=True), degree.shape)
-
-
-def make_adjacency(tile_mask, counts):
+            for i in range(ROWS // TILE):
+                rows = slice(i * TILE, (i + 1) * TILE)
+                strip = []
+                for k in range(ROWS // TILE):
+                    stored = mask[i, (step * (CHUNK // ROWS) + j) * (ROWS // TILE) + k].astype(f32)
+                    tile = slots[slot, rows, j * ROWS + k * TILE : j * ROWS + (k + 1) * TILE]
+                    strip.append((tile.astype(f32) * stored).astype(bf16))
+                strip = jnp.concatenate(strip, axis=1)
+                adj[rows, pl.ds(base, ROWS)] = strip
+                part = jnp.dot(strip, pick, preferred_element_type=f32)
+                degree[rows, :] += part
+                adj2[rows, pl.ds(place, TILE)] = jnp.where(inside, part, 0.0).astype(bf16)
+
+    place = pl.ds(pl.multiple_of(me * TILE, TILE), TILE)
+    adj2[:, place] = (adj2[:, place].astype(f32) + chosen.astype(f32)).astype(bf16)
+    row = lax.broadcasted_iota(jnp.int32, (ROWS, ROWS), 0)
+    col = lax.broadcasted_iota(jnp.int32, (ROWS, ROWS), 1)
+    place = pl.ds(pl.multiple_of(me * ROWS, ROWS), ROWS)
+    adj[:, place] = (adj[:, place].astype(f32) + (row == col).astype(f32)).astype(bf16)
+    degree[...] = jnp.broadcast_to(degree[:, SHARE : SHARE + 1] + 1.0, degree.shape)
+
+
+def make_adjacency(tile_mask, counts, *after):
     counts = pltpu.with_memory_space_constraint(counts, pltpu.HBM)
     return pl.pallas_call(
         adjacency_kernel,
-        in_specs=[SM, pl.BlockSpec(memory_space=pltpu.HBM)],
+        in_specs=[SM, pl.BlockSpec(memory_space=pltpu.HBM)] + [ANY] * len(after),
         out_specs=[VM] * 3,
         out_shape=[
             pltpu.VMEM((ROWS, NV * ROWS), bf16),
@@ -128,34 +141,33 @@
             pltpu.VMEM((ROWS, TILE), f32),
         ],
         scratch_shapes=[pltpu.VMEM((SLOTS, ROWS, CHUNK), jnp.int32), pltpu.SemaphoreType.DMA((SLOTS,))],
-        compiler_params=params(),
+        compiler_params=params(24),
         cost_estimate=cost(2.4e9, 31e6),
         name="adjacency",
-    )(tile_mask, counts)
-
-
-def pack_kernel(w_in, w_out_t, b_in, after, mine, other):
-    core = lax.rem(here()[0], 2)
+    )(tile_mask, counts, *after)
+
+
+def pack_kernel(w_in, w_out_t, b_in, whole, mine):
     zero = jnp.zeros((192 - CLS, TILE), f32)
-    for out, half in ((mine, core), (other, 1 - core)):
+    for half in range(2):
+        lanes = slice(TILE * half, TILE * (half + 1))
         for k in range(NF):
-            lanes = pl.ds(pl.multiple_of(256 * k + TILE * half, TILE), TILE)
-            out[0:192, k * TILE : (k + 1) * TILE] = w_in[:, lanes]
-        lanes = pl.ds(pl.multiple_of(TILE * half, TILE), TILE)
+            whole[half, 0:192, k * TILE : (k + 1) * TILE] = w_in[:, 256 * k + TILE * half : 256 * k + TILE * (half + 1)]
         w = jnp.concatenate([w_out_t[:, lanes].astype(f32), zero], axis=0)
         for k in range(NF):
-            out[192:240, k * TILE : (k + 1) * TILE] = w[48 * k : 48 * (k + 1)].astype(bf16)
+            whole[half, 192:240, k * TILE : (k + 1) * TILE] = w[48 * k : 48 * (k + 1)].astype(bf16)
         b = jnp.broadcast_to(b_in[:, lanes], (16, TILE))
         hi = b.astype(bf16).astype(f32)
         mid = (b - hi).astype(bf16).astype(f32)
         low = b - hi - mid
         row = lax.broadcasted_iota(jnp.int32, (16, TILE), 0)
         b = jnp.where(row == 0, hi, jnp.where(row == 1, mid, jnp.where(row == 2, low, 0.0)))
-        out[240:256, 0:TILE] = b.astype(bf16)
-        out[240:256, TILE:] = jnp.zeros((16, 512 - TILE), bf16)
-
-
-def stack_kernel(a, b, c, d, after, out):
+        whole[half, 240:256, 0:TILE] = b.astype(bf16)
+        whole[half, 240:256, TILE:] = jnp.zeros((16, 512 - TILE), bf16)
+    mine[...] = whole[lax.rem(here()[0], 2)]
+
+
+def stack_kernel(a, b, c, d, after, after_too, out):
     for i, part in enumerate((a, b, c, d)):
         out[i] = part[...]
 
@@ -194,22 +206,32 @@
     return cost(2 * 384 * 384 * 256 * n, n * 450e3)
 
 
-def hidden_kernel(g0, g1, g2, g3, n0, n1, n2, n3, f0, f1, f2, f3, z_out, hid):
-    feat = here()[1]
-    gs = (g0, g1, g2, g3)
+def hidden_kernel(g0, g1, g2, g3, own, side, other_side, near, far, z_out, hid):
+    me, feat = here()
+    core = lax.rem(me, 2)
+    even = core == 0
+    ga = jnp.where(even, g1[...].astype(f32), g3[...].astype(f32)).astype(bf16)
+    gb = jnp.where(even, g3[...].astype(f32), g1[...].astype(f32)).astype(bf16)
+    down, up = lax.rem(feat + NF - 1, NF), lax.rem(feat + 1, NF)
+    across = lax.rem(feat + 2, NF)
     total = jnp.zeros((SHARE, 192), f32)
-    for parts in ((n0, n1, n2, n3), (f0, f1, f2, f3)):
+    for half, opposite in ((core, near), (1 - core, far)):
+        parts = (
+            (g0[...], own.at[half], feat),
+            (ga, side.at[half], jnp.where(even, down, up)),
+            (gb, other_side.at[half], jnp.where(even, up, down)),
+            (g2[...], opposite, across),
+        )
         pre = jnp.zeros((SHARE, 512), f32)
-        for s in range(NF):
-            pre = pre + jnp.dot(gs[s][...], parts[s][0:192, :], preferred_element_type=f32)
+        for g, part, _ in parts:
+            pre = pre + jnp.dot(g, part[0:192, :], preferred_element_type=f32)
         hid[...] = pre
-        for s in range(NF):
-            owner = lax.rem(feat + NF - s, NF)
+        for _, part, owner in parts:
             lanes = pl.ds(pl.multiple_of(owner * TILE, TILE), TILE)
-            b = parts[s][240:256, 0:TILE].astype(f32)
+            b = part[240:256, 0:TILE].astype(f32)
             bias = b[0:1] + b[1:2] + b[2:3]
             unit = jnp.maximum(hid[:, lanes] + bias, 0.0).astype(bf16)
-            w = parts[s][192:240, :]
+            w = part[192:240, :]
             w = jnp.concatenate([w[:, k * TILE : (k + 1) * TILE] for k in range(NF)], axis=0)
             total = total + lax.dot_general(unit, w, NT, preferred_element_type=f32)
     z_out[0:SHARE, :] = total[:, :TILE].astype(bf16)
@@ -241,24 +263,27 @@
 
 
 def local(features, counts, tile_mask, w_in, b_in, w_out, b_out):
-    adj, adj2, degree = make_adjacency(tile_mask, counts)
+    whole, mine_half = pl.pallas_call(
+        pack_kernel,
+        out_shape=[jax.ShapeDtypeStruct((2, 256, 512), bf16), jax.ShapeDtypeStruct((256, 512), bf16)],
+        in_specs=[VM] * 3, out_specs=[VM] * 2,
+        compiler_params=params(), cost_estimate=cost(1e5, 1.2e6), name="pack",
+    )(w_in, w_out.T, b_in.reshape(1, 256))
+    side = both_sides(whole)
+    near = along_feat(mine_half, 2)
+    adj, adj2, degree = make_adjacency(tile_mask, counts, mine_half)
 
     mine = features.T
     ring = [first_axis(mine, s) for s in (1, 3, 2)]
     four = pl.pallas_call(
         stack_kernel, out_shape=jax.ShapeDtypeStruct((NF, 192, ROWS), bf16),
-        in_specs=[VM] * 4 + [pl.BlockSpec(memory_space=pl.ANY)], out_specs=VM,
+        in_specs=[VM] * 4 + [ANY] * 2, out_specs=VM,
         compiler_params=params(), cost_estimate=cost(1e5, 1.2e6), name="stack",
-    )(mine, *ring, degree)
+    )(mine, *ring, degree, side)
     rows = {t: second_axis(four, t) for t in (1, 3, 2)}
 
-    near, far = pl.pallas_call(
-        pack_kernel, out_shape=[jax.ShapeDtypeStruct((256, 512), bf16)] * 2,
-        in_specs=[VM] * 3 + [pl.BlockSpec(memory_space=pl.ANY)], out_specs=[VM] * 2,
-        compiler_params=params(), cost_estimate=cost(1e5, 1.2e6), name="pack",
-    )(w_in, w_out.T, b_in.reshape(1, 256), four)
-    near = [near] + [along_feat(near, s) for s in (1, 2, 3)]
-    far = [far] + [swap(w) for w in near[1:]]
+    near, rows[3] = lax.optimization_barrier((near, rows[3]))
+    other_side, far = swap(side), swap(near)
 
     total_shape = jax.ShapeDtypeStruct((ROWS, 192), f32)
     pieces = [four, swap(four)]
@@ -283,10 +308,10 @@
     g = [means[0]] + [along_feat(means[s], s) for s in (1, 2, 3)]
     z_block = pl.pallas_call(
         hidden_kernel, out_shape=jax.ShapeDtypeStruct((TILE, TILE), bf16),
-        in_specs=[VM] * 12, out_specs=VM,
+        in_specs=[VM] * 9, out_specs=VM,
         scratch_shapes=[pltpu.VMEM((SHARE, 512), f32)],
         compiler_params=params(), cost_estimate=cost(2 * 96 * 768 * 1024, 2e6), name="hidden",
-    )(*g, *near, *far)
+    )(*g, whole, side, other_side, near, far)
 
     z_four = jnp.stack([z_block] + [first_axis(z_block, s) for s in (1, 3, 2)])
     z_rows = [z_four] + [second_axis(z_four, t) for t in (1, 3, 2)]

time: 104 us -> 88.2 us (0.85)
  starting transfers between devices: 57.8 us -> 45.5 us
  Pallas kernels: 20.3 us -> 15.9 us
  local copies, waits for them, and re-layouts: 0.71 us -> 3.25 us
  waiting for transfers between devices: 24.8 us -> 23.2 us
    ppermute x11 -> x10, starting transfers between devices: 23.4 us -> 16.4 us  [swap(): return lax.ppermute(value, 'vert', positions(lambda x, z, c: (x, z, 1 - c)))]
    ppermute x9 -> x7, starting transfers between devices: 17.3 us -> 11.9 us  [along_feat(): lax.ppermute(value, 'feat', [(i, (i + shift) % NF) for i in range(NF)])]
    pallas_call x1, Pallas kernels: 12.9 us -> 8.48 us  [make_adjacency(): pl.pallas_call(adjacency_kernel, in_specs=[SM, pl.BlockSpec(memory_space=...]
    ppermute x0 -> x1, starting transfers between devices: none -> 3.63 us  [both_sides(): return lax.ppermute(value, ('feat', 'vert'), pairs)]
    ppermute x6, starting transfers between devices: 9.99 us -> 6.67 us  [first_axis(): lax.ppermute(value, 'vert', positions(lambda x, z, c: (x + shift * (1 - c...]
    ppermute x9 -> x7, waiting for transfers between devices: 16.3 us -> 13.6 us  [along_feat(): lax.ppermute(value, 'feat', [(i, (i + shift) % NF) for i in range(NF)])]
    unnamed x12, local copies, waits for them, and re-layouts: 0.7 us -> 3.25 us
  transfers between devices with their start and end apart: 32 -> 30, of which waited for: 11 -> 11; matrix products, arithmetic and copies ran while one was open for 0% -> 0% of each run, Pallas kernels for 16% -> 14%
where the time goes in v3:
time: 88.2 us; the launch traced here: 88 us
  starting transfers between devices  45.5 us (52%)
  waiting for transfers between devices  23.2 us (26%)
  Pallas kernels  15.9 us (18%)
  local copies, waits for them, and re-layouts  3.25 us (4%)
    ppermute x10, starting transfers between devices, swap(): return lax.ppermute(value, 'vert', positions(lambda x, z, c: (x, z, 1 - c)))  16.4 us
    ppermute x7, waiting for transfers between devices, along_feat(): lax.ppermute(value, 'feat', [(i, (i + shift) % NF) for i in range(NF)])  13.6 us
    ppermute x7, starting transfers between devices, along_feat(): lax.ppermute(value, 'feat', [(i, (i + shift) % NF) for i in range(NF)])  11.9 us
    pallas_call x1, Pallas kernels, make_adjacency(): pl.pallas_call(adjacency_kernel, in_specs=[SM, pl.BlockSpec(memory_space=...  8.48 us
    ppermute x6, starting transfers between devices, second_axis(): lax.ppermute(value, 'vert', positions(lambda x, z, c: (x + shift * c, z +...  6.89 us
    ppermute x6, starting transfers between devices, first_axis(): lax.ppermute(value, 'vert', positions(lambda x, z, c: (x + shift * (1 - c...  6.67 us
    ppermute x6, waiting for transfers between devices, second_axis(): lax.ppermute(value, 'vert', positions(lambda x, z, c: (x + shift * c, z +...  5.07 us
    ppermute x1, starting transfers between devices, both_sides(): return lax.ppermute(value, ('feat', 'vert'), pairs)  3.63 us
  transfers between devices with their start and end apart: 30, of which 11 were waited for; matrix products, arithmetic and copies ran while one was open for 0% of the time, Pallas kernels for 14%

profile of v3, /device:TPU:1, one launch (start us, length us, event | category | flops | bytes accessed | tf_op | source)
XLA Modules:
  0.0 88.0 jit_solution(2194306769287440667)
XLA Ops:
  0.0 1.0 %copy-done = bf16[192,1024]{1,0:T(8,128)(2,1)S(1)} copy-done((bf16[192,1024]{1,0:T(8,128)(2,1)S(1)}, bf16[192,1024]{1,0:T(8,128)(2,1)}, u32[]{:S(2)}) %copy-start) | copy-done | bytes 393240
  1.0 0.9 %copy-done.2 = bf16[256,153]{0,1:T(8,128)(2,1)S(1)} copy-done((bf16[256,153]{0,1:T(8,128)(2,1)S(1)}, bf16[256,153]{0,1:T(8,128)(2,1)}, u32[]{:S(2)}) %copy-start.2) | copy-done | bytes 78360
  1.9 0.7 copy-done.4
  2.6 0.1 pack.1
  2.7 3.6 %collective-permute-start.3 = (bf16[2,256,512]{2,1,0:T(8,128)(2,1)S(1)}, bf16[2,256,512]{2,1,0:T(8,128)(2,1)S(1)}, u32[]{:S(2)}, u32[]{:S(2)}) collective-permute-start(bf16[2,256,512]{2,1,0:T(8,128)(2,1)S(1)} %get-tuple-element.22.own), channel_id=1, source_target_pairs={{0,32},{32,64},{64,96},{96,0},{1,97},{33,1},{65,33},{97,65},{2,34}... | collective-permute-start | bytes 1572872 | tf_op jit(solution)/shard_map/ppermute | solution.py:73
  6.3 1.6 %collective-permute-start = (bf16[192,384]{1,0:T(8,128)(2,1)}, bf16[192,384]{1,0:T(8,128)(2,1)S(1)}, u32[]{:S(2)}, u32[]{:S(2)}) collective-permute-start(bf16[192,384]{1,0:T(8,128)(2,1)} %bitcast.9), channel_id=1, source_target_pairs={{0,8},{1,3},{2,10},{3,5},{4,12},{5,7},{6,14},{7,1},{8,16},{9,11},{... | collective-permute-start | bytes 442376 | tf_op jit(solution)/shard_map/ppermute | solution.py:56
  8.0 2.1 %collective-permute-start.1 = (bf16[192,384]{1,0:T(8,128)(2,1)}, bf16[192,384]{1,0:T(8,128)(2,1)S(1)}, u32[]{:S(2)}, u32[]{:S(2)}) collective-permute-start(bf16[192,384]{1,0:T(8,128)(2,1)} %bitcast.10), channel_id=1, source_target_pairs={{0,24},{1,7},{2,26},{3,1},{4,28},{5,3},{6,30},{7,5},{8,0},{9,15},{... | collective-permute-start | bytes 442376 | tf_op jit(solution)/shard_map/ppermute | solution.py:56
  10.1 1.3 %collective-permute-start.2 = (bf16[192,384]{1,0:T(8,128)(2,1)}, bf16[192,384]{1,0:T(8,128)(2,1)S(1)}, u32[]{:S(2)}, u32[]{:S(2)}) collective-permute-start(bf16[192,384]{1,0:T(8,128)(2,1)} %bitcast.11), channel_id=1, source_target_pairs={{0,16},{1,5},{2,18},{3,7},{4,20},{5,1},{6,22},{7,3},{8,24},{9,13},... | collective-permute-start | bytes 442376 | tf_op jit(solution)/shard_map/ppermute | solution.py:56
  11.4 0.7 copy-done.3
  12.1 8.5 %adjacency.1 = (bf16[384,12288]{1,0:T(8,128)(2,1)S(1)}, bf16[384,4096]{1,0:T(8,128)(2,1)S(1)}, f32[384,128]{1,0:T(8,128)S(1)}) custom-call(s32[3,96]{1,0:T(4,128)S(1)} %copy-done.3, s32[384,12288]{1,0:T(8,128)} %counts.1, bf16[256,512]{1,0:T(8,128)(2,1)S(1)} %get-tuple-element.18.refs_0_), custom_call_target="tpu_custom_call" | custom-call | flops 2400000000 | bytes 31000000 | tf_op jit(solution)/shard_map/adjacency/pallas_call | solution.py:134
  20.6 0.0 collective-permute-done.1.c
  20.6 0.0 collective-permute-done.2.d
  20.6 0.1 stack.21.refs_0_
  20.7 2.5 %collective-permute-start.9 = (bf16[4,192,384]{2,1,0:T(8,128)(2,1)S(1)}, bf16[4,192,384]{2,1,0:T(8,128)(2,1)S(1)}, u32[]{:S(2)}, u32[]{:S(2)}) collective-permute-start(bf16[4,192,384]{2,1,0:T(8,128)(2,1)S(1)} %stack.21.refs_0_), channel_id=1, source_target_pairs={{0,6},{1,25},{2,0},{3,27},{4,2},{5,29},{6,4},{7,31},{8,14},{9,1},{... | collective-permute-start | bytes 1769480 | tf_op jit(solution)/shard_map/ppermute | solution.py:60
  23.2 0.0 collective-permute-start.6
  23.2 1.1 %collective-permute-start.4 = (bf16[4,192,384]{2,1,0:T(8,128)(2,1)S(1)}, bf16[4,192,384]{2,1,0:T(8,128)(2,1)S(1)}, u32[]{:S(2)}, u32[]{:S(2)}) collective-permute-start(bf16[4,192,384]{2,1,0:T(8,128)(2,1)S(1)} %stack.21.refs_0_), channel_id=1, source_target_pairs={{0,1},{1,0},{2,3},{3,2},{4,5},{5,4},{6,7},{7,6},{8,9},{9,8},{10,11... | collective-permute-start | bytes 1769480 | tf_op jit(solution)/shard_map/ppermute | solution.py:64
  24.3 1.4 %collective-permute-start.5 = (bf16[4,192,384]{2,1,0:T(8,128)(2,1)S(1)}, bf16[4,192,384]{2,1,0:T(8,128)(2,1)S(1)}, u32[]{:S(2)}, u32[]{:S(2)}) collective-permute-start(bf16[4,192,384]{2,1,0:T(8,128)(2,1)S(1)} %stack.21.refs_0_), channel_id=1, source_target_pairs={{0,4},{1,17},{2,6},{3,19},{4,0},{5,21},{6,2},{7,23},{8,12},{9,25},... | collective-permute-start | bytes 1769480 | tf_op jit(solution)/shard_map/ppermute | solution.py:60
  25.7 2.6 %collective-permute-start.8 = (bf16[256,512]{1,0:T(8,128)(2,1)S(1)}, bf16[256,512]{1,0:T(8,128)(2,1)S(1)}, u32[]{:S(2)}, u32[]{:S(2)}) collective-permute-start(bf16[256,512]{1,0:T(8,128)(2,1)S(1)} %get-tuple-element.18.refs_0_), channel_id=1, source_target_pairs={{0,64},{32,96},{64,0},{96,32},{1,65},{33,97},{65,1},{97,33},{2,66}... | collective-permute-start | bytes 786440 | tf_op jit(solution)/shard_map/ppermute | solution.py:68
  28.4 6.4 %collective-permute-done.8.near = bf16[256,512]{1,0:T(8,128)(2,1)S(1)} collective-permute-done((bf16[256,512]{1,0:T(8,128)(2,1)S(1)}, bf16[256,512]{1,0:T(8,128)(2,1)S(1)}, u32[]{:S(2)}, u32[]{:S(2)}) %collective-permute-start.8) | collective-permute-done | bytes 262176 | tf_op jit(solution)/shard_map/ppermute | solution.py:68
  34.7 1.6 %collective-permute-done.9.refs_2_ = bf16[4,192,384]{2,1,0:T(8,128)(2,1)S(1)} collective-permute-done((bf16[4,192,384]{2,1,0:T(8,128)(2,1)S(1)}, bf16[4,192,384]{2,1,0:T(8,128)(2,1)S(1)}, u32[]{:S(2)}, u32[]{:S(2)}) %collective-permute-start.9) | collective-permute-done | bytes 589856 | tf_op jit(solution)/shard_map/ppermute | solution.py:60
  36.4 3.4 %collective-permute-done.6.refs_0_ = bf16[4,192,384]{2,1,0:T(8,128)(2,1)S(1)} collective-permute-done((bf16[4,192,384]{2,1,0:T(8,128)(2,1)S(1)}, bf16[4,192,384]{2,1,0:T(8,128)(2,1)S(1)}, u32[]{:S(2)}, u32[]{:S(2)}) %collective-permute-start.6) | collective-permute-done | bytes 589856 | tf_op jit(solution)/shard_map/ppermute | solution.py:60
  39.8 1.9 %collective-permute-start.7 = (bf16[4,192,384]{2,1,0:T(8,128)(2,1)S(1)}, bf16[4,192,384]{2,1,0:T(8,128)(2,1)S(1)}, u32[]{:S(2)}, u32[]{:S(2)}) collective-permute-start(bf16[4,192,384]{2,1,0:T(8,128)(2,1)S(1)} %collective-permute-done.6.refs_0_), channel_id=1, source_target_pairs={{0,1},{1,0},{2,3},{3,2},{4,5},{5,4},{6,7},{7,6},{8,9},{9,8},{10,11... | collective-permute-start | bytes 1769480 | tf_op jit(solution)/shard_map/ppermute | solution.py:64
  41.7 0.0 collective-permute-start.10
  41.7 0.0 collective-permute-done.4.refs_1_
  41.7 1.0 %product_first.1.before = f32[384,192]{1,0:T(8,128)S(1)} custom-call(bf16[384,12288]{1,0:T(8,128)(2,1)S(1)} %get-tuple-element.21.adj, bf16[4,192,384]{2,1,0:T(8,128)(2,1)S(1)} %stack.21.refs_0_, bf16[4,192,384]{2,1,0:T(8,128)(2,1)S(1)} %collective-permute-done.4.refs_1_), custom_call_target="tpu_custom_call" | custom-call | flops 603979776 | bytes 3600000 | tf_op jit(solution)/shard_map/product_first/pallas_call | solution.py:290
  42.7 0.0 collective-permute-done.5.refs_0_
  42.7 0.6 collective-permute-start.11
  43.3 0.1 collective-permute-start.15
  43.4 0.4 collective-permute-start.16
  43.8 0.0 collective-permute-done.7.refs_1_
  43.8 0.4 collective-permute-done.10.refs_3_
  44.2 1.8 %product_next.1.before = f32[384,192]{1,0:T(8,128)S(1)} custom-call(bf16[384,12288]{1,0:T(8,128)(2,1)S(1)} %get-tuple-element.21.adj, f32[384,192]{1,0:T(8,128)S(1)} %product_first.1.before, bf16[4,192,384]{2,1,0:T(8,128)(2,1)S(1)} %collective-permute-done.6.refs_0_, bf16[4,192,384]{2,1,0:T(8,128)(2,1)S(1)} %collective-permute-done.7.refs_1_, ...), custom_call_target="tpu_custom_call" | custom-call | flops 1207959552 | bytes 7200000 | tf_op jit(solution)/shard_map/product_next/pallas_call | solution.py:296
  46.0 0.0 copy-start.5
  46.0 1.0 %product_last.1 = (bf16[96,192]{1,0:T(8,128)(2,1)S(1)}, bf16[96,192]{1,0:T(8,128)(2,1)S(1)}, bf16[96,192]{1,0:T(8,128)(2,1)S(1)}, bf16[96,192]{1,0:T(8,128)(2,1)S(1)}) custom-call(bf16[384,12288]{1,0:T(8,128)(2,1)S(1)} %get-tuple-element.21.adj, f32[384,192]{1,0:T(8,128)S(1)} %product_next.1.before, f32[384,128]{1,0:T(8,128)S(1)} %get-tuple-element.20.after.degree, ...), custom_call_target="tpu_custom_call" | custom-call | flops 603979776 | bytes 3600000 | tf_op jit(solution)/shard_map/product_last/pallas_call | solution.py:301
  47.1 1.4 %collective-permute-start.12 = (bf16[96,192]{1,0:T(8,128)(2,1)S(1)}, bf16[96,192]{1,0:T(8,128)(2,1)S(1)}, u32[]{:S(2)}, u32[]{:S(2)}) collective-permute-start(bf16[96,192]{1,0:T(8,128)(2,1)S(1)} %get-tuple-element.27), channel_id=1, source_target_pairs={{0,32},{32,64},{64,96},{96,0},{1,33},{33,65},{65,97},{97,1},{2,34}... | collective-permute-start | bytes 110600 | tf_op jit(solution)/shard_map/ppermute | solution.py:68
  48.4 1.4 %collective-permute-start.13 = (bf16[96,192]{1,0:T(8,128)(2,1)S(1)}, bf16[96,192]{1,0:T(8,128)(2,1)S(1)}, u32[]{:S(2)}, u32[]{:S(2)}) collective-permute-start(bf16[96,192]{1,0:T(8,128)(2,1)S(1)} %get-tuple-element.28), channel_id=1, source_target_pairs={{0,64},{32,96},{64,0},{96,32},{1,65},{33,97},{65,1},{97,33},{2,66}... | collective-permute-start | bytes 110600 | tf_op jit(solution)/shard_map/ppermute | solution.py:68
  49.9 2.0 %collective-permute-start.14 = (bf16[96,192]{1,0:T(8,128)(2,1)S(1)}, bf16[96,192]{1,0:T(8,128)(2,1)S(1)}, u32[]{:S(2)}, u32[]{:S(2)}) collective-permute-start(bf16[96,192]{1,0:T(8,128)(2,1)S(1)} %get-tuple-element.29), channel_id=1, source_target_pairs={{0,96},{32,0},{64,32},{96,64},{1,97},{33,1},{65,33},{97,65},{2,98}... | collective-permute-start | bytes 110600 | tf_op jit(solution)/shard_map/ppermute | solution.py:68
  51.8 0.0 collective-permute-done.15.other_side
  51.8 0.0 collective-permute-done.16.far
  51.8 1.0 %collective-permute-done.13.g2 = bf16[96,192]{1,0:T(8,128)(2,1)S(1)} collective-permute-done((bf16[96,192]{1,0:T(8,128)(2,1)S(1)}, bf16[96,192]{1,0:T(8,128)(2,1)S(1)}, u32[]{:S(2)}, u32[]{:S(2)}) %collective-permute-start.13) | collective-permute-done | bytes 36896 | tf_op jit(solution)/shard_map/ppermute | solution.py:68
  52.9 0.5 collective-permute-done.14.g3
  53.4 1.0 %hidden.1 = bf16[128,128]{1,0:T(8,128)(2,1)S(1)} custom-call(bf16[96,192]{1,0:T(8,128)(2,1)S(1)} %get-tuple-element.26.g0, bf16[96,192]{1,0:T(8,128)(2,1)S(1)} %collective-permute-done.12.g1, bf16[96,192]{1,0:T(8,128)(2,1)S(1)} %collective-permute-done.13.g2, bf16[96,192]{1,0:T(8,128)(2,1)S(1)} %collective-permute-done.14.g3, ...), custom_call_target="tpu_custom_call" | custom-call | flops 150994944 | bytes 2000000 | tf_op jit(solution)/shard_map/hidden/pallas_call | solution.py:309
  54.5 0.1 collective-permute-start.19
  54.5 0.7 collective-permute-start.18
  55.3 0.8 collective-permute-start.17
  56.1 2.7 %collective-permute-done.19 = bf16[128,128]{1,0:T(8,128)(2,1)S(1)} collective-permute-done((bf16[128,128]{1,0:T(8,128)(2,1)S(1)}, bf16[128,128]{1,0:T(8,128)(2,1)S(1)}, u32[]{:S(2)}, u32[]{:S(2)}) %collective-permute-start.19) | collective-permute-done | bytes 32800 | tf_op jit(solution)/shard_map/ppermute | solution.py:56
  58.8 0.4 collective-permute-done.17
  59.3 0.3 collective-permute-start.21
  59.6 2.4 %collective-permute-start.23 = (bf16[4,128,128]{2,1,0:T(8,128)(2,1)S(1)}, bf16[4,128,128]{2,1,0:T(8,128)(2,1)S(1)}, u32[]{:S(2)}, u32[]{:S(2)}) collective-permute-start(bf16[4,128,128]{2,1,0:T(8,128)(2,1)S(1)} %pad_maximum_fusion.refs_0_), channel_id=1, source_target_pairs={{0,6},{1,25},{2,0},{3,27},{4,2},{5,29},{6,4},{7,31},{8,14},{9,1},{... | collective-permute-start | bytes 393224 | tf_op jit(solution)/shard_map/ppermute | solution.py:60
  62.0 0.2 collective-permute-start.25
  62.2 5.8 %collective-permute-start.20 = (bf16[4,128,128]{2,1,0:T(8,128)(2,1)S(1)}, bf16[4,128,128]{2,1,0:T(8,128)(2,1)S(1)}, u32[]{:S(2)}, u32[]{:S(2)}) collective-permute-start(bf16[4,128,128]{2,1,0:T(8,128)(2,1)S(1)} %pad_maximum_fusion.refs_0_), channel_id=1, source_target_pairs={{0,1},{1,0},{2,3},{3,2},{4,5},{5,4},{6,7},{7,6},{8,9},{9,8},{10,11... | collective-permute-start | bytes 393224 | tf_op jit(solution)/shard_map/ppermute | solution.py:64
  68.0 0.0 collective-permute-done.21.refs_2_
  68.0 2.9 %collective-permute-start.22 = (bf16[4,128,128]{2,1,0:T(8,128)(2,1)S(1)}, bf16[4,128,128]{2,1,0:T(8,128)(2,1)S(1)}, u32[]{:S(2)}, u32[]{:S(2)}) collective-permute-start(bf16[4,128,128]{2,1,0:T(8,128)(2,1)S(1)} %collective-permute-done.21.refs_2_), channel_id=1, source_target_pairs={{0,1},{1,0},{2,3},{3,2},{4,5},{5,4},{6,7},{7,6},{8,9},{9,8},{10,11... | collective-permute-start | bytes 393224 | tf_op jit(solution)/shard_map/ppermute | solution.py:64
  70.9 0.0 collective-permute-done.23.refs_4_
  70.9 1.0 %collective-permute-start.24 = (bf16[4,128,128]{2,1,0:T(8,128)(2,1)S(1)}, bf16[4,128,128]{2,1,0:T(8,128)(2,1)S(1)}, u32[]{:S(2)}, u32[]{:S(2)}) collective-permute-start(bf16[4,128,128]{2,1,0:T(8,128)(2,1)S(1)} %collective-permute-done.23.refs_4_), channel_id=1, source_target_pairs={{0,1},{1,0},{2,3},{3,2},{4,5},{5,4},{6,7},{7,6},{8,9},{9,8},{10,11... | collective-permute-start | bytes 393224 | tf_op jit(solution)/shard_map/ppermute | solution.py:64
  71.9 2.5 %collective-permute-start.26 = (bf16[4,128,128]{2,1,0:T(8,128)(2,1)S(1)}, bf16[4,128,128]{2,1,0:T(8,128)(2,1)S(1)}, u32[]{:S(2)}, u32[]{:S(2)}) collective-permute-start(bf16[4,128,128]{2,1,0:T(8,128)(2,1)S(1)} %collective-permute-done.25.refs_6_), channel_id=1, source_target_pairs={{0,1},{1,0},{2,3},{3,2},{4,5},{5,4},{6,7},{7,6},{8,9},{9,8},{10,11... | collective-permute-start | bytes 393224 | tf_op jit(solution)/shard_map/ppermute | solution.py:64
  74.5 1.0 %collective-permute-done.26.refs_7_ = bf16[4,128,128]{2,1,0:T(8,128)(2,1)S(1)} collective-permute-done((bf16[4,128,128]{2,1,0:T(8,128)(2,1)S(1)}, bf16[4,128,128]{2,1,0:T(8,128)(2,1)S(1)}, u32[]{:S(2)}, u32[]{:S(2)}) %collective-permute-start.26) | collective-permute-done | bytes 131104 | tf_op jit(solution)/shard_map/ppermute | solution.py:64
  75.4 1.5 %scores.1.p0 = bf16[160,384]{1,0:T(8,128)(2,1)S(1)} custom-call(bf16[384,4096]{1,0:T(8,128)(2,1)S(1)} %get-tuple-element.19.adj2, f32[384,128]{1,0:T(8,128)S(1)} %get-tuple-element.20.after.degree, bf16[4,128,128]{2,1,0:T(8,128)(2,1)S(1)} %pad_maximum_fusion.refs_0_, bf16[4,128,128]{2,1,0:T(8,128)(2,1)S(1)} %collective-permute-done.20.refs_1_, ...), custom_call_target="tpu_custom_call" | custom-call | flops 805306368 | bytes 5000000 | tf_op jit(solution)/shard_map/scores/pallas_call | solution.py:319
  76.9 1.2 %collective-permute-start.27 = (bf16[160,384]{1,0:T(8,128)(2,1)S(1)}, bf16[160,384]{1,0:T(8,128)(2,1)S(1)}, u32[]{:S(2)}, u32[]{:S(2)}) collective-permute-start(bf16[160,384]{1,0:T(8,128)(2,1)S(1)} %scores.1.p0), channel_id=1, source_target_pairs={{0,32},{32,64},{64,96},{96,0},{1,33},{33,65},{65,97},{97,1},{2,34}... | collective-permute-start | bytes 368648 | tf_op jit(solution)/shard_map/ppermute | solution.py:68
  78.1 3.3 %collective-permute-start.28 = (bf16[160,384]{1,0:T(8,128)(2,1)S(1)}, bf16[160,384]{1,0:T(8,128)(2,1)S(1)}, u32[]{:S(2)}, u32[]{:S(2)}) collective-permute-start(bf16[160,384]{1,0:T(8,128)(2,1)S(1)} %scores.1.p0), channel_id=1, source_target_pairs={{0,64},{32,96},{64,0},{96,32},{1,65},{33,97},{65,1},{97,33},{2,66}... | collective-permute-start | bytes 368648 | tf_op jit(solution)/shard_map/ppermute | solution.py:68
  81.4 0.0 collective-permute-start.29
  81.4 2.2 %collective-permute-done.27.p1 = bf16[160,384]{1,0:T(8,128)(2,1)S(1)} collective-permute-done((bf16[160,384]{1,0:T(8,128)(2,1)S(1)}, bf16[160,384]{1,0:T(8,128)(2,1)S(1)}, u32[]{:S(2)}, u32[]{:S(2)}) %collective-permute-start.27) | collective-permute-done | bytes 122912 | tf_op jit(solution)/shard_map/ppermute | solution.py:68
  83.6 3.5 %collective-permute-done.28.p2 = bf16[160,384]{1,0:T(8,128)(2,1)S(1)} collective-permute-done((bf16[160,384]{1,0:T(8,128)(2,1)S(1)}, bf16[160,384]{1,0:T(8,128)(2,1)S(1)}, u32[]{:S(2)}, u32[]{:S(2)}) %collective-permute-start.28) | collective-permute-done | bytes 122912 | tf_op jit(solution)/shard_map/ppermute | solution.py:68
  87.1 0.9 sum.1
  (19 shorter events, 0.1 us)
Async XLA Ops:
  0.0 1.0 %copy-start = (bf16[192,1024]{1,0:T(8,128)(2,1)S(1)}, bf16[192,1024]{1,0:T(8,128)(2,1)}, u32[]{:S(2)}) copy-start(bf16[192,1024]{1,0:T(8,128)(2,1)} %w_in.1) | copy-start | bytes 1179652
  1.0 0.9 %copy-start.2 = (bf16[256,153]{0,1:T(8,128)(2,1)S(1)}, bf16[256,153]{0,1:T(8,128)(2,1)}, u32[]{:S(2)}) copy-start(bf16[256,153]{0,1:T(8,128)(2,1)} %param.12) | copy-start | bytes 235012
  1.9 0.7 copy-start.4
  2.7 17.9 %collective-permute-start.3 = (bf16[2,256,512]{2,1,0:T(8,128)(2,1)S(1)}, bf16[2,256,512]{2,1,0:T(8,128)(2,1)S(1)}, u32[]{:S(2)}, u32[]{:S(2)}) collective-permute-start(bf16[2,256,512]{2,1,0:T(8,128)(2,1)S(1)} %get-tuple-element.22.own), channel_id=1, source_target_pairs={{0,32},{32,64},{64,96},{96,0},{1,97},{33,1},{65,33},{97,65},{2,34}... | collective-permute-start | bytes 1572872 | tf_op jit(solution)/shard_map/ppermute | solution.py:73
  6.3 14.2 %collective-permute-start = (bf16[192,384]{1,0:T(8,128)(2,1)}, bf16[192,384]{1,0:T(8,128)(2,1)S(1)}, u32[]{:S(2)}, u32[]{:S(2)}) collective-permute-start(bf16[192,384]{1,0:T(8,128)(2,1)} %bitcast.9), channel_id=1, source_target_pairs={{0,8},{1,3},{2,10},{3,5},{4,12},{5,7},{6,14},{7,1},{8,16},{9,11},{... | collective-permute-start | bytes 442376 | tf_op jit(solution)/shard_map/ppermute | solution.py:56
  8.0 12.6 %collective-permute-start.1 = (bf16[192,384]{1,0:T(8,128)(2,1)}, bf16[192,384]{1,0:T(8,128)(2,1)S(1)}, u32[]{:S(2)}, u32[]{:S(2)}) collective-permute-start(bf16[192,384]{1,0:T(8,128)(2,1)} %bitcast.10), channel_id=1, source_target_pairs={{0,24},{1,7},{2,26},{3,1},{4,28},{5,3},{6,30},{7,5},{8,0},{9,15},{... | collective-permute-start | bytes 442376 | tf_op jit(solution)/shard_map/ppermute | solution.py:56
  10.1 10.5 %collective-permute-start.2 = (bf16[192,384]{1,0:T(8,128)(2,1)}, bf16[192,384]{1,0:T(8,128)(2,1)S(1)}, u32[]{:S(2)}, u32[]{:S(2)}) collective-permute-start(bf16[192,384]{1,0:T(8,128)(2,1)} %bitcast.11), channel_id=1, source_target_pairs={{0,16},{1,5},{2,18},{3,7},{4,20},{5,1},{6,22},{7,3},{8,24},{9,13},... | collective-permute-start | bytes 442376 | tf_op jit(solution)/shard_map/ppermute | solution.py:56
  11.4 0.7 copy-start.3
  12.1 8.5 %copy-start.1 = (bf16[384,192]{0,1:T(8,128)(2,1)S(1)}, bf16[384,192]{0,1:T(8,128)(2,1)}, u32[]{:S(2)}) copy-start(bf16[384,192]{0,1:T(8,128)(2,1)} %param.7) | copy-start | bytes 442372
  20.7 15.7 %collective-permute-start.9 = (bf16[4,192,384]{2,1,0:T(8,128)(2,1)S(1)}, bf16[4,192,384]{2,1,0:T(8,128)(2,1)S(1)}, u32[]{:S(2)}, u32[]{:S(2)}) collective-permute-start(bf16[4,192,384]{2,1,0:T(8,128)(2,1)S(1)} %stack.21.refs_0_), channel_id=1, source_target_pairs={{0,6},{1,25},{2,0},{3,27},{4,2},{5,29},{6,4},{7,31},{8,14},{9,1},{... | collective-permute-start | bytes 1769480 | tf_op jit(solution)/shard_map/ppermute | solution.py:60
  23.2 16.6 %collective-permute-start.6 = (bf16[4,192,384]{2,1,0:T(8,128)(2,1)S(1)}, bf16[4,192,384]{2,1,0:T(8,128)(2,1)S(1)}, u32[]{:S(2)}, u32[]{:S(2)}) collective-permute-start(bf16[4,192,384]{2,1,0:T(8,128)(2,1)S(1)} %stack.21.refs_0_), channel_id=1, source_target_pairs={{0,2},{1,9},{2,4},{3,11},{4,6},{5,13},{6,0},{7,15},{8,10},{9,17},{... | collective-permute-start | bytes 1769480 | tf_op jit(solution)/shard_map/ppermute | solution.py:60
  23.2 18.5 %collective-permute-start.4 = (bf16[4,192,384]{2,1,0:T(8,128)(2,1)S(1)}, bf16[4,192,384]{2,1,0:T(8,128)(2,1)S(1)}, u32[]{:S(2)}, u32[]{:S(2)}) collective-permute-start(bf16[4,192,384]{2,1,0:T(8,128)(2,1)S(1)} %stack.21.refs_0_), channel_id=1, source_target_pairs={{0,1},{1,0},{2,3},{3,2},{4,5},{5,4},{6,7},{7,6},{8,9},{9,8},{10,11... | collective-permute-start | bytes 1769480 | tf_op jit(solution)/shard_map/ppermute | solution.py:64
  24.3 18.4 %collective-permute-start.5 = (bf16[4,192,384]{2,1,0:T(8,128)(2,1)S(1)}, bf16[4,192,384]{2,1,0:T(8,128)(2,1)S(1)}, u32[]{:S(2)}, u32[]{:S(2)}) collective-permute-start(bf16[4,192,384]{2,1,0:T(8,128)(2,1)S(1)} %stack.21.refs_0_), channel_id=1, source_target_pairs={{0,4},{1,17},{2,6},{3,19},{4,0},{5,21},{6,2},{7,23},{8,12},{9,25},... | collective-permute-start | bytes 1769480 | tf_op jit(solution)/shard_map/ppermute | solution.py:60
  25.7 9.0 %collective-permute-start.8 = (bf16[256,512]{1,0:T(8,128)(2,1)S(1)}, bf16[256,512]{1,0:T(8,128)(2,1)S(1)}, u32[]{:S(2)}, u32[]{:S(2)}) collective-permute-start(bf16[256,512]{1,0:T(8,128)(2,1)S(1)} %get-tuple-element.18.refs_0_), channel_id=1, source_target_pairs={{0,64},{32,96},{64,0},{96,32},{1,65},{33,97},{65,1},{97,33},{2,66}... | collective-permute-start | bytes 786440 | tf_op jit(solution)/shard_map/ppermute | solution.py:68
  39.8 4.1 %collective-permute-start.7 = (bf16[4,192,384]{2,1,0:T(8,128)(2,1)S(1)}, bf16[4,192,384]{2,1,0:T(8,128)(2,1)S(1)}, u32[]{:S(2)}, u32[]{:S(2)}) collective-permute-start(bf16[4,192,384]{2,1,0:T(8,128)(2,1)S(1)} %collective-permute-done.6.refs_0_), channel_id=1, source_target_pairs={{0,1},{1,0},{2,3},{3,2},{4,5},{5,4},{6,7},{7,6},{8,9},{9,8},{10,11... | collective-permute-start | bytes 1769480 | tf_op jit(solution)/shard_map/ppermute | solution.py:64
  41.7 2.5 %collective-permute-start.10 = (bf16[4,192,384]{2,1,0:T(8,128)(2,1)S(1)}, bf16[4,192,384]{2,1,0:T(8,128)(2,1)S(1)}, u32[]{:S(2)}, u32[]{:S(2)}) collective-permute-start(bf16[4,192,384]{2,1,0:T(8,128)(2,1)S(1)} %collective-permute-done.9.refs_2_), channel_id=1, source_target_pairs={{0,1},{1,0},{2,3},{3,2},{4,5},{5,4},{6,7},{7,6},{8,9},{9,8},{10,11... | collective-permute-start | bytes 1769480 | tf_op jit(solution)/shard_map/ppermute | solution.py:64
  42.7 3.3 %collective-permute-start.11 = (bf16[4,192,384]{2,1,0:T(8,128)(2,1)S(1)}, bf16[4,192,384]{2,1,0:T(8,128)(2,1)S(1)}, u32[]{:S(2)}, u32[]{:S(2)}) collective-permute-start(bf16[4,192,384]{2,1,0:T(8,128)(2,1)S(1)} %collective-permute-done.5.refs_0_), channel_id=1, source_target_pairs={{0,1},{1,0},{2,3},{3,2},{4,5},{5,4},{6,7},{7,6},{8,9},{9,8},{10,11... | collective-permute-start | bytes 1769480 | tf_op jit(solution)/shard_map/ppermute | solution.py:64
  43.3 8.5 %collective-permute-start.15 = (bf16[2,256,512]{2,1,0:T(8,128)(2,1)S(1)}, bf16[2,256,512]{2,1,0:T(8,128)(2,1)S(1)}, u32[]{:S(2)}, u32[]{:S(2)}) collective-permute-start(bf16[2,256,512]{2,1,0:T(8,128)(2,1)S(1)} %collective-permute-done.3.after_too.side), channel_id=1, source_target_pairs={{0,1},{1,0},{2,3},{3,2},{4,5},{5,4},{6,7},{7,6},{8,9},{9,8},{10,11... | collective-permute-start | bytes 1572872 | tf_op jit(solution)/shard_map/ppermute | solution.py:64
  43.4 8.4 %collective-permute-start.16 = (bf16[256,512]{1,0:T(8,128)(2,1)S(1)}, bf16[256,512]{1,0:T(8,128)(2,1)S(1)}, u32[]{:S(2)}, u32[]{:S(2)}) collective-permute-start(bf16[256,512]{1,0:T(8,128)(2,1)S(1)} %collective-permute-done.8.near), channel_id=1, source_target_pairs={{0,1},{1,0},{2,3},{3,2},{4,5},{5,4},{6,7},{7,6},{8,9},{9,8},{10,11... | collective-permute-start | bytes 786440 | tf_op jit(solution)/shard_map/ppermute | solution.py:64
  46.0 35.4 %copy-start.5 = (f32[153]{0:T(256)S(1)}, f32[153]{0:T(256)}, u32[]{:S(2)}) copy-start(f32[153]{0:T(256)} %param.13) | copy-start | bytes 1840
  47.1 4.8 %collective-permute-start.12 = (bf16[96,192]{1,0:T(8,128)(2,1)S(1)}, bf16[96,192]{1,0:T(8,128)(2,1)S(1)}, u32[]{:S(2)}, u32[]{:S(2)}) collective-permute-start(bf16[96,192]{1,0:T(8,128)(2,1)S(1)} %get-tuple-element.27), channel_id=1, source_target_pairs={{0,32},{32,64},{64,96},{96,0},{1,33},{33,65},{65,97},{97,1},{2,34}... | collective-permute-start | bytes 110600 | tf_op jit(solution)/shard_map/ppermute | solution.py:68
  48.4 4.4 %collective-permute-start.13 = (bf16[96,192]{1,0:T(8,128)(2,1)S(1)}, bf16[96,192]{1,0:T(8,128)(2,1)S(1)}, u32[]{:S(2)}, u32[]{:S(2)}) collective-permute-start(bf16[96,192]{1,0:T(8,128)(2,1)S(1)} %get-tuple-element.28), channel_id=1, source_target_pairs={{0,64},{32,96},{64,0},{96,32},{1,65},{33,97},{65,1},{97,33},{2,66}... | collective-permute-start | bytes 110600 | tf_op jit(solution)/shard_map/ppermute | solution.py:68
  49.9 3.6 %collective-permute-start.14 = (bf16[96,192]{1,0:T(8,128)(2,1)S(1)}, bf16[96,192]{1,0:T(8,128)(2,1)S(1)}, u32[]{:S(2)}, u32[]{:S(2)}) collective-permute-start(bf16[96,192]{1,0:T(8,128)(2,1)S(1)} %get-tuple-element.29), channel_id=1, source_target_pairs={{0,96},{32,0},{64,32},{96,64},{1,97},{33,1},{65,33},{97,65},{2,98}... | collective-permute-start | bytes 110600 | tf_op jit(solution)/shard_map/ppermute | solution.py:68
  54.5 4.3 %collective-permute-start.19 = (bf16[128,128]{1,0:T(8,128)(2,1)S(1)}, bf16[128,128]{1,0:T(8,128)(2,1)S(1)}, u32[]{:S(2)}, u32[]{:S(2)}) collective-permute-start(bf16[128,128]{1,0:T(8,128)(2,1)S(1)} %hidden.1), channel_id=1, source_target_pairs={{0,16},{1,5},{2,18},{3,7},{4,20},{5,1},{6,22},{7,3},{8,24},{9,13},... | collective-permute-start | bytes 98312 | tf_op jit(solution)/shard_map/ppermute | solution.py:56
  54.5 4.3 %collective-permute-start.18 = (bf16[128,128]{1,0:T(8,128)(2,1)S(1)}, bf16[128,128]{1,0:T(8,128)(2,1)S(1)}, u32[]{:S(2)}, u32[]{:S(2)}) collective-permute-start(bf16[128,128]{1,0:T(8,128)(2,1)S(1)} %hidden.1), channel_id=1, source_target_pairs={{0,24},{1,7},{2,26},{3,1},{4,28},{5,3},{6,30},{7,5},{8,0},{9,15},{... | collective-permute-start | bytes 98312 | tf_op jit(solution)/shard_map/ppermute | solution.py:56
  55.3 4.0 %collective-permute-start.17 = (bf16[128,128]{1,0:T(8,128)(2,1)S(1)}, bf16[128,128]{1,0:T(8,128)(2,1)S(1)}, u32[]{:S(2)}, u32[]{:S(2)}) collective-permute-start(bf16[128,128]{1,0:T(8,128)(2,1)S(1)} %hidden.1), channel_id=1, source_target_pairs={{0,8},{1,3},{2,10},{3,5},{4,12},{5,7},{6,14},{7,1},{8,16},{9,11},{... | collective-permute-start | bytes 98312 | tf_op jit(solution)/shard_map/ppermute | solution.py:56
  59.3 8.7 %collective-permute-start.21 = (bf16[4,128,128]{2,1,0:T(8,128)(2,1)S(1)}, bf16[4,128,128]{2,1,0:T(8,128)(2,1)S(1)}, u32[]{:S(2)}, u32[]{:S(2)}) collective-permute-start(bf16[4,128,128]{2,1,0:T(8,128)(2,1)S(1)} %pad_maximum_fusion.refs_0_), channel_id=1, source_target_pairs={{0,2},{1,9},{2,4},{3,11},{4,6},{5,13},{6,0},{7,15},{8,10},{9,17},{... | collective-permute-start | bytes 393224 | tf_op jit(solution)/shard_map/ppermute | solution.py:60
  59.6 11.4 %collective-permute-start.23 = (bf16[4,128,128]{2,1,0:T(8,128)(2,1)S(1)}, bf16[4,128,128]{2,1,0:T(8,128)(2,1)S(1)}, u32[]{:S(2)}, u32[]{:S(2)}) collective-permute-start(bf16[4,128,128]{2,1,0:T(8,128)(2,1)S(1)} %pad_maximum_fusion.refs_0_), channel_id=1, source_target_pairs={{0,6},{1,25},{2,0},{3,27},{4,2},{5,29},{6,4},{7,31},{8,14},{9,1},{... | collective-permute-start | bytes 393224 | tf_op jit(solution)/shard_map/ppermute | solution.py:60
  62.0 9.9 %collective-permute-start.25 = (bf16[4,128,128]{2,1,0:T(8,128)(2,1)S(1)}, bf16[4,128,128]{2,1,0:T(8,128)(2,1)S(1)}, u32[]{:S(2)}, u32[]{:S(2)}) collective-permute-start(bf16[4,128,128]{2,1,0:T(8,128)(2,1)S(1)} %pad_maximum_fusion.refs_0_), channel_id=1, source_target_pairs={{0,4},{1,17},{2,6},{3,19},{4,0},{5,21},{6,2},{7,23},{8,12},{9,25},... | collective-permute-start | bytes 393224 | tf_op jit(solution)/shard_map/ppermute | solution.py:60
  62.2 12.3 %collective-permute-start.20 = (bf16[4,128,128]{2,1,0:T(8,128)(2,1)S(1)}, bf16[4,128,128]{2,1,0:T(8,128)(2,1)S(1)}, u32[]{:S(2)}, u32[]{:S(2)}) collective-permute-start(bf16[4,128,128]{2,1,0:T(8,128)(2,1)S(1)} %pad_maximum_fusion.refs_0_), channel_id=1, source_target_pairs={{0,1},{1,0},{2,3},{3,2},{4,5},{5,4},{6,7},{7,6},{8,9},{9,8},{10,11... | collective-permute-start | bytes 393224 | tf_op jit(solution)/shard_map/ppermute | solution.py:64
  68.0 6.5 %collective-permute-start.22 = (bf16[4,128,128]{2,1,0:T(8,128)(2,1)S(1)}, bf16[4,128,128]{2,1,0:T(8,128)(2,1)S(1)}, u32[]{:S(2)}, u32[]{:S(2)}) collective-permute-start(bf16[4,128,128]{2,1,0:T(8,128)(2,1)S(1)} %collective-permute-done.21.refs_2_), channel_id=1, source_target_pairs={{0,1},{1,0},{2,3},{3,2},{4,5},{5,4},{6,7},{7,6},{8,9},{9,8},{10,11... | collective-permute-start | bytes 393224 | tf_op jit(solution)/shard_map/ppermute | solution.py:64
  70.9 3.5 %collective-permute-start.24 = (bf16[4,128,128]{2,1,0:T(8,128)(2,1)S(1)}, bf16[4,128,128]{2,1,0:T(8,128)(2,1)S(1)}, u32[]{:S(2)}, u32[]{:S(2)}) collective-permute-start(bf16[4,128,128]{2,1,0:T(8,128)(2,1)S(1)} %collective-permute-done.23.refs_4_), channel_id=1, source_target_pairs={{0,1},{1,0},{2,3},{3,2},{4,5},{5,4},{6,7},{7,6},{8,9},{9,8},{10,11... | collective-permute-start | bytes 393224 | tf_op jit(solution)/shard_map/ppermute | solution.py:64
  71.9 3.5 %collective-permute-start.26 = (bf16[4,128,128]{2,1,0:T(8,128)(2,1)S(1)}, bf16[4,128,128]{2,1,0:T(8,128)(2,1)S(1)}, u32[]{:S(2)}, u32[]{:S(2)}) collective-permute-start(bf16[4,128,128]{2,1,0:T(8,128)(2,1)S(1)} %collective-permute-done.25.refs_6_), channel_id=1, source_target_pairs={{0,1},{1,0},{2,3},{3,2},{4,5},{5,4},{6,7},{7,6},{8,9},{9,8},{10,11... | collective-permute-start | bytes 393224 | tf_op jit(solution)/shard_map/ppermute | solution.py:64
  76.9 6.7 %collective-permute-start.27 = (bf16[160,384]{1,0:T(8,128)(2,1)S(1)}, bf16[160,384]{1,0:T(8,128)(2,1)S(1)}, u32[]{:S(2)}, u32[]{:S(2)}) collective-permute-start(bf16[160,384]{1,0:T(8,128)(2,1)S(1)} %scores.1.p0), channel_id=1, source_target_pairs={{0,32},{32,64},{64,96},{96,0},{1,33},{33,65},{65,97},{97,1},{2,34}... | collective-permute-start | bytes 368648 | tf_op jit(solution)/shard_map/ppermute | solution.py:68
  78.1 9.0 %collective-permute-start.28 = (bf16[160,384]{1,0:T(8,128)(2,1)S(1)}, bf16[160,384]{1,0:T(8,128)(2,1)S(1)}, u32[]{:S(2)}, u32[]{:S(2)}) collective-permute-start(bf16[160,384]{1,0:T(8,128)(2,1)S(1)} %scores.1.p0), channel_id=1, source_target_pairs={{0,64},{32,96},{64,0},{96,32},{1,65},{33,97},{65,1},{97,33},{2,66}... | collective-permute-start | bytes 368648 | tf_op jit(solution)/shard_map/ppermute | solution.py:68
  81.4 5.7 %collective-permute-start.29 = (bf16[160,384]{1,0:T(8,128)(2,1)S(1)}, bf16[160,384]{1,0:T(8,128)(2,1)S(1)}, u32[]{:S(2)}, u32[]{:S(2)}) collective-permute-start(bf16[160,384]{1,0:T(8,128)(2,1)S(1)} %scores.1.p0), channel_id=1, source_target_pairs={{0,96},{32,0},{64,32},{96,64},{1,97},{33,1},{65,33},{97,65},{2,98}... | collective-permute-start | bytes 368648 | tf_op jit(solution)/shard_map/ppermute | solution.py:68

commit v4 on v3

--- a/solution.py
+++ b/solution.py
@@ -1,3 +1,5 @@
+import functools
+
 import jax
 import jax.numpy as jnp
 from jax import lax
@@ -16,6 +18,7 @@
 NT = (((1,), (1,)), ((), ()))
 VM = pl.BlockSpec(memory_space=pltpu.VMEM)
 SM = pl.BlockSpec(memory_space=pltpu.SMEM)
+HB = pl.BlockSpec(memory_space=pltpu.HBM)
 ANY = pl.BlockSpec(memory_space=pl.ANY)
 
 
@@ -78,9 +81,17 @@
 SLOTS = 3
 
 
-def adjacency_kernel(mask, counts, *refs):
-    adj, adj2, degree, slots, sems = refs[-5:]
+def adjacency_kernel(part, mask, counts, *refs):
+    if part == 0:
+        w_in, w_out_t, b_in, adj, adj2, degree, whole, mine, slots, sems, mask_sm, one, w1, w2, b1, three = refs
+        extra = [(w_in, w1), (w_out_t, w2), (b_in, b1)]
+    else:
+        adj, adj2, degree, slots, sems, mask_sm, one = refs[4:]
+        extra = []
     me, feat = here()
+    first, last = part * STEPS // 2, (part + 1) * STEPS // 2
+    mask_copy = pltpu.make_async_copy(mask, mask_sm, one)
+    mask_copy.start()
     source_row = lax.broadcasted_iota(jnp.int32, (ROWS, TILE), 0)
     target = lax.broadcasted_iota(jnp.int32, (ROWS, TILE), 1)
     chosen = (source_row == target + feat * SHARE) & (target < SHARE)
@@ -92,16 +103,21 @@
         return pltpu.make_async_copy(counts.at[:, pl.ds(start, CHUNK)], slots.at[slot], sems.at[slot])
 
     for i in range(SLOTS - 1):
-        fetch(i, i).start()
-    degree[...] = jnp.zeros_like(degree)
-
-    @pl.loop(0, STEPS)
+        fetch(first + i, i).start()
+    extra = [pltpu.make_async_copy(a, b, three.at[i]) for i, (a, b) in enumerate(extra)]
+    for copy in extra:
+        copy.start()
+    if part == 0:
+        degree[...] = jnp.zeros_like(degree)
+    mask_copy.wait()
+
+    @pl.loop(first, last)
     def _(step):
-        slot = lax.rem(step, SLOTS)
-
-        @pl.when(step + SLOTS - 1 < STEPS)
+        slot = lax.rem(step - first, SLOTS)
+
+        @pl.when(step + SLOTS - 1 < last)
         def _():
-            fetch(step + SLOTS - 1, lax.rem(step + SLOTS - 1, SLOTS)).start()
+            fetch(step + SLOTS - 1, lax.rem(step - first + SLOTS - 1, SLOTS)).start()
 
         fetch(step, slot).wait()
         for j in range(CHUNK // ROWS):
@@ -111,7 +127,7 @@
                 rows = slice(i * TILE, (i + 1) * TILE)
                 strip = []
                 for k in range(ROWS // TILE):
-                    stored = mask[i, (step * (CHUNK // ROWS) + j) * (ROWS // TILE) + k].astype(f32)
+                    stored = mask_sm[i, (step * (CHUNK // ROWS) + j) * (ROWS // TILE) + k].astype(f32)
                     tile = slots[slot, rows, j * ROWS + k * TILE : j * ROWS + (k + 1) * TILE]
                     strip.append((tile.astype(f32) * stored).astype(bf16))
                 strip = jnp.concatenate(strip, axis=1)
@@ -120,6 +136,11 @@
                 degree[rows, :] += part
                 adj2[rows, pl.ds(place, TILE)] = jnp.where(inside, part, 0.0).astype(bf16)
 
+    for copy in extra:
+        copy.wait()
+    if part == 0:
+        pack(w1, w2, b1, whole, mine)
+        return
     place = pl.ds(pl.multiple_of(me * TILE, TILE), TILE)
     adj2[:, place] = (adj2[:, place].astype(f32) + chosen.astype(f32)).astype(bf16)
     row = lax.broadcasted_iota(jnp.int32, (ROWS, ROWS), 0)
@@ -129,25 +150,55 @@
     degree[...] = jnp.broadcast_to(degree[:, SHARE : SHARE + 1] + 1.0, degree.shape)
 
 
-def make_adjacency(tile_mask, counts, *after):
-    counts = pltpu.with_memory_space_constraint(counts, pltpu.HBM)
+ADJACENCY = [
+    pltpu.VMEM((ROWS, NV * ROWS), bf16),
+    pltpu.VMEM((ROWS, NV * TILE), bf16),
+    pltpu.VMEM((ROWS, TILE), f32),
+]
+ADJACENCY_SCRATCH = [
+    pltpu.VMEM((SLOTS, ROWS, CHUNK), jnp.int32),
+    pltpu.SemaphoreType.DMA((SLOTS,)),
+    pltpu.SMEM((ROWS // TILE, NV * ROWS // TILE), jnp.int32),
+    pltpu.SemaphoreType.DMA(()),
+]
+
+
+def first_half(tile_mask, counts, w_in, w_out_t, b_in):
     return pl.pallas_call(
-        adjacency_kernel,
-        in_specs=[SM, pl.BlockSpec(memory_space=pltpu.HBM)] + [ANY] * len(after),
+        functools.partial(adjacency_kernel, 0),
+        in_specs=[HB] * 5,
+        out_specs=[VM] * 5,
+        out_shape=ADJACENCY + [
+            jax.ShapeDtypeStruct((2, 256, 512), bf16),
+            jax.ShapeDtypeStruct((256, 512), bf16),
+        ],
+        scratch_shapes=ADJACENCY_SCRATCH + [
+            pltpu.VMEM((192, 1024), bf16),
+            pltpu.VMEM((CLS, 256), bf16),
+            pltpu.VMEM((1, 256), f32),
+            pltpu.SemaphoreType.DMA((3,)),
+        ],
+        compiler_params=params(24),
+        cost_estimate=cost(1.2e9, 16e6),
+        name="adjacency_first",
+    )(tile_mask, counts, w_in, w_out_t, b_in)
+
+
+def second_half(tile_mask, counts, adj, adj2, degree, after):
+    return pl.pallas_call(
+        functools.partial(adjacency_kernel, 1),
+        in_specs=[HB] * 2 + [VM] * 3 + [ANY],
         out_specs=[VM] * 3,
-        out_shape=[
-            pltpu.VMEM((ROWS, NV * ROWS), bf16),
-            pltpu.VMEM((ROWS, NV * TILE), bf16),
-            pltpu.VMEM((ROWS, TILE), f32),
-        ],
-        scratch_shapes=[pltpu.VMEM((SLOTS, ROWS, CHUNK), jnp.int32), pltpu.SemaphoreType.DMA((SLOTS,))],
+        out_shape=ADJACENCY,
+        input_output_aliases={2: 0, 3: 1, 4: 2},
+        scratch_shapes=ADJACENCY_SCRATCH,
         compiler_params=params(24),
-        cost_estimate=cost(2.4e9, 31e6),
-        name="adjacency",
-    )(tile_mask, counts, *after)
-
-
-def pack_kernel(w_in, w_out_t, b_in, whole, mine):
+        cost_estimate=cost(1.2e9, 16e6),
+        name="adjacency_second",
+    )(tile_mask, counts, adj, adj2, degree, after)
+
+
+def pack(w_in, w_out_t, b_in, whole, mine):
     zero = jnp.zeros((192 - CLS, TILE), f32)
     for half in range(2):
         lanes = slice(TILE * half, TILE * (half + 1))
@@ -167,7 +218,7 @@
     mine[...] = whole[lax.rem(here()[0], 2)]
 
 
-def stack_kernel(a, b, c, d, after, after_too, out):
+def stack_kernel(a, b, c, d, after, out):
     for i, part in enumerate((a, b, c, d)):
         out[i] = part[...]
 
@@ -184,7 +235,7 @@
 
 
 def product_first(adj, *refs):
-    refs[-1][...] = add_blocks((0,), adj, jnp.zeros(refs[-1].shape, f32), refs[:-1])
+    refs[-1][...] = add_blocks((0,), adj, jnp.zeros(refs[-1].shape, f32), refs[:-2])
 
 
 def product_next(adj, before, *refs):
@@ -263,35 +314,35 @@
 
 
 def local(features, counts, tile_mask, w_in, b_in, w_out, b_out):
-    whole, mine_half = pl.pallas_call(
-        pack_kernel,
-        out_shape=[jax.ShapeDtypeStruct((2, 256, 512), bf16), jax.ShapeDtypeStruct((256, 512), bf16)],
-        in_specs=[VM] * 3, out_specs=[VM] * 2,
-        compiler_params=params(), cost_estimate=cost(1e5, 1.2e6), name="pack",
-    )(w_in, w_out.T, b_in.reshape(1, 256))
+    tile_mask, counts, *weights = (
+        pltpu.with_memory_space_constraint(a, pltpu.HBM)
+        for a in (tile_mask, counts, w_in, w_out.T, b_in.reshape(1, 256))
+    )
+    *adjacency, whole, mine_half = first_half(tile_mask, counts, *weights)
     side = both_sides(whole)
     near = along_feat(mine_half, 2)
-    adj, adj2, degree = make_adjacency(tile_mask, counts, mine_half)
 
     mine = features.T
-    ring = [first_axis(mine, s) for s in (1, 3, 2)]
+    ring = [first_axis(mine, s) for s in (2, 1, 3)]
     four = pl.pallas_call(
         stack_kernel, out_shape=jax.ShapeDtypeStruct((NF, 192, ROWS), bf16),
-        in_specs=[VM] * 4 + [ANY] * 2, out_specs=VM,
+        in_specs=[VM] * 4 + [ANY], out_specs=VM,
         compiler_params=params(), cost_estimate=cost(1e5, 1.2e6), name="stack",
-    )(mine, *ring, degree, side)
-    rows = {t: second_axis(four, t) for t in (1, 3, 2)}
-
-    near, rows[3] = lax.optimization_barrier((near, rows[3]))
-    other_side, far = swap(side), swap(near)
+    )(mine, ring[1], ring[2], ring[0], mine_half)
+    rows = {t: second_axis(four, t) for t in (2, 1, 3)}
+
+    adj, adj2, degree = second_half(tile_mask, counts, *adjacency, mine_half)
 
     total_shape = jax.ShapeDtypeStruct((ROWS, 192), f32)
     pieces = [four, swap(four)]
     total = pl.pallas_call(
-        product_first, out_shape=total_shape, in_specs=[VM] * 3, out_specs=VM,
+        product_first, out_shape=total_shape, in_specs=[VM] * 3 + [ANY], out_specs=VM,
         compiler_params=params(), cost_estimate=blocks_cost(pieces), name="product_first",
-    )(adj, *pieces)
-    total, rows[2] = lax.optimization_barrier((total, rows[2]))
+    )(adj, *pieces, near)
+    for t in (1, 2, 3):
+        rows[t] = lax.optimization_barrier((total, rows[t]))[1]
+    side, near, _ = lax.optimization_barrier((side, near, total))
+    other_side, far = swap(side), swap(near)
     pieces = [rows[1], swap(rows[1]), rows[3], swap(rows[3])]
     total = pl.pallas_call(
         product_next, out_shape=total_shape, in_specs=[VM] * 6, out_specs=VM,

time: 88.2 us -> 79.1 us (0.90)
  waiting for transfers between devices: 23.2 us -> 15.8 us
  local copies, waits for them, and re-layouts: 3.25 us -> 0.01 us
  Pallas kernels: 15.9 us -> 17 us
    ppermute x6, waiting for transfers between devices: 5.07 us -> 0.02 us  [second_axis(): lax.ppermute(value, 'vert', positions(lambda x, z, c: (x + shift * c, z +...]
    ppermute x7, waiting for transfers between devices: 13.6 us -> 10.3 us  [along_feat(): lax.ppermute(value, 'feat', [(i, (i + shift) % NF) for i in range(NF)])]
    unnamed x12 -> x4, local copies, waits for them, and re-layouts: 3.25 us -> 0.01 us
    ppermute x6, starting transfers between devices: 6.67 us -> 8.92 us  [first_axis(): lax.ppermute(value, 'vert', positions(lambda x, z, c: (x + shift * (1 - c...]
    pallas_call x3, Pallas kernels: 9.59 us -> 10.8 us  [the longest x1 4.97 us: first_half(): pl.pallas_call(functools.partial(adjacency_kernel, 0), in_specs=[HB] * 5,...]
    ppermute x1, starting transfers between devices: 3.63 us -> 2.73 us  [both_sides(): return lax.ppermute(value, ('feat', 'vert'), pairs)]
  transfers between devices with their start and end apart: 30 -> 30, of which waited for: 11 -> 9; matrix products, arithmetic and copies ran while one was open for 0% -> 0% of each run, Pallas kernels for 14% -> 17%
where the time goes in v4:
time: 79.1 us; the launch traced here: 78.9 us
  starting transfers between devices  45.9 us (58%)
  Pallas kernels  17 us (21%)
  waiting for transfers between devices  15.8 us (20%)
    ppermute x10, starting transfers between devices, swap(): return lax.ppermute(value, 'vert', positions(lambda x, z, c: (x, z, 1 - c)))  16 us
    ppermute x7, starting transfers between devices, along_feat(): lax.ppermute(value, 'feat', [(i, (i + shift) % NF) for i in range(NF)])  11.5 us
    ppermute x7, waiting for transfers between devices, along_feat(): lax.ppermute(value, 'feat', [(i, (i + shift) % NF) for i in range(NF)])  10.3 us
    ppermute x6, starting transfers between devices, first_axis(): lax.ppermute(value, 'vert', positions(lambda x, z, c: (x + shift * (1 - c...  8.92 us
    ppermute x6, starting transfers between devices, second_axis(): lax.ppermute(value, 'vert', positions(lambda x, z, c: (x + shift * c, z +...  6.7 us
    pallas_call x1, Pallas kernels, first_half(): pl.pallas_call(functools.partial(adjacency_kernel, 0), in_specs=[HB] * 5,...  4.97 us
    pallas_call x1, Pallas kernels, second_half(): pl.pallas_call(functools.partial(adjacency_kernel, 1), in_specs=[HB] * 2...  4.79 us
    ppermute x6, waiting for transfers between devices, first_axis(): lax.ppermute(value, 'vert', positions(lambda x, z, c: (x + shift * (1 - c...  3.98 us
  transfers between devices with their start and end apart: 30, of which 9 were waited for; matrix products, arithmetic and copies ran while one was open for 0% of the time, Pallas kernels for 17%

profile of v4, /device:TPU:1, one launch (start us, length us, event | category | flops | bytes accessed | tf_op | source)
XLA Modules:
  0.0 78.9 jit_solution(8288423013734404260)
XLA Ops:
  0.0 2.5 %collective-permute-start = (bf16[192,384]{1,0:T(8,128)(2,1)}, bf16[192,384]{1,0:T(8,128)(2,1)S(1)}, u32[]{:S(2)}, u32[]{:S(2)}) collective-permute-start(bf16[192,384]{1,0:T(8,128)(2,1)} %bitcast.9), channel_id=1, source_target_pairs={{0,8},{1,3},{2,10},{3,5},{4,12},{5,7},{6,14},{7,1},{8,16},{9,11},{... | collective-permute-start | bytes 442376 | tf_op jit(solution)/shard_map/ppermute | solution.py:59
  2.5 2.1 %collective-permute-start.1 = (bf16[192,384]{1,0:T(8,128)(2,1)}, bf16[192,384]{1,0:T(8,128)(2,1)S(1)}, u32[]{:S(2)}, u32[]{:S(2)}) collective-permute-start(bf16[192,384]{1,0:T(8,128)(2,1)} %bitcast.10), channel_id=1, source_target_pairs={{0,24},{1,7},{2,26},{3,1},{4,28},{5,3},{6,30},{7,5},{8,0},{9,15},{... | collective-permute-start | bytes 442376 | tf_op jit(solution)/shard_map/ppermute | solution.py:59
  4.6 1.3 %collective-permute-start.2 = (bf16[192,384]{1,0:T(8,128)(2,1)}, bf16[192,384]{1,0:T(8,128)(2,1)S(1)}, u32[]{:S(2)}, u32[]{:S(2)}) collective-permute-start(bf16[192,384]{1,0:T(8,128)(2,1)} %bitcast.11), channel_id=1, source_target_pairs={{0,16},{1,5},{2,18},{3,7},{4,20},{5,1},{6,22},{7,3},{8,24},{9,13},... | collective-permute-start | bytes 442376 | tf_op jit(solution)/shard_map/ppermute | solution.py:59
  5.9 5.0 %adjacency_first.1 = (bf16[384,12288]{1,0:T(8,128)(2,1)S(1)}, bf16[384,4096]{1,0:T(8,128)(2,1)S(1)}, f32[384,128]{1,0:T(8,128)S(1)}, bf16[2,256,512]{2,1,0:T(8,128)(2,1)S(1)}, bf16[256,512]{1,0:T(8,128)(2,1)S(1)}) custom-call(s32[3,96]{1,0:T(4,128)} %mask.3, s32[384,12288]{1,0:T(8,128)} %counts.3, bf16[192,1024]{1,0:T(8,128)(2,1)} %refs_0_.1, ...), custom_call_target="tpu_custom_call" | custom-call | flops 1200000000 | bytes 16000000 | tf_op jit(solution)/shard_map/adjacency_first/pallas_call | solution.py:167
  10.9 0.0 collective-permute-done.1.c
  10.9 0.0 collective-permute-done.2.d
  10.9 0.1 stack.21.refs_0_
  11.0 0.7 collective-permute-start.3
  11.7 1.9 %collective-permute-start.7 = (bf16[4,192,384]{2,1,0:T(8,128)(2,1)S(1)}, bf16[4,192,384]{2,1,0:T(8,128)(2,1)S(1)}, u32[]{:S(2)}, u32[]{:S(2)}) collective-permute-start(bf16[4,192,384]{2,1,0:T(8,128)(2,1)S(1)} %stack.21.refs_0_), channel_id=1, source_target_pairs={{0,6},{1,25},{2,0},{3,27},{4,2},{5,29},{6,4},{7,31},{8,14},{9,1},{... | collective-permute-start | bytes 1769480 | tf_op jit(solution)/shard_map/ppermute | solution.py:63
  13.6 0.0 collective-permute-start.5
  13.6 2.9 %collective-permute-start.4 = (bf16[256,512]{1,0:T(8,128)(2,1)S(1)}, bf16[256,512]{1,0:T(8,128)(2,1)S(1)}, u32[]{:S(2)}, u32[]{:S(2)}) collective-permute-start(bf16[256,512]{1,0:T(8,128)(2,1)S(1)} %get-tuple-element.25.refs_3_.after), channel_id=1, source_target_pairs={{0,64},{32,96},{64,0},{96,32},{1,65},{33,97},{65,1},{97,33},{2,66}... | collective-permute-start | bytes 786440 | tf_op jit(solution)/shard_map/ppermute | solution.py:71
  16.5 1.7 %collective-permute-start.9 = (bf16[4,192,384]{2,1,0:T(8,128)(2,1)S(1)}, bf16[4,192,384]{2,1,0:T(8,128)(2,1)S(1)}, u32[]{:S(2)}, u32[]{:S(2)}) collective-permute-start(bf16[4,192,384]{2,1,0:T(8,128)(2,1)S(1)} %stack.21.refs_0_), channel_id=1, source_target_pairs={{0,4},{1,17},{2,6},{3,19},{4,0},{5,21},{6,2},{7,23},{8,12},{9,25},... | collective-permute-start | bytes 1769480 | tf_op jit(solution)/shard_map/ppermute | solution.py:63
  18.3 2.4 %collective-permute-done.4.refs_2_.near = bf16[256,512]{1,0:T(8,128)(2,1)S(1)} collective-permute-done((bf16[256,512]{1,0:T(8,128)(2,1)S(1)}, bf16[256,512]{1,0:T(8,128)(2,1)S(1)}, u32[]{:S(2)}, u32[]{:S(2)}) %collective-permute-start.4) | collective-permute-done | bytes 262176 | tf_op jit(solution)/shard_map/ppermute | solution.py:71
  20.7 2.7 %collective-permute-start.14 = (bf16[2,256,512]{2,1,0:T(8,128)(2,1)S(1)}, bf16[2,256,512]{2,1,0:T(8,128)(2,1)S(1)}, u32[]{:S(2)}, u32[]{:S(2)}) collective-permute-start(bf16[2,256,512]{2,1,0:T(8,128)(2,1)S(1)} %get-tuple-element.36.own), channel_id=1, source_target_pairs={{0,32},{32,64},{64,96},{96,0},{1,97},{33,1},{65,33},{97,65},{2,34}... | collective-permute-start | bytes 1572872 | tf_op jit(solution)/shard_map/ppermute | solution.py:76
  23.4 4.8 %adjacency_second.1 = (bf16[384,12288]{1,0:T(8,128)(2,1)S(1)}, bf16[384,4096]{1,0:T(8,128)(2,1)S(1)}, f32[384,128]{1,0:T(8,128)S(1)}) custom-call(s32[3,96]{1,0:T(4,128)} %mask.3, s32[384,12288]{1,0:T(8,128)} %counts.3, bf16[384,12288]{1,0:T(8,128)(2,1)S(1)} %get-tuple-element.22.refs_0_, ...), custom_call_target="tpu_custom_call", output_to_operand_aliasing={{0}: (2, {}), {1}: (3, {}), {2}: (4, {})} | custom-call | flops 1200000000 | bytes 16000000 | tf_op jit(solution)/shard_map/adjacency_second/pallas_call | solution.py:188
  28.2 0.0 collective-permute-done.3.refs_1_
  28.2 1.0 %product_first.1.before = f32[384,192]{1,0:T(8,128)S(1)} custom-call(bf16[384,12288]{1,0:T(8,128)(2,1)S(1)} %get-tuple-element.28.adj, bf16[4,192,384]{2,1,0:T(8,128)(2,1)S(1)} %stack.21.refs_0_, bf16[4,192,384]{2,1,0:T(8,128)(2,1)S(1)} %collective-permute-done.3.refs_1_, bf16[256,512]{1,0:T(8,128)(2,1)S(1)} %collective-permute-done.4.refs_2_.near), custom_call_target="tpu_custom_call" | custom-call | flops 603979776 | bytes 3600000 | tf_op jit(solution)/shard_map/product_first/pallas_call | solution.py:338
  29.2 2.1 %collective-permute-start.8 = (bf16[4,192,384]{2,1,0:T(8,128)(2,1)S(1)}, bf16[4,192,384]{2,1,0:T(8,128)(2,1)S(1)}, u32[]{:S(2)}, u32[]{:S(2)}) collective-permute-start(bf16[4,192,384]{2,1,0:T(8,128)(2,1)S(1)} %collective-permute-done.7.refs_2_), channel_id=1, source_target_pairs={{0,1},{1,0},{2,3},{3,2},{4,5},{5,4},{6,7},{7,6},{8,9},{9,8},{10,11... | collective-permute-start | bytes 1769480 | tf_op jit(solution)/shard_map/ppermute | solution.py:67
  31.3 0.0 collective-permute-done.5.refs_0_
  31.3 1.9 %collective-permute-start.6 = (bf16[4,192,384]{2,1,0:T(8,128)(2,1)S(1)}, bf16[4,192,384]{2,1,0:T(8,128)(2,1)S(1)}, u32[]{:S(2)}, u32[]{:S(2)}) collective-permute-start(bf16[4,192,384]{2,1,0:T(8,128)(2,1)S(1)} %collective-permute-done.5.refs_0_), channel_id=1, source_target_pairs={{0,1},{1,0},{2,3},{3,2},{4,5},{5,4},{6,7},{7,6},{8,9},{9,8},{10,11... | collective-permute-start | bytes 1769480 | tf_op jit(solution)/shard_map/ppermute | solution.py:67
  33.3 0.0 collective-permute-done.9.refs_0_
  33.3 0.0 collective-permute-start.10
  33.3 0.0 collective-permute-done.14.side
  33.3 1.1 %collective-permute-start.15 = (bf16[2,256,512]{2,1,0:T(8,128)(2,1)S(1)}, bf16[2,256,512]{2,1,0:T(8,128)(2,1)S(1)}, u32[]{:S(2)}, u32[]{:S(2)}) collective-permute-start(bf16[2,256,512]{2,1,0:T(8,128)(2,1)S(1)} %collective-permute-done.14.side), channel_id=1, source_target_pairs={{0,1},{1,0},{2,3},{3,2},{4,5},{5,4},{6,7},{7,6},{8,9},{9,8},{10,11... | collective-permute-start | bytes 1572872 | tf_op jit(solution)/shard_map/ppermute | solution.py:67
  34.4 0.0 collective-permute-start.16
  34.4 0.0 collective-permute-done.8.refs_3_
  34.4 0.5 collective-permute-done.6.refs_1_
  34.9 1.8 %product_next.1.before = f32[384,192]{1,0:T(8,128)S(1)} custom-call(bf16[384,12288]{1,0:T(8,128)(2,1)S(1)} %get-tuple-element.28.adj, f32[384,192]{1,0:T(8,128)S(1)} %product_first.1.before, bf16[4,192,384]{2,1,0:T(8,128)(2,1)S(1)} %collective-permute-done.5.refs_0_, bf16[4,192,384]{2,1,0:T(8,128)(2,1)S(1)} %collective-permute-done.6.refs_1_, ...), custom_call_target="tpu_custom_call" | custom-call | flops 1207959552 | bytes 7200000 | tf_op jit(solution)/shard_map/product_next/pallas_call | solution.py:347
  36.7 0.0 copy-start.1
  36.7 0.0 collective-permute-done.10.refs_1_
  36.7 1.1 %product_last.1 = (bf16[96,192]{1,0:T(8,128)(2,1)S(1)}, bf16[96,192]{1,0:T(8,128)(2,1)S(1)}, bf16[96,192]{1,0:T(8,128)(2,1)S(1)}, bf16[96,192]{1,0:T(8,128)(2,1)S(1)}) custom-call(bf16[384,12288]{1,0:T(8,128)(2,1)S(1)} %get-tuple-element.28.adj, f32[384,192]{1,0:T(8,128)S(1)} %product_next.1.before, f32[384,128]{1,0:T(8,128)S(1)} %get-tuple-element.27.degree, ...), custom_call_target="tpu_custom_call" | custom-call | flops 603979776 | bytes 3600000 | tf_op jit(solution)/shard_map/product_last/pallas_call | solution.py:352
  37.8 1.4 %collective-permute-start.11 = (bf16[96,192]{1,0:T(8,128)(2,1)S(1)}, bf16[96,192]{1,0:T(8,128)(2,1)S(1)}, u32[]{:S(2)}, u32[]{:S(2)}) collective-permute-start(bf16[96,192]{1,0:T(8,128)(2,1)S(1)} %get-tuple-element.33), channel_id=1, source_target_pairs={{0,32},{32,64},{64,96},{96,0},{1,33},{33,65},{65,97},{97,1},{2,34}... | collective-permute-start | bytes 110600 | tf_op jit(solution)/shard_map/ppermute | solution.py:71
  39.2 2.6 %collective-permute-start.12 = (bf16[96,192]{1,0:T(8,128)(2,1)S(1)}, bf16[96,192]{1,0:T(8,128)(2,1)S(1)}, u32[]{:S(2)}, u32[]{:S(2)}) collective-permute-start(bf16[96,192]{1,0:T(8,128)(2,1)S(1)} %get-tuple-element.34), channel_id=1, source_target_pairs={{0,64},{32,96},{64,0},{96,32},{1,65},{33,97},{65,1},{97,33},{2,66}... | collective-permute-start | bytes 110600 | tf_op jit(solution)/shard_map/ppermute | solution.py:71
  41.8 1.1 %collective-permute-start.13 = (bf16[96,192]{1,0:T(8,128)(2,1)S(1)}, bf16[96,192]{1,0:T(8,128)(2,1)S(1)}, u32[]{:S(2)}, u32[]{:S(2)}) collective-permute-start(bf16[96,192]{1,0:T(8,128)(2,1)S(1)} %get-tuple-element.35), channel_id=1, source_target_pairs={{0,96},{32,0},{64,32},{96,64},{1,97},{33,1},{65,33},{97,65},{2,98}... | collective-permute-start | bytes 110600 | tf_op jit(solution)/shard_map/ppermute | solution.py:71
  42.9 0.0 collective-permute-done.16.far
  42.9 0.0 collective-permute-done.15.other_side
  42.9 0.0 collective-permute-done.11.g1
  42.9 1.2 %collective-permute-done.12.g2 = bf16[96,192]{1,0:T(8,128)(2,1)S(1)} collective-permute-done((bf16[96,192]{1,0:T(8,128)(2,1)S(1)}, bf16[96,192]{1,0:T(8,128)(2,1)S(1)}, u32[]{:S(2)}, u32[]{:S(2)}) %collective-permute-start.12) | collective-permute-done | bytes 36896 | tf_op jit(solution)/shard_map/ppermute | solution.py:71
  44.0 1.0 %collective-permute-done.13.g3 = bf16[96,192]{1,0:T(8,128)(2,1)S(1)} collective-permute-done((bf16[96,192]{1,0:T(8,128)(2,1)S(1)}, bf16[96,192]{1,0:T(8,128)(2,1)S(1)}, u32[]{:S(2)}, u32[]{:S(2)}) %collective-permute-start.13) | collective-permute-done | bytes 36896 | tf_op jit(solution)/shard_map/ppermute | solution.py:71
  45.0 1.0 %hidden.1 = bf16[128,128]{1,0:T(8,128)(2,1)S(1)} custom-call(bf16[96,192]{1,0:T(8,128)(2,1)S(1)} %get-tuple-element.32.g0, bf16[96,192]{1,0:T(8,128)(2,1)S(1)} %collective-permute-done.11.g1, bf16[96,192]{1,0:T(8,128)(2,1)S(1)} %collective-permute-done.12.g2, bf16[96,192]{1,0:T(8,128)(2,1)S(1)} %collective-permute-done.13.g3, ...), custom_call_target="tpu_custom_call" | custom-call | flops 150994944 | bytes 2000000 | tf_op jit(solution)/shard_map/hidden/pallas_call | solution.py:360
  46.1 0.1 collective-permute-start.17
  46.1 2.7 %collective-permute-start.18 = (bf16[128,128]{1,0:T(8,128)(2,1)S(1)}, bf16[128,128]{1,0:T(8,128)(2,1)S(1)}, u32[]{:S(2)}, u32[]{:S(2)}) collective-permute-start(bf16[128,128]{1,0:T(8,128)(2,1)S(1)} %hidden.1), channel_id=1, source_target_pairs={{0,24},{1,7},{2,26},{3,1},{4,28},{5,3},{6,30},{7,5},{8,0},{9,15},{... | collective-permute-start | bytes 98312 | tf_op jit(solution)/shard_map/ppermute | solution.py:59
  48.8 0.3 collective-permute-start.19
  49.1 1.0 %collective-permute-done.17 = bf16[128,128]{1,0:T(8,128)(2,1)S(1)} collective-permute-done((bf16[128,128]{1,0:T(8,128)(2,1)S(1)}, bf16[128,128]{1,0:T(8,128)(2,1)S(1)}, u32[]{:S(2)}, u32[]{:S(2)}) %collective-permute-start.17) | collective-permute-done | bytes 32800 | tf_op jit(solution)/shard_map/ppermute | solution.py:59
  50.1 0.0 collective-permute-done.18
  50.1 3.0 %collective-permute-done.19 = bf16[128,128]{1,0:T(8,128)(2,1)S(1)} collective-permute-done((bf16[128,128]{1,0:T(8,128)(2,1)S(1)}, bf16[128,128]{1,0:T(8,128)(2,1)S(1)}, u32[]{:S(2)}, u32[]{:S(2)}) %collective-permute-start.19) | collective-permute-done | bytes 32800 | tf_op jit(solution)/shard_map/ppermute | solution.py:59
  53.1 0.4 collective-permute-start.21
  53.5 2.4 %collective-permute-start.23 = (bf16[4,128,128]{2,1,0:T(8,128)(2,1)S(1)}, bf16[4,128,128]{2,1,0:T(8,128)(2,1)S(1)}, u32[]{:S(2)}, u32[]{:S(2)}) collective-permute-start(bf16[4,128,128]{2,1,0:T(8,128)(2,1)S(1)} %pad_maximum_fusion.refs_0_), channel_id=1, source_target_pairs={{0,6},{1,25},{2,0},{3,27},{4,2},{5,29},{6,4},{7,31},{8,14},{9,1},{... | collective-permute-start | bytes 393224 | tf_op jit(solution)/shard_map/ppermute | solution.py:63
  55.8 0.3 collective-permute-start.25
  56.2 4.3 %collective-permute-start.20 = (bf16[4,128,128]{2,1,0:T(8,128)(2,1)S(1)}, bf16[4,128,128]{2,1,0:T(8,128)(2,1)S(1)}, u32[]{:S(2)}, u32[]{:S(2)}) collective-permute-start(bf16[4,128,128]{2,1,0:T(8,128)(2,1)S(1)} %pad_maximum_fusion.refs_0_), channel_id=1, source_target_pairs={{0,1},{1,0},{2,3},{3,2},{4,5},{5,4},{6,7},{7,6},{8,9},{9,8},{10,11... | collective-permute-start | bytes 393224 | tf_op jit(solution)/shard_map/ppermute | solution.py:67
  60.4 0.0 collective-permute-done.21.refs_2_
  60.4 2.4 %collective-permute-start.22 = (bf16[4,128,128]{2,1,0:T(8,128)(2,1)S(1)}, bf16[4,128,128]{2,1,0:T(8,128)(2,1)S(1)}, u32[]{:S(2)}, u32[]{:S(2)}) collective-permute-start(bf16[4,128,128]{2,1,0:T(8,128)(2,1)S(1)} %collective-permute-done.21.refs_2_), channel_id=1, source_target_pairs={{0,1},{1,0},{2,3},{3,2},{4,5},{5,4},{6,7},{7,6},{8,9},{9,8},{10,11... | collective-permute-start | bytes 393224 | tf_op jit(solution)/shard_map/ppermute | solution.py:67
  62.8 0.0 collective-permute-done.23.refs_4_
  62.8 1.0 %collective-permute-start.24 = (bf16[4,128,128]{2,1,0:T(8,128)(2,1)S(1)}, bf16[4,128,128]{2,1,0:T(8,128)(2,1)S(1)}, u32[]{:S(2)}, u32[]{:S(2)}) collective-permute-start(bf16[4,128,128]{2,1,0:T(8,128)(2,1)S(1)} %collective-permute-done.23.refs_4_), channel_id=1, source_target_pairs={{0,1},{1,0},{2,3},{3,2},{4,5},{5,4},{6,7},{7,6},{8,9},{9,8},{10,11... | collective-permute-start | bytes 393224 | tf_op jit(solution)/shard_map/ppermute | solution.py:67
  63.8 2.5 %collective-permute-start.26 = (bf16[4,128,128]{2,1,0:T(8,128)(2,1)S(1)}, bf16[4,128,128]{2,1,0:T(8,128)(2,1)S(1)}, u32[]{:S(2)}, u32[]{:S(2)}) collective-permute-start(bf16[4,128,128]{2,1,0:T(8,128)(2,1)S(1)} %collective-permute-done.25.refs_6_), channel_id=1, source_target_pairs={{0,1},{1,0},{2,3},{3,2},{4,5},{5,4},{6,7},{7,6},{8,9},{9,8},{10,11... | collective-permute-start | bytes 393224 | tf_op jit(solution)/shard_map/ppermute | solution.py:67
  66.4 1.0 %collective-permute-done.26.refs_7_ = bf16[4,128,128]{2,1,0:T(8,128)(2,1)S(1)} collective-permute-done((bf16[4,128,128]{2,1,0:T(8,128)(2,1)S(1)}, bf16[4,128,128]{2,1,0:T(8,128)(2,1)S(1)}, u32[]{:S(2)}, u32[]{:S(2)}) %collective-permute-start.26) | collective-permute-done | bytes 131104 | tf_op jit(solution)/shard_map/ppermute | solution.py:67
  67.4 1.5 %scores.1.p0 = bf16[160,384]{1,0:T(8,128)(2,1)S(1)} custom-call(bf16[384,4096]{1,0:T(8,128)(2,1)S(1)} %get-tuple-element.26.adj2, f32[384,128]{1,0:T(8,128)S(1)} %get-tuple-element.27.degree, bf16[4,128,128]{2,1,0:T(8,128)(2,1)S(1)} %pad_maximum_fusion.refs_0_, bf16[4,128,128]{2,1,0:T(8,128)(2,1)S(1)} %collective-permute-done.20.refs_1_, ...), custom_call_target="tpu_custom_call" | custom-call | flops 805306368 | bytes 5000000 | tf_op jit(solution)/shard_map/scores/pallas_call | solution.py:370
  68.8 0.1 collective-permute-start.27
  68.9 3.4 %collective-permute-start.28 = (bf16[160,384]{1,0:T(8,128)(2,1)S(1)}, bf16[160,384]{1,0:T(8,128)(2,1)S(1)}, u32[]{:S(2)}, u32[]{:S(2)}) collective-permute-start(bf16[160,384]{1,0:T(8,128)(2,1)S(1)} %scores.1.p0), channel_id=1, source_target_pairs={{0,64},{32,96},{64,0},{96,32},{1,65},{33,97},{65,1},{97,33},{2,66}... | collective-permute-start | bytes 368648 | tf_op jit(solution)/shard_map/ppermute | solution.py:71
  72.4 0.0 collective-permute-start.29
  72.4 2.3 %collective-permute-done.27.p1 = bf16[160,384]{1,0:T(8,128)(2,1)S(1)} collective-permute-done((bf16[160,384]{1,0:T(8,128)(2,1)S(1)}, bf16[160,384]{1,0:T(8,128)(2,1)S(1)}, u32[]{:S(2)}, u32[]{:S(2)}) %collective-permute-start.27) | collective-permute-done | bytes 122912 | tf_op jit(solution)/shard_map/ppermute | solution.py:71
  74.7 3.4 %collective-permute-done.28.p2 = bf16[160,384]{1,0:T(8,128)(2,1)S(1)} collective-permute-done((bf16[160,384]{1,0:T(8,128)(2,1)S(1)}, bf16[160,384]{1,0:T(8,128)(2,1)S(1)}, u32[]{:S(2)}, u32[]{:S(2)}) %collective-permute-start.28) | collective-permute-done | bytes 122912 | tf_op jit(solution)/shard_map/ppermute | solution.py:71
  78.1 0.0 collective-permute-done.29.p3
  78.1 0.9 %sum.1 = f32[153,384]{1,0:T(8,128)} custom-call(bf16[160,384]{1,0:T(8,128)(2,1)S(1)} %scores.1.p0, bf16[160,384]{1,0:T(8,128)(2,1)S(1)} %collective-permute-done.27.p1, bf16[160,384]{1,0:T(8,128)(2,1)S(1)} %collective-permute-done.28.p2, bf16[160,384]{1,0:T(8,128)(2,1)S(1)} %collective-permute-done.29.p3, f32[1,256]{1,0:T(1,128)S(1)} %bitcast.14), custom_call_target="tpu_custom_call" | custom-call | flops 300000 | bytes 800000 | tf_op jit(solution)/shard_map/sum/pallas_call | solution.py:377
  (11 shorter events, 0.0 us)
Async XLA Ops:
  0.0 10.9 %collective-permute-start = (bf16[192,384]{1,0:T(8,128)(2,1)}, bf16[192,384]{1,0:T(8,128)(2,1)S(1)}, u32[]{:S(2)}, u32[]{:S(2)}) collective-permute-start(bf16[192,384]{1,0:T(8,128)(2,1)} %bitcast.9), channel_id=1, source_target_pairs={{0,8},{1,3},{2,10},{3,5},{4,12},{5,7},{6,14},{7,1},{8,16},{9,11},{... | collective-permute-start | bytes 442376 | tf_op jit(solution)/shard_map/ppermute | solution.py:59
  2.5 8.4 %collective-permute-start.1 = (bf16[192,384]{1,0:T(8,128)(2,1)}, bf16[192,384]{1,0:T(8,128)(2,1)S(1)}, u32[]{:S(2)}, u32[]{:S(2)}) collective-permute-start(bf16[192,384]{1,0:T(8,128)(2,1)} %bitcast.10), channel_id=1, source_target_pairs={{0,24},{1,7},{2,26},{3,1},{4,28},{5,3},{6,30},{7,5},{8,0},{9,15},{... | collective-permute-start | bytes 442376 | tf_op jit(solution)/shard_map/ppermute | solution.py:59
  4.6 6.3 %collective-permute-start.2 = (bf16[192,384]{1,0:T(8,128)(2,1)}, bf16[192,384]{1,0:T(8,128)(2,1)S(1)}, u32[]{:S(2)}, u32[]{:S(2)}) collective-permute-start(bf16[192,384]{1,0:T(8,128)(2,1)} %bitcast.11), channel_id=1, source_target_pairs={{0,16},{1,5},{2,18},{3,7},{4,20},{5,1},{6,22},{7,3},{8,24},{9,13},... | collective-permute-start | bytes 442376 | tf_op jit(solution)/shard_map/ppermute | solution.py:59
  5.9 5.0 %copy-start = (bf16[384,192]{0,1:T(8,128)(2,1)S(1)}, bf16[384,192]{0,1:T(8,128)(2,1)}, u32[]{:S(2)}) copy-start(bf16[384,192]{0,1:T(8,128)(2,1)} %param.7) | copy-start | bytes 442372
  11.0 17.2 %collective-permute-start.3 = (bf16[4,192,384]{2,1,0:T(8,128)(2,1)S(1)}, bf16[4,192,384]{2,1,0:T(8,128)(2,1)S(1)}, u32[]{:S(2)}, u32[]{:S(2)}) collective-permute-start(bf16[4,192,384]{2,1,0:T(8,128)(2,1)S(1)} %stack.21.refs_0_), channel_id=1, source_target_pairs={{0,1},{1,0},{2,3},{3,2},{4,5},{5,4},{6,7},{7,6},{8,9},{9,8},{10,11... | collective-permute-start | bytes 1769480 | tf_op jit(solution)/shard_map/ppermute | solution.py:67
  11.7 17.5 %collective-permute-start.7 = (bf16[4,192,384]{2,1,0:T(8,128)(2,1)S(1)}, bf16[4,192,384]{2,1,0:T(8,128)(2,1)S(1)}, u32[]{:S(2)}, u32[]{:S(2)}) collective-permute-start(bf16[4,192,384]{2,1,0:T(8,128)(2,1)S(1)} %stack.21.refs_0_), channel_id=1, source_target_pairs={{0,6},{1,25},{2,0},{3,27},{4,2},{5,29},{6,4},{7,31},{8,14},{9,1},{... | collective-permute-start | bytes 1769480 | tf_op jit(solution)/shard_map/ppermute | solution.py:63
  13.6 17.7 %collective-permute-start.5 = (bf16[4,192,384]{2,1,0:T(8,128)(2,1)S(1)}, bf16[4,192,384]{2,1,0:T(8,128)(2,1)S(1)}, u32[]{:S(2)}, u32[]{:S(2)}) collective-permute-start(bf16[4,192,384]{2,1,0:T(8,128)(2,1)S(1)} %stack.21.refs_0_), channel_id=1, source_target_pairs={{0,2},{1,9},{2,4},{3,11},{4,6},{5,13},{6,0},{7,15},{8,10},{9,17},{... | collective-permute-start | bytes 1769480 | tf_op jit(solution)/shard_map/ppermute | solution.py:63
  13.6 7.1 %collective-permute-start.4 = (bf16[256,512]{1,0:T(8,128)(2,1)S(1)}, bf16[256,512]{1,0:T(8,128)(2,1)S(1)}, u32[]{:S(2)}, u32[]{:S(2)}) collective-permute-start(bf16[256,512]{1,0:T(8,128)(2,1)S(1)} %get-tuple-element.25.refs_3_.after), channel_id=1, source_target_pairs={{0,64},{32,96},{64,0},{96,32},{1,65},{33,97},{65,1},{97,33},{2,66}... | collective-permute-start | bytes 786440 | tf_op jit(solution)/shard_map/ppermute | solution.py:71
  16.5 16.7 %collective-permute-start.9 = (bf16[4,192,384]{2,1,0:T(8,128)(2,1)S(1)}, bf16[4,192,384]{2,1,0:T(8,128)(2,1)S(1)}, u32[]{:S(2)}, u32[]{:S(2)}) collective-permute-start(bf16[4,192,384]{2,1,0:T(8,128)(2,1)S(1)} %stack.21.refs_0_), channel_id=1, source_target_pairs={{0,4},{1,17},{2,6},{3,19},{4,0},{5,21},{6,2},{7,23},{8,12},{9,25},... | collective-permute-start | bytes 1769480 | tf_op jit(solution)/shard_map/ppermute | solution.py:63
  20.7 12.6 %collective-permute-start.14 = (bf16[2,256,512]{2,1,0:T(8,128)(2,1)S(1)}, bf16[2,256,512]{2,1,0:T(8,128)(2,1)S(1)}, u32[]{:S(2)}, u32[]{:S(2)}) collective-permute-start(bf16[2,256,512]{2,1,0:T(8,128)(2,1)S(1)} %get-tuple-element.36.own), channel_id=1, source_target_pairs={{0,32},{32,64},{64,96},{96,0},{1,97},{33,1},{65,33},{97,65},{2,34}... | collective-permute-start | bytes 1572872 | tf_op jit(solution)/shard_map/ppermute | solution.py:76
  29.2 5.1 %collective-permute-start.8 = (bf16[4,192,384]{2,1,0:T(8,128)(2,1)S(1)}, bf16[4,192,384]{2,1,0:T(8,128)(2,1)S(1)}, u32[]{:S(2)}, u32[]{:S(2)}) collective-permute-start(bf16[4,192,384]{2,1,0:T(8,128)(2,1)S(1)} %collective-permute-done.7.refs_2_), channel_id=1, source_target_pairs={{0,1},{1,0},{2,3},{3,2},{4,5},{5,4},{6,7},{7,6},{8,9},{9,8},{10,11... | collective-permute-start | bytes 1769480 | tf_op jit(solution)/shard_map/ppermute | solution.py:67
  31.3 3.6 %collective-permute-start.6 = (bf16[4,192,384]{2,1,0:T(8,128)(2,1)S(1)}, bf16[4,192,384]{2,1,0:T(8,128)(2,1)S(1)}, u32[]{:S(2)}, u32[]{:S(2)}) collective-permute-start(bf16[4,192,384]{2,1,0:T(8,128)(2,1)S(1)} %collective-permute-done.5.refs_0_), channel_id=1, source_target_pairs={{0,1},{1,0},{2,3},{3,2},{4,5},{5,4},{6,7},{7,6},{8,9},{9,8},{10,11... | collective-permute-start | bytes 1769480 | tf_op jit(solution)/shard_map/ppermute | solution.py:67
  33.3 3.5 %collective-permute-start.10 = (bf16[4,192,384]{2,1,0:T(8,128)(2,1)S(1)}, bf16[4,192,384]{2,1,0:T(8,128)(2,1)S(1)}, u32[]{:S(2)}, u32[]{:S(2)}) collective-permute-start(bf16[4,192,384]{2,1,0:T(8,128)(2,1)S(1)} %collective-permute-done.9.refs_0_), channel_id=1, source_target_pairs={{0,1},{1,0},{2,3},{3,2},{4,5},{5,4},{6,7},{7,6},{8,9},{9,8},{10,11... | collective-permute-start | bytes 1769480 | tf_op jit(solution)/shard_map/ppermute | solution.py:67
  33.3 9.6 %collective-permute-start.15 = (bf16[2,256,512]{2,1,0:T(8,128)(2,1)S(1)}, bf16[2,256,512]{2,1,0:T(8,128)(2,1)S(1)}, u32[]{:S(2)}, u32[]{:S(2)}) collective-permute-start(bf16[2,256,512]{2,1,0:T(8,128)(2,1)S(1)} %collective-permute-done.14.side), channel_id=1, source_target_pairs={{0,1},{1,0},{2,3},{3,2},{4,5},{5,4},{6,7},{7,6},{8,9},{9,8},{10,11... | collective-permute-start | bytes 1572872 | tf_op jit(solution)/shard_map/ppermute | solution.py:67
  34.4 8.5 %collective-permute-start.16 = (bf16[256,512]{1,0:T(8,128)(2,1)S(1)}, bf16[256,512]{1,0:T(8,128)(2,1)S(1)}, u32[]{:S(2)}, u32[]{:S(2)}) collective-permute-start(bf16[256,512]{1,0:T(8,128)(2,1)S(1)} %collective-permute-done.4.refs_2_.near), channel_id=1, source_target_pairs={{0,1},{1,0},{2,3},{3,2},{4,5},{5,4},{6,7},{7,6},{8,9},{9,8},{10,11... | collective-permute-start | bytes 786440 | tf_op jit(solution)/shard_map/ppermute | solution.py:67
  36.7 35.6 %copy-start.1 = (f32[153]{0:T(256)S(1)}, f32[153]{0:T(256)}, u32[]{:S(2)}) copy-start(f32[153]{0:T(256)} %param.13) | copy-start | bytes 1840
  37.8 5.1 %collective-permute-start.11 = (bf16[96,192]{1,0:T(8,128)(2,1)S(1)}, bf16[96,192]{1,0:T(8,128)(2,1)S(1)}, u32[]{:S(2)}, u32[]{:S(2)}) collective-permute-start(bf16[96,192]{1,0:T(8,128)(2,1)S(1)} %get-tuple-element.33), channel_id=1, source_target_pairs={{0,32},{32,64},{64,96},{96,0},{1,33},{33,65},{65,97},{97,1},{2,34}... | collective-permute-start | bytes 110600 | tf_op jit(solution)/shard_map/ppermute | solution.py:71
  39.2 4.9 %collective-permute-start.12 = (bf16[96,192]{1,0:T(8,128)(2,1)S(1)}, bf16[96,192]{1,0:T(8,128)(2,1)S(1)}, u32[]{:S(2)}, u32[]{:S(2)}) collective-permute-start(bf16[96,192]{1,0:T(8,128)(2,1)S(1)} %get-tuple-element.34), channel_id=1, source_target_pairs={{0,64},{32,96},{64,0},{96,32},{1,65},{33,97},{65,1},{97,33},{2,66}... | collective-permute-start | bytes 110600 | tf_op jit(solution)/shard_map/ppermute | solution.py:71
  41.8 3.2 %collective-permute-start.13 = (bf16[96,192]{1,0:T(8,128)(2,1)S(1)}, bf16[96,192]{1,0:T(8,128)(2,1)S(1)}, u32[]{:S(2)}, u32[]{:S(2)}) collective-permute-start(bf16[96,192]{1,0:T(8,128)(2,1)S(1)} %get-tuple-element.35), channel_id=1, source_target_pairs={{0,96},{32,0},{64,32},{96,64},{1,97},{33,1},{65,33},{97,65},{2,98}... | collective-permute-start | bytes 110600 | tf_op jit(solution)/shard_map/ppermute | solution.py:71
  46.1 4.0 %collective-permute-start.17 = (bf16[128,128]{1,0:T(8,128)(2,1)S(1)}, bf16[128,128]{1,0:T(8,128)(2,1)S(1)}, u32[]{:S(2)}, u32[]{:S(2)}) collective-permute-start(bf16[128,128]{1,0:T(8,128)(2,1)S(1)} %hidden.1), channel_id=1, source_target_pairs={{0,8},{1,3},{2,10},{3,5},{4,12},{5,7},{6,14},{7,1},{8,16},{9,11},{... | collective-permute-start | bytes 98312 | tf_op jit(solution)/shard_map/ppermute | solution.py:59
  46.1 4.0 %collective-permute-start.18 = (bf16[128,128]{1,0:T(8,128)(2,1)S(1)}, bf16[128,128]{1,0:T(8,128)(2,1)S(1)}, u32[]{:S(2)}, u32[]{:S(2)}) collective-permute-start(bf16[128,128]{1,0:T(8,128)(2,1)S(1)} %hidden.1), channel_id=1, source_target_pairs={{0,24},{1,7},{2,26},{3,1},{4,28},{5,3},{6,30},{7,5},{8,0},{9,15},{... | collective-permute-start | bytes 98312 | tf_op jit(solution)/shard_map/ppermute | solution.py:59
  48.8 4.3 %collective-permute-start.19 = (bf16[128,128]{1,0:T(8,128)(2,1)S(1)}, bf16[128,128]{1,0:T(8,128)(2,1)S(1)}, u32[]{:S(2)}, u32[]{:S(2)}) collective-permute-start(bf16[128,128]{1,0:T(8,128)(2,1)S(1)} %hidden.1), channel_id=1, source_target_pairs={{0,16},{1,5},{2,18},{3,7},{4,20},{5,1},{6,22},{7,3},{8,24},{9,13},... | collective-permute-start | bytes 98312 | tf_op jit(solution)/shard_map/ppermute | solution.py:59
  53.1 7.3 %collective-permute-start.21 = (bf16[4,128,128]{2,1,0:T(8,128)(2,1)S(1)}, bf16[4,128,128]{2,1,0:T(8,128)(2,1)S(1)}, u32[]{:S(2)}, u32[]{:S(2)}) collective-permute-start(bf16[4,128,128]{2,1,0:T(8,128)(2,1)S(1)} %pad_maximum_fusion.refs_0_), channel_id=1, source_target_pairs={{0,2},{1,9},{2,4},{3,11},{4,6},{5,13},{6,0},{7,15},{8,10},{9,17},{... | collective-permute-start | bytes 393224 | tf_op jit(solution)/shard_map/ppermute | solution.py:63
  53.5 9.4 %collective-permute-start.23 = (bf16[4,128,128]{2,1,0:T(8,128)(2,1)S(1)}, bf16[4,128,128]{2,1,0:T(8,128)(2,1)S(1)}, u32[]{:S(2)}, u32[]{:S(2)}) collective-permute-start(bf16[4,128,128]{2,1,0:T(8,128)(2,1)S(1)} %pad_maximum_fusion.refs_0_), channel_id=1, source_target_pairs={{0,6},{1,25},{2,0},{3,27},{4,2},{5,29},{6,4},{7,31},{8,14},{9,1},{... | collective-permute-start | bytes 393224 | tf_op jit(solution)/shard_map/ppermute | solution.py:63
  55.8 8.0 %collective-permute-start.25 = (bf16[4,128,128]{2,1,0:T(8,128)(2,1)S(1)}, bf16[4,128,128]{2,1,0:T(8,128)(2,1)S(1)}, u32[]{:S(2)}, u32[]{:S(2)}) collective-permute-start(bf16[4,128,128]{2,1,0:T(8,128)(2,1)S(1)} %pad_maximum_fusion.refs_0_), channel_id=1, source_target_pairs={{0,4},{1,17},{2,6},{3,19},{4,0},{5,21},{6,2},{7,23},{8,12},{9,25},... | collective-permute-start | bytes 393224 | tf_op jit(solution)/shard_map/ppermute | solution.py:63
  56.2 10.2 %collective-permute-start.20 = (bf16[4,128,128]{2,1,0:T(8,128)(2,1)S(1)}, bf16[4,128,128]{2,1,0:T(8,128)(2,1)S(1)}, u32[]{:S(2)}, u32[]{:S(2)}) collective-permute-start(bf16[4,128,128]{2,1,0:T(8,128)(2,1)S(1)} %pad_maximum_fusion.refs_0_), channel_id=1, source_target_pairs={{0,1},{1,0},{2,3},{3,2},{4,5},{5,4},{6,7},{7,6},{8,9},{9,8},{10,11... | collective-permute-start | bytes 393224 | tf_op jit(solution)/shard_map/ppermute | solution.py:67
  60.4 5.9 %collective-permute-start.22 = (bf16[4,128,128]{2,1,0:T(8,128)(2,1)S(1)}, bf16[4,128,128]{2,1,0:T(8,128)(2,1)S(1)}, u32[]{:S(2)}, u32[]{:S(2)}) collective-permute-start(bf16[4,128,128]{2,1,0:T(8,128)(2,1)S(1)} %collective-permute-done.21.refs_2_), channel_id=1, source_target_pairs={{0,1},{1,0},{2,3},{3,2},{4,5},{5,4},{6,7},{7,6},{8,9},{9,8},{10,11... | collective-permute-start | bytes 393224 | tf_op jit(solution)/shard_map/ppermute | solution.py:67
  62.8 3.5 %collective-permute-start.24 = (bf16[4,128,128]{2,1,0:T(8,128)(2,1)S(1)}, bf16[4,128,128]{2,1,0:T(8,128)(2,1)S(1)}, u32[]{:S(2)}, u32[]{:S(2)}) collective-permute-start(bf16[4,128,128]{2,1,0:T(8,128)(2,1)S(1)} %collective-permute-done.23.refs_4_), channel_id=1, source_target_pairs={{0,1},{1,0},{2,3},{3,2},{4,5},{5,4},{6,7},{7,6},{8,9},{9,8},{10,11... | collective-permute-start | bytes 393224 | tf_op jit(solution)/shard_map/ppermute | solution.py:67
  63.8 3.5 %collective-permute-start.26 = (bf16[4,128,128]{2,1,0:T(8,128)(2,1)S(1)}, bf16[4,128,128]{2,1,0:T(8,128)(2,1)S(1)}, u32[]{:S(2)}, u32[]{:S(2)}) collective-permute-start(bf16[4,128,128]{2,1,0:T(8,128)(2,1)S(1)} %collective-permute-done.25.refs_6_), channel_id=1, source_target_pairs={{0,1},{1,0},{2,3},{3,2},{4,5},{5,4},{6,7},{7,6},{8,9},{9,8},{10,11... | collective-permute-start | bytes 393224 | tf_op jit(solution)/shard_map/ppermute | solution.py:67
  68.8 5.8 %collective-permute-start.27 = (bf16[160,384]{1,0:T(8,128)(2,1)S(1)}, bf16[160,384]{1,0:T(8,128)(2,1)S(1)}, u32[]{:S(2)}, u32[]{:S(2)}) collective-permute-start(bf16[160,384]{1,0:T(8,128)(2,1)S(1)} %scores.1.p0), channel_id=1, source_target_pairs={{0,32},{32,64},{64,96},{96,0},{1,33},{33,65},{65,97},{97,1},{2,34}... | collective-permute-start | bytes 368648 | tf_op jit(solution)/shard_map/ppermute | solution.py:71
  68.9 9.2 %collective-permute-start.28 = (bf16[160,384]{1,0:T(8,128)(2,1)S(1)}, bf16[160,384]{1,0:T(8,128)(2,1)S(1)}, u32[]{:S(2)}, u32[]{:S(2)}) collective-permute-start(bf16[160,384]{1,0:T(8,128)(2,1)S(1)} %scores.1.p0), channel_id=1, source_target_pairs={{0,64},{32,96},{64,0},{96,32},{1,65},{33,97},{65,1},{97,33},{2,66}... | collective-permute-start | bytes 368648 | tf_op jit(solution)/shard_map/ppermute | solution.py:71
  72.4 5.7 %collective-permute-start.29 = (bf16[160,384]{1,0:T(8,128)(2,1)S(1)}, bf16[160,384]{1,0:T(8,128)(2,1)S(1)}, u32[]{:S(2)}, u32[]{:S(2)}) collective-permute-start(bf16[160,384]{1,0:T(8,128)(2,1)S(1)} %scores.1.p0), channel_id=1, source_target_pairs={{0,96},{32,0},{64,32},{96,64},{1,97},{33,1},{65,33},{97,65},{2,98}... | collective-permute-start | bytes 368648 | tf_op jit(solution)/shard_map/ppermute | solution.py:71

commit v5 on v4

--- a/solution.py
+++ b/solution.py
@@ -34,7 +34,7 @@
     return (x * NF + z) * 2 + c
 
 
-SHIFTS = (0, 1, 3, 2)
+SHIFTS = (0, 2, 1, 3)
 
 
 def params(mib=16):
@@ -79,6 +79,7 @@
 CHUNK = 4 * ROWS
 STEPS = NV * ROWS // CHUNK
 SLOTS = 3
+SPLIT = 3
 
 
 def adjacency_kernel(part, mask, counts, *refs):
@@ -89,7 +90,7 @@
         adj, adj2, degree, slots, sems, mask_sm, one = refs[4:]
         extra = []
     me, feat = here()
-    first, last = part * STEPS // 2, (part + 1) * STEPS // 2
+    first, last = (0, SPLIT) if part == 0 else (SPLIT, STEPS)
     mask_copy = pltpu.make_async_copy(mask, mask_sm, one)
     mask_copy.start()
     source_row = lax.broadcasted_iota(jnp.int32, (ROWS, TILE), 0)
@@ -223,29 +224,29 @@
         out[i] = part[...]
 
 
-def add_blocks(shifts, adj, total, pieces):
+def add_blocks(kinds, adj, total, pieces):
     me, _ = here()
-    for p, piece in enumerate(pieces):
+    for (shift, p), piece in zip(kinds, pieces, strict=True):
         core = lax.rem(me + p, 2)
         for b in range(NF):
-            src = source(me, SHIFTS[b], shifts[p // 2], core)
+            src = source(me, SHIFTS[b], shift, core)
             src = pl.multiple_of(src * ROWS, ROWS)
             total = total + lax.dot_general(adj[:, pl.ds(src, ROWS)], piece[b], NT, preferred_element_type=f32)
     return total
 
 
-def product_first(adj, *refs):
-    refs[-1][...] = add_blocks((0,), adj, jnp.zeros(refs[-1].shape, f32), refs[:-2])
-
-
-def product_next(adj, before, *refs):
-    refs[-1][...] = add_blocks((1, 3), adj, before[...], refs[:-1])
-
-
-def product_last(adj, before, degree, *refs):
+def product_first(kinds, adj, *refs):
+    refs[-1][...] = add_blocks(kinds, adj, jnp.zeros(refs[-1].shape, f32), refs[: len(kinds)])
+
+
+def product_next(kinds, adj, before, *refs):
+    refs[-1][...] = add_blocks(kinds, adj, before[...], refs[: len(kinds)])
+
+
+def product_last(kinds, adj, before, degree, *refs):
     pieces, outs, mean = refs[:-5], refs[-5:-1], refs[-1]
     feat = here()[1]
-    total = add_blocks((2,), adj, before[...], pieces)
+    total = add_blocks(kinds, adj, before[...], pieces)
     mean[...] = total / degree[:, :1]
     for s in range(NF):
         q = lax.rem(feat + s, NF)
@@ -319,7 +320,6 @@
         for a in (tile_mask, counts, w_in, w_out.T, b_in.reshape(1, 256))
     )
     *adjacency, whole, mine_half = first_half(tile_mask, counts, *weights)
-    side = both_sides(whole)
     near = along_feat(mine_half, 2)
 
     mine = features.T
@@ -328,35 +328,41 @@
         stack_kernel, out_shape=jax.ShapeDtypeStruct((NF, 192, ROWS), bf16),
         in_specs=[VM] * 4 + [ANY], out_specs=VM,
         compiler_params=params(), cost_estimate=cost(1e5, 1.2e6), name="stack",
-    )(mine, ring[1], ring[2], ring[0], mine_half)
+    )(mine, *ring, mine_half)
     rows = {t: second_axis(four, t) for t in (2, 1, 3)}
 
-    adj, adj2, degree = second_half(tile_mask, counts, *adjacency, mine_half)
+    other_four = swap(four)
+    side = both_sides(whole)
+    adj, adj2, degree = second_half(tile_mask, counts, *adjacency, other_four)
 
     total_shape = jax.ShapeDtypeStruct((ROWS, 192), f32)
-    pieces = [four, swap(four)]
-    total = pl.pallas_call(
-        product_first, out_shape=total_shape, in_specs=[VM] * 3 + [ANY], out_specs=VM,
-        compiler_params=params(), cost_estimate=blocks_cost(pieces), name="product_first",
-    )(adj, *pieces, near)
+    def product(kernel, kinds, pieces, *extra, after=(), name):
+        return pl.pallas_call(
+            functools.partial(kernel, kinds), out_shape=total_shape,
+            in_specs=[VM] * (1 + len(extra) + len(pieces)) + [ANY] * len(after), out_specs=VM,
+            compiler_params=params(), cost_estimate=blocks_cost(pieces), name=name,
+        )(adj, *extra, *pieces, *after)
+
+    total = product(product_first, ((0, 0), (0, 1)), [four, other_four], after=(side,), name="product_first")
     for t in (1, 2, 3):
         rows[t] = lax.optimization_barrier((total, rows[t]))[1]
-    side, near, _ = lax.optimization_barrier((side, near, total))
-    other_side, far = swap(side), swap(near)
-    pieces = [rows[1], swap(rows[1]), rows[3], swap(rows[3])]
-    total = pl.pallas_call(
-        product_next, out_shape=total_shape, in_specs=[VM] * 6, out_specs=VM,
-        compiler_params=params(), cost_estimate=blocks_cost(pieces), name="product_next",
-    )(adj, total, *pieces)
-    pieces = [rows[2], swap(rows[2])]
+    total = product(product_next, ((1, 0), (3, 0)), [rows[1], rows[3]], total, after=(near,), name="product_next")
+    rows[2] = lax.optimization_barrier((total, rows[2]))[1]
+    across = swap(rows[2])
+    pieces = [swap(rows[1]), swap(rows[3]), rows[2]]
+    total = product(product_next, ((1, 1), (3, 1), (2, 0)), pieces, total, name="product_more")
+    pieces = [across]
     means = pl.pallas_call(
-        product_last, out_shape=[jax.ShapeDtypeStruct((SHARE, 192), bf16)] * NF,
-        in_specs=[VM] * 5, out_specs=[VM] * NF,
+        functools.partial(product_last, ((2, 1),)), out_shape=[jax.ShapeDtypeStruct((SHARE, 192), bf16)] * NF,
+        in_specs=[VM] * 4, out_specs=[VM] * NF,
         scratch_shapes=[pltpu.VMEM((ROWS, 192), f32)],
         compiler_params=params(), cost_estimate=blocks_cost(pieces), name="product_last",
     )(adj, total, degree, *pieces)
 
-    g = [means[0]] + [along_feat(means[s], s) for s in (1, 2, 3)]
+    side, near, means = lax.optimization_barrier((side, near, means))
+    other_side, far = swap(side), swap(near)
+    g = {0: means[0]} | {s: along_feat(means[s], s) for s in (2, 1, 3)}
+    g = [g[s] for s in range(NF)]
     z_block = pl.pallas_call(
         hidden_kernel, out_shape=jax.ShapeDtypeStruct((TILE, TILE), bf16),
         in_specs=[VM] * 9, out_specs=VM,
@@ -364,8 +370,10 @@
         compiler_params=params(), cost_estimate=cost(2 * 96 * 768 * 1024, 2e6), name="hidden",
     )(*g, whole, side, other_side, near, far)
 
-    z_four = jnp.stack([z_block] + [first_axis(z_block, s) for s in (1, 3, 2)])
-    z_rows = [z_four] + [second_axis(z_four, t) for t in (1, 3, 2)]
+    ring = {0: z_block} | {s: first_axis(z_block, s) for s in (2, 1, 3)}
+    z_four = jnp.stack([ring[s] for s in SHIFTS])
+    z_rows = {0: z_four} | {t: second_axis(z_four, t) for t in (2, 1, 3)}
+    z_rows = [z_rows[t] for t in SHIFTS]
     z_pieces = [z for row in z_rows for z in (row, swap(row))]
     part = pl.pallas_call(
         scores_kernel, out_shape=jax.ShapeDtypeStruct((160, ROWS), bf16),
@@ -373,7 +381,8 @@
         scratch_shapes=[pltpu.VMEM((NV * TILE, 256), bf16)],
         compiler_params=params(), cost_estimate=cost(2 * 384 * 4096 * 256, 5e6), name="scores",
     )(adj2, degree, *z_pieces)
-    parts = [part] + [along_feat(part, s) for s in (1, 2, 3)]
+    parts = {0: part} | {s: along_feat(part, s) for s in (2, 1, 3)}
+    parts = [parts[s] for s in range(NF)]
     return pl.pallas_call(
         sum_kernel, out_shape=jax.ShapeDtypeStruct((CLS, ROWS), f32),
         in_specs=[VM] * 5, out_specs=VM,

time: 79.1 us -> 77.3 us (0.977)
  starting transfers between devices: 45.9 us -> 42.8 us
  waiting for transfers between devices: 15.8 us -> 16.9 us
    ppermute x1, waiting for transfers between devices: 0.01 us -> 4.26 us  [both_sides(): return lax.ppermute(value, ('feat', 'vert'), pairs)]
    ppermute x10, starting transfers between devices: 16 us -> 13.3 us  [swap(): return lax.ppermute(value, 'vert', positions(lambda x, z, c: (x, z, 1 - c)))]
    ppermute x6, waiting for transfers between devices: 3.98 us -> 1.31 us  [first_axis(): lax.ppermute(value, 'vert', positions(lambda x, z, c: (x + shift * (1 - c...]
    ppermute x7, starting transfers between devices: 11.5 us -> 8.9 us  [along_feat(): lax.ppermute(value, 'feat', [(i, (i + shift) % NF) for i in range(NF)])]
    ppermute x7, waiting for transfers between devices: 10.3 us -> 8.07 us  [along_feat(): lax.ppermute(value, 'feat', [(i, (i + shift) % NF) for i in range(NF)])]
    ppermute x6, starting transfers between devices: 8.92 us -> 10.6 us  [first_axis(): lax.ppermute(value, 'vert', positions(lambda x, z, c: (x + shift * (1 - c...]
    ppermute x6, waiting for transfers between devices: 0.02 us -> 1.08 us  [second_axis(): lax.ppermute(value, 'vert', positions(lambda x, z, c: (x + shift * c, z +...]
    pallas_call x3 -> x4, Pallas kernels: 3.85 us -> 4.03 us  [the longest x3 3.39 us: product(): pl.pallas_call(functools.partial(kernel, kinds), out_shape=total_shape, i...]
  transfers between devices with their start and end apart: 30 -> 30, of which waited for: 9 -> 11; matrix products, arithmetic and copies ran while one was open for 0% -> 0% of each run, Pallas kernels for 17% -> 17%
where the time goes in v5:
time: 77.3 us; the launch traced here: 77.1 us
  starting transfers between devices  42.8 us (55%)
  Pallas kernels  17.2 us (22%)
  waiting for transfers between devices  16.9 us (22%)
    ppermute x10, starting transfers between devices, swap(): return lax.ppermute(value, 'vert', positions(lambda x, z, c: (x, z, 1 - c)))  13.3 us
    ppermute x6, starting transfers between devices, first_axis(): lax.ppermute(value, 'vert', positions(lambda x, z, c: (x + shift * (1 - c...  10.6 us
    ppermute x7, starting transfers between devices, along_feat(): lax.ppermute(value, 'feat', [(i, (i + shift) % NF) for i in range(NF)])  8.9 us
    ppermute x7, waiting for transfers between devices, along_feat(): lax.ppermute(value, 'feat', [(i, (i + shift) % NF) for i in range(NF)])  8.07 us
    ppermute x6, starting transfers between devices, second_axis(): lax.ppermute(value, 'vert', positions(lambda x, z, c: (x + shift * c, z +...  7.27 us
    pallas_call x1, Pallas kernels, second_half(): pl.pallas_call(functools.partial(adjacency_kernel, 1), in_specs=[HB] * 2...  5.54 us
    ppermute x1, waiting for transfers between devices, both_sides(): return lax.ppermute(value, ('feat', 'vert'), pairs)  4.26 us
    pallas_call x1, Pallas kernels, first_half(): pl.pallas_call(functools.partial(adjacency_kernel, 0), in_specs=[HB] * 5,...  4.18 us
  transfers between devices with their start and end apart: 30, of which 11 were waited for; matrix products, arithmetic and copies ran while one was open for 0% of the time, Pallas kernels for 17%

profile of v5, /device:TPU:1, one launch (start us, length us, event | category | flops | bytes accessed | tf_op | source)
XLA Modules:
  0.0 77.1 jit_solution(8343488764666164532)
XLA Ops:
  0.0 4.4 %collective-permute-start = (bf16[192,384]{1,0:T(8,128)(2,1)}, bf16[192,384]{1,0:T(8,128)(2,1)S(1)}, u32[]{:S(2)}, u32[]{:S(2)}) collective-permute-start(bf16[192,384]{1,0:T(8,128)(2,1)} %bitcast.9), channel_id=1, source_target_pairs={{0,16},{1,5},{2,18},{3,7},{4,20},{5,1},{6,22},{7,3},{8,24},{9,13},... | collective-permute-start | bytes 442376 | tf_op jit(solution)/shard_map/ppermute | solution.py:59
  4.4 0.7 collective-permute-start.1
  5.2 1.9 %collective-permute-start.2 = (bf16[192,384]{1,0:T(8,128)(2,1)}, bf16[192,384]{1,0:T(8,128)(2,1)S(1)}, u32[]{:S(2)}, u32[]{:S(2)}) collective-permute-start(bf16[192,384]{1,0:T(8,128)(2,1)} %bitcast.11), channel_id=1, source_target_pairs={{0,24},{1,7},{2,26},{3,1},{4,28},{5,3},{6,30},{7,5},{8,0},{9,15},{... | collective-permute-start | bytes 442376 | tf_op jit(solution)/shard_map/ppermute | solution.py:59
  7.1 4.2 %adjacency_first.1 = (bf16[384,12288]{1,0:T(8,128)(2,1)S(1)}, bf16[384,4096]{1,0:T(8,128)(2,1)S(1)}, f32[384,128]{1,0:T(8,128)S(1)}, bf16[2,256,512]{2,1,0:T(8,128)(2,1)S(1)}, bf16[256,512]{1,0:T(8,128)(2,1)S(1)}) custom-call(s32[3,96]{1,0:T(4,128)} %mask.3, s32[384,12288]{1,0:T(8,128)} %counts.3, bf16[192,1024]{1,0:T(8,128)(2,1)} %refs_0_.1, ...), custom_call_target="tpu_custom_call" | custom-call | flops 1200000000 | bytes 16000000 | tf_op jit(solution)/shard_map/adjacency_first/pallas_call | solution.py:168
  11.3 0.0 collective-permute-done.b
  11.3 0.0 collective-permute-done.1.c
  11.3 0.1 stack.21.refs_0_
  11.4 0.7 collective-permute-start.3
  12.1 2.0 %collective-permute-start.7 = (bf16[4,192,384]{2,1,0:T(8,128)(2,1)S(1)}, bf16[4,192,384]{2,1,0:T(8,128)(2,1)S(1)}, u32[]{:S(2)}, u32[]{:S(2)}) collective-permute-start(bf16[4,192,384]{2,1,0:T(8,128)(2,1)S(1)} %stack.21.refs_0_), channel_id=1, source_target_pairs={{0,6},{1,25},{2,0},{3,27},{4,2},{5,29},{6,4},{7,31},{8,14},{9,1},{... | collective-permute-start | bytes 1769480 | tf_op jit(solution)/shard_map/ppermute | solution.py:63
  14.2 0.0 collective-permute-start.6
  14.2 2.7 %collective-permute-start.4 = (bf16[2,256,512]{2,1,0:T(8,128)(2,1)S(1)}, bf16[2,256,512]{2,1,0:T(8,128)(2,1)S(1)}, u32[]{:S(2)}, u32[]{:S(2)}) collective-permute-start(bf16[2,256,512]{2,1,0:T(8,128)(2,1)S(1)} %get-tuple-element.33.own), channel_id=1, source_target_pairs={{0,32},{32,64},{64,96},{96,0},{1,97},{33,1},{65,33},{97,65},{2,34}... | collective-permute-start | bytes 1572872 | tf_op jit(solution)/shard_map/ppermute | solution.py:76
  16.9 1.6 %collective-permute-start.10 = (bf16[4,192,384]{2,1,0:T(8,128)(2,1)S(1)}, bf16[4,192,384]{2,1,0:T(8,128)(2,1)S(1)}, u32[]{:S(2)}, u32[]{:S(2)}) collective-permute-start(bf16[4,192,384]{2,1,0:T(8,128)(2,1)S(1)} %stack.21.refs_0_), channel_id=1, source_target_pairs={{0,4},{1,17},{2,6},{3,19},{4,0},{5,21},{6,2},{7,23},{8,12},{9,25},... | collective-permute-start | bytes 1769480 | tf_op jit(solution)/shard_map/ppermute | solution.py:63
  18.5 0.0 collective-permute-done.3.refs_3_.refs_1_
  18.5 0.3 collective-permute-start.5
  18.9 5.5 %adjacency_second.1 = (bf16[384,12288]{1,0:T(8,128)(2,1)S(1)}, bf16[384,4096]{1,0:T(8,128)(2,1)S(1)}, f32[384,128]{1,0:T(8,128)S(1)}) custom-call(s32[3,96]{1,0:T(4,128)} %mask.3, s32[384,12288]{1,0:T(8,128)} %counts.3, bf16[384,12288]{1,0:T(8,128)(2,1)S(1)} %get-tuple-element.27.refs_0_, ...), custom_call_target="tpu_custom_call", output_to_operand_aliasing={{0}: (2, {}), {1}: (3, {}), {2}: (4, {})} | custom-call | flops 1200000000 | bytes 16000000 | tf_op jit(solution)/shard_map/adjacency_second/pallas_call | solution.py:189
  24.4 4.3 %collective-permute-done.4.refs_2_.side = bf16[2,256,512]{2,1,0:T(8,128)(2,1)S(1)} collective-permute-done((bf16[2,256,512]{2,1,0:T(8,128)(2,1)S(1)}, bf16[2,256,512]{2,1,0:T(8,128)(2,1)S(1)}, u32[]{:S(2)}, u32[]{:S(2)}) %collective-permute-start.4) | collective-permute-done | bytes 524320 | tf_op jit(solution)/shard_map/ppermute | solution.py:76
  28.7 1.0 %product_first.1.before = f32[384,192]{1,0:T(8,128)S(1)} custom-call(bf16[384,12288]{1,0:T(8,128)(2,1)S(1)} %get-tuple-element.34.adj, bf16[4,192,384]{2,1,0:T(8,128)(2,1)S(1)} %stack.21.refs_0_, bf16[4,192,384]{2,1,0:T(8,128)(2,1)S(1)} %collective-permute-done.3.refs_3_.refs_1_, bf16[2,256,512]{2,1,0:T(8,128)(2,1)S(1)} %collective-permute-done.4.refs_2_.side), custom_call_target="tpu_custom_call" | custom-call | flops 603979776 | bytes 3600000 | tf_op jit(solution)/shard_map/product_first/pallas_call | solution.py:340
  29.7 1.1 %collective-permute-done.6.refs_0_ = bf16[4,192,384]{2,1,0:T(8,128)(2,1)S(1)} collective-permute-done((bf16[4,192,384]{2,1,0:T(8,128)(2,1)S(1)}, bf16[4,192,384]{2,1,0:T(8,128)(2,1)S(1)}, u32[]{:S(2)}, u32[]{:S(2)}) %collective-permute-start.6) | collective-permute-done | bytes 589856 | tf_op jit(solution)/shard_map/ppermute | solution.py:63
  30.7 2.9 %collective-permute-start.9 = (bf16[4,192,384]{2,1,0:T(8,128)(2,1)S(1)}, bf16[4,192,384]{2,1,0:T(8,128)(2,1)S(1)}, u32[]{:S(2)}, u32[]{:S(2)}) collective-permute-start(bf16[4,192,384]{2,1,0:T(8,128)(2,1)S(1)} %collective-permute-done.7.refs_1_), channel_id=1, source_target_pairs={{0,1},{1,0},{2,3},{3,2},{4,5},{5,4},{6,7},{7,6},{8,9},{9,8},{10,11... | collective-permute-start | bytes 1769480 | tf_op jit(solution)/shard_map/ppermute | solution.py:67
  33.7 0.0 collective-permute-start.8
  33.7 0.0 collective-permute-done.10.refs_2_
  33.7 0.0 collective-permute-done.5.refs_2_.near
  33.7 1.0 %product_next.1.before = f32[384,192]{1,0:T(8,128)S(1)} custom-call(bf16[384,12288]{1,0:T(8,128)(2,1)S(1)} %get-tuple-element.34.adj, f32[384,192]{1,0:T(8,128)S(1)} %product_first.1.before, bf16[4,192,384]{2,1,0:T(8,128)(2,1)S(1)} %collective-permute-done.6.refs_0_, bf16[4,192,384]{2,1,0:T(8,128)(2,1)S(1)} %collective-permute-done.7.refs_1_, ...), custom_call_target="tpu_custom_call" | custom-call | flops 603979776 | bytes 3600000 | tf_op jit(solution)/shard_map/product_next/pallas_call | solution.py:340
  34.7 0.6 collective-permute-start.11
  35.3 0.0 collective-permute-done.9.refs_1_
  35.3 0.8 %collective-permute-done.8.refs_0_ = bf16[4,192,384]{2,1,0:T(8,128)(2,1)S(1)} collective-permute-done((bf16[4,192,384]{2,1,0:T(8,128)(2,1)S(1)}, bf16[4,192,384]{2,1,0:T(8,128)(2,1)S(1)}, u32[]{:S(2)}, u32[]{:S(2)}) %collective-permute-start.8) | collective-permute-done | bytes 589856 | tf_op jit(solution)/shard_map/ppermute | solution.py:67
  36.1 1.4 %product_more.1.before = f32[384,192]{1,0:T(8,128)S(1)} custom-call(bf16[384,12288]{1,0:T(8,128)(2,1)S(1)} %get-tuple-element.34.adj, f32[384,192]{1,0:T(8,128)S(1)} %product_next.1.before, bf16[4,192,384]{2,1,0:T(8,128)(2,1)S(1)} %collective-permute-done.8.refs_0_, bf16[4,192,384]{2,1,0:T(8,128)(2,1)S(1)} %collective-permute-done.9.refs_1_, ...), custom_call_target="tpu_custom_call" | custom-call | flops 905969664 | bytes 5400000 | tf_op jit(solution)/shard_map/product_more/pallas_call | solution.py:340
  37.6 0.0 copy-start.1
  37.6 0.0 collective-permute-done.11.refs_0_
  37.6 0.6 product_last.1
  38.2 0.5 collective-permute-start.15
  38.7 0.1 collective-permute-start.16
  38.8 1.3 %collective-permute-start.12 = (bf16[96,192]{1,0:T(8,128)(2,1)S(1)}, bf16[96,192]{1,0:T(8,128)(2,1)S(1)}, u32[]{:S(2)}, u32[]{:S(2)}) collective-permute-start(bf16[96,192]{1,0:T(8,128)(2,1)S(1)} %get-tuple-element.44), channel_id=1, source_target_pairs={{0,32},{32,64},{64,96},{96,0},{1,33},{33,65},{65,97},{97,1},{2,34}... | collective-permute-start | bytes 110600 | tf_op jit(solution)/shard_map/ppermute | solution.py:71
  40.1 2.6 %collective-permute-start.13 = (bf16[96,192]{1,0:T(8,128)(2,1)S(1)}, bf16[96,192]{1,0:T(8,128)(2,1)S(1)}, u32[]{:S(2)}, u32[]{:S(2)}) collective-permute-start(bf16[96,192]{1,0:T(8,128)(2,1)S(1)} %get-tuple-element.45), channel_id=1, source_target_pairs={{0,64},{32,96},{64,0},{96,32},{1,65},{33,97},{65,1},{97,33},{2,66}... | collective-permute-start | bytes 110600 | tf_op jit(solution)/shard_map/ppermute | solution.py:71
  42.7 1.1 %collective-permute-start.14 = (bf16[96,192]{1,0:T(8,128)(2,1)S(1)}, bf16[96,192]{1,0:T(8,128)(2,1)S(1)}, u32[]{:S(2)}, u32[]{:S(2)}) collective-permute-start(bf16[96,192]{1,0:T(8,128)(2,1)S(1)} %get-tuple-element.46), channel_id=1, source_target_pairs={{0,96},{32,0},{64,32},{96,64},{1,97},{33,1},{65,33},{97,65},{2,98}... | collective-permute-start | bytes 110600 | tf_op jit(solution)/shard_map/ppermute | solution.py:71
  43.8 0.0 collective-permute-done.12.g1
  43.8 1.2 %collective-permute-done.13.g2 = bf16[96,192]{1,0:T(8,128)(2,1)S(1)} collective-permute-done((bf16[96,192]{1,0:T(8,128)(2,1)S(1)}, bf16[96,192]{1,0:T(8,128)(2,1)S(1)}, u32[]{:S(2)}, u32[]{:S(2)}) %collective-permute-start.13) | collective-permute-done | bytes 36896 | tf_op jit(solution)/shard_map/ppermute | solution.py:71
  45.0 1.0 %collective-permute-done.14.g3 = bf16[96,192]{1,0:T(8,128)(2,1)S(1)} collective-permute-done((bf16[96,192]{1,0:T(8,128)(2,1)S(1)}, bf16[96,192]{1,0:T(8,128)(2,1)S(1)}, u32[]{:S(2)}, u32[]{:S(2)}) %collective-permute-start.14) | collective-permute-done | bytes 36896 | tf_op jit(solution)/shard_map/ppermute | solution.py:71
  46.0 1.0 %hidden.1 = bf16[128,128]{1,0:T(8,128)(2,1)S(1)} custom-call(bf16[96,192]{1,0:T(8,128)(2,1)S(1)} %get-tuple-element.43.g0, bf16[96,192]{1,0:T(8,128)(2,1)S(1)} %collective-permute-done.12.g1, bf16[96,192]{1,0:T(8,128)(2,1)S(1)} %collective-permute-done.13.g2, bf16[96,192]{1,0:T(8,128)(2,1)S(1)} %collective-permute-done.14.g3, ...), custom_call_target="tpu_custom_call" | custom-call | flops 150994944 | bytes 2000000 | tf_op jit(solution)/shard_map/hidden/pallas_call | solution.py:366
  47.0 0.8 %collective-permute-start.17 = (bf16[128,128]{1,0:T(8,128)(2,1)S(1)}, bf16[128,128]{1,0:T(8,128)(2,1)S(1)}, u32[]{:S(2)}, u32[]{:S(2)}) collective-permute-start(bf16[128,128]{1,0:T(8,128)(2,1)S(1)} %hidden.1), channel_id=1, source_target_pairs={{0,16},{1,5},{2,18},{3,7},{4,20},{5,1},{6,22},{7,3},{8,24},{9,13},... | collective-permute-start | bytes 98312 | tf_op jit(solution)/shard_map/ppermute | solution.py:59
  47.8 0.9 %collective-permute-start.18 = (bf16[128,128]{1,0:T(8,128)(2,1)S(1)}, bf16[128,128]{1,0:T(8,128)(2,1)S(1)}, u32[]{:S(2)}, u32[]{:S(2)}) collective-permute-start(bf16[128,128]{1,0:T(8,128)(2,1)S(1)} %hidden.1), channel_id=1, source_target_pairs={{0,8},{1,3},{2,10},{3,5},{4,12},{5,7},{6,14},{7,1},{8,16},{9,11},{... | collective-permute-start | bytes 98312 | tf_op jit(solution)/shard_map/ppermute | solution.py:59
  48.7 1.8 %collective-permute-start.19 = (bf16[128,128]{1,0:T(8,128)(2,1)S(1)}, bf16[128,128]{1,0:T(8,128)(2,1)S(1)}, u32[]{:S(2)}, u32[]{:S(2)}) collective-permute-start(bf16[128,128]{1,0:T(8,128)(2,1)S(1)} %hidden.1), channel_id=1, source_target_pairs={{0,24},{1,7},{2,26},{3,1},{4,28},{5,3},{6,30},{7,5},{8,0},{9,15},{... | collective-permute-start | bytes 98312 | tf_op jit(solution)/shard_map/ppermute | solution.py:59
  50.5 0.8 %collective-permute-done.17 = bf16[128,128]{1,0:T(8,128)(2,1)S(1)} collective-permute-done((bf16[128,128]{1,0:T(8,128)(2,1)S(1)}, bf16[128,128]{1,0:T(8,128)(2,1)S(1)}, u32[]{:S(2)}, u32[]{:S(2)}) %collective-permute-start.17) | collective-permute-done | bytes 32800 | tf_op jit(solution)/shard_map/ppermute | solution.py:59
  51.4 0.4 collective-permute-done.18
  51.8 0.0 collective-permute-done.19
  51.8 1.0 %collective-permute-start.21 = (bf16[4,128,128]{2,1,0:T(8,128)(2,1)S(1)}, bf16[4,128,128]{2,1,0:T(8,128)(2,1)S(1)}, u32[]{:S(2)}, u32[]{:S(2)}) collective-permute-start(bf16[4,128,128]{2,1,0:T(8,128)(2,1)S(1)} %pad_maximum_fusion.refs_0_), channel_id=1, source_target_pairs={{0,4},{1,17},{2,6},{3,19},{4,0},{5,21},{6,2},{7,23},{8,12},{9,25},... | collective-permute-start | bytes 393224 | tf_op jit(solution)/shard_map/ppermute | solution.py:63
  52.8 2.1 %collective-permute-start.23 = (bf16[4,128,128]{2,1,0:T(8,128)(2,1)S(1)}, bf16[4,128,128]{2,1,0:T(8,128)(2,1)S(1)}, u32[]{:S(2)}, u32[]{:S(2)}) collective-permute-start(bf16[4,128,128]{2,1,0:T(8,128)(2,1)S(1)} %pad_maximum_fusion.refs_0_), channel_id=1, source_target_pairs={{0,2},{1,9},{2,4},{3,11},{4,6},{5,13},{6,0},{7,15},{8,10},{9,17},{... | collective-permute-start | bytes 393224 | tf_op jit(solution)/shard_map/ppermute | solution.py:63
  54.9 0.6 collective-permute-start.25
  55.5 5.0 %collective-permute-start.20 = (bf16[4,128,128]{2,1,0:T(8,128)(2,1)S(1)}, bf16[4,128,128]{2,1,0:T(8,128)(2,1)S(1)}, u32[]{:S(2)}, u32[]{:S(2)}) collective-permute-start(bf16[4,128,128]{2,1,0:T(8,128)(2,1)S(1)} %pad_maximum_fusion.refs_0_), channel_id=1, source_target_pairs={{0,1},{1,0},{2,3},{3,2},{4,5},{5,4},{6,7},{7,6},{8,9},{9,8},{10,11... | collective-permute-start | bytes 393224 | tf_op jit(solution)/shard_map/ppermute | solution.py:67
  60.5 2.1 %collective-permute-start.22 = (bf16[4,128,128]{2,1,0:T(8,128)(2,1)S(1)}, bf16[4,128,128]{2,1,0:T(8,128)(2,1)S(1)}, u32[]{:S(2)}, u32[]{:S(2)}) collective-permute-start(bf16[4,128,128]{2,1,0:T(8,128)(2,1)S(1)} %collective-permute-done.21.refs_2_), channel_id=1, source_target_pairs={{0,1},{1,0},{2,3},{3,2},{4,5},{5,4},{6,7},{7,6},{8,9},{9,8},{10,11... | collective-permute-start | bytes 393224 | tf_op jit(solution)/shard_map/ppermute | solution.py:67
  62.6 1.3 %collective-permute-start.24 = (bf16[4,128,128]{2,1,0:T(8,128)(2,1)S(1)}, bf16[4,128,128]{2,1,0:T(8,128)(2,1)S(1)}, u32[]{:S(2)}, u32[]{:S(2)}) collective-permute-start(bf16[4,128,128]{2,1,0:T(8,128)(2,1)S(1)} %collective-permute-done.23.refs_4_), channel_id=1, source_target_pairs={{0,1},{1,0},{2,3},{3,2},{4,5},{5,4},{6,7},{7,6},{8,9},{9,8},{10,11... | collective-permute-start | bytes 393224 | tf_op jit(solution)/shard_map/ppermute | solution.py:67
  64.0 0.0 collective-permute-done.25.refs_6_
  64.0 0.0 collective-permute-start.26
  64.0 0.0 collective-permute-done.20.refs_1_
  64.0 1.0 %collective-permute-done.24.refs_5_ = bf16[4,128,128]{2,1,0:T(8,128)(2,1)S(1)} collective-permute-done((bf16[4,128,128]{2,1,0:T(8,128)(2,1)S(1)}, bf16[4,128,128]{2,1,0:T(8,128)(2,1)S(1)}, u32[]{:S(2)}, u32[]{:S(2)}) %collective-permute-start.24) | collective-permute-done | bytes 131104 | tf_op jit(solution)/shard_map/ppermute | solution.py:67
  65.0 0.4 collective-permute-done.26.refs_7_
  65.3 1.5 %scores.1.p0 = bf16[160,384]{1,0:T(8,128)(2,1)S(1)} custom-call(bf16[384,4096]{1,0:T(8,128)(2,1)S(1)} %get-tuple-element.31.adj2, f32[384,128]{1,0:T(8,128)S(1)} %get-tuple-element.32.degree, bf16[4,128,128]{2,1,0:T(8,128)(2,1)S(1)} %pad_maximum_fusion.refs_0_, bf16[4,128,128]{2,1,0:T(8,128)(2,1)S(1)} %collective-permute-done.20.refs_1_, ...), custom_call_target="tpu_custom_call" | custom-call | flops 805306368 | bytes 5000000 | tf_op jit(solution)/shard_map/scores/pallas_call | solution.py:378
  66.8 0.1 collective-permute-start.27
  66.9 3.5 %collective-permute-start.28 = (bf16[160,384]{1,0:T(8,128)(2,1)S(1)}, bf16[160,384]{1,0:T(8,128)(2,1)S(1)}, u32[]{:S(2)}, u32[]{:S(2)}) collective-permute-start(bf16[160,384]{1,0:T(8,128)(2,1)S(1)} %scores.1.p0), channel_id=1, source_target_pairs={{0,64},{32,96},{64,0},{96,32},{1,65},{33,97},{65,1},{97,33},{2,66}... | collective-permute-start | bytes 368648 | tf_op jit(solution)/shard_map/ppermute | solution.py:71
  70.4 0.0 collective-permute-start.29
  70.4 2.5 %collective-permute-done.27.p1 = bf16[160,384]{1,0:T(8,128)(2,1)S(1)} collective-permute-done((bf16[160,384]{1,0:T(8,128)(2,1)S(1)}, bf16[160,384]{1,0:T(8,128)(2,1)S(1)}, u32[]{:S(2)}, u32[]{:S(2)}) %collective-permute-start.27) | collective-permute-done | bytes 122912 | tf_op jit(solution)/shard_map/ppermute | solution.py:71
  72.8 3.5 %collective-permute-done.28.p2 = bf16[160,384]{1,0:T(8,128)(2,1)S(1)} collective-permute-done((bf16[160,384]{1,0:T(8,128)(2,1)S(1)}, bf16[160,384]{1,0:T(8,128)(2,1)S(1)}, u32[]{:S(2)}, u32[]{:S(2)}) %collective-permute-start.28) | collective-permute-done | bytes 122912 | tf_op jit(solution)/shard_map/ppermute | solution.py:71
  76.3 0.0 collective-permute-done.29.p3
  76.3 0.9 %sum.1 = f32[153,384]{1,0:T(8,128)} custom-call(bf16[160,384]{1,0:T(8,128)(2,1)S(1)} %scores.1.p0, bf16[160,384]{1,0:T(8,128)(2,1)S(1)} %collective-permute-done.27.p1, bf16[160,384]{1,0:T(8,128)(2,1)S(1)} %collective-permute-done.28.p2, bf16[160,384]{1,0:T(8,128)(2,1)S(1)} %collective-permute-done.29.p3, f32[1,256]{1,0:T(1,128)S(1)} %bitcast.14), custom_call_target="tpu_custom_call" | custom-call | flops 300000 | bytes 800000 | tf_op jit(solution)/shard_map/sum/pallas_call | solution.py:386
  (12 shorter events, 0.0 us)
Async XLA Ops:
  0.0 11.3 %collective-permute-start = (bf16[192,384]{1,0:T(8,128)(2,1)}, bf16[192,384]{1,0:T(8,128)(2,1)S(1)}, u32[]{:S(2)}, u32[]{:S(2)}) collective-permute-start(bf16[192,384]{1,0:T(8,128)(2,1)} %bitcast.9), channel_id=1, source_target_pairs={{0,16},{1,5},{2,18},{3,7},{4,20},{5,1},{6,22},{7,3},{8,24},{9,13},... | collective-permute-start | bytes 442376 | tf_op jit(solution)/shard_map/ppermute | solution.py:59
  4.4 6.9 %collective-permute-start.1 = (bf16[192,384]{1,0:T(8,128)(2,1)}, bf16[192,384]{1,0:T(8,128)(2,1)S(1)}, u32[]{:S(2)}, u32[]{:S(2)}) collective-permute-start(bf16[192,384]{1,0:T(8,128)(2,1)} %bitcast.10), channel_id=1, source_target_pairs={{0,8},{1,3},{2,10},{3,5},{4,12},{5,7},{6,14},{7,1},{8,16},{9,11},{... | collective-permute-start | bytes 442376 | tf_op jit(solution)/shard_map/ppermute | solution.py:59
  5.2 6.2 %collective-permute-start.2 = (bf16[192,384]{1,0:T(8,128)(2,1)}, bf16[192,384]{1,0:T(8,128)(2,1)S(1)}, u32[]{:S(2)}, u32[]{:S(2)}) collective-permute-start(bf16[192,384]{1,0:T(8,128)(2,1)} %bitcast.11), channel_id=1, source_target_pairs={{0,24},{1,7},{2,26},{3,1},{4,28},{5,3},{6,30},{7,5},{8,0},{9,15},{... | collective-permute-start | bytes 442376 | tf_op jit(solution)/shard_map/ppermute | solution.py:59
  7.1 4.2 %copy-start = (bf16[384,192]{0,1:T(8,128)(2,1)S(1)}, bf16[384,192]{0,1:T(8,128)(2,1)}, u32[]{:S(2)}) copy-start(bf16[384,192]{0,1:T(8,128)(2,1)} %param.7) | copy-start | bytes 442372
  11.4 7.1 %collective-permute-start.3 = (bf16[4,192,384]{2,1,0:T(8,128)(2,1)S(1)}, bf16[4,192,384]{2,1,0:T(8,128)(2,1)S(1)}, u32[]{:S(2)}, u32[]{:S(2)}) collective-permute-start(bf16[4,192,384]{2,1,0:T(8,128)(2,1)S(1)} %stack.21.refs_0_), channel_id=1, source_target_pairs={{0,1},{1,0},{2,3},{3,2},{4,5},{5,4},{6,7},{7,6},{8,9},{9,8},{10,11... | collective-permute-start | bytes 1769480 | tf_op jit(solution)/shard_map/ppermute | solution.py:67
  12.1 17.5 %collective-permute-start.7 = (bf16[4,192,384]{2,1,0:T(8,128)(2,1)S(1)}, bf16[4,192,384]{2,1,0:T(8,128)(2,1)S(1)}, u32[]{:S(2)}, u32[]{:S(2)}) collective-permute-start(bf16[4,192,384]{2,1,0:T(8,128)(2,1)S(1)} %stack.21.refs_0_), channel_id=1, source_target_pairs={{0,6},{1,25},{2,0},{3,27},{4,2},{5,29},{6,4},{7,31},{8,14},{9,1},{... | collective-permute-start | bytes 1769480 | tf_op jit(solution)/shard_map/ppermute | solution.py:63
  14.2 16.6 %collective-permute-start.6 = (bf16[4,192,384]{2,1,0:T(8,128)(2,1)S(1)}, bf16[4,192,384]{2,1,0:T(8,128)(2,1)S(1)}, u32[]{:S(2)}, u32[]{:S(2)}) collective-permute-start(bf16[4,192,384]{2,1,0:T(8,128)(2,1)S(1)} %stack.21.refs_0_), channel_id=1, source_target_pairs={{0,2},{1,9},{2,4},{3,11},{4,6},{5,13},{6,0},{7,15},{8,10},{9,17},{... | collective-permute-start | bytes 1769480 | tf_op jit(solution)/shard_map/ppermute | solution.py:63
  14.2 14.5 %collective-permute-start.4 = (bf16[2,256,512]{2,1,0:T(8,128)(2,1)S(1)}, bf16[2,256,512]{2,1,0:T(8,128)(2,1)S(1)}, u32[]{:S(2)}, u32[]{:S(2)}) collective-permute-start(bf16[2,256,512]{2,1,0:T(8,128)(2,1)S(1)} %get-tuple-element.33.own), channel_id=1, source_target_pairs={{0,32},{32,64},{64,96},{96,0},{1,97},{33,1},{65,33},{97,65},{2,34}... | collective-permute-start | bytes 1572872 | tf_op jit(solution)/shard_map/ppermute | solution.py:76
  16.9 16.8 %collective-permute-start.10 = (bf16[4,192,384]{2,1,0:T(8,128)(2,1)S(1)}, bf16[4,192,384]{2,1,0:T(8,128)(2,1)S(1)}, u32[]{:S(2)}, u32[]{:S(2)}) collective-permute-start(bf16[4,192,384]{2,1,0:T(8,128)(2,1)S(1)} %stack.21.refs_0_), channel_id=1, source_target_pairs={{0,4},{1,17},{2,6},{3,19},{4,0},{5,21},{6,2},{7,23},{8,12},{9,25},... | collective-permute-start | bytes 1769480 | tf_op jit(solution)/shard_map/ppermute | solution.py:63
  18.5 15.2 %collective-permute-start.5 = (bf16[256,512]{1,0:T(8,128)(2,1)S(1)}, bf16[256,512]{1,0:T(8,128)(2,1)S(1)}, u32[]{:S(2)}, u32[]{:S(2)}) collective-permute-start(bf16[256,512]{1,0:T(8,128)(2,1)S(1)} %get-tuple-element.30.after), channel_id=1, source_target_pairs={{0,64},{32,96},{64,0},{96,32},{1,65},{33,97},{65,1},{97,33},{2,66}... | collective-permute-start | bytes 786440 | tf_op jit(solution)/shard_map/ppermute | solution.py:71
  30.7 4.6 %collective-permute-start.9 = (bf16[4,192,384]{2,1,0:T(8,128)(2,1)S(1)}, bf16[4,192,384]{2,1,0:T(8,128)(2,1)S(1)}, u32[]{:S(2)}, u32[]{:S(2)}) collective-permute-start(bf16[4,192,384]{2,1,0:T(8,128)(2,1)S(1)} %collective-permute-done.7.refs_1_), channel_id=1, source_target_pairs={{0,1},{1,0},{2,3},{3,2},{4,5},{5,4},{6,7},{7,6},{8,9},{9,8},{10,11... | collective-permute-start | bytes 1769480 | tf_op jit(solution)/shard_map/ppermute | solution.py:67
  33.7 2.5 %collective-permute-start.8 = (bf16[4,192,384]{2,1,0:T(8,128)(2,1)S(1)}, bf16[4,192,384]{2,1,0:T(8,128)(2,1)S(1)}, u32[]{:S(2)}, u32[]{:S(2)}) collective-permute-start(bf16[4,192,384]{2,1,0:T(8,128)(2,1)S(1)} %collective-permute-done.6.refs_0_), channel_id=1, source_target_pairs={{0,1},{1,0},{2,3},{3,2},{4,5},{5,4},{6,7},{7,6},{8,9},{9,8},{10,11... | collective-permute-start | bytes 1769480 | tf_op jit(solution)/shard_map/ppermute | solution.py:67
  34.7 2.9 %collective-permute-start.11 = (bf16[4,192,384]{2,1,0:T(8,128)(2,1)S(1)}, bf16[4,192,384]{2,1,0:T(8,128)(2,1)S(1)}, u32[]{:S(2)}, u32[]{:S(2)}) collective-permute-start(bf16[4,192,384]{2,1,0:T(8,128)(2,1)S(1)} %collective-permute-done.10.refs_2_), channel_id=1, source_target_pairs={{0,1},{1,0},{2,3},{3,2},{4,5},{5,4},{6,7},{7,6},{8,9},{9,8},{10,11... | collective-permute-start | bytes 1769480 | tf_op jit(solution)/shard_map/ppermute | solution.py:67
  37.6 32.8 %copy-start.1 = (f32[153]{0:T(256)S(1)}, f32[153]{0:T(256)}, u32[]{:S(2)}) copy-start(f32[153]{0:T(256)} %param.13) | copy-start | bytes 1840
  38.2 7.8 %collective-permute-start.15 = (bf16[2,256,512]{2,1,0:T(8,128)(2,1)S(1)}, bf16[2,256,512]{2,1,0:T(8,128)(2,1)S(1)}, u32[]{:S(2)}, u32[]{:S(2)}) collective-permute-start(bf16[2,256,512]{2,1,0:T(8,128)(2,1)S(1)} %collective-permute-done.4.refs_2_.side), channel_id=1, source_target_pairs={{0,1},{1,0},{2,3},{3,2},{4,5},{5,4},{6,7},{7,6},{8,9},{9,8},{10,11... | collective-permute-start | bytes 1572872 | tf_op jit(solution)/shard_map/ppermute | solution.py:67
  38.7 7.3 %collective-permute-start.16 = (bf16[256,512]{1,0:T(8,128)(2,1)S(1)}, bf16[256,512]{1,0:T(8,128)(2,1)S(1)}, u32[]{:S(2)}, u32[]{:S(2)}) collective-permute-start(bf16[256,512]{1,0:T(8,128)(2,1)S(1)} %collective-permute-done.5.refs_2_.near), channel_id=1, source_target_pairs={{0,1},{1,0},{2,3},{3,2},{4,5},{5,4},{6,7},{7,6},{8,9},{9,8},{10,11... | collective-permute-start | bytes 786440 | tf_op jit(solution)/shard_map/ppermute | solution.py:67
  38.8 5.0 %collective-permute-start.12 = (bf16[96,192]{1,0:T(8,128)(2,1)S(1)}, bf16[96,192]{1,0:T(8,128)(2,1)S(1)}, u32[]{:S(2)}, u32[]{:S(2)}) collective-permute-start(bf16[96,192]{1,0:T(8,128)(2,1)S(1)} %get-tuple-element.44), channel_id=1, source_target_pairs={{0,32},{32,64},{64,96},{96,0},{1,33},{33,65},{65,97},{97,1},{2,34}... | collective-permute-start | bytes 110600 | tf_op jit(solution)/shard_map/ppermute | solution.py:71
  40.1 4.9 %collective-permute-start.13 = (bf16[96,192]{1,0:T(8,128)(2,1)S(1)}, bf16[96,192]{1,0:T(8,128)(2,1)S(1)}, u32[]{:S(2)}, u32[]{:S(2)}) collective-permute-start(bf16[96,192]{1,0:T(8,128)(2,1)S(1)} %get-tuple-element.45), channel_id=1, source_target_pairs={{0,64},{32,96},{64,0},{96,32},{1,65},{33,97},{65,1},{97,33},{2,66}... | collective-permute-start | bytes 110600 | tf_op jit(solution)/shard_map/ppermute | solution.py:71
  42.7 3.2 %collective-permute-start.14 = (bf16[96,192]{1,0:T(8,128)(2,1)S(1)}, bf16[96,192]{1,0:T(8,128)(2,1)S(1)}, u32[]{:S(2)}, u32[]{:S(2)}) collective-permute-start(bf16[96,192]{1,0:T(8,128)(2,1)S(1)} %get-tuple-element.46), channel_id=1, source_target_pairs={{0,96},{32,0},{64,32},{96,64},{1,97},{33,1},{65,33},{97,65},{2,98}... | collective-permute-start | bytes 110600 | tf_op jit(solution)/shard_map/ppermute | solution.py:71
  47.0 4.3 %collective-permute-start.17 = (bf16[128,128]{1,0:T(8,128)(2,1)S(1)}, bf16[128,128]{1,0:T(8,128)(2,1)S(1)}, u32[]{:S(2)}, u32[]{:S(2)}) collective-permute-start(bf16[128,128]{1,0:T(8,128)(2,1)S(1)} %hidden.1), channel_id=1, source_target_pairs={{0,16},{1,5},{2,18},{3,7},{4,20},{5,1},{6,22},{7,3},{8,24},{9,13},... | collective-permute-start | bytes 98312 | tf_op jit(solution)/shard_map/ppermute | solution.py:59
  47.8 4.0 %collective-permute-start.18 = (bf16[128,128]{1,0:T(8,128)(2,1)S(1)}, bf16[128,128]{1,0:T(8,128)(2,1)S(1)}, u32[]{:S(2)}, u32[]{:S(2)}) collective-permute-start(bf16[128,128]{1,0:T(8,128)(2,1)S(1)} %hidden.1), channel_id=1, source_target_pairs={{0,8},{1,3},{2,10},{3,5},{4,12},{5,7},{6,14},{7,1},{8,16},{9,11},{... | collective-permute-start | bytes 98312 | tf_op jit(solution)/shard_map/ppermute | solution.py:59
  48.7 3.1 %collective-permute-start.19 = (bf16[128,128]{1,0:T(8,128)(2,1)S(1)}, bf16[128,128]{1,0:T(8,128)(2,1)S(1)}, u32[]{:S(2)}, u32[]{:S(2)}) collective-permute-start(bf16[128,128]{1,0:T(8,128)(2,1)S(1)} %hidden.1), channel_id=1, source_target_pairs={{0,24},{1,7},{2,26},{3,1},{4,28},{5,3},{6,30},{7,5},{8,0},{9,15},{... | collective-permute-start | bytes 98312 | tf_op jit(solution)/shard_map/ppermute | solution.py:59
  51.8 8.6 %collective-permute-start.21 = (bf16[4,128,128]{2,1,0:T(8,128)(2,1)S(1)}, bf16[4,128,128]{2,1,0:T(8,128)(2,1)S(1)}, u32[]{:S(2)}, u32[]{:S(2)}) collective-permute-start(bf16[4,128,128]{2,1,0:T(8,128)(2,1)S(1)} %pad_maximum_fusion.refs_0_), channel_id=1, source_target_pairs={{0,4},{1,17},{2,6},{3,19},{4,0},{5,21},{6,2},{7,23},{8,12},{9,25},... | collective-permute-start | bytes 393224 | tf_op jit(solution)/shard_map/ppermute | solution.py:63
  52.8 9.8 %collective-permute-start.23 = (bf16[4,128,128]{2,1,0:T(8,128)(2,1)S(1)}, bf16[4,128,128]{2,1,0:T(8,128)(2,1)S(1)}, u32[]{:S(2)}, u32[]{:S(2)}) collective-permute-start(bf16[4,128,128]{2,1,0:T(8,128)(2,1)S(1)} %pad_maximum_fusion.refs_0_), channel_id=1, source_target_pairs={{0,2},{1,9},{2,4},{3,11},{4,6},{5,13},{6,0},{7,15},{8,10},{9,17},{... | collective-permute-start | bytes 393224 | tf_op jit(solution)/shard_map/ppermute | solution.py:63
  54.9 9.1 %collective-permute-start.25 = (bf16[4,128,128]{2,1,0:T(8,128)(2,1)S(1)}, bf16[4,128,128]{2,1,0:T(8,128)(2,1)S(1)}, u32[]{:S(2)}, u32[]{:S(2)}) collective-permute-start(bf16[4,128,128]{2,1,0:T(8,128)(2,1)S(1)} %pad_maximum_fusion.refs_0_), channel_id=1, source_target_pairs={{0,6},{1,25},{2,0},{3,27},{4,2},{5,29},{6,4},{7,31},{8,14},{9,1},{... | collective-permute-start | bytes 393224 | tf_op jit(solution)/shard_map/ppermute | solution.py:63
  55.5 8.5 %collective-permute-start.20 = (bf16[4,128,128]{2,1,0:T(8,128)(2,1)S(1)}, bf16[4,128,128]{2,1,0:T(8,128)(2,1)S(1)}, u32[]{:S(2)}, u32[]{:S(2)}) collective-permute-start(bf16[4,128,128]{2,1,0:T(8,128)(2,1)S(1)} %pad_maximum_fusion.refs_0_), channel_id=1, source_target_pairs={{0,1},{1,0},{2,3},{3,2},{4,5},{5,4},{6,7},{7,6},{8,9},{9,8},{10,11... | collective-permute-start | bytes 393224 | tf_op jit(solution)/shard_map/ppermute | solution.py:67
  60.5 3.5 %collective-permute-start.22 = (bf16[4,128,128]{2,1,0:T(8,128)(2,1)S(1)}, bf16[4,128,128]{2,1,0:T(8,128)(2,1)S(1)}, u32[]{:S(2)}, u32[]{:S(2)}) collective-permute-start(bf16[4,128,128]{2,1,0:T(8,128)(2,1)S(1)} %collective-permute-done.21.refs_2_), channel_id=1, source_target_pairs={{0,1},{1,0},{2,3},{3,2},{4,5},{5,4},{6,7},{7,6},{8,9},{9,8},{10,11... | collective-permute-start | bytes 393224 | tf_op jit(solution)/shard_map/ppermute | solution.py:67
  62.6 2.3 %collective-permute-start.24 = (bf16[4,128,128]{2,1,0:T(8,128)(2,1)S(1)}, bf16[4,128,128]{2,1,0:T(8,128)(2,1)S(1)}, u32[]{:S(2)}, u32[]{:S(2)}) collective-permute-start(bf16[4,128,128]{2,1,0:T(8,128)(2,1)S(1)} %collective-permute-done.23.refs_4_), channel_id=1, source_target_pairs={{0,1},{1,0},{2,3},{3,2},{4,5},{5,4},{6,7},{7,6},{8,9},{9,8},{10,11... | collective-permute-start | bytes 393224 | tf_op jit(solution)/shard_map/ppermute | solution.py:67
  64.0 1.3 %collective-permute-start.26 = (bf16[4,128,128]{2,1,0:T(8,128)(2,1)S(1)}, bf16[4,128,128]{2,1,0:T(8,128)(2,1)S(1)}, u32[]{:S(2)}, u32[]{:S(2)}) collective-permute-start(bf16[4,128,128]{2,1,0:T(8,128)(2,1)S(1)} %collective-permute-done.25.refs_6_), channel_id=1, source_target_pairs={{0,1},{1,0},{2,3},{3,2},{4,5},{5,4},{6,7},{7,6},{8,9},{9,8},{10,11... | collective-permute-start | bytes 393224 | tf_op jit(solution)/shard_map/ppermute | solution.py:67
  66.8 6.0 %collective-permute-start.27 = (bf16[160,384]{1,0:T(8,128)(2,1)S(1)}, bf16[160,384]{1,0:T(8,128)(2,1)S(1)}, u32[]{:S(2)}, u32[]{:S(2)}) collective-permute-start(bf16[160,384]{1,0:T(8,128)(2,1)S(1)} %scores.1.p0), channel_id=1, source_target_pairs={{0,32},{32,64},{64,96},{96,0},{1,33},{33,65},{65,97},{97,1},{2,34}... | collective-permute-start | bytes 368648 | tf_op jit(solution)/shard_map/ppermute | solution.py:71
  66.9 9.4 %collective-permute-start.28 = (bf16[160,384]{1,0:T(8,128)(2,1)S(1)}, bf16[160,384]{1,0:T(8,128)(2,1)S(1)}, u32[]{:S(2)}, u32[]{:S(2)}) collective-permute-start(bf16[160,384]{1,0:T(8,128)(2,1)S(1)} %scores.1.p0), channel_id=1, source_target_pairs={{0,64},{32,96},{64,0},{96,32},{1,65},{33,97},{65,1},{97,33},{2,66}... | collective-permute-start | bytes 368648 | tf_op jit(solution)/shard_map/ppermute | solution.py:71
  70.4 5.9 %collective-permute-start.29 = (bf16[160,384]{1,0:T(8,128)(2,1)S(1)}, bf16[160,384]{1,0:T(8,128)(2,1)S(1)}, u32[]{:S(2)}, u32[]{:S(2)}) collective-permute-start(bf16[160,384]{1,0:T(8,128)(2,1)S(1)} %scores.1.p0), channel_id=1, source_target_pairs={{0,96},{32,0},{64,32},{96,64},{1,97},{33,1},{65,33},{97,65},{2,98}... | collective-permute-start | bytes 368648 | tf_op jit(solution)/shard_map/ppermute | solution.py:71

commit v6 on v5

--- a/solution.py
+++ b/solution.py
@@ -148,7 +148,7 @@
     col = lax.broadcasted_iota(jnp.int32, (ROWS, ROWS), 1)
     place = pl.ds(pl.multiple_of(me * ROWS, ROWS), ROWS)
     adj[:, place] = (adj[:, place].astype(f32) + (row == col).astype(f32)).astype(bf16)
-    degree[...] = jnp.broadcast_to(degree[:, SHARE : SHARE + 1] + 1.0, degree.shape)
+    degree[...] = jnp.broadcast_to(1.0 / (degree[:, SHARE : SHARE + 1] + 1.0), degree.shape)
 
 
 ADJACENCY = [
@@ -247,7 +247,7 @@
     pieces, outs, mean = refs[:-5], refs[-5:-1], refs[-1]
     feat = here()[1]
     total = add_blocks(kinds, adj, before[...], pieces)
-    mean[...] = total / degree[:, :1]
+    mean[...] = total * degree[:, :1]
     for s in range(NF):
         q = lax.rem(feat + s, NF)
         outs[s][...] = mean[pl.ds(pl.multiple_of(q * SHARE, SHARE), SHARE), :].astype(bf16)
@@ -292,19 +292,27 @@
     z_out[SHARE:, :] = packed.astype(bf16)
 
 
-def scores_kernel(adj2, degree, *refs):
-    pieces, out, z_all = refs[:-2], refs[-2], refs[-1]
+def unpack(kinds, pieces, z_all):
     me, _ = here()
-    for p, piece in enumerate(pieces):
+    for (shift, p), piece in zip(kinds, pieces, strict=True):
         for b in range(NF):
-            src = source(me, SHIFTS[b], SHIFTS[p // 2], lax.rem(me + p, 2))
+            src = source(me, SHIFTS[b], shift, lax.rem(me + p, 2))
             src = pl.multiple_of(src * TILE, TILE)
             z_all[pl.ds(src, TILE), :TILE] = piece[b]
             tail = piece[b, SHARE:, :].astype(f32)
             tail = jnp.concatenate([tail[:, 0:32], tail[:, 32:64], tail[:, 64:96], jnp.zeros((32, 32), f32)], axis=0)
             tail = jnp.concatenate([tail, jnp.zeros((TILE, 96), f32)], axis=1)
             z_all[pl.ds(src, TILE), TILE:] = tail.astype(bf16)
-    part = jnp.dot(adj2[...], z_all[...], preferred_element_type=f32) / degree[:, :1]
+
+
+def unpack_kernel(kinds, *refs):
+    unpack(kinds, refs[: len(kinds)], refs[-1])
+
+
+def scores_kernel(kinds, adj2, inverse, before, *refs):
+    out, z_all = refs[-2], refs[-1]
+    unpack(kinds, refs[: len(kinds)], z_all)
+    part = jnp.dot(adj2[...], z_all[...], preferred_element_type=f32) * inverse[:, :1]
     out[...] = part.T[0:160].astype(bf16)
 
 
@@ -374,13 +382,22 @@
     z_four = jnp.stack([ring[s] for s in SHIFTS])
     z_rows = {0: z_four} | {t: second_axis(z_four, t) for t in (2, 1, 3)}
     z_rows = [z_rows[t] for t in SHIFTS]
-    z_pieces = [z for row in z_rows for z in (row, swap(row))]
-    part = pl.pallas_call(
-        scores_kernel, out_shape=jax.ShapeDtypeStruct((160, ROWS), bf16),
-        in_specs=[VM] * 10, out_specs=VM,
-        scratch_shapes=[pltpu.VMEM((NV * TILE, 256), bf16)],
+    z_rows = dict(zip(SHIFTS, z_rows, strict=True))
+    z_other = {t: swap(z_rows[t]) for t in SHIFTS}
+    z_shape = pltpu.VMEM((NV * TILE, 256), bf16)
+    early = ((0, 0), (0, 1), (2, 0), (1, 0), (3, 0))
+    late = ((2, 1), (1, 1), (3, 1))
+    z_all = pl.pallas_call(
+        functools.partial(unpack_kernel, early), out_shape=z_shape,
+        in_specs=[VM] * len(early), out_specs=VM,
+        compiler_params=params(), cost_estimate=cost(1e5, 2e6), name="unpack",
+    )(*((z_rows, z_other)[p][t] for t, p in early))
+    part, _ = pl.pallas_call(
+        functools.partial(scores_kernel, late),
+        out_shape=[jax.ShapeDtypeStruct((160, ROWS), bf16), z_shape],
+        in_specs=[VM] * (3 + len(late)), out_specs=[VM] * 2, input_output_aliases={2: 1},
         compiler_params=params(), cost_estimate=cost(2 * 384 * 4096 * 256, 5e6), name="scores",
-    )(adj2, degree, *z_pieces)
+    )(adj2, degree, z_all, *((z_rows, z_other)[p][t] for t, p in late))
     parts = {0: part} | {s: along_feat(part, s) for s in (2, 1, 3)}
     parts = [parts[s] for s in range(NF)]
     return pl.pallas_call(

time: 77.3 us -> 77 us (level)
  no operation moved by 1% of the time
where the time goes in v6:
time: 77 us; the launch traced here: 76.9 us
  starting transfers between devices  42.8 us (56%)
  Pallas kernels  17.2 us (22%)
  waiting for transfers between devices  16.6 us (22%)
    ppermute x10, starting transfers between devices, swap(): return lax.ppermute(value, 'vert', positions(lambda x, z, c: (x, z, 1 - c)))  13.3 us
    ppermute x6, starting transfers between devices, first_axis(): lax.ppermute(value, 'vert', positions(lambda x, z, c: (x + shift * (1 - c...  10.6 us
    ppermute x7, starting transfers between devices, along_feat(): lax.ppermute(value, 'feat', [(i, (i + shift) % NF) for i in range(NF)])  8.89 us
    ppermute x7, waiting for transfers between devices, along_feat(): lax.ppermute(value, 'feat', [(i, (i + shift) % NF) for i in range(NF)])  8.07 us
    ppermute x6, starting transfers between devices, second_axis(): lax.ppermute(value, 'vert', positions(lambda x, z, c: (x + shift * c, z +...  7.27 us
    pallas_call x1, Pallas kernels, second_half(): pl.pallas_call(functools.partial(adjacency_kernel, 1), in_specs=[HB] * 2...  5.54 us
    ppermute x1, waiting for transfers between devices, both_sides(): return lax.ppermute(value, ('feat', 'vert'), pairs)  4.26 us
    pallas_call x1, Pallas kernels, first_half(): pl.pallas_call(functools.partial(adjacency_kernel, 0), in_specs=[HB] * 5,...  4.18 us
  transfers between devices with their start and end apart: 30, of which 11 were waited for; matrix products, arithmetic and copies ran while one was open for 0% of the time, Pallas kernels for 17%

profile of v6, /device:TPU:1, one launch (start us, length us, event | category | flops | bytes accessed | tf_op | source)
XLA Modules:
  0.0 76.9 jit_solution(14459384143368376683)
XLA Ops:
  0.0 4.4 %collective-permute-start = (bf16[192,384]{1,0:T(8,128)(2,1)}, bf16[192,384]{1,0:T(8,128)(2,1)S(1)}, u32[]{:S(2)}, u32[]{:S(2)}) collective-permute-start(bf16[192,384]{1,0:T(8,128)(2,1)} %bitcast.9), channel_id=1, source_target_pairs={{0,16},{1,5},{2,18},{3,7},{4,20},{5,1},{6,22},{7,3},{8,24},{9,13},... | collective-permute-start | bytes 442376 | tf_op jit(solution)/shard_map/ppermute | solution.py:59
  4.4 0.7 collective-permute-start.1
  5.2 1.9 %collective-permute-start.2 = (bf16[192,384]{1,0:T(8,128)(2,1)}, bf16[192,384]{1,0:T(8,128)(2,1)S(1)}, u32[]{:S(2)}, u32[]{:S(2)}) collective-permute-start(bf16[192,384]{1,0:T(8,128)(2,1)} %bitcast.11), channel_id=1, source_target_pairs={{0,24},{1,7},{2,26},{3,1},{4,28},{5,3},{6,30},{7,5},{8,0},{9,15},{... | collective-permute-start | bytes 442376 | tf_op jit(solution)/shard_map/ppermute | solution.py:59
  7.1 4.2 %adjacency_first.1 = (bf16[384,12288]{1,0:T(8,128)(2,1)S(1)}, bf16[384,4096]{1,0:T(8,128)(2,1)S(1)}, f32[384,128]{1,0:T(8,128)S(1)}, bf16[2,256,512]{2,1,0:T(8,128)(2,1)S(1)}, bf16[256,512]{1,0:T(8,128)(2,1)S(1)}) custom-call(s32[3,96]{1,0:T(4,128)} %mask.3, s32[384,12288]{1,0:T(8,128)} %counts.3, bf16[192,1024]{1,0:T(8,128)(2,1)} %refs_0_.1, ...), custom_call_target="tpu_custom_call" | custom-call | flops 1200000000 | bytes 16000000 | tf_op jit(solution)/shard_map/adjacency_first/pallas_call | solution.py:168
  11.3 0.0 collective-permute-done.b
  11.3 0.0 collective-permute-done.2.d
  11.3 0.1 stack.21.refs_0_
  11.4 0.7 collective-permute-start.3
  12.1 2.0 %collective-permute-start.7 = (bf16[4,192,384]{2,1,0:T(8,128)(2,1)S(1)}, bf16[4,192,384]{2,1,0:T(8,128)(2,1)S(1)}, u32[]{:S(2)}, u32[]{:S(2)}) collective-permute-start(bf16[4,192,384]{2,1,0:T(8,128)(2,1)S(1)} %stack.21.refs_0_), channel_id=1, source_target_pairs={{0,6},{1,25},{2,0},{3,27},{4,2},{5,29},{6,4},{7,31},{8,14},{9,1},{... | collective-permute-start | bytes 1769480 | tf_op jit(solution)/shard_map/ppermute | solution.py:63
  14.2 0.0 collective-permute-start.6
  14.2 2.7 %collective-permute-start.4 = (bf16[2,256,512]{2,1,0:T(8,128)(2,1)S(1)}, bf16[2,256,512]{2,1,0:T(8,128)(2,1)S(1)}, u32[]{:S(2)}, u32[]{:S(2)}) collective-permute-start(bf16[2,256,512]{2,1,0:T(8,128)(2,1)S(1)} %get-tuple-element.34.own), channel_id=1, source_target_pairs={{0,32},{32,64},{64,96},{96,0},{1,97},{33,1},{65,33},{97,65},{2,34}... | collective-permute-start | bytes 1572872 | tf_op jit(solution)/shard_map/ppermute | solution.py:76
  16.9 1.6 %collective-permute-start.10 = (bf16[4,192,384]{2,1,0:T(8,128)(2,1)S(1)}, bf16[4,192,384]{2,1,0:T(8,128)(2,1)S(1)}, u32[]{:S(2)}, u32[]{:S(2)}) collective-permute-start(bf16[4,192,384]{2,1,0:T(8,128)(2,1)S(1)} %stack.21.refs_0_), channel_id=1, source_target_pairs={{0,4},{1,17},{2,6},{3,19},{4,0},{5,21},{6,2},{7,23},{8,12},{9,25},... | collective-permute-start | bytes 1769480 | tf_op jit(solution)/shard_map/ppermute | solution.py:63
  18.5 0.3 collective-permute-start.5
  18.9 5.5 %adjacency_second.1 = (bf16[384,12288]{1,0:T(8,128)(2,1)S(1)}, bf16[384,4096]{1,0:T(8,128)(2,1)S(1)}, f32[384,128]{1,0:T(8,128)S(1)}) custom-call(s32[3,96]{1,0:T(4,128)} %mask.3, s32[384,12288]{1,0:T(8,128)} %counts.3, bf16[384,12288]{1,0:T(8,128)(2,1)S(1)} %get-tuple-element.28.refs_0_, ...), custom_call_target="tpu_custom_call", output_to_operand_aliasing={{0}: (2, {}), {1}: (3, {}), {2}: (4, {})} | custom-call | flops 1200000000 | bytes 16000000 | tf_op jit(solution)/shard_map/adjacency_second/pallas_call | solution.py:189
  24.4 4.3 %collective-permute-done.4.refs_2_.side = bf16[2,256,512]{2,1,0:T(8,128)(2,1)S(1)} collective-permute-done((bf16[2,256,512]{2,1,0:T(8,128)(2,1)S(1)}, bf16[2,256,512]{2,1,0:T(8,128)(2,1)S(1)}, u32[]{:S(2)}, u32[]{:S(2)}) %collective-permute-start.4) | collective-permute-done | bytes 524320 | tf_op jit(solution)/shard_map/ppermute | solution.py:76
  28.7 1.0 %product_first.1.before = f32[384,192]{1,0:T(8,128)S(1)} custom-call(bf16[384,12288]{1,0:T(8,128)(2,1)S(1)} %get-tuple-element.35.adj, bf16[4,192,384]{2,1,0:T(8,128)(2,1)S(1)} %stack.21.refs_0_, bf16[4,192,384]{2,1,0:T(8,128)(2,1)S(1)} %collective-permute-done.3.refs_3_.refs_1_, bf16[2,256,512]{2,1,0:T(8,128)(2,1)S(1)} %collective-permute-done.4.refs_2_.side), custom_call_target="tpu_custom_call" | custom-call | flops 603979776 | bytes 3600000 | tf_op jit(solution)/shard_map/product_first/pallas_call | solution.py:348
  29.7 0.0 collective-permute-done.7.refs_1_
  29.7 1.1 %collective-permute-done.6.refs_0_ = bf16[4,192,384]{2,1,0:T(8,128)(2,1)S(1)} collective-permute-done((bf16[4,192,384]{2,1,0:T(8,128)(2,1)S(1)}, bf16[4,192,384]{2,1,0:T(8,128)(2,1)S(1)}, u32[]{:S(2)}, u32[]{:S(2)}) %collective-permute-start.6) | collective-permute-done | bytes 589856 | tf_op jit(solution)/shard_map/ppermute | solution.py:63
  30.7 2.9 %collective-permute-start.9 = (bf16[4,192,384]{2,1,0:T(8,128)(2,1)S(1)}, bf16[4,192,384]{2,1,0:T(8,128)(2,1)S(1)}, u32[]{:S(2)}, u32[]{:S(2)}) collective-permute-start(bf16[4,192,384]{2,1,0:T(8,128)(2,1)S(1)} %collective-permute-done.7.refs_1_), channel_id=1, source_target_pairs={{0,1},{1,0},{2,3},{3,2},{4,5},{5,4},{6,7},{7,6},{8,9},{9,8},{10,11... | collective-permute-start | bytes 1769480 | tf_op jit(solution)/shard_map/ppermute | solution.py:67
  33.7 0.0 collective-permute-start.8
  33.7 0.0 collective-permute-done.10.refs_2_
  33.7 0.0 collective-permute-done.5.refs_2_.near
  33.7 1.0 %product_next.1.before = f32[384,192]{1,0:T(8,128)S(1)} custom-call(bf16[384,12288]{1,0:T(8,128)(2,1)S(1)} %get-tuple-element.35.adj, f32[384,192]{1,0:T(8,128)S(1)} %product_first.1.before, bf16[4,192,384]{2,1,0:T(8,128)(2,1)S(1)} %collective-permute-done.6.refs_0_, bf16[4,192,384]{2,1,0:T(8,128)(2,1)S(1)} %collective-permute-done.7.refs_1_, ...), custom_call_target="tpu_custom_call" | custom-call | flops 603979776 | bytes 3600000 | tf_op jit(solution)/shard_map/product_next/pallas_call | solution.py:348
  34.7 0.6 collective-permute-start.11
  35.3 0.0 collective-permute-done.9.refs_1_
  35.3 0.8 %collective-permute-done.8.refs_0_ = bf16[4,192,384]{2,1,0:T(8,128)(2,1)S(1)} collective-permute-done((bf16[4,192,384]{2,1,0:T(8,128)(2,1)S(1)}, bf16[4,192,384]{2,1,0:T(8,128)(2,1)S(1)}, u32[]{:S(2)}, u32[]{:S(2)}) %collective-permute-start.8) | collective-permute-done | bytes 589856 | tf_op jit(solution)/shard_map/ppermute | solution.py:67
  36.1 1.4 %product_more.1.before = f32[384,192]{1,0:T(8,128)S(1)} custom-call(bf16[384,12288]{1,0:T(8,128)(2,1)S(1)} %get-tuple-element.35.adj, f32[384,192]{1,0:T(8,128)S(1)} %product_next.1.before, bf16[4,192,384]{2,1,0:T(8,128)(2,1)S(1)} %collective-permute-done.8.refs_0_, bf16[4,192,384]{2,1,0:T(8,128)(2,1)S(1)} %collective-permute-done.9.refs_1_, ...), custom_call_target="tpu_custom_call" | custom-call | flops 905969664 | bytes 5400000 | tf_op jit(solution)/shard_map/product_more/pallas_call | solution.py:348
  37.6 0.6 product_last.1
  38.2 0.5 collective-permute-start.15
  38.7 0.1 collective-permute-start.16
  38.8 1.3 %collective-permute-start.12 = (bf16[96,192]{1,0:T(8,128)(2,1)S(1)}, bf16[96,192]{1,0:T(8,128)(2,1)S(1)}, u32[]{:S(2)}, u32[]{:S(2)}) collective-permute-start(bf16[96,192]{1,0:T(8,128)(2,1)S(1)} %get-tuple-element.45), channel_id=1, source_target_pairs={{0,32},{32,64},{64,96},{96,0},{1,33},{33,65},{65,97},{97,1},{2,34}... | collective-permute-start | bytes 110600 | tf_op jit(solution)/shard_map/ppermute | solution.py:71
  40.1 2.6 %collective-permute-start.13 = (bf16[96,192]{1,0:T(8,128)(2,1)S(1)}, bf16[96,192]{1,0:T(8,128)(2,1)S(1)}, u32[]{:S(2)}, u32[]{:S(2)}) collective-permute-start(bf16[96,192]{1,0:T(8,128)(2,1)S(1)} %get-tuple-element.46), channel_id=1, source_target_pairs={{0,64},{32,96},{64,0},{96,32},{1,65},{33,97},{65,1},{97,33},{2,66}... | collective-permute-start | bytes 110600 | tf_op jit(solution)/shard_map/ppermute | solution.py:71
  42.7 1.1 %collective-permute-start.14 = (bf16[96,192]{1,0:T(8,128)(2,1)S(1)}, bf16[96,192]{1,0:T(8,128)(2,1)S(1)}, u32[]{:S(2)}, u32[]{:S(2)}) collective-permute-start(bf16[96,192]{1,0:T(8,128)(2,1)S(1)} %get-tuple-element.47), channel_id=1, source_target_pairs={{0,96},{32,0},{64,32},{96,64},{1,97},{33,1},{65,33},{97,65},{2,98}... | collective-permute-start | bytes 110600 | tf_op jit(solution)/shard_map/ppermute | solution.py:71
  43.8 0.0 collective-permute-done.12.g1
  43.8 1.2 %collective-permute-done.13.g2 = bf16[96,192]{1,0:T(8,128)(2,1)S(1)} collective-permute-done((bf16[96,192]{1,0:T(8,128)(2,1)S(1)}, bf16[96,192]{1,0:T(8,128)(2,1)S(1)}, u32[]{:S(2)}, u32[]{:S(2)}) %collective-permute-start.13) | collective-permute-done | bytes 36896 | tf_op jit(solution)/shard_map/ppermute | solution.py:71
  45.0 1.0 %collective-permute-done.14.g3 = bf16[96,192]{1,0:T(8,128)(2,1)S(1)} collective-permute-done((bf16[96,192]{1,0:T(8,128)(2,1)S(1)}, bf16[96,192]{1,0:T(8,128)(2,1)S(1)}, u32[]{:S(2)}, u32[]{:S(2)}) %collective-permute-start.14) | collective-permute-done | bytes 36896 | tf_op jit(solution)/shard_map/ppermute | solution.py:71
  46.0 0.0 collective-permute-done.16.far
  46.0 0.0 collective-permute-done.15.other_side
  46.0 1.0 %hidden.1 = bf16[128,128]{1,0:T(8,128)(2,1)S(1)} custom-call(bf16[96,192]{1,0:T(8,128)(2,1)S(1)} %get-tuple-element.44.g0, bf16[96,192]{1,0:T(8,128)(2,1)S(1)} %collective-permute-done.12.g1, bf16[96,192]{1,0:T(8,128)(2,1)S(1)} %collective-permute-done.13.g2, bf16[96,192]{1,0:T(8,128)(2,1)S(1)} %collective-permute-done.14.g3, ...), custom_call_target="tpu_custom_call" | custom-call | flops 150994944 | bytes 2000000 | tf_op jit(solution)/shard_map/hidden/pallas_call | solution.py:374
  47.0 0.8 %collective-permute-start.17 = (bf16[128,128]{1,0:T(8,128)(2,1)S(1)}, bf16[128,128]{1,0:T(8,128)(2,1)S(1)}, u32[]{:S(2)}, u32[]{:S(2)}) collective-permute-start(bf16[128,128]{1,0:T(8,128)(2,1)S(1)} %hidden.1), channel_id=1, source_target_pairs={{0,16},{1,5},{2,18},{3,7},{4,20},{5,1},{6,22},{7,3},{8,24},{9,13},... | collective-permute-start | bytes 98312 | tf_op jit(solution)/shard_map/ppermute | solution.py:59
  47.8 0.9 %collective-permute-start.18 = (bf16[128,128]{1,0:T(8,128)(2,1)S(1)}, bf16[128,128]{1,0:T(8,128)(2,1)S(1)}, u32[]{:S(2)}, u32[]{:S(2)}) collective-permute-start(bf16[128,128]{1,0:T(8,128)(2,1)S(1)} %hidden.1), channel_id=1, source_target_pairs={{0,8},{1,3},{2,10},{3,5},{4,12},{5,7},{6,14},{7,1},{8,16},{9,11},{... | collective-permute-start | bytes 98312 | tf_op jit(solution)/shard_map/ppermute | solution.py:59
  48.7 1.8 %collective-permute-start.19 = (bf16[128,128]{1,0:T(8,128)(2,1)S(1)}, bf16[128,128]{1,0:T(8,128)(2,1)S(1)}, u32[]{:S(2)}, u32[]{:S(2)}) collective-permute-start(bf16[128,128]{1,0:T(8,128)(2,1)S(1)} %hidden.1), channel_id=1, source_target_pairs={{0,24},{1,7},{2,26},{3,1},{4,28},{5,3},{6,30},{7,5},{8,0},{9,15},{... | collective-permute-start | bytes 98312 | tf_op jit(solution)/shard_map/ppermute | solution.py:59
  50.5 0.9 %collective-permute-done.17 = bf16[128,128]{1,0:T(8,128)(2,1)S(1)} collective-permute-done((bf16[128,128]{1,0:T(8,128)(2,1)S(1)}, bf16[128,128]{1,0:T(8,128)(2,1)S(1)}, u32[]{:S(2)}, u32[]{:S(2)}) %collective-permute-start.17) | collective-permute-done | bytes 32800 | tf_op jit(solution)/shard_map/ppermute | solution.py:59
  51.4 0.4 collective-permute-done.18
  51.8 1.0 %collective-permute-start.21 = (bf16[4,128,128]{2,1,0:T(8,128)(2,1)S(1)}, bf16[4,128,128]{2,1,0:T(8,128)(2,1)S(1)}, u32[]{:S(2)}, u32[]{:S(2)}) collective-permute-start(bf16[4,128,128]{2,1,0:T(8,128)(2,1)S(1)} %pad_maximum_fusion.refs_0_), channel_id=1, source_target_pairs={{0,4},{1,17},{2,6},{3,19},{4,0},{5,21},{6,2},{7,23},{8,12},{9,25},... | collective-permute-start | bytes 393224 | tf_op jit(solution)/shard_map/ppermute | solution.py:63
  52.8 2.1 %collective-permute-start.22 = (bf16[4,128,128]{2,1,0:T(8,128)(2,1)S(1)}, bf16[4,128,128]{2,1,0:T(8,128)(2,1)S(1)}, u32[]{:S(2)}, u32[]{:S(2)}) collective-permute-start(bf16[4,128,128]{2,1,0:T(8,128)(2,1)S(1)} %pad_maximum_fusion.refs_0_), channel_id=1, source_target_pairs={{0,2},{1,9},{2,4},{3,11},{4,6},{5,13},{6,0},{7,15},{8,10},{9,17},{... | collective-permute-start | bytes 393224 | tf_op jit(solution)/shard_map/ppermute | solution.py:63
  54.9 0.6 collective-permute-start.23
  55.5 5.0 %collective-permute-start.20 = (bf16[4,128,128]{2,1,0:T(8,128)(2,1)S(1)}, bf16[4,128,128]{2,1,0:T(8,128)(2,1)S(1)}, u32[]{:S(2)}, u32[]{:S(2)}) collective-permute-start(bf16[4,128,128]{2,1,0:T(8,128)(2,1)S(1)} %pad_maximum_fusion.refs_0_), channel_id=1, source_target_pairs={{0,1},{1,0},{2,3},{3,2},{4,5},{5,4},{6,7},{7,6},{8,9},{9,8},{10,11... | collective-permute-start | bytes 393224 | tf_op jit(solution)/shard_map/ppermute | solution.py:67
  60.5 0.0 collective-permute-done.21.refs_2_
  60.5 2.1 %collective-permute-start.24 = (bf16[4,128,128]{2,1,0:T(8,128)(2,1)S(1)}, bf16[4,128,128]{2,1,0:T(8,128)(2,1)S(1)}, u32[]{:S(2)}, u32[]{:S(2)}) collective-permute-start(bf16[4,128,128]{2,1,0:T(8,128)(2,1)S(1)} %collective-permute-done.21.refs_2_), channel_id=1, source_target_pairs={{0,1},{1,0},{2,3},{3,2},{4,5},{5,4},{6,7},{7,6},{8,9},{9,8},{10,11... | collective-permute-start | bytes 393224 | tf_op jit(solution)/shard_map/ppermute | solution.py:67
  62.6 1.3 %collective-permute-start.25 = (bf16[4,128,128]{2,1,0:T(8,128)(2,1)S(1)}, bf16[4,128,128]{2,1,0:T(8,128)(2,1)S(1)}, u32[]{:S(2)}, u32[]{:S(2)}) collective-permute-start(bf16[4,128,128]{2,1,0:T(8,128)(2,1)S(1)} %collective-permute-done.22.refs_3_), channel_id=1, source_target_pairs={{0,1},{1,0},{2,3},{3,2},{4,5},{5,4},{6,7},{7,6},{8,9},{9,8},{10,11... | collective-permute-start | bytes 393224 | tf_op jit(solution)/shard_map/ppermute | solution.py:67
  64.0 0.0 collective-permute-done.23.refs_4_
  64.0 0.0 collective-permute-start.26
  64.0 0.0 collective-permute-done.20.refs_1_
  64.0 0.3 unpack.1.before
  64.3 0.0 copy-start.1
  64.3 0.7 collective-permute-done.25.refs_1_
  64.9 0.4 collective-permute-done.26.refs_2_
  65.3 1.2 %scores.1 = (bf16[160,384]{1,0:T(8,128)(2,1)S(1)}, bf16[4096,256]{1,0:T(8,128)(2,1)S(1)}) custom-call(bf16[384,4096]{1,0:T(8,128)(2,1)S(1)} %get-tuple-element.32.adj2, f32[384,128]{1,0:T(8,128)S(1)} %get-tuple-element.33.degree.inverse, bf16[4096,256]{1,0:T(8,128)(2,1)S(1)} %unpack.1.before, ...), custom_call_target="tpu_custom_call", output_to_operand_aliasing={{1}: (2, {})} | custom-call | flops 805306368 | bytes 5000000 | tf_op jit(solution)/shard_map/scores/pallas_call | solution.py:395
  66.5 0.1 collective-permute-start.27
  66.6 3.5 %collective-permute-start.28 = (bf16[160,384]{1,0:T(8,128)(2,1)S(1)}, bf16[160,384]{1,0:T(8,128)(2,1)S(1)}, u32[]{:S(2)}, u32[]{:S(2)}) collective-permute-start(bf16[160,384]{1,0:T(8,128)(2,1)S(1)} %get-tuple-element.50.p0), channel_id=1, source_target_pairs={{0,64},{32,96},{64,0},{96,32},{1,65},{33,97},{65,1},{97,33},{2,66}... | collective-permute-start | bytes 368648 | tf_op jit(solution)/shard_map/ppermute | solution.py:71
  70.1 2.5 %collective-permute-done.27.p1 = bf16[160,384]{1,0:T(8,128)(2,1)S(1)} collective-permute-done((bf16[160,384]{1,0:T(8,128)(2,1)S(1)}, bf16[160,384]{1,0:T(8,128)(2,1)S(1)}, u32[]{:S(2)}, u32[]{:S(2)}) %collective-permute-start.27) | collective-permute-done | bytes 122912 | tf_op jit(solution)/shard_map/ppermute | solution.py:71
  72.6 3.4 %collective-permute-done.28.p2 = bf16[160,384]{1,0:T(8,128)(2,1)S(1)} collective-permute-done((bf16[160,384]{1,0:T(8,128)(2,1)S(1)}, bf16[160,384]{1,0:T(8,128)(2,1)S(1)}, u32[]{:S(2)}, u32[]{:S(2)}) %collective-permute-start.28) | collective-permute-done | bytes 122912 | tf_op jit(solution)/shard_map/ppermute | solution.py:71
  76.0 0.9 %sum.1 = f32[153,384]{1,0:T(8,128)} custom-call(bf16[160,384]{1,0:T(8,128)(2,1)S(1)} %get-tuple-element.50.p0, bf16[160,384]{1,0:T(8,128)(2,1)S(1)} %collective-permute-done.27.p1, bf16[160,384]{1,0:T(8,128)(2,1)S(1)} %collective-permute-done.28.p2, bf16[160,384]{1,0:T(8,128)(2,1)S(1)} %collective-permute-done.29.p3, f32[1,256]{1,0:T(1,128)S(1)} %bitcast.14), custom_call_target="tpu_custom_call" | custom-call | flops 300000 | bytes 800000 | tf_op jit(solution)/shard_map/sum/pallas_call | solution.py:403
  (13 shorter events, 0.0 us)
Async XLA Ops:
  0.0 11.3 %collective-permute-start = (bf16[192,384]{1,0:T(8,128)(2,1)}, bf16[192,384]{1,0:T(8,128)(2,1)S(1)}, u32[]{:S(2)}, u32[]{:S(2)}) collective-permute-start(bf16[192,384]{1,0:T(8,128)(2,1)} %bitcast.9), channel_id=1, source_target_pairs={{0,16},{1,5},{2,18},{3,7},{4,20},{5,1},{6,22},{7,3},{8,24},{9,13},... | collective-permute-start | bytes 442376 | tf_op jit(solution)/shard_map/ppermute | solution.py:59
  4.4 6.9 %collective-permute-start.1 = (bf16[192,384]{1,0:T(8,128)(2,1)}, bf16[192,384]{1,0:T(8,128)(2,1)S(1)}, u32[]{:S(2)}, u32[]{:S(2)}) collective-permute-start(bf16[192,384]{1,0:T(8,128)(2,1)} %bitcast.10), channel_id=1, source_target_pairs={{0,8},{1,3},{2,10},{3,5},{4,12},{5,7},{6,14},{7,1},{8,16},{9,11},{... | collective-permute-start | bytes 442376 | tf_op jit(solution)/shard_map/ppermute | solution.py:59
  5.2 6.2 %collective-permute-start.2 = (bf16[192,384]{1,0:T(8,128)(2,1)}, bf16[192,384]{1,0:T(8,128)(2,1)S(1)}, u32[]{:S(2)}, u32[]{:S(2)}) collective-permute-start(bf16[192,384]{1,0:T(8,128)(2,1)} %bitcast.11), channel_id=1, source_target_pairs={{0,24},{1,7},{2,26},{3,1},{4,28},{5,3},{6,30},{7,5},{8,0},{9,15},{... | collective-permute-start | bytes 442376 | tf_op jit(solution)/shard_map/ppermute | solution.py:59
  7.1 4.2 %copy-start = (bf16[384,192]{0,1:T(8,128)(2,1)S(1)}, bf16[384,192]{0,1:T(8,128)(2,1)}, u32[]{:S(2)}) copy-start(bf16[384,192]{0,1:T(8,128)(2,1)} %param.7) | copy-start | bytes 442372
  11.4 7.1 %collective-permute-start.3 = (bf16[4,192,384]{2,1,0:T(8,128)(2,1)S(1)}, bf16[4,192,384]{2,1,0:T(8,128)(2,1)S(1)}, u32[]{:S(2)}, u32[]{:S(2)}) collective-permute-start(bf16[4,192,384]{2,1,0:T(8,128)(2,1)S(1)} %stack.21.refs_0_), channel_id=1, source_target_pairs={{0,1},{1,0},{2,3},{3,2},{4,5},{5,4},{6,7},{7,6},{8,9},{9,8},{10,11... | collective-permute-start | bytes 1769480 | tf_op jit(solution)/shard_map/ppermute | solution.py:67
  12.1 17.5 %collective-permute-start.7 = (bf16[4,192,384]{2,1,0:T(8,128)(2,1)S(1)}, bf16[4,192,384]{2,1,0:T(8,128)(2,1)S(1)}, u32[]{:S(2)}, u32[]{:S(2)}) collective-permute-start(bf16[4,192,384]{2,1,0:T(8,128)(2,1)S(1)} %stack.21.refs_0_), channel_id=1, source_target_pairs={{0,6},{1,25},{2,0},{3,27},{4,2},{5,29},{6,4},{7,31},{8,14},{9,1},{... | collective-permute-start | bytes 1769480 | tf_op jit(solution)/shard_map/ppermute | solution.py:63
  14.2 16.6 %collective-permute-start.6 = (bf16[4,192,384]{2,1,0:T(8,128)(2,1)S(1)}, bf16[4,192,384]{2,1,0:T(8,128)(2,1)S(1)}, u32[]{:S(2)}, u32[]{:S(2)}) collective-permute-start(bf16[4,192,384]{2,1,0:T(8,128)(2,1)S(1)} %stack.21.refs_0_), channel_id=1, source_target_pairs={{0,2},{1,9},{2,4},{3,11},{4,6},{5,13},{6,0},{7,15},{8,10},{9,17},{... | collective-permute-start | bytes 1769480 | tf_op jit(solution)/shard_map/ppermute | solution.py:63
  14.2 14.5 %collective-permute-start.4 = (bf16[2,256,512]{2,1,0:T(8,128)(2,1)S(1)}, bf16[2,256,512]{2,1,0:T(8,128)(2,1)S(1)}, u32[]{:S(2)}, u32[]{:S(2)}) collective-permute-start(bf16[2,256,512]{2,1,0:T(8,128)(2,1)S(1)} %get-tuple-element.34.own), channel_id=1, source_target_pairs={{0,32},{32,64},{64,96},{96,0},{1,97},{33,1},{65,33},{97,65},{2,34}... | collective-permute-start | bytes 1572872 | tf_op jit(solution)/shard_map/ppermute | solution.py:76
  16.9 16.8 %collective-permute-start.10 = (bf16[4,192,384]{2,1,0:T(8,128)(2,1)S(1)}, bf16[4,192,384]{2,1,0:T(8,128)(2,1)S(1)}, u32[]{:S(2)}, u32[]{:S(2)}) collective-permute-start(bf16[4,192,384]{2,1,0:T(8,128)(2,1)S(1)} %stack.21.refs_0_), channel_id=1, source_target_pairs={{0,4},{1,17},{2,6},{3,19},{4,0},{5,21},{6,2},{7,23},{8,12},{9,25},... | collective-permute-start | bytes 1769480 | tf_op jit(solution)/shard_map/ppermute | solution.py:63
  18.5 15.2 %collective-permute-start.5 = (bf16[256,512]{1,0:T(8,128)(2,1)S(1)}, bf16[256,512]{1,0:T(8,128)(2,1)S(1)}, u32[]{:S(2)}, u32[]{:S(2)}) collective-permute-start(bf16[256,512]{1,0:T(8,128)(2,1)S(1)} %get-tuple-element.31.after), channel_id=1, source_target_pairs={{0,64},{32,96},{64,0},{96,32},{1,65},{33,97},{65,1},{97,33},{2,66}... | collective-permute-start | bytes 786440 | tf_op jit(solution)/shard_map/ppermute | solution.py:71
  30.7 4.6 %collective-permute-start.9 = (bf16[4,192,384]{2,1,0:T(8,128)(2,1)S(1)}, bf16[4,192,384]{2,1,0:T(8,128)(2,1)S(1)}, u32[]{:S(2)}, u32[]{:S(2)}) collective-permute-start(bf16[4,192,384]{2,1,0:T(8,128)(2,1)S(1)} %collective-permute-done.7.refs_1_), channel_id=1, source_target_pairs={{0,1},{1,0},{2,3},{3,2},{4,5},{5,4},{6,7},{7,6},{8,9},{9,8},{10,11... | collective-permute-start | bytes 1769480 | tf_op jit(solution)/shard_map/ppermute | solution.py:67
  33.7 2.5 %collective-permute-start.8 = (bf16[4,192,384]{2,1,0:T(8,128)(2,1)S(1)}, bf16[4,192,384]{2,1,0:T(8,128)(2,1)S(1)}, u32[]{:S(2)}, u32[]{:S(2)}) collective-permute-start(bf16[4,192,384]{2,1,0:T(8,128)(2,1)S(1)} %collective-permute-done.6.refs_0_), channel_id=1, source_target_pairs={{0,1},{1,0},{2,3},{3,2},{4,5},{5,4},{6,7},{7,6},{8,9},{9,8},{10,11... | collective-permute-start | bytes 1769480 | tf_op jit(solution)/shard_map/ppermute | solution.py:67
  34.7 2.9 %collective-permute-start.11 = (bf16[4,192,384]{2,1,0:T(8,128)(2,1)S(1)}, bf16[4,192,384]{2,1,0:T(8,128)(2,1)S(1)}, u32[]{:S(2)}, u32[]{:S(2)}) collective-permute-start(bf16[4,192,384]{2,1,0:T(8,128)(2,1)S(1)} %collective-permute-done.10.refs_2_), channel_id=1, source_target_pairs={{0,1},{1,0},{2,3},{3,2},{4,5},{5,4},{6,7},{7,6},{8,9},{9,8},{10,11... | collective-permute-start | bytes 1769480 | tf_op jit(solution)/shard_map/ppermute | solution.py:67
  38.2 7.8 %collective-permute-start.15 = (bf16[2,256,512]{2,1,0:T(8,128)(2,1)S(1)}, bf16[2,256,512]{2,1,0:T(8,128)(2,1)S(1)}, u32[]{:S(2)}, u32[]{:S(2)}) collective-permute-start(bf16[2,256,512]{2,1,0:T(8,128)(2,1)S(1)} %collective-permute-done.4.refs_2_.side), channel_id=1, source_target_pairs={{0,1},{1,0},{2,3},{3,2},{4,5},{5,4},{6,7},{7,6},{8,9},{9,8},{10,11... | collective-permute-start | bytes 1572872 | tf_op jit(solution)/shard_map/ppermute | solution.py:67
  38.7 7.3 %collective-permute-start.16 = (bf16[256,512]{1,0:T(8,128)(2,1)S(1)}, bf16[256,512]{1,0:T(8,128)(2,1)S(1)}, u32[]{:S(2)}, u32[]{:S(2)}) collective-permute-start(bf16[256,512]{1,0:T(8,128)(2,1)S(1)} %collective-permute-done.5.refs_2_.near), channel_id=1, source_target_pairs={{0,1},{1,0},{2,3},{3,2},{4,5},{5,4},{6,7},{7,6},{8,9},{9,8},{10,11... | collective-permute-start | bytes 786440 | tf_op jit(solution)/shard_map/ppermute | solution.py:67
  38.8 5.0 %collective-permute-start.12 = (bf16[96,192]{1,0:T(8,128)(2,1)S(1)}, bf16[96,192]{1,0:T(8,128)(2,1)S(1)}, u32[]{:S(2)}, u32[]{:S(2)}) collective-permute-start(bf16[96,192]{1,0:T(8,128)(2,1)S(1)} %get-tuple-element.45), channel_id=1, source_target_pairs={{0,32},{32,64},{64,96},{96,0},{1,33},{33,65},{65,97},{97,1},{2,34}... | collective-permute-start | bytes 110600 | tf_op jit(solution)/shard_map/ppermute | solution.py:71
  40.1 4.9 %collective-permute-start.13 = (bf16[96,192]{1,0:T(8,128)(2,1)S(1)}, bf16[96,192]{1,0:T(8,128)(2,1)S(1)}, u32[]{:S(2)}, u32[]{:S(2)}) collective-permute-start(bf16[96,192]{1,0:T(8,128)(2,1)S(1)} %get-tuple-element.46), channel_id=1, source_target_pairs={{0,64},{32,96},{64,0},{96,32},{1,65},{33,97},{65,1},{97,33},{2,66}... | collective-permute-start | bytes 110600 | tf_op jit(solution)/shard_map/ppermute | solution.py:71
  42.7 3.2 %collective-permute-start.14 = (bf16[96,192]{1,0:T(8,128)(2,1)S(1)}, bf16[96,192]{1,0:T(8,128)(2,1)S(1)}, u32[]{:S(2)}, u32[]{:S(2)}) collective-permute-start(bf16[96,192]{1,0:T(8,128)(2,1)S(1)} %get-tuple-element.47), channel_id=1, source_target_pairs={{0,96},{32,0},{64,32},{96,64},{1,97},{33,1},{65,33},{97,65},{2,98}... | collective-permute-start | bytes 110600 | tf_op jit(solution)/shard_map/ppermute | solution.py:71
  47.0 4.3 %collective-permute-start.17 = (bf16[128,128]{1,0:T(8,128)(2,1)S(1)}, bf16[128,128]{1,0:T(8,128)(2,1)S(1)}, u32[]{:S(2)}, u32[]{:S(2)}) collective-permute-start(bf16[128,128]{1,0:T(8,128)(2,1)S(1)} %hidden.1), channel_id=1, source_target_pairs={{0,16},{1,5},{2,18},{3,7},{4,20},{5,1},{6,22},{7,3},{8,24},{9,13},... | collective-permute-start | bytes 98312 | tf_op jit(solution)/shard_map/ppermute | solution.py:59
  47.8 4.0 %collective-permute-start.18 = (bf16[128,128]{1,0:T(8,128)(2,1)S(1)}, bf16[128,128]{1,0:T(8,128)(2,1)S(1)}, u32[]{:S(2)}, u32[]{:S(2)}) collective-permute-start(bf16[128,128]{1,0:T(8,128)(2,1)S(1)} %hidden.1), channel_id=1, source_target_pairs={{0,8},{1,3},{2,10},{3,5},{4,12},{5,7},{6,14},{7,1},{8,16},{9,11},{... | collective-permute-start | bytes 98312 | tf_op jit(solution)/shard_map/ppermute | solution.py:59
  48.7 3.1 %collective-permute-start.19 = (bf16[128,128]{1,0:T(8,128)(2,1)S(1)}, bf16[128,128]{1,0:T(8,128)(2,1)S(1)}, u32[]{:S(2)}, u32[]{:S(2)}) collective-permute-start(bf16[128,128]{1,0:T(8,128)(2,1)S(1)} %hidden.1), channel_id=1, source_target_pairs={{0,24},{1,7},{2,26},{3,1},{4,28},{5,3},{6,30},{7,5},{8,0},{9,15},{... | collective-permute-start | bytes 98312 | tf_op jit(solution)/shard_map/ppermute | solution.py:59
  51.8 8.6 %collective-permute-start.21 = (bf16[4,128,128]{2,1,0:T(8,128)(2,1)S(1)}, bf16[4,128,128]{2,1,0:T(8,128)(2,1)S(1)}, u32[]{:S(2)}, u32[]{:S(2)}) collective-permute-start(bf16[4,128,128]{2,1,0:T(8,128)(2,1)S(1)} %pad_maximum_fusion.refs_0_), channel_id=1, source_target_pairs={{0,4},{1,17},{2,6},{3,19},{4,0},{5,21},{6,2},{7,23},{8,12},{9,25},... | collective-permute-start | bytes 393224 | tf_op jit(solution)/shard_map/ppermute | solution.py:63
  52.8 9.8 %collective-permute-start.22 = (bf16[4,128,128]{2,1,0:T(8,128)(2,1)S(1)}, bf16[4,128,128]{2,1,0:T(8,128)(2,1)S(1)}, u32[]{:S(2)}, u32[]{:S(2)}) collective-permute-start(bf16[4,128,128]{2,1,0:T(8,128)(2,1)S(1)} %pad_maximum_fusion.refs_0_), channel_id=1, source_target_pairs={{0,2},{1,9},{2,4},{3,11},{4,6},{5,13},{6,0},{7,15},{8,10},{9,17},{... | collective-permute-start | bytes 393224 | tf_op jit(solution)/shard_map/ppermute | solution.py:63
  54.9 9.1 %collective-permute-start.23 = (bf16[4,128,128]{2,1,0:T(8,128)(2,1)S(1)}, bf16[4,128,128]{2,1,0:T(8,128)(2,1)S(1)}, u32[]{:S(2)}, u32[]{:S(2)}) collective-permute-start(bf16[4,128,128]{2,1,0:T(8,128)(2,1)S(1)} %pad_maximum_fusion.refs_0_), channel_id=1, source_target_pairs={{0,6},{1,25},{2,0},{3,27},{4,2},{5,29},{6,4},{7,31},{8,14},{9,1},{... | collective-permute-start | bytes 393224 | tf_op jit(solution)/shard_map/ppermute | solution.py:63
  55.5 8.5 %collective-permute-start.20 = (bf16[4,128,128]{2,1,0:T(8,128)(2,1)S(1)}, bf16[4,128,128]{2,1,0:T(8,128)(2,1)S(1)}, u32[]{:S(2)}, u32[]{:S(2)}) collective-permute-start(bf16[4,128,128]{2,1,0:T(8,128)(2,1)S(1)} %pad_maximum_fusion.refs_0_), channel_id=1, source_target_pairs={{0,1},{1,0},{2,3},{3,2},{4,5},{5,4},{6,7},{7,6},{8,9},{9,8},{10,11... | collective-permute-start | bytes 393224 | tf_op jit(solution)/shard_map/ppermute | solution.py:67
  60.5 3.8 %collective-permute-start.24 = (bf16[4,128,128]{2,1,0:T(8,128)(2,1)S(1)}, bf16[4,128,128]{2,1,0:T(8,128)(2,1)S(1)}, u32[]{:S(2)}, u32[]{:S(2)}) collective-permute-start(bf16[4,128,128]{2,1,0:T(8,128)(2,1)S(1)} %collective-permute-done.21.refs_2_), channel_id=1, source_target_pairs={{0,1},{1,0},{2,3},{3,2},{4,5},{5,4},{6,7},{7,6},{8,9},{9,8},{10,11... | collective-permute-start | bytes 393224 | tf_op jit(solution)/shard_map/ppermute | solution.py:67
  62.6 2.3 %collective-permute-start.25 = (bf16[4,128,128]{2,1,0:T(8,128)(2,1)S(1)}, bf16[4,128,128]{2,1,0:T(8,128)(2,1)S(1)}, u32[]{:S(2)}, u32[]{:S(2)}) collective-permute-start(bf16[4,128,128]{2,1,0:T(8,128)(2,1)S(1)} %collective-permute-done.22.refs_3_), channel_id=1, source_target_pairs={{0,1},{1,0},{2,3},{3,2},{4,5},{5,4},{6,7},{7,6},{8,9},{9,8},{10,11... | collective-permute-start | bytes 393224 | tf_op jit(solution)/shard_map/ppermute | solution.py:67
  64.0 1.3 %collective-permute-start.26 = (bf16[4,128,128]{2,1,0:T(8,128)(2,1)S(1)}, bf16[4,128,128]{2,1,0:T(8,128)(2,1)S(1)}, u32[]{:S(2)}, u32[]{:S(2)}) collective-permute-start(bf16[4,128,128]{2,1,0:T(8,128)(2,1)S(1)} %collective-permute-done.23.refs_4_), channel_id=1, source_target_pairs={{0,1},{1,0},{2,3},{3,2},{4,5},{5,4},{6,7},{7,6},{8,9},{9,8},{10,11... | collective-permute-start | bytes 393224 | tf_op jit(solution)/shard_map/ppermute | solution.py:67
  64.3 5.9 %copy-start.1 = (f32[153]{0:T(256)S(1)}, f32[153]{0:T(256)}, u32[]{:S(2)}) copy-start(f32[153]{0:T(256)} %param.13) | copy-start | bytes 1840
  66.5 6.0 %collective-permute-start.27 = (bf16[160,384]{1,0:T(8,128)(2,1)S(1)}, bf16[160,384]{1,0:T(8,128)(2,1)S(1)}, u32[]{:S(2)}, u32[]{:S(2)}) collective-permute-start(bf16[160,384]{1,0:T(8,128)(2,1)S(1)} %get-tuple-element.50.p0), channel_id=1, source_target_pairs={{0,32},{32,64},{64,96},{96,0},{1,33},{33,65},{65,97},{97,1},{2,34}... | collective-permute-start | bytes 368648 | tf_op jit(solution)/shard_map/ppermute | solution.py:71
  66.6 9.4 %collective-permute-start.28 = (bf16[160,384]{1,0:T(8,128)(2,1)S(1)}, bf16[160,384]{1,0:T(8,128)(2,1)S(1)}, u32[]{:S(2)}, u32[]{:S(2)}) collective-permute-start(bf16[160,384]{1,0:T(8,128)(2,1)S(1)} %get-tuple-element.50.p0), channel_id=1, source_target_pairs={{0,64},{32,96},{64,0},{96,32},{1,65},{33,97},{65,1},{97,33},{2,66}... | collective-permute-start | bytes 368648 | tf_op jit(solution)/shard_map/ppermute | solution.py:71
  70.1 5.9 %collective-permute-start.29 = (bf16[160,384]{1,0:T(8,128)(2,1)S(1)}, bf16[160,384]{1,0:T(8,128)(2,1)S(1)}, u32[]{:S(2)}, u32[]{:S(2)}) collective-permute-start(bf16[160,384]{1,0:T(8,128)(2,1)S(1)} %get-tuple-element.50.p0), channel_id=1, source_target_pairs={{0,96},{32,0},{64,32},{96,64},{1,97},{33,1},{65,33},{97,65},{2,98}... | collective-permute-start | bytes 368648 | tf_op jit(solution)/shard_map/ppermute | solution.py:71

commit v7 on v6

--- a/solution.py
+++ b/solution.py
@@ -244,7 +244,7 @@
 
 
 def product_last(kinds, adj, before, degree, *refs):
-    pieces, outs, mean = refs[:-5], refs[-5:-1], refs[-1]
+    pieces, outs, mean = refs[: len(kinds)], refs[-5:-1], refs[-1]
     feat = here()[1]
     total = add_blocks(kinds, adj, before[...], pieces)
     mean[...] = total * degree[:, :1]
@@ -356,19 +356,19 @@
         rows[t] = lax.optimization_barrier((total, rows[t]))[1]
     total = product(product_next, ((1, 0), (3, 0)), [rows[1], rows[3]], total, after=(near,), name="product_next")
     rows[2] = lax.optimization_barrier((total, rows[2]))[1]
+    other_side = swap(lax.optimization_barrier((side, total))[0])
+    far = swap(lax.optimization_barrier((near, total))[0])
     across = swap(rows[2])
     pieces = [swap(rows[1]), swap(rows[3]), rows[2]]
     total = product(product_next, ((1, 1), (3, 1), (2, 0)), pieces, total, name="product_more")
     pieces = [across]
     means = pl.pallas_call(
         functools.partial(product_last, ((2, 1),)), out_shape=[jax.ShapeDtypeStruct((SHARE, 192), bf16)] * NF,
-        in_specs=[VM] * 4, out_specs=[VM] * NF,
+        in_specs=[VM] * 4 + [ANY] * 2, out_specs=[VM] * NF,
         scratch_shapes=[pltpu.VMEM((ROWS, 192), f32)],
         compiler_params=params(), cost_estimate=blocks_cost(pieces), name="product_last",
-    )(adj, total, degree, *pieces)
-
-    side, near, means = lax.optimization_barrier((side, near, means))
-    other_side, far = swap(side), swap(near)
+    )(adj, total, degree, *pieces, other_side, far)
+
     g = {0: means[0]} | {s: along_feat(means[s], s) for s in (2, 1, 3)}
     g = [g[s] for s in range(NF)]
     z_block = pl.pallas_call(

time: 77 us -> 77 us (level)
  transfers between devices with their start and end apart: 30 -> 30, of which waited for: 11 -> 12; matrix products, arithmetic and copies ran while one was open for 0% -> 0% of each run, Pallas kernels for 17% -> 17%
where the time goes in v7:
time: 77 us; the launch traced here: 76.9 us
  starting transfers between devices  42.8 us (56%)
  Pallas kernels  17.2 us (22%)
  waiting for transfers between devices  16.7 us (22%)
    ppermute x10, starting transfers between devices, swap(): return lax.ppermute(value, 'vert', positions(lambda x, z, c: (x, z, 1 - c)))  13.2 us
    ppermute x6, starting transfers between devices, first_axis(): lax.ppermute(value, 'vert', positions(lambda x, z, c: (x + shift * (1 - c...  10.6 us
    ppermute x7, starting transfers between devices, along_feat(): lax.ppermute(value, 'feat', [(i, (i + shift) % NF) for i in range(NF)])  8.93 us
    ppermute x7, waiting for transfers between devices, along_feat(): lax.ppermute(value, 'feat', [(i, (i + shift) % NF) for i in range(NF)])  8.07 us
    ppermute x6, starting transfers between devices, second_axis(): lax.ppermute(value, 'vert', positions(lambda x, z, c: (x + shift * c, z +...  7.27 us
    pallas_call x1, Pallas kernels, second_half(): pl.pallas_call(functools.partial(adjacency_kernel, 1), in_specs=[HB] * 2...  5.54 us
    ppermute x1, waiting for transfers between devices, both_sides(): return lax.ppermute(value, ('feat', 'vert'), pairs)  4.26 us
    pallas_call x1, Pallas kernels, first_half(): pl.pallas_call(functools.partial(adjacency_kernel, 0), in_specs=[HB] * 5,...  4.18 us
  transfers between devices with their start and end apart: 30, of which 12 were waited for; matrix products, arithmetic and copies ran while one was open for 0% of the time, Pallas kernels for 17%

profile of v7, /device:TPU:1, one launch (start us, length us, event | category | flops | bytes accessed | tf_op | source)
XLA Modules:
  0.0 76.9 jit_solution(14311309586293682183)
XLA Ops:
  0.0 4.4 %collective-permute-start = (bf16[192,384]{1,0:T(8,128)(2,1)}, bf16[192,384]{1,0:T(8,128)(2,1)S(1)}, u32[]{:S(2)}, u32[]{:S(2)}) collective-permute-start(bf16[192,384]{1,0:T(8,128)(2,1)} %bitcast.9), channel_id=1, source_target_pairs={{0,16},{1,5},{2,18},{3,7},{4,20},{5,1},{6,22},{7,3},{8,24},{9,13},... | collective-permute-start | bytes 442376 | tf_op jit(solution)/shard_map/ppermute | solution.py:59
  4.4 0.7 collective-permute-start.1
  5.2 1.9 %collective-permute-start.2 = (bf16[192,384]{1,0:T(8,128)(2,1)}, bf16[192,384]{1,0:T(8,128)(2,1)S(1)}, u32[]{:S(2)}, u32[]{:S(2)}) collective-permute-start(bf16[192,384]{1,0:T(8,128)(2,1)} %bitcast.11), channel_id=1, source_target_pairs={{0,24},{1,7},{2,26},{3,1},{4,28},{5,3},{6,30},{7,5},{8,0},{9,15},{... | collective-permute-start | bytes 442376 | tf_op jit(solution)/shard_map/ppermute | solution.py:59
  7.1 4.2 %adjacency_first.1 = (bf16[384,12288]{1,0:T(8,128)(2,1)S(1)}, bf16[384,4096]{1,0:T(8,128)(2,1)S(1)}, f32[384,128]{1,0:T(8,128)S(1)}, bf16[2,256,512]{2,1,0:T(8,128)(2,1)S(1)}, bf16[256,512]{1,0:T(8,128)(2,1)S(1)}) custom-call(s32[3,96]{1,0:T(4,128)} %mask.3, s32[384,12288]{1,0:T(8,128)} %counts.3, bf16[192,1024]{1,0:T(8,128)(2,1)} %refs_0_.1, ...), custom_call_target="tpu_custom_call" | custom-call | flops 1200000000 | bytes 16000000 | tf_op jit(solution)/shard_map/adjacency_first/pallas_call | solution.py:168
  11.3 0.0 collective-permute-done.1.c
  11.3 0.0 collective-permute-done.2.d
  11.3 0.1 stack.21.refs_0_
  11.4 0.7 collective-permute-start.3
  12.1 2.0 %collective-permute-start.6 = (bf16[4,192,384]{2,1,0:T(8,128)(2,1)S(1)}, bf16[4,192,384]{2,1,0:T(8,128)(2,1)S(1)}, u32[]{:S(2)}, u32[]{:S(2)}) collective-permute-start(bf16[4,192,384]{2,1,0:T(8,128)(2,1)S(1)} %stack.21.refs_0_), channel_id=1, source_target_pairs={{0,6},{1,25},{2,0},{3,27},{4,2},{5,29},{6,4},{7,31},{8,14},{9,1},{... | collective-permute-start | bytes 1769480 | tf_op jit(solution)/shard_map/ppermute | solution.py:63
  14.2 0.0 collective-permute-start.5
  14.2 2.7 %collective-permute-start.4 = (bf16[2,256,512]{2,1,0:T(8,128)(2,1)S(1)}, bf16[2,256,512]{2,1,0:T(8,128)(2,1)S(1)}, u32[]{:S(2)}, u32[]{:S(2)}) collective-permute-start(bf16[2,256,512]{2,1,0:T(8,128)(2,1)S(1)} %get-tuple-element.31.own), channel_id=1, source_target_pairs={{0,32},{32,64},{64,96},{96,0},{1,97},{33,1},{65,33},{97,65},{2,34}... | collective-permute-start | bytes 1572872 | tf_op jit(solution)/shard_map/ppermute | solution.py:76
  16.9 1.6 %collective-permute-start.10 = (bf16[4,192,384]{2,1,0:T(8,128)(2,1)S(1)}, bf16[4,192,384]{2,1,0:T(8,128)(2,1)S(1)}, u32[]{:S(2)}, u32[]{:S(2)}) collective-permute-start(bf16[4,192,384]{2,1,0:T(8,128)(2,1)S(1)} %stack.21.refs_0_), channel_id=1, source_target_pairs={{0,4},{1,17},{2,6},{3,19},{4,0},{5,21},{6,2},{7,23},{8,12},{9,25},... | collective-permute-start | bytes 1769480 | tf_op jit(solution)/shard_map/ppermute | solution.py:63
  18.5 0.0 collective-permute-done.3.refs_3_.refs_1_
  18.5 0.3 collective-permute-start.7
  18.9 5.5 %adjacency_second.1 = (bf16[384,12288]{1,0:T(8,128)(2,1)S(1)}, bf16[384,4096]{1,0:T(8,128)(2,1)S(1)}, f32[384,128]{1,0:T(8,128)S(1)}) custom-call(s32[3,96]{1,0:T(4,128)} %mask.3, s32[384,12288]{1,0:T(8,128)} %counts.3, bf16[384,12288]{1,0:T(8,128)(2,1)S(1)} %get-tuple-element.24.refs_0_, ...), custom_call_target="tpu_custom_call", output_to_operand_aliasing={{0}: (2, {}), {1}: (3, {}), {2}: (4, {})} | custom-call | flops 1200000000 | bytes 16000000 | tf_op jit(solution)/shard_map/adjacency_second/pallas_call | solution.py:189
  24.4 4.3 %collective-permute-done.4.refs_2_.side = bf16[2,256,512]{2,1,0:T(8,128)(2,1)S(1)} collective-permute-done((bf16[2,256,512]{2,1,0:T(8,128)(2,1)S(1)}, bf16[2,256,512]{2,1,0:T(8,128)(2,1)S(1)}, u32[]{:S(2)}, u32[]{:S(2)}) %collective-permute-start.4) | collective-permute-done | bytes 524320 | tf_op jit(solution)/shard_map/ppermute | solution.py:76
  28.7 1.0 %product_first.1.before = f32[384,192]{1,0:T(8,128)S(1)} custom-call(bf16[384,12288]{1,0:T(8,128)(2,1)S(1)} %get-tuple-element.30.adj, bf16[4,192,384]{2,1,0:T(8,128)(2,1)S(1)} %stack.21.refs_0_, bf16[4,192,384]{2,1,0:T(8,128)(2,1)S(1)} %collective-permute-done.3.refs_3_.refs_1_, bf16[2,256,512]{2,1,0:T(8,128)(2,1)S(1)} %collective-permute-done.4.refs_2_.side), custom_call_target="tpu_custom_call" | custom-call | flops 603979776 | bytes 3600000 | tf_op jit(solution)/shard_map/product_first/pallas_call | solution.py:348
  29.7 0.0 collective-permute-done.6.refs_1_
  29.7 1.1 %collective-permute-done.5.refs_0_ = bf16[4,192,384]{2,1,0:T(8,128)(2,1)S(1)} collective-permute-done((bf16[4,192,384]{2,1,0:T(8,128)(2,1)S(1)}, bf16[4,192,384]{2,1,0:T(8,128)(2,1)S(1)}, u32[]{:S(2)}, u32[]{:S(2)}) %collective-permute-start.5) | collective-permute-done | bytes 589856 | tf_op jit(solution)/shard_map/ppermute | solution.py:63
  30.7 2.9 %collective-permute-start.9 = (bf16[4,192,384]{2,1,0:T(8,128)(2,1)S(1)}, bf16[4,192,384]{2,1,0:T(8,128)(2,1)S(1)}, u32[]{:S(2)}, u32[]{:S(2)}) collective-permute-start(bf16[4,192,384]{2,1,0:T(8,128)(2,1)S(1)} %collective-permute-done.6.refs_1_), channel_id=1, source_target_pairs={{0,1},{1,0},{2,3},{3,2},{4,5},{5,4},{6,7},{7,6},{8,9},{9,8},{10,11... | collective-permute-start | bytes 1769480 | tf_op jit(solution)/shard_map/ppermute | solution.py:67
  33.7 0.0 collective-permute-start.8
  33.7 0.0 collective-permute-done.10.refs_2_
  33.7 0.0 collective-permute-done.7.refs_2_.near
  33.7 1.0 %product_next.1.before = f32[384,192]{1,0:T(8,128)S(1)} custom-call(bf16[384,12288]{1,0:T(8,128)(2,1)S(1)} %get-tuple-element.30.adj, f32[384,192]{1,0:T(8,128)S(1)} %product_first.1.before, bf16[4,192,384]{2,1,0:T(8,128)(2,1)S(1)} %collective-permute-done.5.refs_0_, bf16[4,192,384]{2,1,0:T(8,128)(2,1)S(1)} %collective-permute-done.6.refs_1_, ...), custom_call_target="tpu_custom_call" | custom-call | flops 603979776 | bytes 3600000 | tf_op jit(solution)/shard_map/product_next/pallas_call | solution.py:348
  34.7 0.6 collective-permute-start.11
  35.3 0.1 collective-permute-start.12
  35.4 0.4 collective-permute-start.13
  35.8 0.0 collective-permute-done.9.refs_1_
  35.8 0.4 collective-permute-done.8.refs_0_
  36.1 1.4 %product_more.1.before = f32[384,192]{1,0:T(8,128)S(1)} custom-call(bf16[384,12288]{1,0:T(8,128)(2,1)S(1)} %get-tuple-element.30.adj, f32[384,192]{1,0:T(8,128)S(1)} %product_next.1.before, bf16[4,192,384]{2,1,0:T(8,128)(2,1)S(1)} %collective-permute-done.8.refs_0_, bf16[4,192,384]{2,1,0:T(8,128)(2,1)S(1)} %collective-permute-done.9.refs_1_, ...), custom_call_target="tpu_custom_call" | custom-call | flops 905969664 | bytes 5400000 | tf_op jit(solution)/shard_map/product_more/pallas_call | solution.py:348
  37.6 0.6 collective-permute-done.13.refs_2_.far
  38.1 0.0 collective-permute-done.12.refs_1_.other_side
  38.1 0.6 product_last.1
  38.8 1.4 %collective-permute-start.14 = (bf16[96,192]{1,0:T(8,128)(2,1)S(1)}, bf16[96,192]{1,0:T(8,128)(2,1)S(1)}, u32[]{:S(2)}, u32[]{:S(2)}) collective-permute-start(bf16[96,192]{1,0:T(8,128)(2,1)S(1)} %get-tuple-element.39), channel_id=1, source_target_pairs={{0,32},{32,64},{64,96},{96,0},{1,33},{33,65},{65,97},{97,1},{2,34}... | collective-permute-start | bytes 110600 | tf_op jit(solution)/shard_map/ppermute | solution.py:71
  40.1 2.6 %collective-permute-start.15 = (bf16[96,192]{1,0:T(8,128)(2,1)S(1)}, bf16[96,192]{1,0:T(8,128)(2,1)S(1)}, u32[]{:S(2)}, u32[]{:S(2)}) collective-permute-start(bf16[96,192]{1,0:T(8,128)(2,1)S(1)} %get-tuple-element.40), channel_id=1, source_target_pairs={{0,64},{32,96},{64,0},{96,32},{1,65},{33,97},{65,1},{97,33},{2,66}... | collective-permute-start | bytes 110600 | tf_op jit(solution)/shard_map/ppermute | solution.py:71
  42.8 1.1 %collective-permute-start.16 = (bf16[96,192]{1,0:T(8,128)(2,1)S(1)}, bf16[96,192]{1,0:T(8,128)(2,1)S(1)}, u32[]{:S(2)}, u32[]{:S(2)}) collective-permute-start(bf16[96,192]{1,0:T(8,128)(2,1)S(1)} %get-tuple-element.41), channel_id=1, source_target_pairs={{0,96},{32,0},{64,32},{96,64},{1,97},{33,1},{65,33},{97,65},{2,98}... | collective-permute-start | bytes 110600 | tf_op jit(solution)/shard_map/ppermute | solution.py:71
  43.8 0.0 collective-permute-done.14.g1
  43.8 1.2 %collective-permute-done.15.g2 = bf16[96,192]{1,0:T(8,128)(2,1)S(1)} collective-permute-done((bf16[96,192]{1,0:T(8,128)(2,1)S(1)}, bf16[96,192]{1,0:T(8,128)(2,1)S(1)}, u32[]{:S(2)}, u32[]{:S(2)}) %collective-permute-start.15) | collective-permute-done | bytes 36896 | tf_op jit(solution)/shard_map/ppermute | solution.py:71
  45.0 1.0 %collective-permute-done.16.g3 = bf16[96,192]{1,0:T(8,128)(2,1)S(1)} collective-permute-done((bf16[96,192]{1,0:T(8,128)(2,1)S(1)}, bf16[96,192]{1,0:T(8,128)(2,1)S(1)}, u32[]{:S(2)}, u32[]{:S(2)}) %collective-permute-start.16) | collective-permute-done | bytes 36896 | tf_op jit(solution)/shard_map/ppermute | solution.py:71
  46.0 1.0 %hidden.1 = bf16[128,128]{1,0:T(8,128)(2,1)S(1)} custom-call(bf16[96,192]{1,0:T(8,128)(2,1)S(1)} %get-tuple-element.38.g0, bf16[96,192]{1,0:T(8,128)(2,1)S(1)} %collective-permute-done.14.g1, bf16[96,192]{1,0:T(8,128)(2,1)S(1)} %collective-permute-done.15.g2, bf16[96,192]{1,0:T(8,128)(2,1)S(1)} %collective-permute-done.16.g3, ...), custom_call_target="tpu_custom_call" | custom-call | flops 150994944 | bytes 2000000 | tf_op jit(solution)/shard_map/hidden/pallas_call | solution.py:374
  47.0 0.8 %collective-permute-start.17 = (bf16[128,128]{1,0:T(8,128)(2,1)S(1)}, bf16[128,128]{1,0:T(8,128)(2,1)S(1)}, u32[]{:S(2)}, u32[]{:S(2)}) collective-permute-start(bf16[128,128]{1,0:T(8,128)(2,1)S(1)} %hidden.1), channel_id=1, source_target_pairs={{0,16},{1,5},{2,18},{3,7},{4,20},{5,1},{6,22},{7,3},{8,24},{9,13},... | collective-permute-start | bytes 98312 | tf_op jit(solution)/shard_map/ppermute | solution.py:59
  47.9 1.0 %collective-permute-start.18 = (bf16[128,128]{1,0:T(8,128)(2,1)S(1)}, bf16[128,128]{1,0:T(8,128)(2,1)S(1)}, u32[]{:S(2)}, u32[]{:S(2)}) collective-permute-start(bf16[128,128]{1,0:T(8,128)(2,1)S(1)} %hidden.1), channel_id=1, source_target_pairs={{0,8},{1,3},{2,10},{3,5},{4,12},{5,7},{6,14},{7,1},{8,16},{9,11},{... | collective-permute-start | bytes 98312 | tf_op jit(solution)/shard_map/ppermute | solution.py:59
  48.9 1.7 %collective-permute-start.19 = (bf16[128,128]{1,0:T(8,128)(2,1)S(1)}, bf16[128,128]{1,0:T(8,128)(2,1)S(1)}, u32[]{:S(2)}, u32[]{:S(2)}) collective-permute-start(bf16[128,128]{1,0:T(8,128)(2,1)S(1)} %hidden.1), channel_id=1, source_target_pairs={{0,24},{1,7},{2,26},{3,1},{4,28},{5,3},{6,30},{7,5},{8,0},{9,15},{... | collective-permute-start | bytes 98312 | tf_op jit(solution)/shard_map/ppermute | solution.py:59
  50.5 0.8 %collective-permute-done.17 = bf16[128,128]{1,0:T(8,128)(2,1)S(1)} collective-permute-done((bf16[128,128]{1,0:T(8,128)(2,1)S(1)}, bf16[128,128]{1,0:T(8,128)(2,1)S(1)}, u32[]{:S(2)}, u32[]{:S(2)}) %collective-permute-start.17) | collective-permute-done | bytes 32800 | tf_op jit(solution)/shard_map/ppermute | solution.py:59
  51.4 0.4 collective-permute-done.18
  51.9 1.0 %collective-permute-start.21 = (bf16[4,128,128]{2,1,0:T(8,128)(2,1)S(1)}, bf16[4,128,128]{2,1,0:T(8,128)(2,1)S(1)}, u32[]{:S(2)}, u32[]{:S(2)}) collective-permute-start(bf16[4,128,128]{2,1,0:T(8,128)(2,1)S(1)} %pad_maximum_fusion.refs_0_), channel_id=1, source_target_pairs={{0,4},{1,17},{2,6},{3,19},{4,0},{5,21},{6,2},{7,23},{8,12},{9,25},... | collective-permute-start | bytes 393224 | tf_op jit(solution)/shard_map/ppermute | solution.py:63
  52.8 2.1 %collective-permute-start.22 = (bf16[4,128,128]{2,1,0:T(8,128)(2,1)S(1)}, bf16[4,128,128]{2,1,0:T(8,128)(2,1)S(1)}, u32[]{:S(2)}, u32[]{:S(2)}) collective-permute-start(bf16[4,128,128]{2,1,0:T(8,128)(2,1)S(1)} %pad_maximum_fusion.refs_0_), channel_id=1, source_target_pairs={{0,2},{1,9},{2,4},{3,11},{4,6},{5,13},{6,0},{7,15},{8,10},{9,17},{... | collective-permute-start | bytes 393224 | tf_op jit(solution)/shard_map/ppermute | solution.py:63
  54.9 0.6 collective-permute-start.23
  55.5 5.0 %collective-permute-start.20 = (bf16[4,128,128]{2,1,0:T(8,128)(2,1)S(1)}, bf16[4,128,128]{2,1,0:T(8,128)(2,1)S(1)}, u32[]{:S(2)}, u32[]{:S(2)}) collective-permute-start(bf16[4,128,128]{2,1,0:T(8,128)(2,1)S(1)} %pad_maximum_fusion.refs_0_), channel_id=1, source_target_pairs={{0,1},{1,0},{2,3},{3,2},{4,5},{5,4},{6,7},{7,6},{8,9},{9,8},{10,11... | collective-permute-start | bytes 393224 | tf_op jit(solution)/shard_map/ppermute | solution.py:67
  60.5 2.1 %collective-permute-start.24 = (bf16[4,128,128]{2,1,0:T(8,128)(2,1)S(1)}, bf16[4,128,128]{2,1,0:T(8,128)(2,1)S(1)}, u32[]{:S(2)}, u32[]{:S(2)}) collective-permute-start(bf16[4,128,128]{2,1,0:T(8,128)(2,1)S(1)} %collective-permute-done.21.refs_2_), channel_id=1, source_target_pairs={{0,1},{1,0},{2,3},{3,2},{4,5},{5,4},{6,7},{7,6},{8,9},{9,8},{10,11... | collective-permute-start | bytes 393224 | tf_op jit(solution)/shard_map/ppermute | solution.py:67
  62.6 1.3 %collective-permute-start.25 = (bf16[4,128,128]{2,1,0:T(8,128)(2,1)S(1)}, bf16[4,128,128]{2,1,0:T(8,128)(2,1)S(1)}, u32[]{:S(2)}, u32[]{:S(2)}) collective-permute-start(bf16[4,128,128]{2,1,0:T(8,128)(2,1)S(1)} %collective-permute-done.22.refs_3_), channel_id=1, source_target_pairs={{0,1},{1,0},{2,3},{3,2},{4,5},{5,4},{6,7},{7,6},{8,9},{9,8},{10,11... | collective-permute-start | bytes 393224 | tf_op jit(solution)/shard_map/ppermute | solution.py:67
  64.0 0.0 collective-permute-done.23.refs_4_
  64.0 0.0 collective-permute-start.26
  64.0 0.0 collective-permute-done.20.refs_1_
  64.0 0.3 unpack.1.before
  64.3 0.0 copy-start.1
  64.3 0.7 collective-permute-done.25.refs_1_
  65.0 0.4 collective-permute-done.26.refs_2_
  65.3 1.2 %scores.1 = (bf16[160,384]{1,0:T(8,128)(2,1)S(1)}, bf16[4096,256]{1,0:T(8,128)(2,1)S(1)}) custom-call(bf16[384,4096]{1,0:T(8,128)(2,1)S(1)} %get-tuple-element.28.adj2, f32[384,128]{1,0:T(8,128)S(1)} %get-tuple-element.29.degree.inverse, bf16[4096,256]{1,0:T(8,128)(2,1)S(1)} %unpack.1.before, ...), custom_call_target="tpu_custom_call", output_to_operand_aliasing={{1}: (2, {})} | custom-call | flops 805306368 | bytes 5000000 | tf_op jit(solution)/shard_map/scores/pallas_call | solution.py:395
  66.6 0.1 collective-permute-start.27
  66.7 3.4 %collective-permute-start.28 = (bf16[160,384]{1,0:T(8,128)(2,1)S(1)}, bf16[160,384]{1,0:T(8,128)(2,1)S(1)}, u32[]{:S(2)}, u32[]{:S(2)}) collective-permute-start(bf16[160,384]{1,0:T(8,128)(2,1)S(1)} %get-tuple-element.42.p0), channel_id=1, source_target_pairs={{0,64},{32,96},{64,0},{96,32},{1,65},{33,97},{65,1},{97,33},{2,66}... | collective-permute-start | bytes 368648 | tf_op jit(solution)/shard_map/ppermute | solution.py:71
  70.1 2.5 %collective-permute-done.27.p1 = bf16[160,384]{1,0:T(8,128)(2,1)S(1)} collective-permute-done((bf16[160,384]{1,0:T(8,128)(2,1)S(1)}, bf16[160,384]{1,0:T(8,128)(2,1)S(1)}, u32[]{:S(2)}, u32[]{:S(2)}) %collective-permute-start.27) | collective-permute-done | bytes 122912 | tf_op jit(solution)/shard_map/ppermute | solution.py:71
  72.6 3.4 %collective-permute-done.28.p2 = bf16[160,384]{1,0:T(8,128)(2,1)S(1)} collective-permute-done((bf16[160,384]{1,0:T(8,128)(2,1)S(1)}, bf16[160,384]{1,0:T(8,128)(2,1)S(1)}, u32[]{:S(2)}, u32[]{:S(2)}) %collective-permute-start.28) | collective-permute-done | bytes 122912 | tf_op jit(solution)/shard_map/ppermute | solution.py:71
  76.0 0.9 %sum.1 = f32[153,384]{1,0:T(8,128)} custom-call(bf16[160,384]{1,0:T(8,128)(2,1)S(1)} %get-tuple-element.42.p0, bf16[160,384]{1,0:T(8,128)(2,1)S(1)} %collective-permute-done.27.p1, bf16[160,384]{1,0:T(8,128)(2,1)S(1)} %collective-permute-done.28.p2, bf16[160,384]{1,0:T(8,128)(2,1)S(1)} %collective-permute-done.29.p3, f32[1,256]{1,0:T(1,128)S(1)} %bitcast.14), custom_call_target="tpu_custom_call" | custom-call | flops 300000 | bytes 800000 | tf_op jit(solution)/shard_map/sum/pallas_call | solution.py:403
  (13 shorter events, 0.0 us)
Async XLA Ops:
  0.0 11.3 %collective-permute-start = (bf16[192,384]{1,0:T(8,128)(2,1)}, bf16[192,384]{1,0:T(8,128)(2,1)S(1)}, u32[]{:S(2)}, u32[]{:S(2)}) collective-permute-start(bf16[192,384]{1,0:T(8,128)(2,1)} %bitcast.9), channel_id=1, source_target_pairs={{0,16},{1,5},{2,18},{3,7},{4,20},{5,1},{6,22},{7,3},{8,24},{9,13},... | collective-permute-start | bytes 442376 | tf_op jit(solution)/shard_map/ppermute | solution.py:59
  4.4 6.9 %collective-permute-start.1 = (bf16[192,384]{1,0:T(8,128)(2,1)}, bf16[192,384]{1,0:T(8,128)(2,1)S(1)}, u32[]{:S(2)}, u32[]{:S(2)}) collective-permute-start(bf16[192,384]{1,0:T(8,128)(2,1)} %bitcast.10), channel_id=1, source_target_pairs={{0,8},{1,3},{2,10},{3,5},{4,12},{5,7},{6,14},{7,1},{8,16},{9,11},{... | collective-permute-start | bytes 442376 | tf_op jit(solution)/shard_map/ppermute | solution.py:59
  5.2 6.2 %collective-permute-start.2 = (bf16[192,384]{1,0:T(8,128)(2,1)}, bf16[192,384]{1,0:T(8,128)(2,1)S(1)}, u32[]{:S(2)}, u32[]{:S(2)}) collective-permute-start(bf16[192,384]{1,0:T(8,128)(2,1)} %bitcast.11), channel_id=1, source_target_pairs={{0,24},{1,7},{2,26},{3,1},{4,28},{5,3},{6,30},{7,5},{8,0},{9,15},{... | collective-permute-start | bytes 442376 | tf_op jit(solution)/shard_map/ppermute | solution.py:59
  7.1 4.2 %copy-start = (bf16[384,192]{0,1:T(8,128)(2,1)S(1)}, bf16[384,192]{0,1:T(8,128)(2,1)}, u32[]{:S(2)}) copy-start(bf16[384,192]{0,1:T(8,128)(2,1)} %param.7) | copy-start | bytes 442372
  11.4 7.1 %collective-permute-start.3 = (bf16[4,192,384]{2,1,0:T(8,128)(2,1)S(1)}, bf16[4,192,384]{2,1,0:T(8,128)(2,1)S(1)}, u32[]{:S(2)}, u32[]{:S(2)}) collective-permute-start(bf16[4,192,384]{2,1,0:T(8,128)(2,1)S(1)} %stack.21.refs_0_), channel_id=1, source_target_pairs={{0,1},{1,0},{2,3},{3,2},{4,5},{5,4},{6,7},{7,6},{8,9},{9,8},{10,11... | collective-permute-start | bytes 1769480 | tf_op jit(solution)/shard_map/ppermute | solution.py:67
  12.1 17.5 %collective-permute-start.6 = (bf16[4,192,384]{2,1,0:T(8,128)(2,1)S(1)}, bf16[4,192,384]{2,1,0:T(8,128)(2,1)S(1)}, u32[]{:S(2)}, u32[]{:S(2)}) collective-permute-start(bf16[4,192,384]{2,1,0:T(8,128)(2,1)S(1)} %stack.21.refs_0_), channel_id=1, source_target_pairs={{0,6},{1,25},{2,0},{3,27},{4,2},{5,29},{6,4},{7,31},{8,14},{9,1},{... | collective-permute-start | bytes 1769480 | tf_op jit(solution)/shard_map/ppermute | solution.py:63
  14.2 16.6 %collective-permute-start.5 = (bf16[4,192,384]{2,1,0:T(8,128)(2,1)S(1)}, bf16[4,192,384]{2,1,0:T(8,128)(2,1)S(1)}, u32[]{:S(2)}, u32[]{:S(2)}) collective-permute-start(bf16[4,192,384]{2,1,0:T(8,128)(2,1)S(1)} %stack.21.refs_0_), channel_id=1, source_target_pairs={{0,2},{1,9},{2,4},{3,11},{4,6},{5,13},{6,0},{7,15},{8,10},{9,17},{... | collective-permute-start | bytes 1769480 | tf_op jit(solution)/shard_map/ppermute | solution.py:63
  14.2 14.5 %collective-permute-start.4 = (bf16[2,256,512]{2,1,0:T(8,128)(2,1)S(1)}, bf16[2,256,512]{2,1,0:T(8,128)(2,1)S(1)}, u32[]{:S(2)}, u32[]{:S(2)}) collective-permute-start(bf16[2,256,512]{2,1,0:T(8,128)(2,1)S(1)} %get-tuple-element.31.own), channel_id=1, source_target_pairs={{0,32},{32,64},{64,96},{96,0},{1,97},{33,1},{65,33},{97,65},{2,34}... | collective-permute-start | bytes 1572872 | tf_op jit(solution)/shard_map/ppermute | solution.py:76
  16.9 16.8 %collective-permute-start.10 = (bf16[4,192,384]{2,1,0:T(8,128)(2,1)S(1)}, bf16[4,192,384]{2,1,0:T(8,128)(2,1)S(1)}, u32[]{:S(2)}, u32[]{:S(2)}) collective-permute-start(bf16[4,192,384]{2,1,0:T(8,128)(2,1)S(1)} %stack.21.refs_0_), channel_id=1, source_target_pairs={{0,4},{1,17},{2,6},{3,19},{4,0},{5,21},{6,2},{7,23},{8,12},{9,25},... | collective-permute-start | bytes 1769480 | tf_op jit(solution)/shard_map/ppermute | solution.py:63
  18.5 15.2 %collective-permute-start.7 = (bf16[256,512]{1,0:T(8,128)(2,1)S(1)}, bf16[256,512]{1,0:T(8,128)(2,1)S(1)}, u32[]{:S(2)}, u32[]{:S(2)}) collective-permute-start(bf16[256,512]{1,0:T(8,128)(2,1)S(1)} %get-tuple-element.27.after), channel_id=1, source_target_pairs={{0,64},{32,96},{64,0},{96,32},{1,65},{33,97},{65,1},{97,33},{2,66}... | collective-permute-start | bytes 786440 | tf_op jit(solution)/shard_map/ppermute | solution.py:71
  30.7 5.0 %collective-permute-start.9 = (bf16[4,192,384]{2,1,0:T(8,128)(2,1)S(1)}, bf16[4,192,384]{2,1,0:T(8,128)(2,1)S(1)}, u32[]{:S(2)}, u32[]{:S(2)}) collective-permute-start(bf16[4,192,384]{2,1,0:T(8,128)(2,1)S(1)} %collective-permute-done.6.refs_1_), channel_id=1, source_target_pairs={{0,1},{1,0},{2,3},{3,2},{4,5},{5,4},{6,7},{7,6},{8,9},{9,8},{10,11... | collective-permute-start | bytes 1769480 | tf_op jit(solution)/shard_map/ppermute | solution.py:67
  33.7 2.5 %collective-permute-start.8 = (bf16[4,192,384]{2,1,0:T(8,128)(2,1)S(1)}, bf16[4,192,384]{2,1,0:T(8,128)(2,1)S(1)}, u32[]{:S(2)}, u32[]{:S(2)}) collective-permute-start(bf16[4,192,384]{2,1,0:T(8,128)(2,1)S(1)} %collective-permute-done.5.refs_0_), channel_id=1, source_target_pairs={{0,1},{1,0},{2,3},{3,2},{4,5},{5,4},{6,7},{7,6},{8,9},{9,8},{10,11... | collective-permute-start | bytes 1769480 | tf_op jit(solution)/shard_map/ppermute | solution.py:67
  34.7 3.4 %collective-permute-start.11 = (bf16[4,192,384]{2,1,0:T(8,128)(2,1)S(1)}, bf16[4,192,384]{2,1,0:T(8,128)(2,1)S(1)}, u32[]{:S(2)}, u32[]{:S(2)}) collective-permute-start(bf16[4,192,384]{2,1,0:T(8,128)(2,1)S(1)} %collective-permute-done.10.refs_2_), channel_id=1, source_target_pairs={{0,1},{1,0},{2,3},{3,2},{4,5},{5,4},{6,7},{7,6},{8,9},{9,8},{10,11... | collective-permute-start | bytes 1769480 | tf_op jit(solution)/shard_map/ppermute | solution.py:67
  35.3 2.8 %collective-permute-start.12 = (bf16[2,256,512]{2,1,0:T(8,128)(2,1)S(1)}, bf16[2,256,512]{2,1,0:T(8,128)(2,1)S(1)}, u32[]{:S(2)}, u32[]{:S(2)}) collective-permute-start(bf16[2,256,512]{2,1,0:T(8,128)(2,1)S(1)} %collective-permute-done.4.refs_2_.side), channel_id=1, source_target_pairs={{0,1},{1,0},{2,3},{3,2},{4,5},{5,4},{6,7},{7,6},{8,9},{9,8},{10,11... | collective-permute-start | bytes 1572872 | tf_op jit(solution)/shard_map/ppermute | solution.py:67
  35.4 2.7 %collective-permute-start.13 = (bf16[256,512]{1,0:T(8,128)(2,1)S(1)}, bf16[256,512]{1,0:T(8,128)(2,1)S(1)}, u32[]{:S(2)}, u32[]{:S(2)}) collective-permute-start(bf16[256,512]{1,0:T(8,128)(2,1)S(1)} %collective-permute-done.7.refs_2_.near), channel_id=1, source_target_pairs={{0,1},{1,0},{2,3},{3,2},{4,5},{5,4},{6,7},{7,6},{8,9},{9,8},{10,11... | collective-permute-start | bytes 786440 | tf_op jit(solution)/shard_map/ppermute | solution.py:67
  38.8 5.1 %collective-permute-start.14 = (bf16[96,192]{1,0:T(8,128)(2,1)S(1)}, bf16[96,192]{1,0:T(8,128)(2,1)S(1)}, u32[]{:S(2)}, u32[]{:S(2)}) collective-permute-start(bf16[96,192]{1,0:T(8,128)(2,1)S(1)} %get-tuple-element.39), channel_id=1, source_target_pairs={{0,32},{32,64},{64,96},{96,0},{1,33},{33,65},{65,97},{97,1},{2,34}... | collective-permute-start | bytes 110600 | tf_op jit(solution)/shard_map/ppermute | solution.py:71
  40.1 4.9 %collective-permute-start.15 = (bf16[96,192]{1,0:T(8,128)(2,1)S(1)}, bf16[96,192]{1,0:T(8,128)(2,1)S(1)}, u32[]{:S(2)}, u32[]{:S(2)}) collective-permute-start(bf16[96,192]{1,0:T(8,128)(2,1)S(1)} %get-tuple-element.40), channel_id=1, source_target_pairs={{0,64},{32,96},{64,0},{96,32},{1,65},{33,97},{65,1},{97,33},{2,66}... | collective-permute-start | bytes 110600 | tf_op jit(solution)/shard_map/ppermute | solution.py:71
  42.8 3.2 %collective-permute-start.16 = (bf16[96,192]{1,0:T(8,128)(2,1)S(1)}, bf16[96,192]{1,0:T(8,128)(2,1)S(1)}, u32[]{:S(2)}, u32[]{:S(2)}) collective-permute-start(bf16[96,192]{1,0:T(8,128)(2,1)S(1)} %get-tuple-element.41), channel_id=1, source_target_pairs={{0,96},{32,0},{64,32},{96,64},{1,97},{33,1},{65,33},{97,65},{2,98}... | collective-permute-start | bytes 110600 | tf_op jit(solution)/shard_map/ppermute | solution.py:71
  47.0 4.3 %collective-permute-start.17 = (bf16[128,128]{1,0:T(8,128)(2,1)S(1)}, bf16[128,128]{1,0:T(8,128)(2,1)S(1)}, u32[]{:S(2)}, u32[]{:S(2)}) collective-permute-start(bf16[128,128]{1,0:T(8,128)(2,1)S(1)} %hidden.1), channel_id=1, source_target_pairs={{0,16},{1,5},{2,18},{3,7},{4,20},{5,1},{6,22},{7,3},{8,24},{9,13},... | collective-permute-start | bytes 98312 | tf_op jit(solution)/shard_map/ppermute | solution.py:59
  47.9 4.0 %collective-permute-start.18 = (bf16[128,128]{1,0:T(8,128)(2,1)S(1)}, bf16[128,128]{1,0:T(8,128)(2,1)S(1)}, u32[]{:S(2)}, u32[]{:S(2)}) collective-permute-start(bf16[128,128]{1,0:T(8,128)(2,1)S(1)} %hidden.1), channel_id=1, source_target_pairs={{0,8},{1,3},{2,10},{3,5},{4,12},{5,7},{6,14},{7,1},{8,16},{9,11},{... | collective-permute-start | bytes 98312 | tf_op jit(solution)/shard_map/ppermute | solution.py:59
  48.9 3.0 %collective-permute-start.19 = (bf16[128,128]{1,0:T(8,128)(2,1)S(1)}, bf16[128,128]{1,0:T(8,128)(2,1)S(1)}, u32[]{:S(2)}, u32[]{:S(2)}) collective-permute-start(bf16[128,128]{1,0:T(8,128)(2,1)S(1)} %hidden.1), channel_id=1, source_target_pairs={{0,24},{1,7},{2,26},{3,1},{4,28},{5,3},{6,30},{7,5},{8,0},{9,15},{... | collective-permute-start | bytes 98312 | tf_op jit(solution)/shard_map/ppermute | solution.py:59
  51.9 8.6 %collective-permute-start.21 = (bf16[4,128,128]{2,1,0:T(8,128)(2,1)S(1)}, bf16[4,128,128]{2,1,0:T(8,128)(2,1)S(1)}, u32[]{:S(2)}, u32[]{:S(2)}) collective-permute-start(bf16[4,128,128]{2,1,0:T(8,128)(2,1)S(1)} %pad_maximum_fusion.refs_0_), channel_id=1, source_target_pairs={{0,4},{1,17},{2,6},{3,19},{4,0},{5,21},{6,2},{7,23},{8,12},{9,25},... | collective-permute-start | bytes 393224 | tf_op jit(solution)/shard_map/ppermute | solution.py:63
  52.8 9.8 %collective-permute-start.22 = (bf16[4,128,128]{2,1,0:T(8,128)(2,1)S(1)}, bf16[4,128,128]{2,1,0:T(8,128)(2,1)S(1)}, u32[]{:S(2)}, u32[]{:S(2)}) collective-permute-start(bf16[4,128,128]{2,1,0:T(8,128)(2,1)S(1)} %pad_maximum_fusion.refs_0_), channel_id=1, source_target_pairs={{0,2},{1,9},{2,4},{3,11},{4,6},{5,13},{6,0},{7,15},{8,10},{9,17},{... | collective-permute-start | bytes 393224 | tf_op jit(solution)/shard_map/ppermute | solution.py:63
  54.9 9.1 %collective-permute-start.23 = (bf16[4,128,128]{2,1,0:T(8,128)(2,1)S(1)}, bf16[4,128,128]{2,1,0:T(8,128)(2,1)S(1)}, u32[]{:S(2)}, u32[]{:S(2)}) collective-permute-start(bf16[4,128,128]{2,1,0:T(8,128)(2,1)S(1)} %pad_maximum_fusion.refs_0_), channel_id=1, source_target_pairs={{0,6},{1,25},{2,0},{3,27},{4,2},{5,29},{6,4},{7,31},{8,14},{9,1},{... | collective-permute-start | bytes 393224 | tf_op jit(solution)/shard_map/ppermute | solution.py:63
  55.5 8.5 %collective-permute-start.20 = (bf16[4,128,128]{2,1,0:T(8,128)(2,1)S(1)}, bf16[4,128,128]{2,1,0:T(8,128)(2,1)S(1)}, u32[]{:S(2)}, u32[]{:S(2)}) collective-permute-start(bf16[4,128,128]{2,1,0:T(8,128)(2,1)S(1)} %pad_maximum_fusion.refs_0_), channel_id=1, source_target_pairs={{0,1},{1,0},{2,3},{3,2},{4,5},{5,4},{6,7},{7,6},{8,9},{9,8},{10,11... | collective-permute-start | bytes 393224 | tf_op jit(solution)/shard_map/ppermute | solution.py:67
  60.5 3.8 %collective-permute-start.24 = (bf16[4,128,128]{2,1,0:T(8,128)(2,1)S(1)}, bf16[4,128,128]{2,1,0:T(8,128)(2,1)S(1)}, u32[]{:S(2)}, u32[]{:S(2)}) collective-permute-start(bf16[4,128,128]{2,1,0:T(8,128)(2,1)S(1)} %collective-permute-done.21.refs_2_), channel_id=1, source_target_pairs={{0,1},{1,0},{2,3},{3,2},{4,5},{5,4},{6,7},{7,6},{8,9},{9,8},{10,11... | collective-permute-start | bytes 393224 | tf_op jit(solution)/shard_map/ppermute | solution.py:67
  62.6 2.3 %collective-permute-start.25 = (bf16[4,128,128]{2,1,0:T(8,128)(2,1)S(1)}, bf16[4,128,128]{2,1,0:T(8,128)(2,1)S(1)}, u32[]{:S(2)}, u32[]{:S(2)}) collective-permute-start(bf16[4,128,128]{2,1,0:T(8,128)(2,1)S(1)} %collective-permute-done.22.refs_3_), channel_id=1, source_target_pairs={{0,1},{1,0},{2,3},{3,2},{4,5},{5,4},{6,7},{7,6},{8,9},{9,8},{10,11... | collective-permute-start | bytes 393224 | tf_op jit(solution)/shard_map/ppermute | solution.py:67
  64.0 1.3 %collective-permute-start.26 = (bf16[4,128,128]{2,1,0:T(8,128)(2,1)S(1)}, bf16[4,128,128]{2,1,0:T(8,128)(2,1)S(1)}, u32[]{:S(2)}, u32[]{:S(2)}) collective-permute-start(bf16[4,128,128]{2,1,0:T(8,128)(2,1)S(1)} %collective-permute-done.23.refs_4_), channel_id=1, source_target_pairs={{0,1},{1,0},{2,3},{3,2},{4,5},{5,4},{6,7},{7,6},{8,9},{9,8},{10,11... | collective-permute-start | bytes 393224 | tf_op jit(solution)/shard_map/ppermute | solution.py:67
  64.3 5.8 %copy-start.1 = (f32[153]{0:T(256)S(1)}, f32[153]{0:T(256)}, u32[]{:S(2)}) copy-start(f32[153]{0:T(256)} %param.13) | copy-start | bytes 1840
  66.6 6.0 %collective-permute-start.27 = (bf16[160,384]{1,0:T(8,128)(2,1)S(1)}, bf16[160,384]{1,0:T(8,128)(2,1)S(1)}, u32[]{:S(2)}, u32[]{:S(2)}) collective-permute-start(bf16[160,384]{1,0:T(8,128)(2,1)S(1)} %get-tuple-element.42.p0), channel_id=1, source_target_pairs={{0,32},{32,64},{64,96},{96,0},{1,33},{33,65},{65,97},{97,1},{2,34}... | collective-permute-start | bytes 368648 | tf_op jit(solution)/shard_map/ppermute | solution.py:71
  66.7 9.4 %collective-permute-start.28 = (bf16[160,384]{1,0:T(8,128)(2,1)S(1)}, bf16[160,384]{1,0:T(8,128)(2,1)S(1)}, u32[]{:S(2)}, u32[]{:S(2)}) collective-permute-start(bf16[160,384]{1,0:T(8,128)(2,1)S(1)} %get-tuple-element.42.p0), channel_id=1, source_target_pairs={{0,64},{32,96},{64,0},{96,32},{1,65},{33,97},{65,1},{97,33},{2,66}... | collective-permute-start | bytes 368648 | tf_op jit(solution)/shard_map/ppermute | solution.py:71
  70.1 5.9 %collective-permute-start.29 = (bf16[160,384]{1,0:T(8,128)(2,1)S(1)}, bf16[160,384]{1,0:T(8,128)(2,1)S(1)}, u32[]{:S(2)}, u32[]{:S(2)}) collective-permute-start(bf16[160,384]{1,0:T(8,128)(2,1)S(1)} %get-tuple-element.42.p0), channel_id=1, source_target_pairs={{0,96},{32,0},{64,32},{96,64},{1,97},{33,1},{65,33},{97,65},{2,98}... | collective-permute-start | bytes 368648 | tf_op jit(solution)/shard_map/ppermute | solution.py:71

commit v8 on v7

--- a/solution.py
+++ b/solution.py
@@ -316,7 +316,7 @@
     out[...] = part.T[0:160].astype(bf16)
 
 
-def sum_kernel(p0, p1, p2, p3, b_out, out):
+def sum_kernel(p0, p2, p1, p3, b_out, out):
     total = (p0[...].astype(f32) + p2[...].astype(f32)) + (p1[...].astype(f32) + p3[...].astype(f32))
     bias = jnp.broadcast_to(b_out[...], (TILE, 256)).T[:, 0:1]
     out[...] = total[0:CLS] + bias[0:CLS]
@@ -399,7 +399,7 @@
         compiler_params=params(), cost_estimate=cost(2 * 384 * 4096 * 256, 5e6), name="scores",
     )(adj2, degree, z_all, *((z_rows, z_other)[p][t] for t, p in late))
     parts = {0: part} | {s: along_feat(part, s) for s in (2, 1, 3)}
-    parts = [parts[s] for s in range(NF)]
+    parts = [parts[s] for s in SHIFTS]
     return pl.pallas_call(
         sum_kernel, out_shape=jax.ShapeDtypeStruct((CLS, ROWS), f32),
         in_specs=[VM] * 5, out_specs=VM,

time: 77 us -> 77 us (level)
  no operation moved by 1% of the time
where the time goes in v8:
time: 77 us; the launch traced here: 76.9 us
  starting transfers between devices  43.2 us (56%)
  Pallas kernels  17.2 us (22%)
  waiting for transfers between devices  16.3 us (21%)
    ppermute x10, starting transfers between devices, swap(): return lax.ppermute(value, 'vert', positions(lambda x, z, c: (x, z, 1 - c)))  13.2 us
    ppermute x6, starting transfers between devices, first_axis(): lax.ppermute(value, 'vert', positions(lambda x, z, c: (x + shift * (1 - c...  10.6 us
    ppermute x7, starting transfers between devices, along_feat(): lax.ppermute(value, 'feat', [(i, (i + shift) % NF) for i in range(NF)])  9.39 us
    ppermute x7, waiting for transfers between devices, along_feat(): lax.ppermute(value, 'feat', [(i, (i + shift) % NF) for i in range(NF)])  7.65 us
    ppermute x6, starting transfers between devices, second_axis(): lax.ppermute(value, 'vert', positions(lambda x, z, c: (x + shift * c, z +...  7.27 us
    pallas_call x1, Pallas kernels, second_half(): pl.pallas_call(functools.partial(adjacency_kernel, 1), in_specs=[HB] * 2...  5.54 us
    ppermute x1, waiting for transfers between devices, both_sides(): return lax.ppermute(value, ('feat', 'vert'), pairs)  4.26 us
    pallas_call x1, Pallas kernels, first_half(): pl.pallas_call(functools.partial(adjacency_kernel, 0), in_specs=[HB] * 5,...  4.18 us
  transfers between devices with their start and end apart: 30, of which 12 were waited for; matrix products, arithmetic and copies ran while one was open for 0% of the time, Pallas kernels for 17%

profile of v8, /device:TPU:1, one launch (start us, length us, event | category | flops | bytes accessed | tf_op | source)
XLA Modules:
  0.0 76.9 jit_solution(1185234453456471017)
XLA Ops:
  0.0 4.4 %collective-permute-start = (bf16[192,384]{1,0:T(8,128)(2,1)}, bf16[192,384]{1,0:T(8,128)(2,1)S(1)}, u32[]{:S(2)}, u32[]{:S(2)}) collective-permute-start(bf16[192,384]{1,0:T(8,128)(2,1)} %bitcast.9), channel_id=1, source_target_pairs={{0,16},{1,5},{2,18},{3,7},{4,20},{5,1},{6,22},{7,3},{8,24},{9,13},... | collective-permute-start | bytes 442376 | tf_op jit(solution)/shard_map/ppermute | solution.py:59
  4.4 0.7 collective-permute-start.1
  5.2 1.9 %collective-permute-start.2 = (bf16[192,384]{1,0:T(8,128)(2,1)}, bf16[192,384]{1,0:T(8,128)(2,1)S(1)}, u32[]{:S(2)}, u32[]{:S(2)}) collective-permute-start(bf16[192,384]{1,0:T(8,128)(2,1)} %bitcast.11), channel_id=1, source_target_pairs={{0,24},{1,7},{2,26},{3,1},{4,28},{5,3},{6,30},{7,5},{8,0},{9,15},{... | collective-permute-start | bytes 442376 | tf_op jit(solution)/shard_map/ppermute | solution.py:59
  7.1 4.2 %adjacency_first.1 = (bf16[384,12288]{1,0:T(8,128)(2,1)S(1)}, bf16[384,4096]{1,0:T(8,128)(2,1)S(1)}, f32[384,128]{1,0:T(8,128)S(1)}, bf16[2,256,512]{2,1,0:T(8,128)(2,1)S(1)}, bf16[256,512]{1,0:T(8,128)(2,1)S(1)}) custom-call(s32[3,96]{1,0:T(4,128)} %mask.3, s32[384,12288]{1,0:T(8,128)} %counts.3, bf16[192,1024]{1,0:T(8,128)(2,1)} %refs_0_.1, ...), custom_call_target="tpu_custom_call" | custom-call | flops 1200000000 | bytes 16000000 | tf_op jit(solution)/shard_map/adjacency_first/pallas_call | solution.py:168
  11.3 0.0 collective-permute-done.b
  11.3 0.0 collective-permute-done.1.c
  11.3 0.0 collective-permute-done.2.d
  11.3 0.1 stack.21.refs_0_
  11.4 0.7 collective-permute-start.3
  12.1 2.0 %collective-permute-start.6 = (bf16[4,192,384]{2,1,0:T(8,128)(2,1)S(1)}, bf16[4,192,384]{2,1,0:T(8,128)(2,1)S(1)}, u32[]{:S(2)}, u32[]{:S(2)}) collective-permute-start(bf16[4,192,384]{2,1,0:T(8,128)(2,1)S(1)} %stack.21.refs_0_), channel_id=1, source_target_pairs={{0,6},{1,25},{2,0},{3,27},{4,2},{5,29},{6,4},{7,31},{8,14},{9,1},{... | collective-permute-start | bytes 1769480 | tf_op jit(solution)/shard_map/ppermute | solution.py:63
  14.2 0.0 collective-permute-start.5
  14.2 2.7 %collective-permute-start.4 = (bf16[2,256,512]{2,1,0:T(8,128)(2,1)S(1)}, bf16[2,256,512]{2,1,0:T(8,128)(2,1)S(1)}, u32[]{:S(2)}, u32[]{:S(2)}) collective-permute-start(bf16[2,256,512]{2,1,0:T(8,128)(2,1)S(1)} %get-tuple-element.31.own), channel_id=1, source_target_pairs={{0,32},{32,64},{64,96},{96,0},{1,97},{33,1},{65,33},{97,65},{2,34}... | collective-permute-start | bytes 1572872 | tf_op jit(solution)/shard_map/ppermute | solution.py:76
  16.9 1.6 %collective-permute-start.10 = (bf16[4,192,384]{2,1,0:T(8,128)(2,1)S(1)}, bf16[4,192,384]{2,1,0:T(8,128)(2,1)S(1)}, u32[]{:S(2)}, u32[]{:S(2)}) collective-permute-start(bf16[4,192,384]{2,1,0:T(8,128)(2,1)S(1)} %stack.21.refs_0_), channel_id=1, source_target_pairs={{0,4},{1,17},{2,6},{3,19},{4,0},{5,21},{6,2},{7,23},{8,12},{9,25},... | collective-permute-start | bytes 1769480 | tf_op jit(solution)/shard_map/ppermute | solution.py:63
  18.5 0.3 collective-permute-start.7
  18.9 5.5 %adjacency_second.1 = (bf16[384,12288]{1,0:T(8,128)(2,1)S(1)}, bf16[384,4096]{1,0:T(8,128)(2,1)S(1)}, f32[384,128]{1,0:T(8,128)S(1)}) custom-call(s32[3,96]{1,0:T(4,128)} %mask.3, s32[384,12288]{1,0:T(8,128)} %counts.3, bf16[384,12288]{1,0:T(8,128)(2,1)S(1)} %get-tuple-element.24.refs_0_, ...), custom_call_target="tpu_custom_call", output_to_operand_aliasing={{0}: (2, {}), {1}: (3, {}), {2}: (4, {})} | custom-call | flops 1200000000 | bytes 16000000 | tf_op jit(solution)/shard_map/adjacency_second/pallas_call | solution.py:189
  24.4 4.3 %collective-permute-done.4.refs_2_.side = bf16[2,256,512]{2,1,0:T(8,128)(2,1)S(1)} collective-permute-done((bf16[2,256,512]{2,1,0:T(8,128)(2,1)S(1)}, bf16[2,256,512]{2,1,0:T(8,128)(2,1)S(1)}, u32[]{:S(2)}, u32[]{:S(2)}) %collective-permute-start.4) | collective-permute-done | bytes 524320 | tf_op jit(solution)/shard_map/ppermute | solution.py:76
  28.7 1.0 %product_first.1.before = f32[384,192]{1,0:T(8,128)S(1)} custom-call(bf16[384,12288]{1,0:T(8,128)(2,1)S(1)} %get-tuple-element.30.adj, bf16[4,192,384]{2,1,0:T(8,128)(2,1)S(1)} %stack.21.refs_0_, bf16[4,192,384]{2,1,0:T(8,128)(2,1)S(1)} %collective-permute-done.3.refs_3_.refs_1_, bf16[2,256,512]{2,1,0:T(8,128)(2,1)S(1)} %collective-permute-done.4.refs_2_.side), custom_call_target="tpu_custom_call" | custom-call | flops 603979776 | bytes 3600000 | tf_op jit(solution)/shard_map/product_first/pallas_call | solution.py:348
  29.7 0.0 collective-permute-done.6.refs_1_
  29.7 1.1 %collective-permute-done.5.refs_0_ = bf16[4,192,384]{2,1,0:T(8,128)(2,1)S(1)} collective-permute-done((bf16[4,192,384]{2,1,0:T(8,128)(2,1)S(1)}, bf16[4,192,384]{2,1,0:T(8,128)(2,1)S(1)}, u32[]{:S(2)}, u32[]{:S(2)}) %collective-permute-start.5) | collective-permute-done | bytes 589856 | tf_op jit(solution)/shard_map/ppermute | solution.py:63
  30.7 2.9 %collective-permute-start.9 = (bf16[4,192,384]{2,1,0:T(8,128)(2,1)S(1)}, bf16[4,192,384]{2,1,0:T(8,128)(2,1)S(1)}, u32[]{:S(2)}, u32[]{:S(2)}) collective-permute-start(bf16[4,192,384]{2,1,0:T(8,128)(2,1)S(1)} %collective-permute-done.6.refs_1_), channel_id=1, source_target_pairs={{0,1},{1,0},{2,3},{3,2},{4,5},{5,4},{6,7},{7,6},{8,9},{9,8},{10,11... | collective-permute-start | bytes 1769480 | tf_op jit(solution)/shard_map/ppermute | solution.py:67
  33.7 0.0 collective-permute-start.8
  33.7 1.0 %product_next.1.before = f32[384,192]{1,0:T(8,128)S(1)} custom-call(bf16[384,12288]{1,0:T(8,128)(2,1)S(1)} %get-tuple-element.30.adj, f32[384,192]{1,0:T(8,128)S(1)} %product_first.1.before, bf16[4,192,384]{2,1,0:T(8,128)(2,1)S(1)} %collective-permute-done.5.refs_0_, bf16[4,192,384]{2,1,0:T(8,128)(2,1)S(1)} %collective-permute-done.6.refs_1_, ...), custom_call_target="tpu_custom_call" | custom-call | flops 603979776 | bytes 3600000 | tf_op jit(solution)/shard_map/product_next/pallas_call | solution.py:348
  34.7 0.6 collective-permute-start.11
  35.3 0.1 collective-permute-start.12
  35.4 0.4 collective-permute-start.13
  35.8 0.4 collective-permute-done.8.refs_0_
  36.1 1.4 %product_more.1.before = f32[384,192]{1,0:T(8,128)S(1)} custom-call(bf16[384,12288]{1,0:T(8,128)(2,1)S(1)} %get-tuple-element.30.adj, f32[384,192]{1,0:T(8,128)S(1)} %product_next.1.before, bf16[4,192,384]{2,1,0:T(8,128)(2,1)S(1)} %collective-permute-done.8.refs_0_, bf16[4,192,384]{2,1,0:T(8,128)(2,1)S(1)} %collective-permute-done.9.refs_1_, ...), custom_call_target="tpu_custom_call" | custom-call | flops 905969664 | bytes 5400000 | tf_op jit(solution)/shard_map/product_more/pallas_call | solution.py:348
  37.6 0.6 collective-permute-done.13.refs_2_.far
  38.1 0.0 collective-permute-done.11.refs_0_
  38.1 0.6 product_last.1
  38.8 1.4 %collective-permute-start.14 = (bf16[96,192]{1,0:T(8,128)(2,1)S(1)}, bf16[96,192]{1,0:T(8,128)(2,1)S(1)}, u32[]{:S(2)}, u32[]{:S(2)}) collective-permute-start(bf16[96,192]{1,0:T(8,128)(2,1)S(1)} %get-tuple-element.39), channel_id=1, source_target_pairs={{0,32},{32,64},{64,96},{96,0},{1,33},{33,65},{65,97},{97,1},{2,34}... | collective-permute-start | bytes 110600 | tf_op jit(solution)/shard_map/ppermute | solution.py:71
  40.1 2.6 %collective-permute-start.15 = (bf16[96,192]{1,0:T(8,128)(2,1)S(1)}, bf16[96,192]{1,0:T(8,128)(2,1)S(1)}, u32[]{:S(2)}, u32[]{:S(2)}) collective-permute-start(bf16[96,192]{1,0:T(8,128)(2,1)S(1)} %get-tuple-element.40), channel_id=1, source_target_pairs={{0,64},{32,96},{64,0},{96,32},{1,65},{33,97},{65,1},{97,33},{2,66}... | collective-permute-start | bytes 110600 | tf_op jit(solution)/shard_map/ppermute | solution.py:71
  42.8 1.1 %collective-permute-start.16 = (bf16[96,192]{1,0:T(8,128)(2,1)S(1)}, bf16[96,192]{1,0:T(8,128)(2,1)S(1)}, u32[]{:S(2)}, u32[]{:S(2)}) collective-permute-start(bf16[96,192]{1,0:T(8,128)(2,1)S(1)} %get-tuple-element.41), channel_id=1, source_target_pairs={{0,96},{32,0},{64,32},{96,64},{1,97},{33,1},{65,33},{97,65},{2,98}... | collective-permute-start | bytes 110600 | tf_op jit(solution)/shard_map/ppermute | solution.py:71
  43.8 1.2 %collective-permute-done.15.g2 = bf16[96,192]{1,0:T(8,128)(2,1)S(1)} collective-permute-done((bf16[96,192]{1,0:T(8,128)(2,1)S(1)}, bf16[96,192]{1,0:T(8,128)(2,1)S(1)}, u32[]{:S(2)}, u32[]{:S(2)}) %collective-permute-start.15) | collective-permute-done | bytes 36896 | tf_op jit(solution)/shard_map/ppermute | solution.py:71
  45.0 1.0 %collective-permute-done.16.g3 = bf16[96,192]{1,0:T(8,128)(2,1)S(1)} collective-permute-done((bf16[96,192]{1,0:T(8,128)(2,1)S(1)}, bf16[96,192]{1,0:T(8,128)(2,1)S(1)}, u32[]{:S(2)}, u32[]{:S(2)}) %collective-permute-start.16) | collective-permute-done | bytes 36896 | tf_op jit(solution)/shard_map/ppermute | solution.py:71
  46.0 1.0 %hidden.1 = bf16[128,128]{1,0:T(8,128)(2,1)S(1)} custom-call(bf16[96,192]{1,0:T(8,128)(2,1)S(1)} %get-tuple-element.38.g0, bf16[96,192]{1,0:T(8,128)(2,1)S(1)} %collective-permute-done.14.g1, bf16[96,192]{1,0:T(8,128)(2,1)S(1)} %collective-permute-done.15.g2, bf16[96,192]{1,0:T(8,128)(2,1)S(1)} %collective-permute-done.16.g3, ...), custom_call_target="tpu_custom_call" | custom-call | flops 150994944 | bytes 2000000 | tf_op jit(solution)/shard_map/hidden/pallas_call | solution.py:374
  47.0 0.8 %collective-permute-start.17 = (bf16[128,128]{1,0:T(8,128)(2,1)S(1)}, bf16[128,128]{1,0:T(8,128)(2,1)S(1)}, u32[]{:S(2)}, u32[]{:S(2)}) collective-permute-start(bf16[128,128]{1,0:T(8,128)(2,1)S(1)} %hidden.1), channel_id=1, source_target_pairs={{0,16},{1,5},{2,18},{3,7},{4,20},{5,1},{6,22},{7,3},{8,24},{9,13},... | collective-permute-start | bytes 98312 | tf_op jit(solution)/shard_map/ppermute | solution.py:59
  47.9 1.0 %collective-permute-start.18 = (bf16[128,128]{1,0:T(8,128)(2,1)S(1)}, bf16[128,128]{1,0:T(8,128)(2,1)S(1)}, u32[]{:S(2)}, u32[]{:S(2)}) collective-permute-start(bf16[128,128]{1,0:T(8,128)(2,1)S(1)} %hidden.1), channel_id=1, source_target_pairs={{0,8},{1,3},{2,10},{3,5},{4,12},{5,7},{6,14},{7,1},{8,16},{9,11},{... | collective-permute-start | bytes 98312 | tf_op jit(solution)/shard_map/ppermute | solution.py:59
  48.9 1.7 %collective-permute-start.19 = (bf16[128,128]{1,0:T(8,128)(2,1)S(1)}, bf16[128,128]{1,0:T(8,128)(2,1)S(1)}, u32[]{:S(2)}, u32[]{:S(2)}) collective-permute-start(bf16[128,128]{1,0:T(8,128)(2,1)S(1)} %hidden.1), channel_id=1, source_target_pairs={{0,24},{1,7},{2,26},{3,1},{4,28},{5,3},{6,30},{7,5},{8,0},{9,15},{... | collective-permute-start | bytes 98312 | tf_op jit(solution)/shard_map/ppermute | solution.py:59
  50.5 0.8 %collective-permute-done.17 = bf16[128,128]{1,0:T(8,128)(2,1)S(1)} collective-permute-done((bf16[128,128]{1,0:T(8,128)(2,1)S(1)}, bf16[128,128]{1,0:T(8,128)(2,1)S(1)}, u32[]{:S(2)}, u32[]{:S(2)}) %collective-permute-start.17) | collective-permute-done | bytes 32800 | tf_op jit(solution)/shard_map/ppermute | solution.py:59
  51.4 0.4 collective-permute-done.18
  51.8 0.0 collective-permute-done.19
  51.9 1.0 %collective-permute-start.21 = (bf16[4,128,128]{2,1,0:T(8,128)(2,1)S(1)}, bf16[4,128,128]{2,1,0:T(8,128)(2,1)S(1)}, u32[]{:S(2)}, u32[]{:S(2)}) collective-permute-start(bf16[4,128,128]{2,1,0:T(8,128)(2,1)S(1)} %pad_maximum_fusion.refs_0_), channel_id=1, source_target_pairs={{0,4},{1,17},{2,6},{3,19},{4,0},{5,21},{6,2},{7,23},{8,12},{9,25},... | collective-permute-start | bytes 393224 | tf_op jit(solution)/shard_map/ppermute | solution.py:63
  52.8 2.1 %collective-permute-start.22 = (bf16[4,128,128]{2,1,0:T(8,128)(2,1)S(1)}, bf16[4,128,128]{2,1,0:T(8,128)(2,1)S(1)}, u32[]{:S(2)}, u32[]{:S(2)}) collective-permute-start(bf16[4,128,128]{2,1,0:T(8,128)(2,1)S(1)} %pad_maximum_fusion.refs_0_), channel_id=1, source_target_pairs={{0,2},{1,9},{2,4},{3,11},{4,6},{5,13},{6,0},{7,15},{8,10},{9,17},{... | collective-permute-start | bytes 393224 | tf_op jit(solution)/shard_map/ppermute | solution.py:63
  54.9 0.6 collective-permute-start.23
  55.5 5.0 %collective-permute-start.20 = (bf16[4,128,128]{2,1,0:T(8,128)(2,1)S(1)}, bf16[4,128,128]{2,1,0:T(8,128)(2,1)S(1)}, u32[]{:S(2)}, u32[]{:S(2)}) collective-permute-start(bf16[4,128,128]{2,1,0:T(8,128)(2,1)S(1)} %pad_maximum_fusion.refs_0_), channel_id=1, source_target_pairs={{0,1},{1,0},{2,3},{3,2},{4,5},{5,4},{6,7},{7,6},{8,9},{9,8},{10,11... | collective-permute-start | bytes 393224 | tf_op jit(solution)/shard_map/ppermute | solution.py:67
  60.5 0.0 collective-permute-done.21.refs_2_
  60.5 2.1 %collective-permute-start.24 = (bf16[4,128,128]{2,1,0:T(8,128)(2,1)S(1)}, bf16[4,128,128]{2,1,0:T(8,128)(2,1)S(1)}, u32[]{:S(2)}, u32[]{:S(2)}) collective-permute-start(bf16[4,128,128]{2,1,0:T(8,128)(2,1)S(1)} %collective-permute-done.21.refs_2_), channel_id=1, source_target_pairs={{0,1},{1,0},{2,3},{3,2},{4,5},{5,4},{6,7},{7,6},{8,9},{9,8},{10,11... | collective-permute-start | bytes 393224 | tf_op jit(solution)/shard_map/ppermute | solution.py:67
  62.6 0.0 collective-permute-done.22.refs_3_
  62.6 1.3 %collective-permute-start.25 = (bf16[4,128,128]{2,1,0:T(8,128)(2,1)S(1)}, bf16[4,128,128]{2,1,0:T(8,128)(2,1)S(1)}, u32[]{:S(2)}, u32[]{:S(2)}) collective-permute-start(bf16[4,128,128]{2,1,0:T(8,128)(2,1)S(1)} %collective-permute-done.22.refs_3_), channel_id=1, source_target_pairs={{0,1},{1,0},{2,3},{3,2},{4,5},{5,4},{6,7},{7,6},{8,9},{9,8},{10,11... | collective-permute-start | bytes 393224 | tf_op jit(solution)/shard_map/ppermute | solution.py:67
  64.0 0.0 collective-permute-start.26
  64.0 0.3 unpack.1.before
  64.3 0.0 copy-start.1
  64.3 0.0 collective-permute-done.24.refs_0_
  64.3 0.7 collective-permute-done.25.refs_1_
  65.0 0.4 collective-permute-done.26.refs_2_
  65.3 1.2 %scores.1 = (bf16[160,384]{1,0:T(8,128)(2,1)S(1)}, bf16[4096,256]{1,0:T(8,128)(2,1)S(1)}) custom-call(bf16[384,4096]{1,0:T(8,128)(2,1)S(1)} %get-tuple-element.28.adj2, f32[384,128]{1,0:T(8,128)S(1)} %get-tuple-element.29.degree.inverse, bf16[4096,256]{1,0:T(8,128)(2,1)S(1)} %unpack.1.before, ...), custom_call_target="tpu_custom_call", output_to_operand_aliasing={{1}: (2, {})} | custom-call | flops 805306368 | bytes 5000000 | tf_op jit(solution)/shard_map/scores/pallas_call | solution.py:395
  66.6 1.3 %collective-permute-start.27 = (bf16[160,384]{1,0:T(8,128)(2,1)S(1)}, bf16[160,384]{1,0:T(8,128)(2,1)S(1)}, u32[]{:S(2)}, u32[]{:S(2)}) collective-permute-start(bf16[160,384]{1,0:T(8,128)(2,1)S(1)} %get-tuple-element.42.p0), channel_id=1, source_target_pairs={{0,64},{32,96},{64,0},{96,32},{1,65},{33,97},{65,1},{97,33},{2,66}... | collective-permute-start | bytes 368648 | tf_op jit(solution)/shard_map/ppermute | solution.py:71
  67.9 1.6 %collective-permute-start.28 = (bf16[160,384]{1,0:T(8,128)(2,1)S(1)}, bf16[160,384]{1,0:T(8,128)(2,1)S(1)}, u32[]{:S(2)}, u32[]{:S(2)}) collective-permute-start(bf16[160,384]{1,0:T(8,128)(2,1)S(1)} %get-tuple-element.42.p0), channel_id=1, source_target_pairs={{0,32},{32,64},{64,96},{96,0},{1,33},{33,65},{65,97},{97,1},{2,34}... | collective-permute-start | bytes 368648 | tf_op jit(solution)/shard_map/ppermute | solution.py:71
  69.5 1.1 %collective-permute-start.29 = (bf16[160,384]{1,0:T(8,128)(2,1)S(1)}, bf16[160,384]{1,0:T(8,128)(2,1)S(1)}, u32[]{:S(2)}, u32[]{:S(2)}) collective-permute-start(bf16[160,384]{1,0:T(8,128)(2,1)S(1)} %get-tuple-element.42.p0), channel_id=1, source_target_pairs={{0,96},{32,0},{64,32},{96,64},{1,97},{33,1},{65,33},{97,65},{2,98}... | collective-permute-start | bytes 368648 | tf_op jit(solution)/shard_map/ppermute | solution.py:71
  70.6 2.3 %collective-permute-done.27.p2 = bf16[160,384]{1,0:T(8,128)(2,1)S(1)} collective-permute-done((bf16[160,384]{1,0:T(8,128)(2,1)S(1)}, bf16[160,384]{1,0:T(8,128)(2,1)S(1)}, u32[]{:S(2)}, u32[]{:S(2)}) %collective-permute-start.27) | collective-permute-done | bytes 122912 | tf_op jit(solution)/shard_map/ppermute | solution.py:71
  72.9 3.1 %collective-permute-done.28.p1 = bf16[160,384]{1,0:T(8,128)(2,1)S(1)} collective-permute-done((bf16[160,384]{1,0:T(8,128)(2,1)S(1)}, bf16[160,384]{1,0:T(8,128)(2,1)S(1)}, u32[]{:S(2)}, u32[]{:S(2)}) %collective-permute-start.28) | collective-permute-done | bytes 122912 | tf_op jit(solution)/shard_map/ppermute | solution.py:71
  76.0 0.0 collective-permute-done.29.p3
  76.0 0.9 %sum.1 = f32[153,384]{1,0:T(8,128)} custom-call(bf16[160,384]{1,0:T(8,128)(2,1)S(1)} %get-tuple-element.42.p0, bf16[160,384]{1,0:T(8,128)(2,1)S(1)} %collective-permute-done.27.p2, bf16[160,384]{1,0:T(8,128)(2,1)S(1)} %collective-permute-done.28.p1, bf16[160,384]{1,0:T(8,128)(2,1)S(1)} %collective-permute-done.29.p3, f32[1,256]{1,0:T(1,128)S(1)} %bitcast.14), custom_call_target="tpu_custom_call" | custom-call | flops 300000 | bytes 800000 | tf_op jit(solution)/shard_map/sum/pallas_call | solution.py:403
  (13 shorter events, 0.0 us)
Async XLA Ops:
  0.0 11.3 %collective-permute-start = (bf16[192,384]{1,0:T(8,128)(2,1)}, bf16[192,384]{1,0:T(8,128)(2,1)S(1)}, u32[]{:S(2)}, u32[]{:S(2)}) collective-permute-start(bf16[192,384]{1,0:T(8,128)(2,1)} %bitcast.9), channel_id=1, source_target_pairs={{0,16},{1,5},{2,18},{3,7},{4,20},{5,1},{6,22},{7,3},{8,24},{9,13},... | collective-permute-start | bytes 442376 | tf_op jit(solution)/shard_map/ppermute | solution.py:59
  4.4 6.9 %collective-permute-start.1 = (bf16[192,384]{1,0:T(8,128)(2,1)}, bf16[192,384]{1,0:T(8,128)(2,1)S(1)}, u32[]{:S(2)}, u32[]{:S(2)}) collective-permute-start(bf16[192,384]{1,0:T(8,128)(2,1)} %bitcast.10), channel_id=1, source_target_pairs={{0,8},{1,3},{2,10},{3,5},{4,12},{5,7},{6,14},{7,1},{8,16},{9,11},{... | collective-permute-start | bytes 442376 | tf_op jit(solution)/shard_map/ppermute | solution.py:59
  5.2 6.2 %collective-permute-start.2 = (bf16[192,384]{1,0:T(8,128)(2,1)}, bf16[192,384]{1,0:T(8,128)(2,1)S(1)}, u32[]{:S(2)}, u32[]{:S(2)}) collective-permute-start(bf16[192,384]{1,0:T(8,128)(2,1)} %bitcast.11), channel_id=1, source_target_pairs={{0,24},{1,7},{2,26},{3,1},{4,28},{5,3},{6,30},{7,5},{8,0},{9,15},{... | collective-permute-start | bytes 442376 | tf_op jit(solution)/shard_map/ppermute | solution.py:59
  7.1 4.2 %copy-start = (bf16[384,192]{0,1:T(8,128)(2,1)S(1)}, bf16[384,192]{0,1:T(8,128)(2,1)}, u32[]{:S(2)}) copy-start(bf16[384,192]{0,1:T(8,128)(2,1)} %param.7) | copy-start | bytes 442372
  11.4 7.1 %collective-permute-start.3 = (bf16[4,192,384]{2,1,0:T(8,128)(2,1)S(1)}, bf16[4,192,384]{2,1,0:T(8,128)(2,1)S(1)}, u32[]{:S(2)}, u32[]{:S(2)}) collective-permute-start(bf16[4,192,384]{2,1,0:T(8,128)(2,1)S(1)} %stack.21.refs_0_), channel_id=1, source_target_pairs={{0,1},{1,0},{2,3},{3,2},{4,5},{5,4},{6,7},{7,6},{8,9},{9,8},{10,11... | collective-permute-start | bytes 1769480 | tf_op jit(solution)/shard_map/ppermute | solution.py:67
  12.1 17.5 %collective-permute-start.6 = (bf16[4,192,384]{2,1,0:T(8,128)(2,1)S(1)}, bf16[4,192,384]{2,1,0:T(8,128)(2,1)S(1)}, u32[]{:S(2)}, u32[]{:S(2)}) collective-permute-start(bf16[4,192,384]{2,1,0:T(8,128)(2,1)S(1)} %stack.21.refs_0_), channel_id=1, source_target_pairs={{0,6},{1,25},{2,0},{3,27},{4,2},{5,29},{6,4},{7,31},{8,14},{9,1},{... | collective-permute-start | bytes 1769480 | tf_op jit(solution)/shard_map/ppermute | solution.py:63
  14.2 16.6 %collective-permute-start.5 = (bf16[4,192,384]{2,1,0:T(8,128)(2,1)S(1)}, bf16[4,192,384]{2,1,0:T(8,128)(2,1)S(1)}, u32[]{:S(2)}, u32[]{:S(2)}) collective-permute-start(bf16[4,192,384]{2,1,0:T(8,128)(2,1)S(1)} %stack.21.refs_0_), channel_id=1, source_target_pairs={{0,2},{1,9},{2,4},{3,11},{4,6},{5,13},{6,0},{7,15},{8,10},{9,17},{... | collective-permute-start | bytes 1769480 | tf_op jit(solution)/shard_map/ppermute | solution.py:63
  14.2 14.5 %collective-permute-start.4 = (bf16[2,256,512]{2,1,0:T(8,128)(2,1)S(1)}, bf16[2,256,512]{2,1,0:T(8,128)(2,1)S(1)}, u32[]{:S(2)}, u32[]{:S(2)}) collective-permute-start(bf16[2,256,512]{2,1,0:T(8,128)(2,1)S(1)} %get-tuple-element.31.own), channel_id=1, source_target_pairs={{0,32},{32,64},{64,96},{96,0},{1,97},{33,1},{65,33},{97,65},{2,34}... | collective-permute-start | bytes 1572872 | tf_op jit(solution)/shard_map/ppermute | solution.py:76
  16.9 16.8 %collective-permute-start.10 = (bf16[4,192,384]{2,1,0:T(8,128)(2,1)S(1)}, bf16[4,192,384]{2,1,0:T(8,128)(2,1)S(1)}, u32[]{:S(2)}, u32[]{:S(2)}) collective-permute-start(bf16[4,192,384]{2,1,0:T(8,128)(2,1)S(1)} %stack.21.refs_0_), channel_id=1, source_target_pairs={{0,4},{1,17},{2,6},{3,19},{4,0},{5,21},{6,2},{7,23},{8,12},{9,25},... | collective-permute-start | bytes 1769480 | tf_op jit(solution)/shard_map/ppermute | solution.py:63
  18.5 15.2 %collective-permute-start.7 = (bf16[256,512]{1,0:T(8,128)(2,1)S(1)}, bf16[256,512]{1,0:T(8,128)(2,1)S(1)}, u32[]{:S(2)}, u32[]{:S(2)}) collective-permute-start(bf16[256,512]{1,0:T(8,128)(2,1)S(1)} %get-tuple-element.27.after), channel_id=1, source_target_pairs={{0,64},{32,96},{64,0},{96,32},{1,65},{33,97},{65,1},{97,33},{2,66}... | collective-permute-start | bytes 786440 | tf_op jit(solution)/shard_map/ppermute | solution.py:71
  30.7 5.0 %collective-permute-start.9 = (bf16[4,192,384]{2,1,0:T(8,128)(2,1)S(1)}, bf16[4,192,384]{2,1,0:T(8,128)(2,1)S(1)}, u32[]{:S(2)}, u32[]{:S(2)}) collective-permute-start(bf16[4,192,384]{2,1,0:T(8,128)(2,1)S(1)} %collective-permute-done.6.refs_1_), channel_id=1, source_target_pairs={{0,1},{1,0},{2,3},{3,2},{4,5},{5,4},{6,7},{7,6},{8,9},{9,8},{10,11... | collective-permute-start | bytes 1769480 | tf_op jit(solution)/shard_map/ppermute | solution.py:67
  33.7 2.5 %collective-permute-start.8 = (bf16[4,192,384]{2,1,0:T(8,128)(2,1)S(1)}, bf16[4,192,384]{2,1,0:T(8,128)(2,1)S(1)}, u32[]{:S(2)}, u32[]{:S(2)}) collective-permute-start(bf16[4,192,384]{2,1,0:T(8,128)(2,1)S(1)} %collective-permute-done.5.refs_0_), channel_id=1, source_target_pairs={{0,1},{1,0},{2,3},{3,2},{4,5},{5,4},{6,7},{7,6},{8,9},{9,8},{10,11... | collective-permute-start | bytes 1769480 | tf_op jit(solution)/shard_map/ppermute | solution.py:67
  34.7 3.4 %collective-permute-start.11 = (bf16[4,192,384]{2,1,0:T(8,128)(2,1)S(1)}, bf16[4,192,384]{2,1,0:T(8,128)(2,1)S(1)}, u32[]{:S(2)}, u32[]{:S(2)}) collective-permute-start(bf16[4,192,384]{2,1,0:T(8,128)(2,1)S(1)} %collective-permute-done.10.refs_2_), channel_id=1, source_target_pairs={{0,1},{1,0},{2,3},{3,2},{4,5},{5,4},{6,7},{7,6},{8,9},{9,8},{10,11... | collective-permute-start | bytes 1769480 | tf_op jit(solution)/shard_map/ppermute | solution.py:67
  35.3 2.8 %collective-permute-start.12 = (bf16[2,256,512]{2,1,0:T(8,128)(2,1)S(1)}, bf16[2,256,512]{2,1,0:T(8,128)(2,1)S(1)}, u32[]{:S(2)}, u32[]{:S(2)}) collective-permute-start(bf16[2,256,512]{2,1,0:T(8,128)(2,1)S(1)} %collective-permute-done.4.refs_2_.side), channel_id=1, source_target_pairs={{0,1},{1,0},{2,3},{3,2},{4,5},{5,4},{6,7},{7,6},{8,9},{9,8},{10,11... | collective-permute-start | bytes 1572872 | tf_op jit(solution)/shard_map/ppermute | solution.py:67
  35.4 2.7 %collective-permute-start.13 = (bf16[256,512]{1,0:T(8,128)(2,1)S(1)}, bf16[256,512]{1,0:T(8,128)(2,1)S(1)}, u32[]{:S(2)}, u32[]{:S(2)}) collective-permute-start(bf16[256,512]{1,0:T(8,128)(2,1)S(1)} %collective-permute-done.7.refs_2_.near), channel_id=1, source_target_pairs={{0,1},{1,0},{2,3},{3,2},{4,5},{5,4},{6,7},{7,6},{8,9},{9,8},{10,11... | collective-permute-start | bytes 786440 | tf_op jit(solution)/shard_map/ppermute | solution.py:67
  38.8 5.1 %collective-permute-start.14 = (bf16[96,192]{1,0:T(8,128)(2,1)S(1)}, bf16[96,192]{1,0:T(8,128)(2,1)S(1)}, u32[]{:S(2)}, u32[]{:S(2)}) collective-permute-start(bf16[96,192]{1,0:T(8,128)(2,1)S(1)} %get-tuple-element.39), channel_id=1, source_target_pairs={{0,32},{32,64},{64,96},{96,0},{1,33},{33,65},{65,97},{97,1},{2,34}... | collective-permute-start | bytes 110600 | tf_op jit(solution)/shard_map/ppermute | solution.py:71
  40.1 4.9 %collective-permute-start.15 = (bf16[96,192]{1,0:T(8,128)(2,1)S(1)}, bf16[96,192]{1,0:T(8,128)(2,1)S(1)}, u32[]{:S(2)}, u32[]{:S(2)}) collective-permute-start(bf16[96,192]{1,0:T(8,128)(2,1)S(1)} %get-tuple-element.40), channel_id=1, source_target_pairs={{0,64},{32,96},{64,0},{96,32},{1,65},{33,97},{65,1},{97,33},{2,66}... | collective-permute-start | bytes 110600 | tf_op jit(solution)/shard_map/ppermute | solution.py:71
  42.8 3.2 %collective-permute-start.16 = (bf16[96,192]{1,0:T(8,128)(2,1)S(1)}, bf16[96,192]{1,0:T(8,128)(2,1)S(1)}, u32[]{:S(2)}, u32[]{:S(2)}) collective-permute-start(bf16[96,192]{1,0:T(8,128)(2,1)S(1)} %get-tuple-element.41), channel_id=1, source_target_pairs={{0,96},{32,0},{64,32},{96,64},{1,97},{33,1},{65,33},{97,65},{2,98}... | collective-permute-start | bytes 110600 | tf_op jit(solution)/shard_map/ppermute | solution.py:71
  47.0 4.3 %collective-permute-start.17 = (bf16[128,128]{1,0:T(8,128)(2,1)S(1)}, bf16[128,128]{1,0:T(8,128)(2,1)S(1)}, u32[]{:S(2)}, u32[]{:S(2)}) collective-permute-start(bf16[128,128]{1,0:T(8,128)(2,1)S(1)} %hidden.1), channel_id=1, source_target_pairs={{0,16},{1,5},{2,18},{3,7},{4,20},{5,1},{6,22},{7,3},{8,24},{9,13},... | collective-permute-start | bytes 98312 | tf_op jit(solution)/shard_map/ppermute | solution.py:59
  47.9 4.0 %collective-permute-start.18 = (bf16[128,128]{1,0:T(8,128)(2,1)S(1)}, bf16[128,128]{1,0:T(8,128)(2,1)S(1)}, u32[]{:S(2)}, u32[]{:S(2)}) collective-permute-start(bf16[128,128]{1,0:T(8,128)(2,1)S(1)} %hidden.1), channel_id=1, source_target_pairs={{0,8},{1,3},{2,10},{3,5},{4,12},{5,7},{6,14},{7,1},{8,16},{9,11},{... | collective-permute-start | bytes 98312 | tf_op jit(solution)/shard_map/ppermute | solution.py:59
  48.9 3.0 %collective-permute-start.19 = (bf16[128,128]{1,0:T(8,128)(2,1)S(1)}, bf16[128,128]{1,0:T(8,128)(2,1)S(1)}, u32[]{:S(2)}, u32[]{:S(2)}) collective-permute-start(bf16[128,128]{1,0:T(8,128)(2,1)S(1)} %hidden.1), channel_id=1, source_target_pairs={{0,24},{1,7},{2,26},{3,1},{4,28},{5,3},{6,30},{7,5},{8,0},{9,15},{... | collective-permute-start | bytes 98312 | tf_op jit(solution)/shard_map/ppermute | solution.py:59
  51.9 8.6 %collective-permute-start.21 = (bf16[4,128,128]{2,1,0:T(8,128)(2,1)S(1)}, bf16[4,128,128]{2,1,0:T(8,128)(2,1)S(1)}, u32[]{:S(2)}, u32[]{:S(2)}) collective-permute-start(bf16[4,128,128]{2,1,0:T(8,128)(2,1)S(1)} %pad_maximum_fusion.refs_0_), channel_id=1, source_target_pairs={{0,4},{1,17},{2,6},{3,19},{4,0},{5,21},{6,2},{7,23},{8,12},{9,25},... | collective-permute-start | bytes 393224 | tf_op jit(solution)/shard_map/ppermute | solution.py:63
  52.8 9.8 %collective-permute-start.22 = (bf16[4,128,128]{2,1,0:T(8,128)(2,1)S(1)}, bf16[4,128,128]{2,1,0:T(8,128)(2,1)S(1)}, u32[]{:S(2)}, u32[]{:S(2)}) collective-permute-start(bf16[4,128,128]{2,1,0:T(8,128)(2,1)S(1)} %pad_maximum_fusion.refs_0_), channel_id=1, source_target_pairs={{0,2},{1,9},{2,4},{3,11},{4,6},{5,13},{6,0},{7,15},{8,10},{9,17},{... | collective-permute-start | bytes 393224 | tf_op jit(solution)/shard_map/ppermute | solution.py:63
  54.9 9.1 %collective-permute-start.23 = (bf16[4,128,128]{2,1,0:T(8,128)(2,1)S(1)}, bf16[4,128,128]{2,1,0:T(8,128)(2,1)S(1)}, u32[]{:S(2)}, u32[]{:S(2)}) collective-permute-start(bf16[4,128,128]{2,1,0:T(8,128)(2,1)S(1)} %pad_maximum_fusion.refs_0_), channel_id=1, source_target_pairs={{0,6},{1,25},{2,0},{3,27},{4,2},{5,29},{6,4},{7,31},{8,14},{9,1},{... | collective-permute-start | bytes 393224 | tf_op jit(solution)/shard_map/ppermute | solution.py:63
  55.5 8.5 %collective-permute-start.20 = (bf16[4,128,128]{2,1,0:T(8,128)(2,1)S(1)}, bf16[4,128,128]{2,1,0:T(8,128)(2,1)S(1)}, u32[]{:S(2)}, u32[]{:S(2)}) collective-permute-start(bf16[4,128,128]{2,1,0:T(8,128)(2,1)S(1)} %pad_maximum_fusion.refs_0_), channel_id=1, source_target_pairs={{0,1},{1,0},{2,3},{3,2},{4,5},{5,4},{6,7},{7,6},{8,9},{9,8},{10,11... | collective-permute-start | bytes 393224 | tf_op jit(solution)/shard_map/ppermute | solution.py:67
  60.5 3.8 %collective-permute-start.24 = (bf16[4,128,128]{2,1,0:T(8,128)(2,1)S(1)}, bf16[4,128,128]{2,1,0:T(8,128)(2,1)S(1)}, u32[]{:S(2)}, u32[]{:S(2)}) collective-permute-start(bf16[4,128,128]{2,1,0:T(8,128)(2,1)S(1)} %collective-permute-done.21.refs_2_), channel_id=1, source_target_pairs={{0,1},{1,0},{2,3},{3,2},{4,5},{5,4},{6,7},{7,6},{8,9},{9,8},{10,11... | collective-permute-start | bytes 393224 | tf_op jit(solution)/shard_map/ppermute | solution.py:67
  62.6 2.3 %collective-permute-start.25 = (bf16[4,128,128]{2,1,0:T(8,128)(2,1)S(1)}, bf16[4,128,128]{2,1,0:T(8,128)(2,1)S(1)}, u32[]{:S(2)}, u32[]{:S(2)}) collective-permute-start(bf16[4,128,128]{2,1,0:T(8,128)(2,1)S(1)} %collective-permute-done.22.refs_3_), channel_id=1, source_target_pairs={{0,1},{1,0},{2,3},{3,2},{4,5},{5,4},{6,7},{7,6},{8,9},{9,8},{10,11... | collective-permute-start | bytes 393224 | tf_op jit(solution)/shard_map/ppermute | solution.py:67
  64.0 1.3 %collective-permute-start.26 = (bf16[4,128,128]{2,1,0:T(8,128)(2,1)S(1)}, bf16[4,128,128]{2,1,0:T(8,128)(2,1)S(1)}, u32[]{:S(2)}, u32[]{:S(2)}) collective-permute-start(bf16[4,128,128]{2,1,0:T(8,128)(2,1)S(1)} %collective-permute-done.23.refs_4_), channel_id=1, source_target_pairs={{0,1},{1,0},{2,3},{3,2},{4,5},{5,4},{6,7},{7,6},{8,9},{9,8},{10,11... | collective-permute-start | bytes 393224 | tf_op jit(solution)/shard_map/ppermute | solution.py:67
  64.3 6.3 %copy-start.1 = (f32[153]{0:T(256)S(1)}, f32[153]{0:T(256)}, u32[]{:S(2)}) copy-start(f32[153]{0:T(256)} %param.13) | copy-start | bytes 1840
  66.6 6.3 %collective-permute-start.27 = (bf16[160,384]{1,0:T(8,128)(2,1)S(1)}, bf16[160,384]{1,0:T(8,128)(2,1)S(1)}, u32[]{:S(2)}, u32[]{:S(2)}) collective-permute-start(bf16[160,384]{1,0:T(8,128)(2,1)S(1)} %get-tuple-element.42.p0), channel_id=1, source_target_pairs={{0,64},{32,96},{64,0},{96,32},{1,65},{33,97},{65,1},{97,33},{2,66}... | collective-permute-start | bytes 368648 | tf_op jit(solution)/shard_map/ppermute | solution.py:71
  67.9 8.2 %collective-permute-start.28 = (bf16[160,384]{1,0:T(8,128)(2,1)S(1)}, bf16[160,384]{1,0:T(8,128)(2,1)S(1)}, u32[]{:S(2)}, u32[]{:S(2)}) collective-permute-start(bf16[160,384]{1,0:T(8,128)(2,1)S(1)} %get-tuple-element.42.p0), channel_id=1, source_target_pairs={{0,32},{32,64},{64,96},{96,0},{1,33},{33,65},{65,97},{97,1},{2,34}... | collective-permute-start | bytes 368648 | tf_op jit(solution)/shard_map/ppermute | solution.py:71
  69.5 6.5 %collective-permute-start.29 = (bf16[160,384]{1,0:T(8,128)(2,1)S(1)}, bf16[160,384]{1,0:T(8,128)(2,1)S(1)}, u32[]{:S(2)}, u32[]{:S(2)}) collective-permute-start(bf16[160,384]{1,0:T(8,128)(2,1)S(1)} %get-tuple-element.42.p0), channel_id=1, source_target_pairs={{0,96},{32,0},{64,32},{96,64},{1,97},{33,1},{65,33},{97,65},{2,98}... | collective-permute-start | bytes 368648 | tf_op jit(solution)/shard_map/ppermute | solution.py:71
